TPU v7x, 256 devices: a whole 4x4x8 slice. The times are simulated.
256 devices in a mesh: dp: 16 (over x, z_lo, core), ctx: 16 (over y, z_hi).
Axes of the slice: x: 4, y: 4, z: 8 (z_hi: 4, z_lo: 2; z = z_hi * 2 + z_lo), core: 2. Of those that a mesh axis runs over, the one named last changes fastest.
Arguments:
- tokens: bfloat16 [16, 16, 2, 96, 1024], P('dp', 'ctx'), may hold values from -48 to 48
- sweep_tiles: int32 [16, 4], P('dp'), may hold values from 1 to 16, 32 in all within a row
- weights: bfloat16 [4, 1024, 512], replicated
- cotangent: bfloat16 [16, 16, 2, 96, 1024], P('dp', 'ctx'), may hold values from -6 to 6
Outputs:
- attn_out: bfloat16 [16, 16, 2, 96, 1024], P('dp', 'ctx')
- input_grad: bfloat16 [16, 16, 2, 96, 1024], P('dp', 'ctx')
- weight_grads: bfloat16 [4, 1024, 512], P(None, 'ctx')
Inputs may be any that keep to these rules, and one draw needn't show every extreme that they name: `sweep_tiles`: each row sums to 32 tiles and its largest entry is exactly 16.
All inputs are finite; a program needn't handle non-finite values.
Results may differ from a plain program's by a relative error of at most 0.035.
The roundings to bfloat16 on the way count: a program that leaves them out, or rounds other values in their place, can miss the bound.
Values may be sent and summed in bfloat16 or wider, within the bound.
No kernel may reach another device: no remote copies, remote signals or barrier semaphores. Data moves between devices by JAX's collectives and lax.ppermute only.
A program may use at most 64 MiB of HBM per device.

v0:
```python
import math

import jax
import jax.numpy as jnp
from jax import lax
from jax.sharding import PartitionSpec as P

D = 1024
HEADS = 8
HEAD = 64


NEGATIVE = -1e30


def token_positions(storage, span_len, ranks):
    owner = storage // (2 * span_len)
    second = storage // span_len % 2
    within = storage % span_len
    segment = jnp.where(second == 0, owner, 2 * ranks - 1 - owner)
    return segment * span_len + within


def sweep_numbers(places, bounds):
    return jnp.sum((places[:, None] >= bounds[None, :]).astype(jnp.int32), axis=1)


def block_scores(query_heads, key_block):
    key_heads = key_block.reshape(key_block.shape[0], HEADS, HEAD)
    return jnp.einsum(
        "qhe,khe->hqk", query_heads, key_heads, preferred_element_type=jnp.float32
    ) * HEAD ** (-0.5)


def per_device(tokens, sweep_tiles, weights, cotangent):
    ranks = lax.axis_size("ctx")
    groups = lax.axis_size("dp")
    rank_now = lax.axis_index("ctx")
    span_len = tokens.shape[3]
    local_rows = 2 * span_len
    total_rows = ranks * local_rows
    hidden_width = HEADS * HEAD
    inputs = tokens.reshape(local_rows, D)
    upstream = cotangent.reshape(local_rows, D)
    bounds = jnp.cumsum(sweep_tiles.reshape(-1)) * span_len
    query_place = token_positions(
        rank_now * local_rows + jnp.arange(local_rows, dtype=jnp.int32), span_len, ranks
    )
    query_sweep = sweep_numbers(query_place, bounds)
    w_query, w_key, w_value, w_output = (weights[0], weights[1], weights[2], weights[3])
    queries = jnp.dot(inputs, w_query, preferred_element_type=jnp.float32).astype(jnp.bfloat16)
    keys_local = jnp.dot(inputs, w_key, preferred_element_type=jnp.float32).astype(jnp.bfloat16)
    values_local = jnp.dot(inputs, w_value, preferred_element_type=jnp.float32).astype(jnp.bfloat16)
    query_heads = queries.reshape(local_rows, HEADS, HEAD)

    def block_allowed(offset, width):
        key_place = token_positions(offset + jnp.arange(width, dtype=jnp.int32), span_len, ranks)
        key_sweep = sweep_numbers(key_place, bounds)
        return (query_sweep[:, None] == key_sweep[None, :]) & (
            key_place[None, :] <= query_place[:, None]
        )

    start_state = (
        jnp.full((HEADS, local_rows), NEGATIVE, jnp.float32),
        jnp.zeros((HEADS, local_rows), jnp.float32),
        jnp.zeros((local_rows, HEADS, HEAD), jnp.float32),
    )
    key_piece = lax.all_gather(keys_local, "ctx", axis=0, tiled=True)
    value_piece = lax.all_gather(values_local, "ctx", axis=0, tiled=True)
    count = key_piece.shape[0]
    attend_width = math.gcd(count, 512)
    blocks = count // attend_width
    key_blocks = key_piece.reshape(blocks, attend_width, hidden_width)
    value_blocks = value_piece.reshape(blocks, attend_width, hidden_width)
    offsets = jnp.arange(blocks, dtype=jnp.int32) * attend_width

    def one_block(state_in, block_items):
        key_block, value_block, offset = block_items
        allowed = block_allowed(offset, attend_width)
        run_max, run_sum, run_accum = state_in
        scores = jnp.where(allowed[None], block_scores(query_heads, key_block), NEGATIVE)
        new_max = jnp.maximum(run_max, jnp.max(scores, axis=-1))
        factor = jnp.exp(run_max - new_max)
        expo = jnp.where(allowed[None], jnp.exp(scores - new_max[..., None]), 0.0)
        new_sum = run_sum * factor + jnp.sum(expo, axis=-1)
        value_heads = value_block.reshape(attend_width, HEADS, HEAD)
        update = jnp.einsum(
            "hqk,khe->qhe",
            expo.astype(jnp.bfloat16),
            value_heads,
            preferred_element_type=jnp.float32,
        )
        state_out = (new_max, new_sum, run_accum * factor.T[:, :, None] + update)
        return (state_out, None)

    state_end, unused = lax.scan(one_block, start_state, (key_blocks, value_blocks, offsets))
    run_max, run_sum, run_accum = state_end
    context = (
        (run_accum / run_sum.T[:, :, None]).astype(jnp.bfloat16).reshape(local_rows, hidden_width)
    )
    log_total = run_max + jnp.log(run_sum)
    attn_out = jnp.dot(context, w_output.T, preferred_element_type=jnp.float32).astype(jnp.bfloat16)
    keys_all, values_all = (
        lax.all_gather(keys_local, "ctx", axis=0, tiled=True),
        lax.all_gather(values_local, "ctx", axis=0, tiled=True),
    )
    context_grad = jnp.dot(upstream, w_output, preferred_element_type=jnp.float32).astype(
        jnp.bfloat16
    )
    grad_heads = context_grad.reshape(local_rows, HEADS, HEAD)
    context_heads = context.reshape(local_rows, HEADS, HEAD)
    delta = jnp.einsum(
        "qhe,qhe->hq", grad_heads.astype(jnp.float32), context_heads.astype(jnp.float32)
    )
    width = math.gcd(total_rows, 512)
    blocks = total_rows // width
    key_blocks = keys_all.reshape(blocks, width, hidden_width)
    value_blocks = values_all.reshape(blocks, width, hidden_width)
    offsets = jnp.arange(blocks, dtype=jnp.int32) * width

    def backward_block(grad_in, block_items):
        key_block, value_block, offset = block_items
        allowed = block_allowed(offset, width)
        scores = block_scores(query_heads, key_block)
        probs = jnp.where(allowed[None], jnp.exp(scores - log_total[..., None]), 0.0)
        probs_low = probs.astype(jnp.bfloat16)
        value_heads = value_block.reshape(width, HEADS, HEAD)
        key_heads = key_block.reshape(width, HEADS, HEAD)
        prob_grad = jnp.einsum(
            "qhe,khe->hqk", grad_heads, value_heads, preferred_element_type=jnp.float32
        )
        score_grad = (probs * (prob_grad - delta[..., None]) * HEAD ** (-0.5)).astype(jnp.bfloat16)
        grad_new = grad_in + jnp.einsum(
            "hqk,khe->qhe", score_grad, key_heads, preferred_element_type=jnp.float32
        )
        key_term = jnp.einsum(
            "hqk,qhe->khe", score_grad, query_heads, preferred_element_type=jnp.float32
        )
        value_term = jnp.einsum(
            "hqk,qhe->khe", probs_low, grad_heads, preferred_element_type=jnp.float32
        )
        stacked = jnp.stack(
            [key_term.reshape(width, hidden_width), value_term.reshape(width, hidden_width)], axis=1
        )
        return (grad_new, stacked)

    query_accum, pair_terms = lax.scan(
        backward_block,
        jnp.zeros((local_rows, HEADS, HEAD), jnp.float32),
        (key_blocks, value_blocks, offsets),
    )
    pair_terms = pair_terms.reshape(total_rows, 2, hidden_width)
    own_terms = lax.psum_scatter(
        pair_terms.astype(jnp.bfloat16), "ctx", scatter_dimension=0, tiled=True
    ).astype(jnp.float32)
    key_grad = own_terms[:, 0].astype(jnp.bfloat16)
    value_grad = own_terms[:, 1].astype(jnp.bfloat16)
    query_grad = query_accum.astype(jnp.bfloat16).reshape(local_rows, hidden_width)
    input_grad = jnp.dot(query_grad, w_query.T, preferred_element_type=jnp.float32)
    input_grad = input_grad + jnp.dot(key_grad, w_key.T, preferred_element_type=jnp.float32)
    input_grad = input_grad + jnp.dot(value_grad, w_value.T, preferred_element_type=jnp.float32)
    input_grad = input_grad.astype(jnp.bfloat16)
    factor = float(groups * total_rows) ** (-0.5)
    grad_terms = jnp.stack(
        [
            jnp.dot(inputs.T, query_grad, preferred_element_type=jnp.float32),
            jnp.dot(inputs.T, key_grad, preferred_element_type=jnp.float32),
            jnp.dot(inputs.T, value_grad, preferred_element_type=jnp.float32),
            jnp.dot(upstream.T, context, preferred_element_type=jnp.float32),
        ]
    )
    summed = lax.psum(grad_terms.astype(jnp.bfloat16), "dp")
    own_rows = lax.psum_scatter(summed, "ctx", scatter_dimension=1, tiled=True).astype(jnp.float32)
    weight_grads = (own_rows * factor).astype(jnp.bfloat16)
    return (attn_out.reshape(tokens.shape), input_grad.reshape(tokens.shape), weight_grads)


def solution(mesh):
    placed = (
        P("dp", "ctx", None, None, None),
        P("dp", None),
        P(),
        P("dp", "ctx", None, None, None),
    )
    return jax.shard_map(
        per_device,
        mesh=mesh,
        in_specs=placed,
        out_specs=(
            P("dp", "ctx", None, None, None),
            P("dp", "ctx", None, None, None),
            P(None, "ctx", None),
        ),
        check_vma=False,
    )
```

profile of v0, /device:TPU:1, one launch (start us, length us, event | category | flops | bytes accessed | tf_op | source)
XLA Modules:
  0.0 772.1 jit_solution(2769489773628216215)
XLA Ops:
  8.2 2.3 convolution_convert_fusion.8
  10.5 2.3 convolution_convert_fusion.6
  12.9 1.6 convolution_convert_fusion.5
  15.6 1.6 convolution_convert_fusion.7
  20.4 62.1 %all-gather.3.cloned.1.call-done = bf16[3072,512]{1,0:T(8,128)(2,1)} async-done(((bf16[192,512]{1,0:T(8,128)(2,1)}), bf16[3072,512]{1,0:T(8,128)(2,1)}) %all-gather.3.cloned.1.call-update) | async-done | bytes 3145744 | tf_op jit(solution)/shard_map/all_gather | solution.py:68
  82.5 4.7 copy.33
  87.2 63.5 %all-gather.5.cloned.1.call-done = bf16[3072,512]{1,0:T(8,128)(2,1)} async-done(((bf16[192,512]{1,0:T(8,128)(2,1)}), bf16[3072,512]{1,0:T(8,128)(2,1)}) %all-gather.5.cloned.1.call-update) | async-done | bytes 3145744 | tf_op jit(solution)/shard_map/all_gather | solution.py:69
  150.8 4.7 copy.34
  155.5 67.7 %while.34 = (s32[]{:T(128)}, f32[8,192]{1,0:T(8,128)S(1)}, f32[8,192]{1,0:T(8,128)}, f32[192,8,64]{0,2,1:T(8,128)}, s32[192]{0:T(256)}, /*index=5*/s32[6]{0:T(12...) while((s32[]{:T(128)}, f32[8,192]{1,0:T(8,128)S(1)}, ...), condition=%wide.region_6.7_spmd.clone, body=%wide.region_2.6_spmd.clone.sunk | while | flops 212179520 | bytes 20148860 | solution.py:96
  158.9 2.1 constant_dynamic-slice_fusion.7
  161.0 1.7 fusion.138
  162.9 2.0 fusion.140
  170.2 2.1 constant_dynamic-slice_fusion.7
  172.3 1.7 fusion.138
  174.1 2.0 fusion.140
  181.5 2.1 constant_dynamic-slice_fusion.7
  183.6 1.7 fusion.138
  185.4 2.0 fusion.140
  192.8 2.1 constant_dynamic-slice_fusion.7
  194.9 1.7 fusion.138
  196.7 2.0 fusion.140
  204.0 2.1 constant_dynamic-slice_fusion.7
  206.2 1.7 fusion.138
  208.0 2.0 fusion.140
  215.3 2.1 constant_dynamic-slice_fusion.7
  217.4 1.7 fusion.138
  219.3 2.0 fusion.140
  223.9 1.9 fusion.75
  225.8 79.8 %while.35 = (s32[]{:T(128)}, f32[192,8,64]{0,2,1:T(8,128)}, bf16[6,512,2,512]{3,1,0,2:T(8,128)(2,1)}, bf16[6,512,512]{1,2,0:T(8,128)(2,1)}, s32[192]{0:T(256)}, ...) while((s32[]{:T(128)}, f32[192,8,64]{0,2,1:T(8,128)}, ...), condition=%wide.region_9.10_spmd.clone, body=%wide.region_7.9_spmd.clone.sunk | while | flops 513013312 | bytes 56949360 | solution.py:147
  227.1 1.6 fusion.153
  228.7 1.5 dynamic_slice.61
  240.4 1.6 fusion.153
  241.9 1.5 dynamic_slice.61
  253.6 1.6 fusion.153
  255.2 1.5 dynamic_slice.61
  267.0 1.6 fusion.153
  280.3 1.6 fusion.153
  293.6 1.6 fusion.153
  307.6 104.0 %reduce-scatter.2.cloned.1.call-done = bf16[192,2,512]{2,0,1:T(8,128)(2,1)} async-done(((bf16[3072,2,512]{2,0,1:T(8,128)(2,1)}), bf16[192,2,512]{2,0,1:T(8,128)(2,1)}) %reduce-scatter.2.cloned.1.call-update) | async-done | bytes 393232 | tf_op jit(solution)/shard_map/reduce_scatter | solution.py:153
  414.5 2.2 pad_maximum_fusion
  416.7 7.8 %copy.39 = bf16[4,1024,512]{2,0,1:T(4,128)(2,1)} copy(bf16[4,1024,512]{1,2,0:T(8,128)(2,1)} %pad_maximum_fusion) | data formatting | bytes 8388608 | tf_op jit(solution)/shard_map/stack | solution.py:164
  426.5 2.5 convolution_convert_fusion.4
  428.9 1.7 fusion.62
  430.7 1.7 convolution_add_fusion.1
  432.4 203.4 %all-reduce.6.cloned.1.call-done = bf16[4,1024,512]{2,0,1:T(4,128)(2,1)} async-done(((bf16[4,1024,512]{2,0,1:T(4,128)(2,1)}), bf16[4,1024,512]{2,0,1:T(4,128)(2,1)}) %all-reduce.6.cloned.1.call-update) | async-done | bytes 4194320
  635.8 1.7 constant_dynamic-slice_fusion.4
  637.6 2.5 fusion.57
  640.0 123.7 %all-reduce.4.cloned.1.call-done = bf16[4,64,512]{2,0,1:T(4,128)(2,1)} async-done(((bf16[4,64,512]{2,0,1:T(4,128)(2,1)}), bf16[4,64,512]{2,0,1:T(4,128)(2,1)}) %all-reduce.4.cloned.1.call-update) | async-done | bytes 262160 | tf_op jit(solution)/shard_map/psum | solution.py:172
  (332 shorter events, 110.6 us)
Async XLA Ops:
  7.2 5.8 copy-start.17
  7.2 75.3 %all-gather.3.cloned.1.call-start = ((), (), s32[]{:S(2)}) async-start(), calls=%async_computation.1 | async-start | bytes 3342336 | tf_op jit(solution)/shard_map/all_gather | solution.py:68
  8.2 7.2 copy-start.19
  10.5 140.3 %all-gather.5.cloned.1.call-start = ((), (), s32[]{:S(2)}) async-start(), calls=%async_computation.2 | async-start | bytes 3342336 | tf_op jit(solution)/shard_map/all_gather | solution.py:69
  12.8 398.8 %reduce-scatter.2.cloned.1.call-start = ((), (), s32[]{:S(2)}) async-start(), calls=%async_computation.3 | async-start | bytes 6684672 | tf_op jit(solution)/shard_map/reduce_scatter | solution.py:153
  158.9 3.9 copy-start.4
  162.8 2.1 copy-start.5
  170.2 3.9 copy-start.4
  174.1 2.1 copy-start.5
  181.5 3.9 copy-start.4
  185.4 2.1 copy-start.5
  192.7 3.9 copy-start.4
  196.7 2.1 copy-start.5
  204.0 3.9 copy-start.4
  215.3 3.9 copy-start.4
  225.8 6.6 copy-start.11
  228.7 5.3 copy-start.1
  234.0 2.1 copy-start.2
  234.0 2.9 copy-start.3
  234.6 2.7 copy-start.7
  239.0 6.6 copy-start.11
  241.9 5.3 copy-start.1
  247.2 2.1 copy-start.2
  247.2 2.9 copy-start.3
  247.9 2.7 copy-start.7
  252.3 6.6 copy-start.11
  255.2 5.3 copy-start.1
  260.5 2.1 copy-start.2
  260.5 2.9 copy-start.3
  261.2 2.7 copy-start.7
  265.6 6.6 copy-start.11
  268.5 5.3 copy-start.1
  273.8 2.1 copy-start.2
  273.9 2.9 copy-start.3
  274.5 2.7 copy-start.7
  278.9 6.6 copy-start.11
  281.8 5.3 copy-start.1
  287.1 2.1 copy-start.2
  287.1 2.9 copy-start.3
  287.8 2.7 copy-start.7
  292.2 6.6 copy-start.11
  295.1 5.3 copy-start.1
  300.4 2.1 copy-start.2
  300.5 2.9 copy-start.3
  301.1 2.7 copy-start.7
  305.6 330.2 %all-reduce.6.cloned.1.call-start = ((), (), s32[]{:S(2)}) async-start(), calls=%async_computation.5 | async-start | bytes 8388608
  424.5 6.1 copy-start.10
  424.6 339.2 %all-reduce.4.cloned.1.call-start = ((), (), s32[]{:S(2)}) async-start(), calls=%async_computation.4 | async-start | bytes 524288 | tf_op jit(solution)/shard_map/psum | solution.py:172
  (43 other events, 66.6 us)
Sparse Core Ops, SparseCore 0:
  11.1 71.4 all-gather.2
  85.0 65.7 all-gather.4
  305.7 105.9 reduce-scatter.1
  424.7 211.0 all-reduce.5
  638.8 124.8 all-reduce.3
where the time goes:
time: 774 us; the launch traced here: 772 us
  waiting for transfers between devices  557 us (72%)
  local copies, waits for them, and re-layouts  85 us (11%)
  matrix products  66.3 us (9%)
  other arithmetic  47.4 us (6%)
  between operations  14.6 us (2%)
    unnamed x6, waiting for transfers between devices  203 us
    psum x1, waiting for transfers between devices, per_device(): summed = lax.psum(grad_terms.astype(jnp.bfloat16), 'dp')  124 us
    reduce_scatter x1, waiting for transfers between devices, per_device(): lax.psum_scatter(pair_terms.astype(jnp.bfloat16), 'ctx', scatter_dimensio...  104 us
    all_gather x1, waiting for transfers between devices, per_device(): value_piece = lax.all_gather(values_local, 'ctx', axis=0, tiled=True)  63.5 us
    all_gather x1, waiting for transfers between devices, per_device(): key_piece = lax.all_gather(keys_local, 'ctx', axis=0, tiled=True)  62.1 us
    dynamic_slice x24, local copies, waits for them, and re-layouts, per_device(): lax.scan(one_block, start_state, (key_blocks, value_blocks, offsets))  37.1 us
    dot_general x12, matrix products, block_scores(): jnp.einsum('qhe,khe->hqk', query_heads, key_heads, preferred_element_type...  19.9 us
  transfers between devices with their start and end apart: 5, of which 5 were waited for; matrix products, arithmetic and copies ran while one was open for 3% of the time, Pallas kernels for 0%

commit v1 on v0

v1 whole, which is shorter than its diff:
```python
import functools

import jax
import jax.numpy as jnp
from jax import lax
from jax.experimental import pallas as pl
from jax.experimental.pallas import tpu as pltpu
from jax.sharding import PartitionSpec as P

D = 1024
HEADS = 8
HEAD = 64
HQ = HEADS * HEAD
SPAN = 96
RANKS = 16
TILES = 2 * RANKS
CHUNK = 256
KEY_ROWS = TILES * SPAN + CHUNK
NEGATIVE = -1e30
VMEM_LIMIT = 48 * 1024 * 1024

CORE_PAIRS = [[2 * i, 2 * i + 1] for i in range(8)]
CORE_SWAP = [(i, i ^ 1) for i in range(16)]
SAME_CORE = [[core + 2 * i for i in range(8)] for core in range(2)]
Y_LINES = [[z + 4 * y for y in range(4)] for z in range(4)]
Z_LINES = [[4 * y + z for z in range(4)] for y in range(4)]


def low_lanes(rows):
    return lax.broadcasted_iota(jnp.int32, (rows, 128), 1) < HEAD


def project_kernel(block_ref, tokens_ref, upstream_ref, weights_ref, out_ref):
    inputs = tokens_ref[...].reshape(2 * SPAN, D)
    upstream = upstream_ref[...].reshape(2 * SPAN, D)

    def product(rows, number):
        return jnp.dot(rows, weights_ref[number], preferred_element_type=jnp.float32)

    queries, keys, values = (product(inputs, number) for number in range(3))
    grads = product(upstream, 3)
    low = low_lanes(2 * SPAN)
    for half, (first, second) in enumerate(((queries, grads), (keys, values))):
        for pair in range(2):
            one = first[:, 128 * pair : 128 * pair + 128]
            two = second[:, 128 * pair : 128 * pair + 128]
            even = jnp.where(low, one, pltpu.roll(two, HEAD, 1)).astype(jnp.bfloat16)
            odd = jnp.where(low, pltpu.roll(one, HEAD, 1), two).astype(jnp.bfloat16)
            for sequence in range(2):
                rows = slice(SPAN * sequence, SPAN * sequence + SPAN)
                place = slice(SPAN * half, SPAN * half + SPAN)
                out_ref[sequence, 2 * pair, place, :] = even[rows]
                out_ref[sequence, 2 * pair + 1, place, :] = odd[rows]


def project(block, tokens_pair, upstream_pair, weights):
    tokens_spec = pl.BlockSpec((2, 1, SPAN, D), lambda j, block: (0, block[0], 0, 0))
    return pl.pallas_call(
        project_kernel,
        out_shape=jax.ShapeDtypeStruct((2, HEADS, 2 * SPAN, 128), jnp.bfloat16),
        grid_spec=pltpu.PrefetchScalarGridSpec(
            num_scalar_prefetch=1,
            grid=(2,),
            in_specs=[
                tokens_spec,
                tokens_spec,
                pl.BlockSpec((4, D, HQ // 2), lambda j, block: (0, 0, j)),
            ],
            out_specs=pl.BlockSpec((2, HEADS // 2, 2 * SPAN, 128), lambda j, block: (0, j, 0, 0)),
        ),
        compiler_params=pltpu.CompilerParams(vmem_limit_bytes=VMEM_LIMIT),
        name="project",
    )(block, tokens_pair, upstream_pair, weights)


def attend_kernel(
    core_ref, tiles_ref, own_ref, other_ref, out_ref, own_grad_ref, other_grad_ref,
    key_ref, grad_ref, score_ref, prob_grad_ref,
):
    core = core_ref[0]
    first = tiles_ref[0]
    second = first + tiles_ref[1]
    third = second + tiles_ref[2]
    grad_ref[...] = jnp.zeros_like(grad_ref)
    key_ref[TILES * SPAN :, :] = jnp.zeros((CHUNK, 128), jnp.bfloat16)

    def own_tile(rank):
        return jnp.where(rank % 2 == core, rank, TILES - 1 - rank)

    def tile_rows(tile):
        return pl.ds(pl.multiple_of(tile * SPAN, SPAN), SPAN)

    for rank in range(RANKS):
        tile = own_tile(rank)
        key_ref[tile_rows(tile), :] = own_ref[rank, SPAN:, :]
        key_ref[tile_rows(TILES - 1 - tile), :] = other_ref[rank]

    low = low_lanes(SPAN)
    scale = HEAD ** -0.5

    def attend(rank, tile, start, chunks):
        base = pl.multiple_of(start * SPAN, SPAN)
        packed = own_ref[rank, :SPAN, :]
        query_only = jnp.where(low, packed, jnp.zeros_like(packed))
        grad_only = jnp.where(low, jnp.zeros_like(packed), packed)
        left = jnp.concatenate([query_only, grad_only], axis=0)
        right = jnp.concatenate([grad_only, query_only], axis=0)

        def rows(j):
            return pl.ds(pl.multiple_of(base + CHUNK * j, 32), CHUNK)

        top = jnp.full((SPAN, 1), NEGATIVE, jnp.float32)
        for j in range(chunks):
            both = lax.dot_general(
                left, key_ref[rows(j), :], (((1,), (1,)), ((), ())),
                preferred_element_type=jnp.float32,
            )
            scores = both[:SPAN] * scale
            if j >= chunks - 2:
                gap = (tile - start) * SPAN - CHUNK * j
                ahead = lax.broadcasted_iota(jnp.int32, (SPAN, CHUNK), 1) - lax.broadcasted_iota(
                    jnp.int32, (SPAN, CHUNK), 0
                )
                scores = jnp.where(ahead <= gap, scores, NEGATIVE)
            place = slice(CHUNK * j, CHUNK * j + CHUNK)
            score_ref[:, place] = scores
            prob_grad_ref[:, place] = both[SPAN:]
            top = jnp.maximum(top, jnp.max(scores, axis=1, keepdims=True))
        total = jnp.zeros((SPAN, 1), jnp.float32)
        accum = jnp.zeros((SPAN, 128), jnp.float32)
        for j in range(chunks):
            place = slice(CHUNK * j, CHUNK * j + CHUNK)
            expo = jnp.exp(score_ref[:, place] - top)
            score_ref[:, place] = expo
            total = total + jnp.sum(expo, axis=1, keepdims=True)
            accum = accum + jnp.dot(
                expo.astype(jnp.bfloat16), key_ref[rows(j), :], preferred_element_type=jnp.float32
            )
        inverse = 1.0 / total
        context = (accum / total).astype(jnp.bfloat16)
        delta = jnp.sum(
            grad_only.astype(jnp.float32) * context.astype(jnp.float32), axis=1, keepdims=True
        )
        query_grad = jnp.zeros((SPAN, 128), jnp.float32)
        for j in range(chunks):
            place = slice(CHUNK * j, CHUNK * j + CHUNK)
            probs = score_ref[:, place] * inverse
            score_grad = (probs * (prob_grad_ref[:, place] - delta) * scale).astype(jnp.bfloat16)
            query_grad = query_grad + jnp.dot(
                score_grad, key_ref[rows(j), :], preferred_element_type=jnp.float32
            )
            stacked = jnp.concatenate([probs.astype(jnp.bfloat16), score_grad], axis=0)
            grad_ref[rows(j), :] += lax.dot_general(
                stacked, right, (((0,), (0,)), ((), ())), preferred_element_type=jnp.float32
            )
        out_ref[rank] = jnp.where(low, query_grad, context.astype(jnp.float32)).astype(jnp.bfloat16)

    def one_tile(rank, carry):
        tile = own_tile(rank)
        start = jnp.where(
            tile >= third, third, jnp.where(tile >= second, second, jnp.where(tile >= first, first, 0))
        )
        chunks = ((tile - start + 1) * SPAN + CHUNK - 1) // CHUNK
        for count in range(1, 7):
            @pl.when(chunks == count)
            def _():
                attend(rank, tile, start, count)
        return carry

    lax.fori_loop(0, RANKS, one_tile, 0)
    for rank in range(RANKS):
        tile = own_tile(rank)
        own_grad_ref[rank] = grad_ref[tile_rows(tile), :]
        other_grad_ref[rank] = grad_ref[tile_rows(TILES - 1 - tile), :].astype(jnp.bfloat16)


def attend(core, tiles, own, other):
    smem = pl.BlockSpec(memory_space=pltpu.SMEM)
    vmem = pl.BlockSpec(memory_space=pltpu.VMEM)
    block = (RANKS, SPAN, 128)
    return pl.pallas_call(
        attend_kernel,
        out_shape=(
            jax.ShapeDtypeStruct(block, jnp.bfloat16),
            jax.ShapeDtypeStruct(block, jnp.float32),
            jax.ShapeDtypeStruct(block, jnp.bfloat16),
        ),
        in_specs=[smem, smem, vmem, vmem],
        out_specs=(vmem, vmem, vmem),
        scratch_shapes=[
            pltpu.VMEM((KEY_ROWS, 128), jnp.bfloat16),
            pltpu.VMEM((KEY_ROWS, 128), jnp.float32),
            pltpu.VMEM((SPAN, 6 * CHUNK), jnp.float32),
            pltpu.VMEM((SPAN, 6 * CHUNK), jnp.float32),
        ],
        compiler_params=pltpu.CompilerParams(vmem_limit_bytes=VMEM_LIMIT),
        name="attend",
    )(core, tiles, own, other)


def weight_kernel(place_ref, grads_ref, tokens_ref, upstream_ref, out_ref, held_ref):
    core, odd = place_ref[0], place_ref[1]
    number, step = pl.program_id(0), pl.program_id(1)

    @pl.when(step == 0)
    def _():
        low = low_lanes(SPAN)
        for sequence in range(2):
            for block in range(2):
                holder = jnp.bitwise_xor(odd, block)
                first = (2 * sequence + block) * SPAN
                rows = pl.ds(pl.multiple_of(number * SPAN, SPAN), SPAN)
                for pair in range(HEADS // 2):
                    one = grads_ref[holder, sequence, 2 * pair, rows, :].astype(jnp.float32)
                    two = grads_ref[holder, sequence, 2 * pair + 1, rows, :].astype(jnp.float32)
                    lower = jnp.where(low, one, pltpu.roll(two, HEAD, 1))
                    upper = jnp.where(low, pltpu.roll(one, HEAD, 1), two)
                    held_ref[first : first + SPAN, 128 * pair : 128 * pair + 128] = jnp.where(
                        core == 0, lower, upper
                    ).astype(jnp.bfloat16)

    use_upstream = jnp.logical_and(core == 1, number == 0)
    left = jnp.where(use_upstream, upstream_ref[...], tokens_ref[...]).reshape(4 * SPAN, D // 4)
    result = lax.dot_general(
        left, held_ref[...], (((0,), (0,)), ((), ())), preferred_element_type=jnp.float32
    ).astype(jnp.bfloat16)
    for rank in range(4):
        for part in range(4):
            row = 64 * rank + 16 * part
            out_ref[part, rank] = result[row : row + 16]


def weight_terms(place, grads, tokens_pair, upstream_pair):
    tokens_spec = pl.BlockSpec((2, 2, SPAN, D // 4), lambda w, j, place: (0, 0, 0, j))
    return pl.pallas_call(
        weight_kernel,
        out_shape=jax.ShapeDtypeStruct((8, RANKS, 16, HQ), jnp.bfloat16),
        grid_spec=pltpu.PrefetchScalarGridSpec(
            num_scalar_prefetch=1,
            grid=(2, 4),
            in_specs=[
                pl.BlockSpec((2, 2, HEADS, 2 * SPAN, 128), lambda w, j, place: (0, 0, 0, 0, 0)),
                tokens_spec,
                tokens_spec,
            ],
            out_specs=pl.BlockSpec((4, 4, 16, HQ), lambda w, j, place: (w, j, 0, 0)),
            scratch_shapes=[pltpu.VMEM((4 * SPAN, HQ), jnp.bfloat16)],
        ),
        compiler_params=pltpu.CompilerParams(vmem_limit_bytes=VMEM_LIMIT),
        name="weight_terms",
    )(place, grads, tokens_pair, upstream_pair)


def output_kernel(place_ref, grads_ref, weights_ref, out_ref, input_grad_ref, held_ref):
    core, odd = place_ref[0], place_ref[1]

    @pl.when(pl.program_id(0) == 0)
    def _():
        low = low_lanes(SPAN)
        for block in range(2):
            holder = jnp.bitwise_xor(odd, block)
            rows = slice(SPAN * block, SPAN * block + SPAN)
            for half in range(2):
                place = slice(SPAN * half, SPAN * half + SPAN)
                for pair in range(HEADS // 2):
                    columns = slice(128 * pair, 128 * pair + 128)
                    one = grads_ref[holder, 0, 2 * pair, place, :].astype(jnp.float32)
                    two = grads_ref[holder, 0, 2 * pair + 1, place, :].astype(jnp.float32)
                    held_ref[2 * half, rows, columns] = jnp.where(
                        low, one, pltpu.roll(two, HEAD, 1)
                    ).astype(jnp.bfloat16)
                    held_ref[2 * half + 1, rows, columns] = jnp.where(
                        low, pltpu.roll(one, HEAD, 1), two
                    ).astype(jnp.bfloat16)

    def product(number, weight):
        return lax.dot_general(
            held_ref[number], weights_ref[weight], (((1,), (1,)), ((), ())),
            preferred_element_type=jnp.float32,
        )

    out_ref[...] = product(1, 3).astype(jnp.bfloat16).reshape(2, SPAN, D // 4)
    input_grad = product(0, 0) + product(2, 1) + product(3, 2)
    input_grad_ref[...] = input_grad.astype(jnp.bfloat16).reshape(2, SPAN, D // 4)


def outputs(place, grads, weights):
    shape = jax.ShapeDtypeStruct((2, SPAN, D), jnp.bfloat16)
    out_spec = pl.BlockSpec((2, SPAN, D // 4), lambda j, place: (0, 0, j))
    return pl.pallas_call(
        output_kernel,
        out_shape=(shape, shape),
        grid_spec=pltpu.PrefetchScalarGridSpec(
            num_scalar_prefetch=1,
            grid=(4,),
            in_specs=[
                pl.BlockSpec(
                    (2, 1, HEADS, 2 * SPAN, 128), lambda j, place: (0, place[0], 0, 0, 0)
                ),
                pl.BlockSpec((4, D // 4, HQ), lambda j, place: (0, j, 0)),
            ],
            out_specs=(out_spec, out_spec),
            scratch_shapes=[pltpu.VMEM((4, 2 * SPAN, HQ), jnp.bfloat16)],
        ),
        compiler_params=pltpu.CompilerParams(vmem_limit_bytes=VMEM_LIMIT),
        cost_estimate=pl.CostEstimate(
            flops=8 * 2 * SPAN * D * HQ, bytes_accessed=7 * 1024 * 1024, transcendentals=0
        ),
        name="outputs",
    )(place, grads, weights)


def per_device(tokens, sweep_tiles, weights, cotangent):
    core = lax.axis_index("dp") % 2
    rank = lax.axis_index("ctx")
    odd = rank % 2
    gather_pair = functools.partial(
        lax.all_gather, axis_name="dp", axis_index_groups=CORE_PAIRS, axis=0, tiled=True
    )
    tokens_pair = gather_pair(tokens.reshape(1, 2, SPAN, D))
    upstream_pair = gather_pair(cotangent.reshape(1, 2, SPAN, D))
    other_tiles = lax.ppermute(sweep_tiles, "dp", CORE_SWAP)
    block = jnp.bitwise_xor(core, odd).astype(jnp.int32).reshape(1)
    packed = project(block, tokens_pair, upstream_pair, weights).reshape(RANKS, 2 * SPAN, 128)
    own = lax.all_to_all(packed, "ctx", 0, 0)
    other = lax.ppermute(own[:, SPAN:], "dp", CORE_SWAP)
    tiles = jnp.where(rank // 8 == core, sweep_tiles, other_tiles).reshape(-1)
    query_part, own_grad, other_grad = attend(core.astype(jnp.int32).reshape(1), tiles, own, other)
    arrived = lax.ppermute(other_grad, "dp", CORE_SWAP)
    key_part = (own_grad + arrived.astype(jnp.float32)).astype(jnp.bfloat16)
    back = lax.all_to_all(jnp.concatenate([query_part, key_part], axis=1), "ctx", 0, 0)
    grads = gather_pair(back.reshape(1, 2, HEADS, 2 * SPAN, 128))
    place = jnp.stack([core, odd]).astype(jnp.int32)
    terms = weight_terms(place, grads, tokens_pair, upstream_pair)
    terms = lax.all_to_all(terms, "dp", 0, 0, axis_index_groups=SAME_CORE)
    attn_out, input_grad = outputs(place, grads, weights)

    def summed(parts):
        return jnp.sum(parts.astype(jnp.float32), axis=0)

    terms = summed(terms).astype(jnp.bfloat16).reshape(4, 4, 16, HQ)
    terms = lax.all_to_all(terms, "ctx", 0, 0, axis_index_groups=Y_LINES)
    terms = summed(terms).astype(jnp.bfloat16)
    terms = lax.all_to_all(terms, "ctx", 0, 0, axis_index_groups=Z_LINES)
    factor = float(16 * RANKS * 2 * SPAN) ** -0.5
    rows = (summed(terms) * factor).astype(jnp.bfloat16)
    spread = lax.all_to_all(jnp.broadcast_to(rows, (16, 16, HQ)), "dp", 0, 0)
    spread = spread.reshape(2, 4, 2, 16, HQ).transpose(2, 0, 1, 3, 4).reshape(4, 64, HQ)
    weight_grads = jnp.stack([spread[0], spread[1], spread[3], spread[2]])
    return (attn_out.reshape(tokens.shape), input_grad.reshape(tokens.shape), weight_grads)


def solution(mesh):
    placed = (
        P("dp", "ctx", None, None, None),
        P("dp", None),
        P(),
        P("dp", "ctx", None, None, None),
    )
    return jax.shard_map(
        per_device,
        mesh=mesh,
        in_specs=placed,
        out_specs=(
            P("dp", "ctx", None, None, None),
            P("dp", "ctx", None, None, None),
            P(None, "ctx", None),
        ),
        check_vma=False,
    )
```

time: 774 us -> 196 us (0.25)
  waiting for transfers between devices: 557 us -> 15.9 us
  blocking collectives: 0 us -> 119 us
  local copies, waits for them, and re-layouts: 85 us -> 4.4 us
  matrix products: 66.3 us -> 0 us
  other arithmetic: 47.4 us -> 3.11 us
  Pallas kernels: 0 us -> 27 us
  starting transfers between devices: 0.21 us -> 11.3 us
    unnamed x6 -> x1, waiting for transfers between devices: 203 us -> 0.02 us
    psum x1 -> x0, waiting for transfers between devices: 124 us -> none  [per_device(): summed = lax.psum(grad_terms.astype(jnp.bfloat16), 'dp')]
    all_gather x2 -> x1, waiting for transfers between devices: 126 us -> 12 us  [per_device(): grads = gather_pair(back.reshape(1, 2, HEADS, 2 * SPAN, 128))]
    all_to_all x0 -> x5, blocking collectives: none -> 111 us  [the longest x1 31.6 us: per_device(): own = lax.all_to_all(packed, 'ctx', 0, 0)]
    reduce_scatter x1 -> x0, waiting for transfers between devices: 104 us -> none  [per_device(): lax.psum_scatter(pair_terms.astype(jnp.bfloat16), 'ctx', scatter_dimensio...]
    dot_general x54 -> x0, matrix products: 66.3 us -> none  [the longest x12 19.9 us: block_scores(): jnp.einsum('qhe,khe->hqk', query_heads, key_heads, preferred_element_type...]
    dynamic_slice x24 -> x0, local copies, waits for them, and re-layouts: 37.1 us -> none  [per_device(): lax.scan(one_block, start_state, (key_blocks, value_blocks, offsets))]
    pallas_call x0 -> x4, Pallas kernels: none -> 27 us  [the longest x1 15.5 us: attend(): pl.pallas_call(attend_kernel, out_shape=(jax.ShapeDtypeStruct(block, jnp....]
  transfers between devices with their start and end apart: 5 -> 5, of which waited for: 5 -> 4; matrix products, arithmetic and copies ran while one was open for 3% -> 0% of each run, Pallas kernels for 0% -> 2%
where the time goes in v1:
time: 196 us; the launch traced here: 195 us
  blocking collectives  119 us (61%)
  Pallas kernels  27 us (14%)
  waiting for transfers between devices  15.9 us (8%)
  between operations  14.1 us (7%)
  starting transfers between devices  11.3 us (6%)
  local copies, waits for them, and re-layouts  4.4 us (2%)
  other arithmetic  3.11 us (2%)
    all_to_all x1, blocking collectives, per_device(): own = lax.all_to_all(packed, 'ctx', 0, 0)  31.6 us
    all_to_all x1, blocking collectives, per_device(): terms = lax.all_to_all(terms, 'dp', 0, 0, axis_index_groups=SAME_CORE)  30.9 us
    all_to_all x1, blocking collectives, per_device(): lax.all_to_all(jnp.concatenate([query_part, key_part], axis=1), 'ctx', 0, 0)  26.9 us
    pallas_call x1, Pallas kernels, attend(): pl.pallas_call(attend_kernel, out_shape=(jax.ShapeDtypeStruct(block, jnp....  15.5 us
    all_to_all x1, blocking collectives, per_device(): terms = lax.all_to_all(terms, 'ctx', 0, 0, axis_index_groups=Z_LINES)  12.7 us
    all_gather x1, waiting for transfers between devices, per_device(): grads = gather_pair(back.reshape(1, 2, HEADS, 2 * SPAN, 128))  12 us
    all_to_all x1, blocking collectives, per_device(): terms = lax.all_to_all(terms, 'ctx', 0, 0, axis_index_groups=Y_LINES)  9.34 us
    all_to_all x1, starting transfers between devices, per_device(): spread = lax.all_to_all(jnp.broadcast_to(rows, (16, 16, HQ)), 'dp', 0, 0)  7.81 us
  transfers between devices with their start and end apart: 5, of which 4 were waited for; matrix products, arithmetic and copies ran while one was open for 0% of the time, Pallas kernels for 2%

profile of v1, /device:TPU:1, one launch (start us, length us, event | category | flops | bytes accessed | tf_op | source)
XLA Modules:
  0.0 195.2 jit_solution(1670886210339748909)
XLA Ops:
  7.2 0.0 all-gather.4.cloned.1.call-start
  7.2 5.4 %all-gather = bf16[2,1,2,96,1024]{4,3,2,1,0:T(8,128)(2,1)S(1)} all-gather(bf16[1,1,2,96,1024]{4,3,2,1,0:T(8,128)(2,1)} %param.4), channel_id=2, replica_groups={{0,16},{32,48},{64,80},{96,112},{128,144},{160,176},{192,208},{224,240}..., dimensions={0}, use_global_device_ids=true | all-gather | bytes 1179648 | tf_op jit(solution)/shard_map/all_gather | solution.py:320
  12.7 2.6 %all-gather.1 = bf16[2,1,2,96,1024]{4,3,2,1,0:T(8,128)(2,1)S(1)} all-gather(bf16[1,1,2,96,1024]{4,3,2,1,0:T(8,128)(2,1)} %param.7), channel_id=3, replica_groups={{0,16},{32,48},{64,80},{96,112},{128,144},{160,176},{192,208},{224,240}..., dimensions={0}, use_global_device_ids=true | all-gather | bytes 1179648 | tf_op jit(solution)/shard_map/all_gather | solution.py:321
  15.2 3.0 %project.1 = bf16[2,8,192,128]{3,2,1,0:T(8,128)(2,1)S(1)} custom-call(s32[1]{0:T(128)} %bitcast.3.block_ref, bf16[2,2,96,1024]{3,2,1,0:T(8,128)(2,1)S(1)} %bitcast.17, bf16[2,2,96,1024]{3,2,1,0:T(8,128)(2,1)S(1)} %bitcast.19, bf16[4,1024,512]{2,1,0:T(8,128)(2,1)} %weights_ref.3), custom_call_target="tpu_custom_call" | custom-call | tf_op jit(solution)/shard_map/project/pallas_call | solution.py:58
  18.2 0.0 copy-start.3
  18.3 31.6 %all_to_all.30.own_ref = bf16[16,192,128]{2,1,0:T(8,128)(2,1)S(1)} all-to-all(bf16[16,192,128]{2,1,0:T(8,128)(2,1)S(1)} %bitcast.21), channel_id=1, replica_groups=mesh['dp'=16,'ctx'=16] {'ctx'}, dimensions={0} | all-to-all | bytes 1572864 | tf_op jit(solution)/shard_map/all_to_all | solution.py:325
  49.9 3.2 %collective-permute-start.1 = (bf16[16,96,128]{2,1,0:T(8,128)(2,1)S(1)}, bf16[16,96,128]{2,1,0:T(8,128)(2,1)S(1)}, u32[]{:S(2)}, u32[]{:S(2)}) collective-permute-start(bf16[16,96,128]{2,1,0:T(8,128)(2,1)S(1)} %slice.22), channel_id=1, source_target_pairs={{0,16},{16,0},{32,48},{48,32},{64,80},{80,64},{96,112},{112,96},{1... | collective-permute-start | bytes 1179656 | tf_op jit(solution)/shard_map/ppermute | solution.py:326
  53.0 0.0 copy-done.3
  53.0 0.1 collective-permute-start
  53.1 1.2 collective-permute-done
  54.4 0.0 collective-permute-done.1.other_ref
  54.4 15.5 %attend.1 = (bf16[16,96,128]{2,1,0:T(8,128)(2,1)S(1)}, f32[16,96,128]{2,1,0:T(8,128)S(1)}, bf16[16,96,128]{2,1,0:T(8,128)(2,1)S(1)}) custom-call(s32[1]{0:T(128)} %bitcast.core_ref, s32[4]{0:T(128)S(1)} %fusion.tiles_ref, bf16[16,192,128]{2,1,0:T(8,128)(2,1)S(1)} %all_to_all.30.own_ref, bf16[16,96,128]{2,1,0:T(8,128)(2,1)S(1)} %collective-permute-done.1.other_ref), custom_call_target="tpu_custom_call" | custom-call | tf_op jit(solution)/shard_map/attend/pallas_call | solution.py:181
  69.9 0.2 collective-permute-start.2
  70.1 1.7 collective-permute-done.2
  71.7 0.1 add_convert_fusion
  71.8 0.1 pad_maximum_fusion
  71.9 26.9 %all_to_all.31 = bf16[16,192,128]{2,1,0:T(8,128)(2,1)} all-to-all(bf16[16,192,128]{2,1,0:T(8,128)(2,1)S(1)} %pad_maximum_fusion), channel_id=1, replica_groups=mesh['dp'=16,'ctx'=16] {'ctx'}, dimensions={0} | all-to-all | bytes 1572864 | tf_op jit(solution)/shard_map/all_to_all | solution.py:331
  98.8 0.0 all-gather.4.cloned.1.call-update
  98.8 0.1 pad_add_fusion.place_ref
  98.9 12.0 %all-gather.4.cloned.1.call-done.grads_ref = bf16[2,2,8,192,128]{4,3,2,1,0:T(8,128)(2,1)} async-done(((bf16[1,2,8,192,128]{4,3,2,1,0:T(8,128)(2,1)}), bf16[2,2,8,192,128]{4,3,2,1,0:T(8,128)(2,1)}) %all-gather.4.cloned.1.call-update) | async-done | bytes 1572880 | tf_op jit(solution)/shard_map/all_gather | solution.py:332
  110.9 0.0 copy-start.1
  110.9 1.4 copy-done.1
  112.3 4.5 %weight_terms.1 = bf16[8,16,16,512]{3,2,1,0:T(8,128)(2,1)S(1)} custom-call(s32[2]{0:T(128)S(1)} %pad_add_fusion.place_ref, bf16[2,2,8,192,128]{4,3,2,1,0:T(8,128)(2,1)S(1)} %copy-done.1, bf16[2,2,96,1024]{3,2,1,0:T(8,128)(2,1)S(1)} %bitcast.18, bf16[2,2,96,1024]{3,2,1,0:T(8,128)(2,1)S(1)} %bitcast.20), custom_call_target="tpu_custom_call" | custom-call | tf_op jit(solution)/shard_map/weight_terms/pallas_call | solution.py:235
  116.8 30.9 %all_to_all.32 = bf16[8,16,16,512]{3,2,1,0:T(8,128)(2,1)} all-to-all(bf16[8,16,16,512]{3,2,1,0:T(8,128)(2,1)S(1)} %weight_terms.1), channel_id=1, replica_groups={{0,32,64,96,128,160,192,224},{16,48,80,112,144,176,208,240},{1,33,65,97..., dimensions={0} | all-to-all | bytes 4194304 | tf_op jit(solution)/shard_map/all_to_all | solution.py:335
  147.7 0.0 copy-start.2
  147.7 2.1 %reduce_sum.33 = bf16[16,16,512]{2,1,0:T(8,128)(2,1)S(1)} reduce(bf16[8,16,16,512]{3,2,1,0:T(8,128)(2,1)} %all_to_all.32, bf16[]{:T(256)} %constant.42.clone.1), dimensions={0}, to_apply=%region_0.1 | reduce | flops 917504 | bytes 2359298 | tf_op jit(solution)/shard_map/reduce_sum | solution.py:339
  149.7 9.3 %all_to_all.33 = bf16[4,4,16,512]{3,2,1,0:T(8,128)(2,1)S(1)} all-to-all(bf16[4,4,16,512]{3,2,1,0:T(8,128)(2,1)S(1)} %bitcast.25), channel_id=1, replica_groups={{0,4,8,12},{1,5,9,13},{2,6,10,14},{3,7,11,15},{16,20,24,28},{17,21,25,2..., dimensions={0} | all-to-all | bytes 524288 | tf_op jit(solution)/shard_map/all_to_all | solution.py:342
  159.1 12.7 %all_to_all.34 = bf16[4,16,512]{2,1,0:T(8,128)(2,1)S(1)} all-to-all(bf16[4,16,512]{2,1,0:T(8,128)(2,1)S(1)} %reduce_sum.34), channel_id=1, replica_groups={{0,1,2,3},{4,5,6,7},{8,9,10,11},{12,13,14,15},{16,17,18,19},{20,21,22,2..., dimensions={0} | all-to-all | bytes 131072 | tf_op jit(solution)/shard_map/all_to_all | solution.py:344
  171.8 0.7 broadcast_in_dim.3
  172.6 7.8 %all-to-all-start.5 = ((bf16[16,16,512]{2,1,0:T(8,128)(2,1)}), bf16[16,16,512]{2,1,0:T(8,128)(2,1)S(1)}, u32[]{:S(2)}, u32[]{:S(2)}) async-start(bf16[16,16,512]{2,1,0:T(8,128)(2,1)} %broadcast_in_dim.3), calls=%async_computation.5 | async-start | bytes 524288 | tf_op jit(solution)/shard_map/all_to_all | solution.py:347
  180.4 0.0 copy-done.2
  180.4 0.0 copy-start
  180.4 2.2 %copy-done = bf16[4,1024,512]{2,1,0:T(8,128)(2,1)S(1)} copy-done((bf16[4,1024,512]{2,1,0:T(8,128)(2,1)S(1)}, bf16[4,1024,512]{2,1,0:T(8,128)(2,1)}, u32[]{:S(2)}) %copy-start) | copy-done | bytes 4194328
  182.6 4.0 %outputs.1 = (bf16[2,96,1024]{2,1,0:T(8,128)(2,1)}, bf16[2,96,1024]{2,1,0:T(8,128)(2,1)}) custom-call(s32[2]{0:T(128)S(1)} %pad_add_fusion.place_ref, bf16[2,2,8,192,128]{4,3,2,1,0:T(8,128)(2,1)S(1)} %copy-done.2, bf16[4,1024,512]{2,1,0:T(8,128)(2,1)S(1)} %copy-done), custom_call_target="tpu_custom_call" | custom-call | flops 805306368 | bytes 7340032 | tf_op jit(solution)/shard_map/outputs/pallas_call | solution.py:290
  186.6 1.0 all-to-all-done.5
  187.7 0.7 pad_maximum_fusion.1
  (8 shorter events, 0.1 us)
Async XLA Ops:
  7.2 103.7 %all-gather.4.cloned.1.call-start = ((), (), s32[]{:S(2)}) async-start(), calls=%async_computation.6 | async-start | bytes 2359296 | tf_op jit(solution)/shard_map/all_gather | solution.py:332
  18.2 34.8 %copy-start.3 = (s32[1,4]{1,0:T(1,128)S(1)}, s32[1,4]{1,0:T(1,128)}, u32[]{:S(2)}) copy-start(s32[1,4]{1,0:T(1,128)} %param.5) | copy-start | bytes 52
  49.9 4.5 %collective-permute-start.1 = (bf16[16,96,128]{2,1,0:T(8,128)(2,1)S(1)}, bf16[16,96,128]{2,1,0:T(8,128)(2,1)S(1)}, u32[]{:S(2)}, u32[]{:S(2)}) collective-permute-start(bf16[16,96,128]{2,1,0:T(8,128)(2,1)S(1)} %slice.22), channel_id=1, source_target_pairs={{0,16},{16,0},{32,48},{48,32},{64,80},{80,64},{96,112},{112,96},{1... | collective-permute-start | bytes 1179656 | tf_op jit(solution)/shard_map/ppermute | solution.py:326
  53.0 1.3 collective-permute-start
  69.9 1.8 collective-permute-start.2
  110.9 1.4 copy-start.1
  147.7 32.7 %copy-start.2 = (bf16[2,2,8,192,128]{4,3,2,1,0:T(8,128)(2,1)S(1)}, bf16[2,2,8,192,128]{4,3,2,1,0:T(8,128)(2,1)}, u32[]{:S(2)}) copy-start(bf16[2,2,8,192,128]{4,3,2,1,0:T(8,128)(2,1)} %all-gather.4.cloned.1.call-done.grads_ref) | copy-start | bytes 4718596
  172.6 15.0 %all-to-all-start.5 = ((bf16[16,16,512]{2,1,0:T(8,128)(2,1)}), bf16[16,16,512]{2,1,0:T(8,128)(2,1)S(1)}, u32[]{:S(2)}, u32[]{:S(2)}) async-start(bf16[16,16,512]{2,1,0:T(8,128)(2,1)} %broadcast_in_dim.3), calls=%async_computation.5 | async-start | bytes 524288 | tf_op jit(solution)/shard_map/all_to_all | solution.py:347
  180.4 2.2 %copy-start = (bf16[4,1024,512]{2,1,0:T(8,128)(2,1)S(1)}, bf16[4,1024,512]{2,1,0:T(8,128)(2,1)}, u32[]{:S(2)}) copy-start(bf16[4,1024,512]{2,1,0:T(8,128)(2,1)} %weights_ref.3) | copy-start | bytes 12582916
Sparse Core Ops, SparseCore 0:
  98.9 11.8 all-gather.3

commit v2 on v1

--- a/solution.py
+++ b/solution.py
@@ -21,9 +21,8 @@
 
 CORE_PAIRS = [[2 * i, 2 * i + 1] for i in range(8)]
 CORE_SWAP = [(i, i ^ 1) for i in range(16)]
-SAME_CORE = [[core + 2 * i for i in range(8)] for core in range(2)]
-Y_LINES = [[z + 4 * y for y in range(4)] for z in range(4)]
-Z_LINES = [[4 * y + z for z in range(4)] for y in range(4)]
+X_LINES = [[4 * x + 2 * z + core for x in range(4) for core in range(2)] for z in range(2)]
+Z_SWAP = [(i, i ^ 2) for i in range(16)]
 
 
 def low_lanes(rows):
@@ -49,15 +48,15 @@
             for sequence in range(2):
                 rows = slice(SPAN * sequence, SPAN * sequence + SPAN)
                 place = slice(SPAN * half, SPAN * half + SPAN)
-                out_ref[sequence, 2 * pair, place, :] = even[rows]
-                out_ref[sequence, 2 * pair + 1, place, :] = odd[rows]
+                out_ref[2 * pair, sequence, place, :] = even[rows]
+                out_ref[2 * pair + 1, sequence, place, :] = odd[rows]
 
 
 def project(block, tokens_pair, upstream_pair, weights):
     tokens_spec = pl.BlockSpec((2, 1, SPAN, D), lambda j, block: (0, block[0], 0, 0))
     return pl.pallas_call(
         project_kernel,
-        out_shape=jax.ShapeDtypeStruct((2, HEADS, 2 * SPAN, 128), jnp.bfloat16),
+        out_shape=jax.ShapeDtypeStruct((HEADS, 2, 2 * SPAN, 128), jnp.bfloat16),
         grid_spec=pltpu.PrefetchScalarGridSpec(
             num_scalar_prefetch=1,
             grid=(2,),
@@ -66,7 +65,7 @@
                 tokens_spec,
                 pl.BlockSpec((4, D, HQ // 2), lambda j, block: (0, 0, j)),
             ],
-            out_specs=pl.BlockSpec((2, HEADS // 2, 2 * SPAN, 128), lambda j, block: (0, j, 0, 0)),
+            out_specs=pl.BlockSpec((HEADS // 2, 2, 2 * SPAN, 128), lambda j, block: (j, 0, 0, 0)),
         ),
         compiler_params=pltpu.CompilerParams(vmem_limit_bytes=VMEM_LIMIT),
         name="project",
@@ -198,60 +197,80 @@
     )(core, tiles, own, other)
 
 
-def weight_kernel(place_ref, grads_ref, tokens_ref, upstream_ref, out_ref, held_ref):
-    core, odd = place_ref[0], place_ref[1]
-    number, step = pl.program_id(0), pl.program_id(1)
-
-    @pl.when(step == 0)
+def weight_kernel(odd_ref, grads_ref, tokens_ref, upstream_ref, out_ref, held_ref):
+    odd = odd_ref[0]
+
+    @pl.when(pl.program_id(0) == 0)
     def _():
-        low = low_lanes(SPAN)
-        for sequence in range(2):
-            for block in range(2):
-                holder = jnp.bitwise_xor(odd, block)
-                first = (2 * sequence + block) * SPAN
-                rows = pl.ds(pl.multiple_of(number * SPAN, SPAN), SPAN)
-                for pair in range(HEADS // 2):
-                    one = grads_ref[holder, sequence, 2 * pair, rows, :].astype(jnp.float32)
-                    two = grads_ref[holder, sequence, 2 * pair + 1, rows, :].astype(jnp.float32)
-                    lower = jnp.where(low, one, pltpu.roll(two, HEAD, 1))
-                    upper = jnp.where(low, pltpu.roll(one, HEAD, 1), two)
-                    held_ref[first : first + SPAN, 128 * pair : 128 * pair + 128] = jnp.where(
-                        core == 0, lower, upper
-                    ).astype(jnp.bfloat16)
-
-    use_upstream = jnp.logical_and(core == 1, number == 0)
-    left = jnp.where(use_upstream, upstream_ref[...], tokens_ref[...]).reshape(4 * SPAN, D // 4)
-    result = lax.dot_general(
-        left, held_ref[...], (((0,), (0,)), ((), ())), preferred_element_type=jnp.float32
-    ).astype(jnp.bfloat16)
-    for rank in range(4):
-        for part in range(4):
-            row = 64 * rank + 16 * part
-            out_ref[part, rank] = result[row : row + 16]
-
-
-def weight_terms(place, grads, tokens_pair, upstream_pair):
-    tokens_spec = pl.BlockSpec((2, 2, SPAN, D // 4), lambda w, j, place: (0, 0, 0, j))
+        for chip in range(4):
+            for sequence in range(2):
+                for block in range(2):
+                    holder = 2 * chip + jnp.bitwise_xor(odd, block)
+                    first = (4 * chip + 2 * sequence + block) * SPAN
+                    for half in range(2):
+                        held_ref[first : first + SPAN, 128 * half : 128 * half + 128] = grads_ref[
+                            holder, sequence, SPAN * half : SPAN * half + SPAN, :
+                        ]
+
+    def product(rows_ref, columns):
+        rows = rows_ref[...].reshape(16 * SPAN, D // 4)
+        return lax.dot_general(
+            rows, held_ref[:, :columns], (((0,), (0,)), ((), ())), preferred_element_type=jnp.float32
+        )
+
+    by_tokens = product(tokens_ref, 256)
+    by_upstream = product(upstream_ref, 128)
+    first = jnp.where(low_lanes(D // 4), by_tokens[:, :128], by_upstream)
+    out_ref[:, :, :128] = first.astype(jnp.bfloat16).reshape(4, 64, 128)
+    out_ref[:, :, 128:] = by_tokens[:, 128:].astype(jnp.bfloat16).reshape(4, 64, 128)
+
+
+def weight_terms(odd, grads, tokens_line, upstream_line):
+    tokens_spec = pl.BlockSpec((8, 2, SPAN, D // 4), lambda j, odd: (0, 0, 0, j))
     return pl.pallas_call(
         weight_kernel,
-        out_shape=jax.ShapeDtypeStruct((8, RANKS, 16, HQ), jnp.bfloat16),
+        out_shape=jax.ShapeDtypeStruct((RANKS, 64, 256), jnp.bfloat16),
         grid_spec=pltpu.PrefetchScalarGridSpec(
             num_scalar_prefetch=1,
-            grid=(2, 4),
+            grid=(4,),
             in_specs=[
-                pl.BlockSpec((2, 2, HEADS, 2 * SPAN, 128), lambda w, j, place: (0, 0, 0, 0, 0)),
+                pl.BlockSpec((8, 2, 2 * SPAN, 128), lambda j, odd: (0, 0, 0, 0)),
                 tokens_spec,
                 tokens_spec,
             ],
-            out_specs=pl.BlockSpec((4, 4, 16, HQ), lambda w, j, place: (w, j, 0, 0)),
-            scratch_shapes=[pltpu.VMEM((4 * SPAN, HQ), jnp.bfloat16)],
+            out_specs=pl.BlockSpec((4, 64, 256), lambda j, odd: (j, 0, 0)),
+            scratch_shapes=[pltpu.VMEM((16 * SPAN, 256), jnp.bfloat16)],
         ),
         compiler_params=pltpu.CompilerParams(vmem_limit_bytes=VMEM_LIMIT),
         name="weight_terms",
-    )(place, grads, tokens_pair, upstream_pair)
-
-
-def output_kernel(place_ref, grads_ref, weights_ref, out_ref, input_grad_ref, held_ref):
+    )(odd, grads, tokens_line, upstream_line)
+
+
+def spread_kernel(parts_ref, out_ref):
+    low = low_lanes(64)
+    for pair in range(HEADS // 2):
+        columns = slice(128 * pair, 128 * pair + 128)
+        for half, (lower, upper) in enumerate(((0, 3), (1, 2))):
+            lanes = slice(128 * half, 128 * half + 128)
+            one = parts_ref[2 * pair, :, lanes].astype(jnp.float32)
+            two = parts_ref[2 * pair + 1, :, lanes].astype(jnp.float32)
+            out_ref[lower, :, columns] = jnp.where(low, one, pltpu.roll(two, HEAD, 1)).astype(
+                jnp.bfloat16
+            )
+            out_ref[upper, :, columns] = jnp.where(low, pltpu.roll(one, HEAD, 1), two).astype(
+                jnp.bfloat16
+            )
+
+
+def spread_heads(parts):
+    return pl.pallas_call(
+        spread_kernel,
+        out_shape=jax.ShapeDtypeStruct((4, 64, HQ), jnp.bfloat16),
+        name="spread_heads",
+    )(parts)
+
+
+def output_kernel(place_ref, grads_ref, arrived_ref, weights_ref, out_ref, input_grad_ref, held_ref):
     core, odd = place_ref[0], place_ref[1]
 
     @pl.when(pl.program_id(0) == 0)
@@ -264,8 +283,14 @@
                 place = slice(SPAN * half, SPAN * half + SPAN)
                 for pair in range(HEADS // 2):
                     columns = slice(128 * pair, 128 * pair + 128)
-                    one = grads_ref[holder, 0, 2 * pair, place, :].astype(jnp.float32)
-                    two = grads_ref[holder, 0, 2 * pair + 1, place, :].astype(jnp.float32)
+                    one, two = (
+                        jnp.where(
+                            holder == core,
+                            grads_ref[head, 0, place, :].astype(jnp.float32),
+                            arrived_ref[head, place, :].astype(jnp.float32),
+                        )
+                        for head in (2 * pair, 2 * pair + 1)
+                    )
                     held_ref[2 * half, rows, columns] = jnp.where(
                         low, one, pltpu.roll(two, HEAD, 1)
                     ).astype(jnp.bfloat16)
@@ -284,7 +309,7 @@
     input_grad_ref[...] = input_grad.astype(jnp.bfloat16).reshape(2, SPAN, D // 4)
 
 
-def outputs(place, grads, weights):
+def outputs(place, grads, arrived, weights):
     shape = jax.ShapeDtypeStruct((2, SPAN, D), jnp.bfloat16)
     out_spec = pl.BlockSpec((2, SPAN, D // 4), lambda j, place: (0, 0, j))
     return pl.pallas_call(
@@ -294,9 +319,8 @@
             num_scalar_prefetch=1,
             grid=(4,),
             in_specs=[
-                pl.BlockSpec(
-                    (2, 1, HEADS, 2 * SPAN, 128), lambda j, place: (0, place[0], 0, 0, 0)
-                ),
+                pl.BlockSpec((HEADS, 1, 2 * SPAN, 128), lambda j, place: (0, place[0], 0, 0)),
+                pl.BlockSpec((HEADS, 2 * SPAN, 128), lambda j, place: (0, 0, 0)),
                 pl.BlockSpec((4, D // 4, HQ), lambda j, place: (0, j, 0)),
             ],
             out_specs=(out_spec, out_spec),
@@ -307,7 +331,7 @@
             flops=8 * 2 * SPAN * D * HQ, bytes_accessed=7 * 1024 * 1024, transcendentals=0
         ),
         name="outputs",
-    )(place, grads, weights)
+    )(place, grads, arrived, weights)
 
 
 def per_device(tokens, sweep_tiles, weights, cotangent):
@@ -319,34 +343,39 @@
     )
     tokens_pair = gather_pair(tokens.reshape(1, 2, SPAN, D))
     upstream_pair = gather_pair(cotangent.reshape(1, 2, SPAN, D))
+    tokens_line, upstream_line = (
+        lax.all_gather(
+            rows.reshape(1, 2, SPAN, D), "dp", axis_index_groups=X_LINES, axis=0, tiled=True
+        )
+        for rows in (tokens, cotangent)
+    )
     other_tiles = lax.ppermute(sweep_tiles, "dp", CORE_SWAP)
     block = jnp.bitwise_xor(core, odd).astype(jnp.int32).reshape(1)
     packed = project(block, tokens_pair, upstream_pair, weights).reshape(RANKS, 2 * SPAN, 128)
     own = lax.all_to_all(packed, "ctx", 0, 0)
     other = lax.ppermute(own[:, SPAN:], "dp", CORE_SWAP)
-    tiles = jnp.where(rank // 8 == core, sweep_tiles, other_tiles).reshape(-1)
+    tiles = jnp.where(odd == core, sweep_tiles, other_tiles).reshape(-1)
     query_part, own_grad, other_grad = attend(core.astype(jnp.int32).reshape(1), tiles, own, other)
     arrived = lax.ppermute(other_grad, "dp", CORE_SWAP)
     key_part = (own_grad + arrived.astype(jnp.float32)).astype(jnp.bfloat16)
     back = lax.all_to_all(jnp.concatenate([query_part, key_part], axis=1), "ctx", 0, 0)
-    grads = gather_pair(back.reshape(1, 2, HEADS, 2 * SPAN, 128))
+    grads = back.reshape(HEADS, 2, 2 * SPAN, 128)
+    line = lax.all_to_all(grads, "dp", 0, 0, axis_index_groups=X_LINES)
+    terms = weight_terms(odd.astype(jnp.int32).reshape(1), line, tokens_line, upstream_line)
+    terms = lax.all_to_all(terms, "ctx", 0, 0)
+    swapped = lax.ppermute(
+        lax.dynamic_index_in_dim(grads, 1 - core, 1, keepdims=False), "dp", CORE_SWAP
+    )
     place = jnp.stack([core, odd]).astype(jnp.int32)
-    terms = weight_terms(place, grads, tokens_pair, upstream_pair)
-    terms = lax.all_to_all(terms, "dp", 0, 0, axis_index_groups=SAME_CORE)
-    attn_out, input_grad = outputs(place, grads, weights)
-
-    def summed(parts):
-        return jnp.sum(parts.astype(jnp.float32), axis=0)
-
-    terms = summed(terms).astype(jnp.bfloat16).reshape(4, 4, 16, HQ)
-    terms = lax.all_to_all(terms, "ctx", 0, 0, axis_index_groups=Y_LINES)
-    terms = summed(terms).astype(jnp.bfloat16)
-    terms = lax.all_to_all(terms, "ctx", 0, 0, axis_index_groups=Z_LINES)
+    attn_out, input_grad = outputs(place, grads, swapped, weights)
+    rows = lax.reduce_precision(jnp.sum(terms.astype(jnp.float32), axis=0), 8, 7)
+    other_rows = lax.ppermute(rows.astype(jnp.bfloat16), "dp", Z_SWAP)
     factor = float(16 * RANKS * 2 * SPAN) ** -0.5
-    rows = (summed(terms) * factor).astype(jnp.bfloat16)
-    spread = lax.all_to_all(jnp.broadcast_to(rows, (16, 16, HQ)), "dp", 0, 0)
-    spread = spread.reshape(2, 4, 2, 16, HQ).transpose(2, 0, 1, 3, 4).reshape(4, 64, HQ)
-    weight_grads = jnp.stack([spread[0], spread[1], spread[3], spread[2]])
+    rows = ((rows + other_rows.astype(jnp.float32)) * factor).astype(jnp.bfloat16)
+    parts = lax.all_to_all(
+        jnp.broadcast_to(rows, (HEADS, 64, 256)), "dp", 0, 0, axis_index_groups=X_LINES
+    )
+    weight_grads = spread_heads(parts)
     return (attn_out.reshape(tokens.shape), input_grad.reshape(tokens.shape), weight_grads)
 
 

time: 196 us -> 172 us (0.88)
  blocking collectives: 119 us -> 83.7 us
  starting transfers between devices: 11.3 us -> 16.9 us
  waiting for transfers between devices: 15.9 us -> 21 us
  other arithmetic: 3.11 us -> 0.34 us
  Pallas kernels: 27 us -> 29.3 us
    all_to_all x3 -> x1, blocking collectives: 52.9 us -> 18 us  [per_device(): line = lax.all_to_all(grads, 'dp', 0, 0, axis_index_groups=X_LINES)]
    all_to_all x1 -> x2, waiting for transfers between devices: 1.04 us -> 16.7 us  [the longest x1 16.5 us: per_device(): terms = lax.all_to_all(terms, 'ctx', 0, 0)]
    all_gather x1 -> x2, waiting for transfers between devices: 12 us -> 0.01 us  [per_device(): lax.all_gather(rows.reshape(1, 2, SPAN, D), 'dp', axis_index_groups=X_LIN...]
    ppermute x0 -> x2, starting transfers between devices: none -> 2.81 us  [the longest x1 2.72 us: per_device(): lax.ppermute(lax.dynamic_index_in_dim(grads, 1 - core, 1, keepdims=False)...]
    all_to_all x1 -> x2, starting transfers between devices: 7.81 us -> 10.5 us  [the longest x1 6.95 us: per_device(): lax.all_to_all(jnp.broadcast_to(rows, (HEADS, 64, 256)), 'dp', 0, 0, axis...]
    pallas_call x2 -> x3, Pallas kernels: 7.5 us -> 10 us  [the longest x1 5.28 us: weight_terms(): pl.pallas_call(weight_kernel, out_shape=jax.ShapeDtypeStruct((RANKS, 64,...]
    reduce_sum x3 -> x1, other arithmetic: 2.14 us -> 0.08 us  [per_device(): jnp.sum(terms.astype(jnp.float32), axis=0)]
  transfers between devices with their start and end apart: 5 -> 9, of which waited for: 4 -> 4; matrix products, arithmetic and copies ran while one was open for 0% -> 1% of each run, Pallas kernels for 2% -> 13%
where the time goes in v2:
time: 172 us; the launch traced here: 171 us
  blocking collectives  83.7 us (49%)
  Pallas kernels  29.3 us (17%)
  waiting for transfers between devices  21 us (12%)
  starting transfers between devices  16.9 us (10%)
  between operations  14.1 us (8%)
  local copies, waits for them, and re-layouts  5.57 us (3%)
    all_to_all x1, blocking collectives, per_device(): own = lax.all_to_all(packed, 'ctx', 0, 0)  31.6 us
    all_to_all x1, blocking collectives, per_device(): lax.all_to_all(jnp.concatenate([query_part, key_part], axis=1), 'ctx', 0, 0)  26.1 us
    all_to_all x1, blocking collectives, per_device(): line = lax.all_to_all(grads, 'dp', 0, 0, axis_index_groups=X_LINES)  18 us
    all_to_all x1, waiting for transfers between devices, per_device(): terms = lax.all_to_all(terms, 'ctx', 0, 0)  16.5 us
    pallas_call x1, Pallas kernels, attend(): pl.pallas_call(attend_kernel, out_shape=(jax.ShapeDtypeStruct(block, jnp....  15.2 us
    all_to_all x1, starting transfers between devices, per_device(): lax.all_to_all(jnp.broadcast_to(rows, (HEADS, 64, 256)), 'dp', 0, 0, axis...  6.95 us
    all_gather x1, blocking collectives, per_device(): tokens_pair = gather_pair(tokens.reshape(1, 2, SPAN, D))  5.45 us
    pallas_call x1, Pallas kernels, weight_terms(): pl.pallas_call(weight_kernel, out_shape=jax.ShapeDtypeStruct((RANKS, 64,...  5.28 us
  transfers between devices with their start and end apart: 9, of which 4 were waited for; matrix products, arithmetic and copies ran while one was open for 1% of the time, Pallas kernels for 13%

profile of v2, /device:TPU:1, one launch (start us, length us, event | category | flops | bytes accessed | tf_op | source)
XLA Modules:
  0.0 170.9 jit_solution(1540021241912241462)
XLA Ops:
  7.2 0.0 all-gather.7.cloned.1.call-start
  7.2 0.7 all-gather.7.cloned.1.call-update
  7.9 0.0 all-gather.9.cloned.1.call-start
  7.9 0.7 all-gather.9.cloned.1.call-update
  8.7 5.4 %all-gather = bf16[2,1,2,96,1024]{4,3,2,1,0:T(8,128)(2,1)S(1)} all-gather(bf16[1,1,2,96,1024]{4,3,2,1,0:T(8,128)(2,1)} %param.4), channel_id=2, replica_groups={{0,16},{32,48},{64,80},{96,112},{128,144},{160,176},{192,208},{224,240}..., dimensions={0}, use_global_device_ids=true | all-gather | bytes 1179648 | tf_op jit(solution)/shard_map/all_gather | solution.py:344
  14.1 2.6 %all-gather.1 = bf16[2,1,2,96,1024]{4,3,2,1,0:T(8,128)(2,1)S(1)} all-gather(bf16[1,1,2,96,1024]{4,3,2,1,0:T(8,128)(2,1)} %param.7), channel_id=3, replica_groups={{0,16},{32,48},{64,80},{96,112},{128,144},{160,176},{192,208},{224,240}..., dimensions={0}, use_global_device_ids=true | all-gather | bytes 1179648 | tf_op jit(solution)/shard_map/all_gather | solution.py:345
  16.7 0.0 copy-start.3
  16.7 3.0 %project.1 = bf16[8,2,192,128]{3,2,1,0:T(8,128)(2,1)S(1)} custom-call(s32[1]{0:T(128)} %bitcast.3.block_ref, bf16[2,2,96,1024]{3,2,1,0:T(8,128)(2,1)S(1)} %bitcast.20, bf16[2,2,96,1024]{3,2,1,0:T(8,128)(2,1)S(1)} %bitcast.21, bf16[4,1024,512]{2,1,0:T(8,128)(2,1)} %weights_ref.3), custom_call_target="tpu_custom_call" | custom-call | tf_op jit(solution)/shard_map/project/pallas_call | solution.py:57
  19.7 31.6 %all_to_all.25.own_ref = bf16[16,192,128]{2,1,0:T(8,128)(2,1)S(1)} all-to-all(bf16[16,192,128]{2,1,0:T(8,128)(2,1)S(1)} %bitcast.19), channel_id=1, replica_groups=mesh['dp'=16,'ctx'=16] {'ctx'}, dimensions={0} | all-to-all | bytes 1572864 | tf_op jit(solution)/shard_map/all_to_all | solution.py:355
  51.3 3.1 %collective-permute-start.1 = (bf16[16,96,128]{2,1,0:T(8,128)(2,1)S(1)}, bf16[16,96,128]{2,1,0:T(8,128)(2,1)S(1)}, u32[]{:S(2)}, u32[]{:S(2)}) collective-permute-start(bf16[16,96,128]{2,1,0:T(8,128)(2,1)S(1)} %slice.4), channel_id=1, source_target_pairs={{0,16},{16,0},{32,48},{48,32},{64,80},{80,64},{96,112},{112,96},{1... | collective-permute-start | bytes 1179656 | tf_op jit(solution)/shard_map/ppermute | solution.py:356
  54.4 0.0 copy-done.3
  54.4 0.1 collective-permute-start
  54.5 1.2 collective-permute-done
  55.8 0.0 collective-permute-done.1.other_ref
  55.8 15.2 %attend.1 = (bf16[16,96,128]{2,1,0:T(8,128)(2,1)S(1)}, f32[16,96,128]{2,1,0:T(8,128)S(1)}, bf16[16,96,128]{2,1,0:T(8,128)(2,1)S(1)}) custom-call(s32[1]{0:T(128)} %bitcast.core_ref, s32[4]{0:T(128)S(1)} %fusion.tiles_ref, bf16[16,192,128]{2,1,0:T(8,128)(2,1)S(1)} %all_to_all.25.own_ref, bf16[16,96,128]{2,1,0:T(8,128)(2,1)S(1)} %collective-permute-done.1.other_ref), custom_call_target="tpu_custom_call" | custom-call | tf_op jit(solution)/shard_map/attend/pallas_call | solution.py:180
  71.0 0.3 collective-permute-start.2
  71.3 1.7 collective-permute-done.2
  73.0 0.1 add_convert_fusion
  73.1 0.1 pad_maximum_fusion
  73.2 26.1 %all_to_all.26 = bf16[16,192,128]{2,1,0:T(8,128)(2,1)S(1)} all-to-all(bf16[16,192,128]{2,1,0:T(8,128)(2,1)S(1)} %pad_maximum_fusion), channel_id=1, replica_groups=mesh['dp'=16,'ctx'=16] {'ctx'}, dimensions={0} | all-to-all | bytes 1572864 | tf_op jit(solution)/shard_map/all_to_all | solution.py:361
  99.3 18.0 %all_to_all.27.grads_ref = bf16[8,2,192,128]{3,2,1,0:T(8,128)(2,1)S(1)} all-to-all(bf16[8,2,192,128]{3,2,1,0:T(8,128)(2,1)S(1)} %bitcast.15), channel_id=1, replica_groups={{0,16,64,80,128,144,192,208},{32,48,96,112,160,176,224,240},{1,17,65,81..., dimensions={0} | all-to-all | bytes 1572864 | tf_op jit(solution)/shard_map/all_to_all | solution.py:363
  117.2 0.0 all-gather.7.cloned.1.call-done
  117.2 0.0 all-gather.9.cloned.1.call-done
  117.2 0.0 copy-start.1
  117.2 1.9 %copy-done.1 = bf16[8,1,2,96,1024]{4,3,2,1,0:T(8,128)(2,1)S(1)} copy-done((bf16[8,1,2,96,1024]{4,3,2,1,0:T(8,128)(2,1)S(1)}, bf16[8,1,2,96,1024]{4,3,2,1,0:T(8,128)(2,1)}, u32[]{:S(2)}) %copy-start.1) | copy-done | bytes 3145752
  119.1 5.3 %weight_terms.1 = bf16[16,64,256]{2,1,0:T(8,128)(2,1)} custom-call(s32[1]{0:T(128)} %bitcast.1.odd_ref, bf16[8,2,192,128]{3,2,1,0:T(8,128)(2,1)S(1)} %all_to_all.27.grads_ref, bf16[8,2,96,1024]{3,2,1,0:T(8,128)(2,1)S(1)} %bitcast.18, bf16[8,2,96,1024]{3,2,1,0:T(8,128)(2,1)} %bitcast.22), custom_call_target="tpu_custom_call" | custom-call | tf_op jit(solution)/shard_map/weight_terms/pallas_call | solution.py:230
  124.4 3.6 %all-to-all-start.3 = ((bf16[16,64,256]{2,1,0:T(8,128)(2,1)}), bf16[16,64,256]{2,1,0:T(8,128)(2,1)S(1)}, u32[]{:S(2)}, u32[]{:S(2)}) async-start(bf16[16,64,256]{2,1,0:T(8,128)(2,1)} %weight_terms.1), calls=%async_computation.3 | async-start | bytes 1048576 | tf_op jit(solution)/shard_map/all_to_all | solution.py:365
  128.0 16.5 %all-to-all-done.3 = bf16[16,64,256]{2,1,0:T(8,128)(2,1)S(1)} async-done(((bf16[16,64,256]{2,1,0:T(8,128)(2,1)}), bf16[16,64,256]{2,1,0:T(8,128)(2,1)S(1)}, u32[]{:S(2)}, u32[]{:S(2)}) %all-to-all-start.3) | async-done | bytes 524320 | tf_op jit(solution)/shard_map/all_to_all | solution.py:365
  144.4 0.1 convert_reduce_fusion
  144.5 0.1 collective-permute-start.4
  144.7 2.7 %collective-permute-start.3 = (bf16[8,192,128]{2,1,0:T(8,128)(2,1)S(1)}, bf16[8,192,128]{2,1,0:T(8,128)(2,1)S(1)}, u32[]{:S(2)}, u32[]{:S(2)}) collective-permute-start(bf16[8,192,128]{2,1,0:T(8,128)(2,1)S(1)} %dynamic-slice_bitcast_fusion), channel_id=1, source_target_pairs={{0,16},{16,0},{32,48},{48,32},{64,80},{80,64},{96,112},{112,96},{1... | collective-permute-start | bytes 1179656 | tf_op jit(solution)/shard_map/ppermute | solution.py:366
  147.4 0.0 collective-permute-done.4
  147.4 0.7 broadcast_in_dim.3
  148.1 6.9 %all-to-all-start.4 = ((bf16[8,64,256]{2,1,0:T(8,128)(2,1)}), bf16[8,64,256]{2,1,0:T(8,128)(2,1)S(1)}, u32[]{:S(2)}, u32[]{:S(2)}) async-start(bf16[8,64,256]{2,1,0:T(8,128)(2,1)} %broadcast_in_dim.3), calls=%async_computation.4 | async-start | bytes 524288 | tf_op jit(solution)/shard_map/all_to_all | solution.py:375
  155.1 0.1 pad_add_fusion.place_ref
  155.2 0.0 collective-permute-done.3.arrived_ref
  155.2 0.0 copy-start
  155.2 2.2 %copy-done = bf16[4,1024,512]{2,1,0:T(8,128)(2,1)S(1)} copy-done((bf16[4,1024,512]{2,1,0:T(8,128)(2,1)S(1)}, bf16[4,1024,512]{2,1,0:T(8,128)(2,1)}, u32[]{:S(2)}) %copy-start) | copy-done | bytes 4194328
  157.4 4.0 %outputs.1 = (bf16[2,96,1024]{2,1,0:T(8,128)(2,1)}, bf16[2,96,1024]{2,1,0:T(8,128)(2,1)}) custom-call(s32[2]{0:T(128)S(1)} %pad_add_fusion.place_ref, bf16[8,2,192,128]{3,2,1,0:T(8,128)(2,1)S(1)} %bitcast.17, bf16[8,192,128]{2,1,0:T(8,128)(2,1)S(1)} %collective-permute-done.3.arrived_ref, bf16[4,1024,512]{2,1,0:T(8,128)(2,1)S(1)} %copy-done), custom_call_target="tpu_custom_call" | custom-call | flops 805306368 | bytes 7340032 | tf_op jit(solution)/shard_map/outputs/pallas_call | solution.py:315
  161.3 0.3 all-to-all-done.4.parts_ref
  161.6 0.0 copy-start.2
  161.6 0.7 copy-done.2
  162.3 1.8 %spread_heads.1 = bf16[4,64,512]{2,1,0:T(8,128)(2,1)} custom-call(bf16[8,64,256]{2,1,0:T(8,128)(2,1)} %copy-done.2), custom_call_target="tpu_custom_call" | custom-call | tf_op jit(solution)/shard_map/spread_heads/pallas_call | solution.py:266
  (5 shorter events, 0.1 us)
Async XLA Ops:
  7.2 110.1 %all-gather.7.cloned.1.call-start = ((), (), s32[]{:S(2)}) async-start(), calls=%async_computation.5 | async-start | bytes 3538944 | tf_op jit(solution)/shard_map/all_gather | solution.py:347
  7.9 109.3 %all-gather.9.cloned.1.call-start = ((), (), s32[]{:S(2)}) async-start(), calls=%async_computation.6 | async-start | bytes 3538944 | tf_op jit(solution)/shard_map/all_gather | solution.py:347
  16.7 37.7 %copy-start.3 = (s32[1,4]{1,0:T(1,128)S(1)}, s32[1,4]{1,0:T(1,128)}, u32[]{:S(2)}) copy-start(s32[1,4]{1,0:T(1,128)} %param.5) | copy-start | bytes 52
  51.3 4.5 %collective-permute-start.1 = (bf16[16,96,128]{2,1,0:T(8,128)(2,1)S(1)}, bf16[16,96,128]{2,1,0:T(8,128)(2,1)S(1)}, u32[]{:S(2)}, u32[]{:S(2)}) collective-permute-start(bf16[16,96,128]{2,1,0:T(8,128)(2,1)S(1)} %slice.4), channel_id=1, source_target_pairs={{0,16},{16,0},{32,48},{48,32},{64,80},{80,64},{96,112},{112,96},{1... | collective-permute-start | bytes 1179656 | tf_op jit(solution)/shard_map/ppermute | solution.py:356
  54.4 1.3 collective-permute-start
  71.0 2.0 %collective-permute-start.2 = (bf16[16,96,128]{2,1,0:T(8,128)(2,1)S(1)}, bf16[16,96,128]{2,1,0:T(8,128)(2,1)S(1)}, u32[]{:S(2)}, u32[]{:S(2)}) collective-permute-start(bf16[16,96,128]{2,1,0:T(8,128)(2,1)S(1)} %get-tuple-element.10), channel_id=1, source_target_pairs={{0,16},{16,0},{32,48},{48,32},{64,80},{80,64},{96,112},{112,96},{1... | collective-permute-start | bytes 1179656 | tf_op jit(solution)/shard_map/ppermute | solution.py:359
  117.2 1.9 %copy-start.1 = (bf16[8,1,2,96,1024]{4,3,2,1,0:T(8,128)(2,1)S(1)}, bf16[8,1,2,96,1024]{4,3,2,1,0:T(8,128)(2,1)}, u32[]{:S(2)}) copy-start(bf16[8,1,2,96,1024]{4,3,2,1,0:T(8,128)(2,1)} %all-gather.7.cloned.1.call-done) | copy-start | bytes 9437188
  124.4 20.0 %all-to-all-start.3 = ((bf16[16,64,256]{2,1,0:T(8,128)(2,1)}), bf16[16,64,256]{2,1,0:T(8,128)(2,1)S(1)}, u32[]{:S(2)}, u32[]{:S(2)}) async-start(bf16[16,64,256]{2,1,0:T(8,128)(2,1)} %weight_terms.1), calls=%async_computation.3 | async-start | bytes 1048576 | tf_op jit(solution)/shard_map/all_to_all | solution.py:365
  144.5 2.9 %collective-permute-start.4 = (bf16[64,256]{1,0:T(8,128)(2,1)S(1)}, bf16[64,256]{1,0:T(8,128)(2,1)S(1)}, u32[]{:S(2)}, u32[]{:S(2)}) collective-permute-start(bf16[64,256]{1,0:T(8,128)(2,1)S(1)} %reduce-precision_convert_fusion), channel_id=1, source_target_pairs={{0,32},{16,48},{32,0},{48,16},{64,96},{80,112},{96,64},{112,80},{1... | collective-permute-start | bytes 98312 | tf_op jit(solution)/shard_map/ppermute | solution.py:372
  144.7 10.5 %collective-permute-start.3 = (bf16[8,192,128]{2,1,0:T(8,128)(2,1)S(1)}, bf16[8,192,128]{2,1,0:T(8,128)(2,1)S(1)}, u32[]{:S(2)}, u32[]{:S(2)}) collective-permute-start(bf16[8,192,128]{2,1,0:T(8,128)(2,1)S(1)} %dynamic-slice_bitcast_fusion), channel_id=1, source_target_pairs={{0,16},{16,0},{32,48},{48,32},{64,80},{80,64},{96,112},{112,96},{1... | collective-permute-start | bytes 1179656 | tf_op jit(solution)/shard_map/ppermute | solution.py:366
  148.1 13.5 %all-to-all-start.4 = ((bf16[8,64,256]{2,1,0:T(8,128)(2,1)}), bf16[8,64,256]{2,1,0:T(8,128)(2,1)S(1)}, u32[]{:S(2)}, u32[]{:S(2)}) async-start(bf16[8,64,256]{2,1,0:T(8,128)(2,1)} %broadcast_in_dim.3), calls=%async_computation.4 | async-start | bytes 524288 | tf_op jit(solution)/shard_map/all_to_all | solution.py:375
  155.2 2.2 %copy-start = (bf16[4,1024,512]{2,1,0:T(8,128)(2,1)S(1)}, bf16[4,1024,512]{2,1,0:T(8,128)(2,1)}, u32[]{:S(2)}) copy-start(bf16[4,1024,512]{2,1,0:T(8,128)(2,1)} %weights_ref.3) | copy-start | bytes 12582916
  161.6 0.7 copy-start.2
Sparse Core Ops, SparseCore 0:
  9.8 34.4 all-gather.6
  46.2 30.3 all-gather.8

commit v3 on v2

--- a/solution.py
+++ b/solution.py
@@ -1,5 +1,3 @@
-import functools
-
 import jax
 import jax.numpy as jnp
 from jax import lax
@@ -19,9 +17,10 @@
 NEGATIVE = -1e30
 VMEM_LIMIT = 48 * 1024 * 1024
 
-CORE_PAIRS = [[2 * i, 2 * i + 1] for i in range(8)]
 CORE_SWAP = [(i, i ^ 1) for i in range(16)]
 X_LINES = [[4 * x + 2 * z + core for x in range(4) for core in range(2)] for z in range(2)]
+CHIP_LINES = [[4 * x + rest for x in range(4)] for rest in range(4)]
+X_SHIFTS = [[(i, (i + 4 * shift) % 16) for i in range(16)] for shift in range(1, 4)]
 Z_SWAP = [(i, i ^ 2) for i in range(16)]
 
 
@@ -29,9 +28,10 @@
     return lax.broadcasted_iota(jnp.int32, (rows, 128), 1) < HEAD
 
 
-def project_kernel(block_ref, tokens_ref, upstream_ref, weights_ref, out_ref):
-    inputs = tokens_ref[...].reshape(2 * SPAN, D)
-    upstream = upstream_ref[...].reshape(2 * SPAN, D)
+def project_kernel(core_ref, mine_ref, arrived_ref, weights_ref, out_ref):
+    core = core_ref[0]
+    inputs = jnp.concatenate([mine_ref[0], arrived_ref[0]], axis=0)
+    upstream = jnp.concatenate([mine_ref[1], arrived_ref[1]], axis=0)
 
     def product(rows, number):
         return jnp.dot(rows, weights_ref[number], preferred_element_type=jnp.float32)
@@ -40,20 +40,21 @@
     grads = product(upstream, 3)
     low = low_lanes(2 * SPAN)
     for half, (first, second) in enumerate(((queries, grads), (keys, values))):
+        place = slice(SPAN * half, SPAN * half + SPAN)
         for pair in range(2):
             one = first[:, 128 * pair : 128 * pair + 128]
             two = second[:, 128 * pair : 128 * pair + 128]
             even = jnp.where(low, one, pltpu.roll(two, HEAD, 1)).astype(jnp.bfloat16)
             odd = jnp.where(low, pltpu.roll(one, HEAD, 1), two).astype(jnp.bfloat16)
-            for sequence in range(2):
-                rows = slice(SPAN * sequence, SPAN * sequence + SPAN)
-                place = slice(SPAN * half, SPAN * half + SPAN)
+            for part in range(2):
+                rows = slice(SPAN * part, SPAN * part + SPAN)
+                sequence = jnp.bitwise_xor(core, part)
                 out_ref[2 * pair, sequence, place, :] = even[rows]
                 out_ref[2 * pair + 1, sequence, place, :] = odd[rows]
 
 
-def project(block, tokens_pair, upstream_pair, weights):
-    tokens_spec = pl.BlockSpec((2, 1, SPAN, D), lambda j, block: (0, block[0], 0, 0))
+def project(core, mine, arrived, weights):
+    block_spec = pl.BlockSpec((2, SPAN, D), lambda j, core: (0, 0, 0))
     return pl.pallas_call(
         project_kernel,
         out_shape=jax.ShapeDtypeStruct((HEADS, 2, 2 * SPAN, 128), jnp.bfloat16),
@@ -61,15 +62,15 @@
             num_scalar_prefetch=1,
             grid=(2,),
             in_specs=[
-                tokens_spec,
-                tokens_spec,
-                pl.BlockSpec((4, D, HQ // 2), lambda j, block: (0, 0, j)),
+                block_spec,
+                block_spec,
+                pl.BlockSpec((4, D, HQ // 2), lambda j, core: (0, 0, j)),
             ],
-            out_specs=pl.BlockSpec((HEADS // 2, 2, 2 * SPAN, 128), lambda j, block: (j, 0, 0, 0)),
+            out_specs=pl.BlockSpec((HEADS // 2, 2, 2 * SPAN, 128), lambda j, core: (j, 0, 0, 0)),
         ),
         compiler_params=pltpu.CompilerParams(vmem_limit_bytes=VMEM_LIMIT),
         name="project",
-    )(block, tokens_pair, upstream_pair, weights)
+    )(core, mine, arrived, weights)
 
 
 def attend_kernel(
@@ -94,39 +95,50 @@
         key_ref[tile_rows(tile), :] = own_ref[rank, SPAN:, :]
         key_ref[tile_rows(TILES - 1 - tile), :] = other_ref[rank]
 
-    low = low_lanes(SPAN)
-    scale = HEAD ** -0.5
-
-    def attend(rank, tile, start, chunks):
+
+    def tile_start(tile):
+        return jnp.where(
+            tile >= third, third, jnp.where(tile >= second, second, jnp.where(tile >= first, first, 0))
+        )
+
+    def holder(tile):
+        return jnp.where(tile < RANKS, tile, TILES - 1 - tile)
+
+    def two_tiles(tile, chunks):
+        start, next_start = tile_start(tile), tile_start(tile + 2)
         base = pl.multiple_of(start * SPAN, SPAN)
-        packed = own_ref[rank, :SPAN, :]
-        query_only = jnp.where(low, packed, jnp.zeros_like(packed))
+        ranks = (holder(tile), holder(tile + 2))
+        packed = jnp.concatenate([own_ref[rank, :SPAN, :] for rank in ranks], axis=0)
+        low = low_lanes(2 * SPAN)
+        query_only = jnp.where(low, packed, jnp.zeros_like(packed)) * jnp.bfloat16(HEAD ** -0.5)
         grad_only = jnp.where(low, jnp.zeros_like(packed), packed)
         left = jnp.concatenate([query_only, grad_only], axis=0)
         right = jnp.concatenate([grad_only, query_only], axis=0)
+        row = lax.broadcasted_iota(jnp.int32, (2 * SPAN, CHUNK), 0)
+        lane = lax.broadcasted_iota(jnp.int32, (2 * SPAN, CHUNK), 1)
+        upper = row < SPAN
+        last = row + (tile - start) * SPAN + jnp.where(upper, 0, SPAN) - lane
+        earliest = jnp.where(upper, 0, (next_start - start) * SPAN) - lane
 
         def rows(j):
             return pl.ds(pl.multiple_of(base + CHUNK * j, 32), CHUNK)
 
-        top = jnp.full((SPAN, 1), NEGATIVE, jnp.float32)
+        top = jnp.full((2 * SPAN, 1), NEGATIVE, jnp.float32)
         for j in range(chunks):
             both = lax.dot_general(
                 left, key_ref[rows(j), :], (((1,), (1,)), ((), ())),
                 preferred_element_type=jnp.float32,
             )
-            scores = both[:SPAN] * scale
-            if j >= chunks - 2:
-                gap = (tile - start) * SPAN - CHUNK * j
-                ahead = lax.broadcasted_iota(jnp.int32, (SPAN, CHUNK), 1) - lax.broadcasted_iota(
-                    jnp.int32, (SPAN, CHUNK), 0
-                )
-                scores = jnp.where(ahead <= gap, scores, NEGATIVE)
+            allowed = earliest <= CHUNK * j
+            if j >= chunks - 3:
+                allowed = jnp.logical_and(allowed, last >= CHUNK * j)
+            scores = jnp.where(allowed, both[: 2 * SPAN], NEGATIVE)
             place = slice(CHUNK * j, CHUNK * j + CHUNK)
             score_ref[:, place] = scores
-            prob_grad_ref[:, place] = both[SPAN:]
+            prob_grad_ref[:, place] = both[2 * SPAN :]
             top = jnp.maximum(top, jnp.max(scores, axis=1, keepdims=True))
-        total = jnp.zeros((SPAN, 1), jnp.float32)
-        accum = jnp.zeros((SPAN, 128), jnp.float32)
+        total = jnp.zeros((2 * SPAN, 1), jnp.float32)
+        accum = jnp.zeros((2 * SPAN, 128), jnp.float32)
         for j in range(chunks):
             place = slice(CHUNK * j, CHUNK * j + CHUNK)
             expo = jnp.exp(score_ref[:, place] - top)
@@ -140,11 +152,11 @@
         delta = jnp.sum(
             grad_only.astype(jnp.float32) * context.astype(jnp.float32), axis=1, keepdims=True
         )
-        query_grad = jnp.zeros((SPAN, 128), jnp.float32)
+        query_grad = jnp.zeros((2 * SPAN, 128), jnp.float32)
         for j in range(chunks):
             place = slice(CHUNK * j, CHUNK * j + CHUNK)
             probs = score_ref[:, place] * inverse
-            score_grad = (probs * (prob_grad_ref[:, place] - delta) * scale).astype(jnp.bfloat16)
+            score_grad = (probs * (prob_grad_ref[:, place] - delta)).astype(jnp.bfloat16)
             query_grad = query_grad + jnp.dot(
                 score_grad, key_ref[rows(j), :], preferred_element_type=jnp.float32
             )
@@ -152,21 +164,20 @@
             grad_ref[rows(j), :] += lax.dot_general(
                 stacked, right, (((0,), (0,)), ((), ())), preferred_element_type=jnp.float32
             )
-        out_ref[rank] = jnp.where(low, query_grad, context.astype(jnp.float32)).astype(jnp.bfloat16)
-
-    def one_tile(rank, carry):
-        tile = own_tile(rank)
-        start = jnp.where(
-            tile >= third, third, jnp.where(tile >= second, second, jnp.where(tile >= first, first, 0))
-        )
-        chunks = ((tile - start + 1) * SPAN + CHUNK - 1) // CHUNK
-        for count in range(1, 7):
+        merged = jnp.where(low, query_grad * HEAD ** -0.5, context.astype(jnp.float32)).astype(jnp.bfloat16)
+        out_ref[ranks[0]] = merged[:SPAN]
+        out_ref[ranks[1]] = merged[SPAN:]
+
+    def one_step(step, carry):
+        tile = core + 4 * step
+        chunks = ((tile + 3 - tile_start(tile)) * SPAN + CHUNK - 1) // CHUNK
+        for count in range(2, 8):
             @pl.when(chunks == count)
             def _():
-                attend(rank, tile, start, count)
+                two_tiles(tile, count)
         return carry
 
-    lax.fori_loop(0, RANKS, one_tile, 0)
+    lax.fori_loop(0, TILES // 4, one_step, 0)
     for rank in range(RANKS):
         tile = own_tile(rank)
         own_grad_ref[rank] = grad_ref[tile_rows(tile), :]
@@ -189,61 +200,73 @@
         scratch_shapes=[
             pltpu.VMEM((KEY_ROWS, 128), jnp.bfloat16),
             pltpu.VMEM((KEY_ROWS, 128), jnp.float32),
-            pltpu.VMEM((SPAN, 6 * CHUNK), jnp.float32),
-            pltpu.VMEM((SPAN, 6 * CHUNK), jnp.float32),
+            pltpu.VMEM((2 * SPAN, 7 * CHUNK), jnp.float32),
+            pltpu.VMEM((2 * SPAN, 7 * CHUNK), jnp.float32),
         ],
         compiler_params=pltpu.CompilerParams(vmem_limit_bytes=VMEM_LIMIT),
         name="attend",
     )(core, tiles, own, other)
 
 
-def weight_kernel(odd_ref, grads_ref, tokens_ref, upstream_ref, out_ref, held_ref):
-    odd = odd_ref[0]
+def weight_kernel(place_ref, grads_ref, *refs):
+    line_refs, (keep_ref, give_ref, held_ref) = refs[:4], refs[4:]
+    core, column = place_ref[0], place_ref[1]
 
     @pl.when(pl.program_id(0) == 0)
     def _():
-        for chip in range(4):
-            for sequence in range(2):
-                for block in range(2):
-                    holder = 2 * chip + jnp.bitwise_xor(odd, block)
-                    first = (4 * chip + 2 * sequence + block) * SPAN
+        for shift in range(4):
+            chip = jnp.bitwise_and(column + 4 - shift, 3)
+            for part in range(2):
+                sequence = jnp.bitwise_xor(core, part)
+                first = (2 * shift + part) * SPAN
+                for head in range(2):
                     for half in range(2):
-                        held_ref[first : first + SPAN, 128 * half : 128 * half + 128] = grads_ref[
-                            holder, sequence, SPAN * half : SPAN * half + SPAN, :
+                        lanes = 128 * (2 * half + head)
+                        held_ref[first : first + SPAN, lanes : lanes + 128] = grads_ref[
+                            chip, head, sequence, SPAN * half : SPAN * half + SPAN, :
                         ]
 
-    def product(rows_ref, columns):
-        rows = rows_ref[...].reshape(16 * SPAN, D // 4)
+    def product(kind, columns):
+        rows = jnp.concatenate([ref[part, kind] for ref in line_refs for part in range(2)], axis=0)
         return lax.dot_general(
             rows, held_ref[:, :columns], (((0,), (0,)), ((), ())), preferred_element_type=jnp.float32
         )
 
-    by_tokens = product(tokens_ref, 256)
-    by_upstream = product(upstream_ref, 128)
-    first = jnp.where(low_lanes(D // 4), by_tokens[:, :128], by_upstream)
-    out_ref[:, :, :128] = first.astype(jnp.bfloat16).reshape(4, 64, 128)
-    out_ref[:, :, 128:] = by_tokens[:, 128:].astype(jnp.bfloat16).reshape(4, 64, 128)
-
-
-def weight_terms(odd, grads, tokens_line, upstream_line):
-    tokens_spec = pl.BlockSpec((8, 2, SPAN, D // 4), lambda j, odd: (0, 0, 0, j))
+    by_tokens = product(0, 512)
+    by_upstream = product(1, 256)
+    low = low_lanes(D // 4)
+    firsts = [
+        jnp.where(low, by_tokens[:, 128 * i : 128 * i + 128], by_upstream[:, 128 * i : 128 * i + 128])
+        for i in range(2)
+    ]
+    seconds = [by_tokens[:, 256:384], by_tokens[:, 384:]]
+    for lanes, (zero, one) in ((slice(0, 128), firsts), (slice(128, 256), seconds)):
+        kept = jnp.where(core == 0, zero, one).astype(jnp.bfloat16)
+        given = jnp.where(core == 0, one, zero).astype(jnp.bfloat16)
+        keep_ref[:, :, lanes] = kept.reshape(4, 64, 128)
+        give_ref[:, :, lanes] = given.reshape(4, 64, 128)
+
+
+def weight_terms(place, grads, lines):
+    shape = jax.ShapeDtypeStruct((RANKS, 64, 256), jnp.bfloat16)
+    line_spec = pl.BlockSpec((2, 2, SPAN, D // 4), lambda j, place: (0, 0, 0, j))
+    out_spec = pl.BlockSpec((4, 64, 256), lambda j, place: (j, 0, 0))
     return pl.pallas_call(
         weight_kernel,
-        out_shape=jax.ShapeDtypeStruct((RANKS, 64, 256), jnp.bfloat16),
+        out_shape=(shape, shape),
         grid_spec=pltpu.PrefetchScalarGridSpec(
             num_scalar_prefetch=1,
             grid=(4,),
             in_specs=[
-                pl.BlockSpec((8, 2, 2 * SPAN, 128), lambda j, odd: (0, 0, 0, 0)),
-                tokens_spec,
-                tokens_spec,
+                pl.BlockSpec((4, 2, 2, 2 * SPAN, 128), lambda j, place: (0, 0, 0, 0, 0)),
+                line_spec, line_spec, line_spec, line_spec,
             ],
-            out_specs=pl.BlockSpec((4, 64, 256), lambda j, odd: (j, 0, 0)),
-            scratch_shapes=[pltpu.VMEM((16 * SPAN, 256), jnp.bfloat16)],
+            out_specs=(out_spec, out_spec),
+            scratch_shapes=[pltpu.VMEM((8 * SPAN, 512), jnp.bfloat16)],
         ),
         compiler_params=pltpu.CompilerParams(vmem_limit_bytes=VMEM_LIMIT),
         name="weight_terms",
-    )(odd, grads, tokens_line, upstream_line)
+    )(place, grads, *lines)
 
 
 def spread_kernel(parts_ref, out_ref):
@@ -336,38 +359,49 @@
 
 def per_device(tokens, sweep_tiles, weights, cotangent):
     core = lax.axis_index("dp") % 2
+    column = lax.axis_index("dp") // 4
     rank = lax.axis_index("ctx")
     odd = rank % 2
-    gather_pair = functools.partial(
-        lax.all_gather, axis_name="dp", axis_index_groups=CORE_PAIRS, axis=0, tiled=True
-    )
-    tokens_pair = gather_pair(tokens.reshape(1, 2, SPAN, D))
-    upstream_pair = gather_pair(cotangent.reshape(1, 2, SPAN, D))
-    tokens_line, upstream_line = (
-        lax.all_gather(
-            rows.reshape(1, 2, SPAN, D), "dp", axis_index_groups=X_LINES, axis=0, tiled=True
+    block = jnp.bitwise_xor(core, odd)
+
+    def chosen(number):
+        return jnp.stack(
+            [
+                lax.dynamic_index_in_dim(rows.reshape(2, SPAN, D), number, 0, keepdims=False)
+                for rows in (tokens, cotangent)
+            ]
         )
-        for rows in (tokens, cotangent)
-    )
+
+    mine = chosen(block)
+    arrived = lax.ppermute(chosen(1 - block), "dp", CORE_SWAP)
     other_tiles = lax.ppermute(sweep_tiles, "dp", CORE_SWAP)
-    block = jnp.bitwise_xor(core, odd).astype(jnp.int32).reshape(1)
-    packed = project(block, tokens_pair, upstream_pair, weights).reshape(RANKS, 2 * SPAN, 128)
+    core_number = core.astype(jnp.int32).reshape(1)
+    packed = project(core_number, mine, arrived, weights).reshape(RANKS, 2 * SPAN, 128)
+    line = jnp.stack([mine, arrived])
+    lines = [line] + [lax.ppermute(line, "dp", shift) for shift in X_SHIFTS]
     own = lax.all_to_all(packed, "ctx", 0, 0)
     other = lax.ppermute(own[:, SPAN:], "dp", CORE_SWAP)
     tiles = jnp.where(odd == core, sweep_tiles, other_tiles).reshape(-1)
-    query_part, own_grad, other_grad = attend(core.astype(jnp.int32).reshape(1), tiles, own, other)
+    query_part, own_grad, other_grad = attend(core_number, tiles, own, other)
     arrived = lax.ppermute(other_grad, "dp", CORE_SWAP)
     key_part = (own_grad + arrived.astype(jnp.float32)).astype(jnp.bfloat16)
     back = lax.all_to_all(jnp.concatenate([query_part, key_part], axis=1), "ctx", 0, 0)
     grads = back.reshape(HEADS, 2, 2 * SPAN, 128)
-    line = lax.all_to_all(grads, "dp", 0, 0, axis_index_groups=X_LINES)
-    terms = weight_terms(odd.astype(jnp.int32).reshape(1), line, tokens_line, upstream_line)
+    line_grads = lax.all_to_all(
+        back.reshape(4, 2, 2, 2 * SPAN, 128), "dp", 0, 0, axis_index_groups=CHIP_LINES
+    )
+    keep, give = weight_terms(
+        jnp.stack([core, column]).astype(jnp.int32), line_grads, lines
+    )
+    given = lax.ppermute(give, "dp", CORE_SWAP)
+    terms = (keep.astype(jnp.float32) + given.astype(jnp.float32)).astype(jnp.bfloat16)
     terms = lax.all_to_all(terms, "ctx", 0, 0)
     swapped = lax.ppermute(
         lax.dynamic_index_in_dim(grads, 1 - core, 1, keepdims=False), "dp", CORE_SWAP
     )
     place = jnp.stack([core, odd]).astype(jnp.int32)
     attn_out, input_grad = outputs(place, grads, swapped, weights)
+    terms, attn_out, input_grad = lax.optimization_barrier((terms, attn_out, input_grad))
     rows = lax.reduce_precision(jnp.sum(terms.astype(jnp.float32), axis=0), 8, 7)
     other_rows = lax.ppermute(rows.astype(jnp.bfloat16), "dp", Z_SWAP)
     factor = float(16 * RANKS * 2 * SPAN) ** -0.5

time: 172 us -> 165 us (0.959)
  blocking collectives: 83.7 us -> 44.6 us
  waiting for transfers between devices: 21 us -> 57.2 us
  starting transfers between devices: 16.9 us -> 30.7 us
  between operations: 14.1 us -> 0.8 us
  Pallas kernels: 29.3 us -> 22.4 us
  other arithmetic: 0.34 us -> 2.46 us
    all_to_all x2 -> x1, blocking collectives: 44.1 us -> 13 us  [per_device(): lax.all_to_all(jnp.broadcast_to(rows, (HEADS, 64, 256)), 'dp', 0, 0, axis...]
    all_to_all x1 -> x2, waiting for transfers between devices: 0.27 us -> 26.7 us  [the longest x1 19.4 us: per_device(): lax.all_to_all(jnp.concatenate([query_part, key_part], axis=1), 'ctx', 0, 0)]
    ppermute x0 -> x5, waiting for transfers between devices: none -> 16.6 us  [the longest x3 13.7 us: per_device(): lines = [line] + [lax.ppermute(line, 'dp', shift) for shift in X_SHIFTS]]
    all_to_all x1, waiting for transfers between devices: 16.5 us -> 7.29 us  [per_device(): terms = lax.all_to_all(terms, 'ctx', 0, 0)]
    ppermute x0 -> x5, starting transfers between devices: none -> 8.6 us  [the longest x3 3.66 us: per_device(): lines = [line] + [lax.ppermute(line, 'dp', shift) for shift in X_SHIFTS]]
    all_gather x2 -> x0, blocking collectives: 8.02 us -> none  [the longest x1 5.45 us: per_device(): tokens_pair = gather_pair(tokens.reshape(1, 2, SPAN, D))]
    pallas_call x1, Pallas kernels: 15.2 us -> 9.78 us  [attend(): pl.pallas_call(attend_kernel, out_shape=(jax.ShapeDtypeStruct(block, jnp....]
    all_to_all x1, starting transfers between devices: 3.57 us -> 8.94 us  [per_device(): terms = lax.all_to_all(terms, 'ctx', 0, 0)]
  transfers between devices with their start and end apart: 9 -> 13, of which waited for: 4 -> 11; matrix products, arithmetic and copies ran while one was open for 1% -> 1% of each run, Pallas kernels for 13% -> 3%
where the time goes in v3:
time: 165 us
  waiting for transfers between devices  57.2 us (35%)
  blocking collectives  44.6 us (27%)
  starting transfers between devices  30.7 us (19%)
  Pallas kernels  22.4 us (14%)
  local copies, waits for them, and re-layouts  6.75 us (4%)
  other arithmetic  2.46 us (1%)
    all_to_all x1, blocking collectives, per_device(): own = lax.all_to_all(packed, 'ctx', 0, 0)  31.6 us
    all_to_all x1, waiting for transfers between devices, per_device(): lax.all_to_all(jnp.concatenate([query_part, key_part], axis=1), 'ctx', 0, 0)  19.4 us
    ppermute x3, waiting for transfers between devices, per_device(): lines = [line] + [lax.ppermute(line, 'dp', shift) for shift in X_SHIFTS]  13.7 us
    all_to_all x1, blocking collectives, per_device(): lax.all_to_all(jnp.broadcast_to(rows, (HEADS, 64, 256)), 'dp', 0, 0, axis...  13 us
    pallas_call x1, Pallas kernels, attend(): pl.pallas_call(attend_kernel, out_shape=(jax.ShapeDtypeStruct(block, jnp....  9.78 us
    all_to_all x1, starting transfers between devices, per_device(): terms = lax.all_to_all(terms, 'ctx', 0, 0)  8.94 us
    all_to_all x1, waiting for transfers between devices, per_device(): lax.all_to_all(back.reshape(4, 2, 2, 2 * SPAN, 128), 'dp', 0, 0, axis_ind...  7.33 us
    all_to_all x1, waiting for transfers between devices, per_device(): terms = lax.all_to_all(terms, 'ctx', 0, 0)  7.29 us
  transfers between devices with their start and end apart: 13, of which 11 were waited for; matrix products, arithmetic and copies ran while one was open for 1% of the time, Pallas kernels for 3%

profile of v3, /device:TPU:1, one launch (start us, length us, event | category | flops | bytes accessed | tf_op | source)
XLA Modules:
  0.0 164.9 jit_solution(10048745862657349825)
XLA Ops:
  0.7 1.3 dynamic-slice_bitcast_fusion.1
  2.0 3.3 %collective-permute-start.1 = (bf16[2,96,1024]{2,1,0:T(8,128)(2,1)S(1)}, bf16[2,96,1024]{2,1,0:T(8,128)(2,1)S(1)}, u32[]{:S(2)}, u32[]{:S(2)}) collective-permute-start(bf16[2,96,1024]{2,1,0:T(8,128)(2,1)S(1)} %pad_maximum_fusion.3), channel_id=1, source_target_pairs={{0,16},{16,0},{32,48},{48,32},{64,80},{80,64},{96,112},{112,96},{1... | collective-permute-start | bytes 1179656 | tf_op jit(solution)/shard_map/ppermute | solution.py:376
  5.3 0.1 fusion.1
  5.4 1.3 collective-permute-done.1.arrived_ref
  6.7 0.0 copy-start
  6.7 2.2 %copy-done = bf16[4,1024,512]{2,1,0:T(8,128)(2,1)S(1)} copy-done((bf16[4,1024,512]{2,1,0:T(8,128)(2,1)S(1)}, bf16[4,1024,512]{2,1,0:T(8,128)(2,1)}, u32[]{:S(2)}) %copy-start) | copy-done | bytes 4194328
  8.9 1.7 %project.1 = bf16[8,2,192,128]{3,2,1,0:T(8,128)(2,1)S(1)} custom-call(s32[1]{0:T(128)} %bitcast.core_ref, bf16[2,96,1024]{2,1,0:T(8,128)(2,1)S(1)} %get-tuple-element.24.mine_ref, bf16[2,96,1024]{2,1,0:T(8,128)(2,1)S(1)} %collective-permute-done.1.arrived_ref, bf16[4,1024,512]{2,1,0:T(8,128)(2,1)S(1)} %copy-done), custom_call_target="tpu_custom_call" | custom-call | tf_op jit(solution)/shard_map/project/pallas_call | solution.py:58
  10.5 0.0 copy-start.2
  10.5 31.6 %all_to_all.25.own_ref = bf16[16,192,128]{2,1,0:T(8,128)(2,1)S(1)} all-to-all(bf16[16,192,128]{2,1,0:T(8,128)(2,1)S(1)} %bitcast.23), channel_id=1, replica_groups=mesh['dp'=16,'ctx'=16] {'ctx'}, dimensions={0} | all-to-all | bytes 1572864 | tf_op jit(solution)/shard_map/all_to_all | solution.py:382
  42.2 3.2 %collective-permute-start.2 = (bf16[16,96,128]{2,1,0:T(8,128)(2,1)S(1)}, bf16[16,96,128]{2,1,0:T(8,128)(2,1)S(1)}, u32[]{:S(2)}, u32[]{:S(2)}) collective-permute-start(bf16[16,96,128]{2,1,0:T(8,128)(2,1)S(1)} %slice.4), channel_id=1, source_target_pairs={{0,16},{16,0},{32,48},{48,32},{64,80},{80,64},{96,112},{112,96},{1... | collective-permute-start | bytes 1179656 | tf_op jit(solution)/shard_map/ppermute | solution.py:383
  45.3 0.0 copy-done.2
  45.3 0.1 collective-permute-start
  45.4 1.2 collective-permute-done
  46.7 0.0 collective-permute-done.2.other_ref
  46.7 9.8 %attend.1 = (bf16[16,96,128]{2,1,0:T(8,128)(2,1)S(1)}, f32[16,96,128]{2,1,0:T(8,128)S(1)}, bf16[16,96,128]{2,1,0:T(8,128)(2,1)S(1)}) custom-call(s32[1]{0:T(128)} %bitcast.core_ref, s32[4]{0:T(128)S(1)} %fusion.tiles_ref, bf16[16,192,128]{2,1,0:T(8,128)(2,1)S(1)} %all_to_all.25.own_ref, bf16[16,96,128]{2,1,0:T(8,128)(2,1)S(1)} %collective-permute-done.2.other_ref), custom_call_target="tpu_custom_call" | custom-call | tf_op jit(solution)/shard_map/attend/pallas_call | solution.py:191
  56.5 0.7 collective-permute-start.3
  57.2 1.3 collective-permute-done.3
  58.5 0.1 add_convert_fusion.1
  58.6 1.0 pad_maximum_fusion
  59.6 4.3 %all-to-all-start.1 = ((bf16[16,192,128]{2,1,0:T(8,128)(2,1)}), bf16[16,192,128]{2,1,0:T(8,128)(2,1)}, u32[]{:S(2)}, u32[]{:S(2)}) async-start(bf16[16,192,128]{2,1,0:T(8,128)(2,1)} %pad_maximum_fusion), calls=%async_computation.1 | async-start | bytes 1572864 | tf_op jit(solution)/shard_map/all_to_all | solution.py:388
  63.9 0.1 pad_maximum_fusion.1.refs_0_
  64.0 3.0 %collective-permute-start.6 = (bf16[2,2,96,1024]{3,2,1,0:T(8,128)(2,1)S(1)}, bf16[2,2,96,1024]{3,2,1,0:T(8,128)(2,1)S(1)}, u32[]{:S(2)}, u32[]{:S(2)}) collective-permute-start(bf16[2,2,96,1024]{3,2,1,0:T(8,128)(2,1)S(1)} %pad_maximum_fusion.1.refs_0_), channel_id=1, source_target_pairs={{0,192},{16,208},{32,224},{48,240},{64,0},{80,16},{96,32},{112,48}... | collective-permute-start | bytes 2359304 | tf_op jit(solution)/shard_map/ppermute | solution.py:381
  67.0 0.3 collective-permute-start.5
  67.3 0.3 collective-permute-start.4
  67.6 19.4 %all-to-all-done.1 = bf16[16,192,128]{2,1,0:T(8,128)(2,1)} async-done(((bf16[16,192,128]{2,1,0:T(8,128)(2,1)}), bf16[16,192,128]{2,1,0:T(8,128)(2,1)}, u32[]{:S(2)}, u32[]{:S(2)}) %all-to-all-start.1) | async-done | bytes 786464 | tf_op jit(solution)/shard_map/all_to_all | solution.py:388
  87.0 4.1 %all-to-all-start.2 = ((bf16[4,2,2,192,128]{4,3,2,1,0:T(8,128)(2,1)}), bf16[4,2,2,192,128]{4,3,2,1,0:T(8,128)(2,1)S(1)}, u32[]{:S(2)}, u32[]{:S(2)}) async-start(bf16[4,2,2,192,128]{4,3,2,1,0:T(8,128)(2,1)} %bitcast.8), calls=%async_computation.2 | async-start | bytes 1572864 | tf_op jit(solution)/shard_map/all_to_all | solution.py:390
  91.1 0.1 pad_add_fusion.place_ref
  91.2 8.6 %collective-permute-done.6.refs_3_ = bf16[2,2,96,1024]{3,2,1,0:T(8,128)(2,1)S(1)} collective-permute-done((bf16[2,2,96,1024]{3,2,1,0:T(8,128)(2,1)S(1)}, bf16[2,2,96,1024]{3,2,1,0:T(8,128)(2,1)S(1)}, u32[]{:S(2)}, u32[]{:S(2)}) %collective-permute-start.6) | collective-permute-done | bytes 786464 | tf_op jit(solution)/shard_map/ppermute | solution.py:381
  99.8 0.0 collective-permute-done.5.refs_2_
  99.8 5.1 %collective-permute-done.4.refs_1_ = bf16[2,2,96,1024]{3,2,1,0:T(8,128)(2,1)} collective-permute-done((bf16[2,2,96,1024]{3,2,1,0:T(8,128)(2,1)S(1)}, bf16[2,2,96,1024]{3,2,1,0:T(8,128)(2,1)}, u32[]{:S(2)}, u32[]{:S(2)}) %collective-permute-start.4) | collective-permute-done | bytes 786464 | tf_op jit(solution)/shard_map/ppermute | solution.py:381
  104.9 7.3 %all-to-all-done.2.grads_ref = bf16[4,2,2,192,128]{4,3,2,1,0:T(8,128)(2,1)S(1)} async-done(((bf16[4,2,2,192,128]{4,3,2,1,0:T(8,128)(2,1)}), bf16[4,2,2,192,128]{4,3,2,1,0:T(8,128)(2,1)S(1)}, u32[]{:S(2)}, u32[]{:S(2)}) %all-to-all-start.2) | async-done | bytes 786464 | tf_op jit(solution)/shard_map/all_to_all | solution.py:390
  112.2 4.3 %weight_terms.1 = (bf16[16,64,256]{2,1,0:T(8,128)(2,1)S(1)}, bf16[16,64,256]{2,1,0:T(8,128)(2,1)S(1)}) custom-call(s32[2]{0:T(128)S(1)} %pad_add_fusion.place_ref, bf16[4,2,2,192,128]{4,3,2,1,0:T(8,128)(2,1)S(1)} %all-to-all-done.2.grads_ref, bf16[2,2,96,1024]{3,2,1,0:T(8,128)(2,1)S(1)} %pad_maximum_fusion.1.refs_0_, ...), custom_call_target="tpu_custom_call" | custom-call | tf_op jit(solution)/shard_map/weight_terms/pallas_call | solution.py:254
  116.5 1.6 collective-permute-start.7
  118.2 1.5 collective-permute-done.7
  119.7 1.0 add_convert_fusion
  120.7 8.9 %all-to-all-start.3 = ((bf16[16,64,256]{2,1,0:T(8,128)(2,1)}), bf16[16,64,256]{2,1,0:T(8,128)(2,1)S(1)}, u32[]{:S(2)}, u32[]{:S(2)}) async-start(bf16[16,64,256]{2,1,0:T(8,128)(2,1)} %add_convert_fusion), calls=%async_computation.3 | async-start | bytes 1048576 | tf_op jit(solution)/shard_map/all_to_all | solution.py:398
  129.6 1.0 dynamic-slice_bitcast_fusion
  130.6 0.7 collective-permute-start.8
  131.4 0.1 pad_add_fusion.1.place_ref
  131.5 1.3 collective-permute-done.8.arrived_ref
  132.7 2.2 %copy-done.1 = bf16[4,1024,512]{2,1,0:T(8,128)(2,1)S(1)} copy-done((bf16[4,1024,512]{2,1,0:T(8,128)(2,1)S(1)}, bf16[4,1024,512]{2,1,0:T(8,128)(2,1)}, u32[]{:S(2)}) %copy-start.1) | copy-done | bytes 4194328
  134.9 4.9 %outputs.1 = (bf16[2,96,1024]{2,1,0:T(8,128)(2,1)}, bf16[2,96,1024]{2,1,0:T(8,128)(2,1)}) custom-call(s32[2]{0:T(128)S(1)} %pad_add_fusion.1.place_ref, bf16[8,2,192,128]{3,2,1,0:T(8,128)(2,1)} %bitcast.12.grads_ref, bf16[8,192,128]{2,1,0:T(8,128)(2,1)S(1)} %collective-permute-done.8.arrived_ref, bf16[4,1024,512]{2,1,0:T(8,128)(2,1)S(1)} %copy-done.1), custom_call_target="tpu_custom_call" | custom-call | flops 805306368 | bytes 7340032 | tf_op jit(solution)/shard_map/outputs/pallas_call | solution.py:338
  139.8 7.3 %all-to-all-done.3 = bf16[16,64,256]{2,1,0:T(8,128)(2,1)S(1)} async-done(((bf16[16,64,256]{2,1,0:T(8,128)(2,1)}), bf16[16,64,256]{2,1,0:T(8,128)(2,1)S(1)}, u32[]{:S(2)}, u32[]{:S(2)}) %all-to-all-start.3) | async-done | bytes 524320 | tf_op jit(solution)/shard_map/all_to_all | solution.py:398
  147.1 0.1 convert_reduce_fusion
  147.2 0.1 collective-permute-start.9
  147.3 2.8 %collective-permute-done.9 = bf16[64,256]{1,0:T(8,128)(2,1)S(1)} collective-permute-done((bf16[64,256]{1,0:T(8,128)(2,1)S(1)}, bf16[64,256]{1,0:T(8,128)(2,1)S(1)}, u32[]{:S(2)}, u32[]{:S(2)}) %collective-permute-start.9) | collective-permute-done | bytes 32800 | tf_op jit(solution)/shard_map/ppermute | solution.py:406
  150.1 13.0 %all_to_all.26.parts_ref = bf16[8,64,256]{2,1,0:T(8,128)(2,1)} all-to-all(bf16[8,64,256]{2,1,0:T(8,128)(2,1)S(1)} %broadcast_in_dim.3), channel_id=1, replica_groups={{0,16,64,80,128,144,192,208},{32,48,96,112,160,176,224,240},{1,17,65,81..., dimensions={0} | all-to-all | bytes 524288 | tf_op jit(solution)/shard_map/all_to_all | solution.py:409
  163.1 1.8 %spread_heads.1 = bf16[4,64,512]{2,1,0:T(8,128)(2,1)} custom-call(bf16[8,64,256]{2,1,0:T(8,128)(2,1)} %all_to_all.26.parts_ref), custom_call_target="tpu_custom_call" | custom-call | tf_op jit(solution)/shard_map/spread_heads/pallas_call | solution.py:289
  (7 shorter events, 0.1 us)
Async XLA Ops:
  2.0 4.7 %collective-permute-start.1 = (bf16[2,96,1024]{2,1,0:T(8,128)(2,1)S(1)}, bf16[2,96,1024]{2,1,0:T(8,128)(2,1)S(1)}, u32[]{:S(2)}, u32[]{:S(2)}) collective-permute-start(bf16[2,96,1024]{2,1,0:T(8,128)(2,1)S(1)} %pad_maximum_fusion.3), channel_id=1, source_target_pairs={{0,16},{16,0},{32,48},{48,32},{64,80},{80,64},{96,112},{112,96},{1... | collective-permute-start | bytes 1179656 | tf_op jit(solution)/shard_map/ppermute | solution.py:376
  6.7 2.2 %copy-start = (bf16[4,1024,512]{2,1,0:T(8,128)(2,1)S(1)}, bf16[4,1024,512]{2,1,0:T(8,128)(2,1)}, u32[]{:S(2)}) copy-start(bf16[4,1024,512]{2,1,0:T(8,128)(2,1)} %weights_ref.3) | copy-start | bytes 12582916
  10.5 34.8 %copy-start.2 = (s32[1,4]{1,0:T(1,128)S(1)}, s32[1,4]{1,0:T(1,128)}, u32[]{:S(2)}) copy-start(s32[1,4]{1,0:T(1,128)} %param.5) | copy-start | bytes 52
  42.2 4.5 %collective-permute-start.2 = (bf16[16,96,128]{2,1,0:T(8,128)(2,1)S(1)}, bf16[16,96,128]{2,1,0:T(8,128)(2,1)S(1)}, u32[]{:S(2)}, u32[]{:S(2)}) collective-permute-start(bf16[16,96,128]{2,1,0:T(8,128)(2,1)S(1)} %slice.4), channel_id=1, source_target_pairs={{0,16},{16,0},{32,48},{48,32},{64,80},{80,64},{96,112},{112,96},{1... | collective-permute-start | bytes 1179656 | tf_op jit(solution)/shard_map/ppermute | solution.py:383
  45.3 1.3 collective-permute-start
  56.5 2.1 %collective-permute-start.3 = (bf16[16,96,128]{2,1,0:T(8,128)(2,1)S(1)}, bf16[16,96,128]{2,1,0:T(8,128)(2,1)S(1)}, u32[]{:S(2)}, u32[]{:S(2)}) collective-permute-start(bf16[16,96,128]{2,1,0:T(8,128)(2,1)S(1)} %get-tuple-element.15), channel_id=1, source_target_pairs={{0,16},{16,0},{32,48},{48,32},{64,80},{80,64},{96,112},{112,96},{1... | collective-permute-start | bytes 1179656 | tf_op jit(solution)/shard_map/ppermute | solution.py:386
  59.6 27.4 %all-to-all-start.1 = ((bf16[16,192,128]{2,1,0:T(8,128)(2,1)}), bf16[16,192,128]{2,1,0:T(8,128)(2,1)}, u32[]{:S(2)}, u32[]{:S(2)}) async-start(bf16[16,192,128]{2,1,0:T(8,128)(2,1)} %pad_maximum_fusion), calls=%async_computation.1 | async-start | bytes 1572864 | tf_op jit(solution)/shard_map/all_to_all | solution.py:388
  64.0 35.8 %collective-permute-start.6 = (bf16[2,2,96,1024]{3,2,1,0:T(8,128)(2,1)S(1)}, bf16[2,2,96,1024]{3,2,1,0:T(8,128)(2,1)S(1)}, u32[]{:S(2)}, u32[]{:S(2)}) collective-permute-start(bf16[2,2,96,1024]{3,2,1,0:T(8,128)(2,1)S(1)} %pad_maximum_fusion.1.refs_0_), channel_id=1, source_target_pairs={{0,192},{16,208},{32,224},{48,240},{64,0},{80,16},{96,32},{112,48}... | collective-permute-start | bytes 2359304 | tf_op jit(solution)/shard_map/ppermute | solution.py:381
  67.0 32.8 %collective-permute-start.5 = (bf16[2,2,96,1024]{3,2,1,0:T(8,128)(2,1)S(1)}, bf16[2,2,96,1024]{3,2,1,0:T(8,128)(2,1)S(1)}, u32[]{:S(2)}, u32[]{:S(2)}) collective-permute-start(bf16[2,2,96,1024]{3,2,1,0:T(8,128)(2,1)S(1)} %pad_maximum_fusion.1.refs_0_), channel_id=1, source_target_pairs={{0,128},{16,144},{32,160},{48,176},{64,192},{80,208},{96,224},{112... | collective-permute-start | bytes 2359304 | tf_op jit(solution)/shard_map/ppermute | solution.py:381
  67.3 37.6 %collective-permute-start.4 = (bf16[2,2,96,1024]{3,2,1,0:T(8,128)(2,1)S(1)}, bf16[2,2,96,1024]{3,2,1,0:T(8,128)(2,1)}, u32[]{:S(2)}, u32[]{:S(2)}) collective-permute-start(bf16[2,2,96,1024]{3,2,1,0:T(8,128)(2,1)S(1)} %pad_maximum_fusion.1.refs_0_), channel_id=1, source_target_pairs={{0,64},{16,80},{32,96},{48,112},{64,128},{80,144},{96,160},{112,17... | collective-permute-start | bytes 2359304 | tf_op jit(solution)/shard_map/ppermute | solution.py:381
  87.0 25.2 %all-to-all-start.2 = ((bf16[4,2,2,192,128]{4,3,2,1,0:T(8,128)(2,1)}), bf16[4,2,2,192,128]{4,3,2,1,0:T(8,128)(2,1)S(1)}, u32[]{:S(2)}, u32[]{:S(2)}) async-start(bf16[4,2,2,192,128]{4,3,2,1,0:T(8,128)(2,1)} %bitcast.8), calls=%async_computation.2 | async-start | bytes 1572864 | tf_op jit(solution)/shard_map/all_to_all | solution.py:390
  116.5 3.1 %collective-permute-start.7 = (bf16[16,64,256]{2,1,0:T(8,128)(2,1)S(1)}, bf16[16,64,256]{2,1,0:T(8,128)(2,1)S(1)}, u32[]{:S(2)}, u32[]{:S(2)}) collective-permute-start(bf16[16,64,256]{2,1,0:T(8,128)(2,1)S(1)} %get-tuple-element.17), channel_id=1, source_target_pairs={{0,16},{16,0},{32,48},{48,32},{64,80},{80,64},{96,112},{112,96},{1... | collective-permute-start | bytes 1572872 | tf_op jit(solution)/shard_map/ppermute | solution.py:396
  120.7 26.5 %all-to-all-start.3 = ((bf16[16,64,256]{2,1,0:T(8,128)(2,1)}), bf16[16,64,256]{2,1,0:T(8,128)(2,1)S(1)}, u32[]{:S(2)}, u32[]{:S(2)}) async-start(bf16[16,64,256]{2,1,0:T(8,128)(2,1)} %add_convert_fusion), calls=%async_computation.3 | async-start | bytes 1048576 | tf_op jit(solution)/shard_map/all_to_all | solution.py:398
  130.6 2.1 %collective-permute-start.8 = (bf16[8,192,128]{2,1,0:T(8,128)(2,1)S(1)}, bf16[8,192,128]{2,1,0:T(8,128)(2,1)S(1)}, u32[]{:S(2)}, u32[]{:S(2)}) collective-permute-start(bf16[8,192,128]{2,1,0:T(8,128)(2,1)S(1)} %dynamic-slice_bitcast_fusion), channel_id=1, source_target_pairs={{0,16},{16,0},{32,48},{48,32},{64,80},{80,64},{96,112},{112,96},{1... | collective-permute-start | bytes 1179656 | tf_op jit(solution)/shard_map/ppermute | solution.py:399
  132.7 2.2 %copy-start.1 = (bf16[4,1024,512]{2,1,0:T(8,128)(2,1)S(1)}, bf16[4,1024,512]{2,1,0:T(8,128)(2,1)}, u32[]{:S(2)}) copy-start(bf16[4,1024,512]{2,1,0:T(8,128)(2,1)} %weights_ref.3) | copy-start | bytes 12582916
  147.2 2.9 %collective-permute-start.9 = (bf16[64,256]{1,0:T(8,128)(2,1)S(1)}, bf16[64,256]{1,0:T(8,128)(2,1)S(1)}, u32[]{:S(2)}, u32[]{:S(2)}) collective-permute-start(bf16[64,256]{1,0:T(8,128)(2,1)S(1)} %reduce-precision_convert_fusion), channel_id=1, source_target_pairs={{0,32},{16,48},{32,0},{48,16},{64,96},{80,112},{96,64},{112,80},{1... | collective-permute-start | bytes 98312 | tf_op jit(solution)/shard_map/ppermute | solution.py:406

commit v4 on v3

--- a/solution.py
+++ b/solution.py
@@ -16,22 +16,31 @@
 KEY_ROWS = TILES * SPAN + CHUNK
 NEGATIVE = -1e30
 VMEM_LIMIT = 48 * 1024 * 1024
+PROJECT_VMEM = 51 * 1024 * 1024
 
 CORE_SWAP = [(i, i ^ 1) for i in range(16)]
-X_LINES = [[4 * x + 2 * z + core for x in range(4) for core in range(2)] for z in range(2)]
 CHIP_LINES = [[4 * x + rest for x in range(4)] for rest in range(4)]
 X_SHIFTS = [[(i, (i + 4 * shift) % 16) for i in range(16)] for shift in range(1, 4)]
-Z_SWAP = [(i, i ^ 2) for i in range(16)]
 
 
 def low_lanes(rows):
     return lax.broadcasted_iota(jnp.int32, (rows, 128), 1) < HEAD
 
 
-def project_kernel(core_ref, mine_ref, arrived_ref, weights_ref, out_ref):
-    core = core_ref[0]
-    inputs = jnp.concatenate([mine_ref[0], arrived_ref[0]], axis=0)
-    upstream = jnp.concatenate([mine_ref[1], arrived_ref[1]], axis=0)
+def project_kernel(
+    place_ref, tokens_ref, other_tokens_ref, upstream_ref, other_upstream_ref, weights_ref,
+    out_ref, line_ref,
+):
+    core = place_ref[0]
+    inputs = jnp.concatenate([tokens_ref[0], other_tokens_ref[0]], axis=0)
+    upstream = jnp.concatenate([upstream_ref[0], other_upstream_ref[0]], axis=0)
+
+    @pl.when(pl.program_id(0) == 0)
+    def _():
+        line_ref[0, 0] = tokens_ref[0]
+        line_ref[0, 1] = upstream_ref[0]
+        line_ref[1, 0] = other_tokens_ref[0]
+        line_ref[1, 1] = other_upstream_ref[0]
 
     def product(rows, number):
         return jnp.dot(rows, weights_ref[number], preferred_element_type=jnp.float32)
@@ -53,24 +62,29 @@
                 out_ref[2 * pair + 1, sequence, place, :] = odd[rows]
 
 
-def project(core, mine, arrived, weights):
-    block_spec = pl.BlockSpec((2, SPAN, D), lambda j, core: (0, 0, 0))
+def project(place, rows, weights):
+    block_spec = pl.BlockSpec((1, SPAN, D), lambda j, place: (place[1], 0, 0))
     return pl.pallas_call(
         project_kernel,
-        out_shape=jax.ShapeDtypeStruct((HEADS, 2, 2 * SPAN, 128), jnp.bfloat16),
+        out_shape=(
+            jax.ShapeDtypeStruct((HEADS, 2, 2 * SPAN, 128), jnp.bfloat16),
+            jax.ShapeDtypeStruct((2, 2, SPAN, D), jnp.bfloat16),
+        ),
         grid_spec=pltpu.PrefetchScalarGridSpec(
             num_scalar_prefetch=1,
             grid=(2,),
             in_specs=[
-                block_spec,
-                block_spec,
-                pl.BlockSpec((4, D, HQ // 2), lambda j, core: (0, 0, j)),
+                block_spec, block_spec, block_spec, block_spec,
+                pl.BlockSpec((4, D, HQ // 2), lambda j, place: (0, 0, j)),
             ],
-            out_specs=pl.BlockSpec((HEADS // 2, 2, 2 * SPAN, 128), lambda j, core: (j, 0, 0, 0)),
-        ),
-        compiler_params=pltpu.CompilerParams(vmem_limit_bytes=VMEM_LIMIT),
+            out_specs=(
+                pl.BlockSpec((HEADS // 2, 2, 2 * SPAN, 128), lambda j, place: (j, 0, 0, 0)),
+                pl.BlockSpec((2, 2, SPAN, D), lambda j, place: (0, 0, 0, 0)),
+            ),
+        ),
+        compiler_params=pltpu.CompilerParams(vmem_limit_bytes=PROJECT_VMEM),
         name="project",
-    )(core, mine, arrived, weights)
+    )(place, *rows, weights)
 
 
 def attend_kernel(
@@ -271,12 +285,19 @@
 
 def spread_kernel(parts_ref, out_ref):
     low = low_lanes(64)
-    for pair in range(HEADS // 2):
-        columns = slice(128 * pair, 128 * pair + 128)
+    factor = float(16 * RANKS * 2 * SPAN) ** -0.5
+    for column in range(4):
+        columns = slice(128 * column, 128 * column + 128)
         for half, (lower, upper) in enumerate(((0, 3), (1, 2))):
             lanes = slice(128 * half, 128 * half + 128)
-            one = parts_ref[2 * pair, :, lanes].astype(jnp.float32)
-            two = parts_ref[2 * pair + 1, :, lanes].astype(jnp.float32)
+            one, two = (
+                factor
+                * (
+                    parts_ref[column, 0, core, :, lanes].astype(jnp.float32)
+                    + parts_ref[column, 1, core, :, lanes].astype(jnp.float32)
+                )
+                for core in range(2)
+            )
             out_ref[lower, :, columns] = jnp.where(low, one, pltpu.roll(two, HEAD, 1)).astype(
                 jnp.bfloat16
             )
@@ -364,23 +385,23 @@
     odd = rank % 2
     block = jnp.bitwise_xor(core, odd)
 
-    def chosen(number):
-        return jnp.stack(
-            [
-                lax.dynamic_index_in_dim(rows.reshape(2, SPAN, D), number, 0, keepdims=False)
-                for rows in (tokens, cotangent)
-            ]
-        )
-
-    mine = chosen(block)
-    arrived = lax.ppermute(chosen(1 - block), "dp", CORE_SWAP)
+    rows = tokens.reshape(2, SPAN, D)
+    upstream = cotangent.reshape(2, SPAN, D)
+    other_rows = lax.ppermute(rows, "dp", CORE_SWAP)
+    other_upstream = lax.ppermute(upstream, "dp", CORE_SWAP)
     other_tiles = lax.ppermute(sweep_tiles, "dp", CORE_SWAP)
     core_number = core.astype(jnp.int32).reshape(1)
-    packed = project(core_number, mine, arrived, weights).reshape(RANKS, 2 * SPAN, 128)
-    line = jnp.stack([mine, arrived])
-    lines = [line] + [lax.ppermute(line, "dp", shift) for shift in X_SHIFTS]
+    packed, line = project(
+        jnp.stack([core, block]).astype(jnp.int32),
+        (rows, other_rows, upstream, other_upstream),
+        weights,
+    )
+    packed = packed.reshape(RANKS, 2 * SPAN, 128)
+    shifted = [lax.ppermute(line, "dp", shift) for shift in X_SHIFTS]
     own = lax.all_to_all(packed, "ctx", 0, 0)
+    own, *shifted = lax.optimization_barrier((own, *shifted))
     other = lax.ppermute(own[:, SPAN:], "dp", CORE_SWAP)
+    lines = [line, *shifted]
     tiles = jnp.where(odd == core, sweep_tiles, other_tiles).reshape(-1)
     query_part, own_grad, other_grad = attend(core_number, tiles, own, other)
     arrived = lax.ppermute(other_grad, "dp", CORE_SWAP)
@@ -395,21 +416,17 @@
     )
     given = lax.ppermute(give, "dp", CORE_SWAP)
     terms = (keep.astype(jnp.float32) + given.astype(jnp.float32)).astype(jnp.bfloat16)
+    terms, own_grads = lax.optimization_barrier((terms, grads))
     terms = lax.all_to_all(terms, "ctx", 0, 0)
     swapped = lax.ppermute(
         lax.dynamic_index_in_dim(grads, 1 - core, 1, keepdims=False), "dp", CORE_SWAP
     )
     place = jnp.stack([core, odd]).astype(jnp.int32)
-    attn_out, input_grad = outputs(place, grads, swapped, weights)
+    attn_out, input_grad = outputs(place, own_grads, swapped, weights)
     terms, attn_out, input_grad = lax.optimization_barrier((terms, attn_out, input_grad))
-    rows = lax.reduce_precision(jnp.sum(terms.astype(jnp.float32), axis=0), 8, 7)
-    other_rows = lax.ppermute(rows.astype(jnp.bfloat16), "dp", Z_SWAP)
-    factor = float(16 * RANKS * 2 * SPAN) ** -0.5
-    rows = ((rows + other_rows.astype(jnp.float32)) * factor).astype(jnp.bfloat16)
-    parts = lax.all_to_all(
-        jnp.broadcast_to(rows, (HEADS, 64, 256)), "dp", 0, 0, axis_index_groups=X_LINES
-    )
-    weight_grads = spread_heads(parts)
+    rows = jnp.sum(terms.astype(jnp.float32), axis=0).astype(jnp.bfloat16)
+    parts = lax.all_to_all(jnp.broadcast_to(rows, (16, 64, 256)), "dp", 0, 0)
+    weight_grads = spread_heads(parts.reshape(4, 2, 2, 64, 256))
     return (attn_out.reshape(tokens.shape), input_grad.reshape(tokens.shape), weight_grads)
 
 

time: 165 us -> 172 us (1.042)
  starting transfers between devices: 30.7 us -> 34.8 us
  Pallas kernels: 22.4 us -> 24.6 us
    all_to_all x1, waiting for transfers between devices: 19.4 us -> 0.01 us  [per_device(): own = lax.all_to_all(packed, 'ctx', 0, 0)]
    ppermute x5, waiting for transfers between devices: 17.8 us -> 34.6 us  [the longest x3 32.7 us: per_device(): shifted = [lax.ppermute(line, 'dp', shift) for shift in X_SHIFTS]]
    all_to_all x1, starting transfers between devices: 4.28 us -> 9.32 us  [per_device(): own = lax.all_to_all(packed, 'ctx', 0, 0)]
    all_to_all x1, starting transfers between devices: 8.94 us -> 4.47 us  [per_device(): terms = lax.all_to_all(terms, 'ctx', 0, 0)]
    all_to_all x1, starting transfers between devices: 4.08 us -> 6.83 us  [per_device(): lax.all_to_all(back.reshape(4, 2, 2, 2 * SPAN, 128), 'dp', 0, 0, axis_ind...]
    pallas_call x1, Pallas kernels: 1.66 us -> 4.41 us  [project(): pl.pallas_call(project_kernel, out_shape=(jax.ShapeDtypeStruct((HEADS, 2,...]
    all_to_all x1, waiting for transfers between devices: 7.33 us -> 9.9 us  [per_device(): lax.all_to_all(back.reshape(4, 2, 2, 2 * SPAN, 128), 'dp', 0, 0, axis_ind...]
    unnamed x6 -> x14, local copies, waits for them, and re-layouts: 4.38 us -> 6.24 us
where the time goes in v4:
time: 172 us
  waiting for transfers between devices  55.9 us (32%)
  blocking collectives  46.3 us (27%)
  starting transfers between devices  34.8 us (20%)
  Pallas kernels  24.6 us (14%)
  local copies, waits for them, and re-layouts  8.08 us (5%)
    ppermute x3, waiting for transfers between devices, per_device(): shifted = [lax.ppermute(line, 'dp', shift) for shift in X_SHIFTS]  32.7 us
    all_to_all x1, blocking collectives, per_device(): lax.all_to_all(jnp.concatenate([query_part, key_part], axis=1), 'ctx', 0, 0)  29.3 us
    all_to_all x1, blocking collectives, per_device(): parts = lax.all_to_all(jnp.broadcast_to(rows, (16, 64, 256)), 'dp', 0, 0)  17 us
    pallas_call x1, Pallas kernels, attend(): pl.pallas_call(attend_kernel, out_shape=(jax.ShapeDtypeStruct(block, jnp....  10.1 us
    all_to_all x1, waiting for transfers between devices, per_device(): lax.all_to_all(back.reshape(4, 2, 2, 2 * SPAN, 128), 'dp', 0, 0, axis_ind...  9.9 us
    all_to_all x1, starting transfers between devices, per_device(): own = lax.all_to_all(packed, 'ctx', 0, 0)  9.32 us
    all_to_all x1, starting transfers between devices, per_device(): lax.all_to_all(back.reshape(4, 2, 2, 2 * SPAN, 128), 'dp', 0, 0, axis_ind...  6.83 us
    unnamed x14, local copies, waits for them, and re-layouts  6.24 us
  transfers between devices with their start and end apart: 13, of which 11 were waited for; matrix products, arithmetic and copies ran while one was open for 1% of the time, Pallas kernels for 3%

profile of v4, /device:TPU:1, one launch (start us, length us, event | category | flops | bytes accessed | tf_op | source)
XLA Modules:
  0.0 171.8 jit_solution(13732032436758147974)
XLA Ops:
  0.6 3.3 %collective-permute-start.1 = (bf16[2,96,1024]{2,1,0:T(8,128)(2,1)}, bf16[2,96,1024]{2,1,0:T(8,128)(2,1)S(1)}, u32[]{:S(2)}, u32[]{:S(2)}) collective-permute-start(bf16[2,96,1024]{2,1,0:T(8,128)(2,1)} %bitcast.16), channel_id=1, source_target_pairs={{0,16},{16,0},{32,48},{48,32},{64,80},{80,64},{96,112},{112,96},{1... | collective-permute-start | bytes 1179656 | tf_op jit(solution)/shard_map/ppermute | solution.py:390
  4.0 0.1 collective-permute-start.2
  4.1 0.1 pad_add_fusion.1.place_ref
  4.1 1.4 collective-permute-done.1.other_tokens_ref
  5.5 0.6 collective-permute-done.2.other_upstream_ref
  6.1 1.0 copy-done.4
  7.1 1.0 copy-done.5
  8.1 4.4 %project.1 = (bf16[8,2,192,128]{3,2,1,0:T(8,128)(2,1)}, bf16[2,2,96,1024]{3,2,1,0:T(8,128)(2,1)}) custom-call(s32[2]{0:T(128)S(1)} %pad_add_fusion.1.place_ref, bf16[2,96,1024]{2,1,0:T(8,128)(2,1)S(1)} %bitcast.17, bf16[2,96,1024]{2,1,0:T(8,128)(2,1)S(1)} %collective-permute-done.1.other_tokens_ref, bf16[2,96,1024]{2,1,0:T(8,128)(2,1)S(1)} %bitcast.19, ...), custom_call_target="tpu_custom_call" | custom-call | tf_op jit(solution)/shard_map/project/pallas_call | solution.py:67
  12.5 9.3 %all-to-all-start = ((bf16[16,192,128]{2,1,0:T(8,128)(2,1)}), bf16[16,192,128]{2,1,0:T(8,128)(2,1)S(1)}, u32[]{:S(2)}, u32[]{:S(2)}) async-start(bf16[16,192,128]{2,1,0:T(8,128)(2,1)} %bitcast.6), calls=%async_computation | async-start | bytes 1572864 | tf_op jit(solution)/shard_map/all_to_all | solution.py:401
  21.8 0.0 copy-done.1
  21.8 1.3 collective-permute-start.3
  23.1 2.4 %collective-permute-start.4 = (bf16[2,2,96,1024]{3,2,1,0:T(8,128)(2,1)S(1)}, bf16[2,2,96,1024]{3,2,1,0:T(8,128)(2,1)S(1)}, u32[]{:S(2)}, u32[]{:S(2)}) collective-permute-start(bf16[2,2,96,1024]{3,2,1,0:T(8,128)(2,1)S(1)} %copy-done.1), channel_id=1, source_target_pairs={{0,128},{16,144},{32,160},{48,176},{64,192},{80,208},{96,224},{112... | collective-permute-start | bytes 2359304 | tf_op jit(solution)/shard_map/ppermute | solution.py:400
  25.6 1.2 collective-permute-start.5
  26.7 14.8 %collective-permute-done.3.refs_1_ = bf16[2,2,96,1024]{3,2,1,0:T(8,128)(2,1)S(1)} collective-permute-done((bf16[2,2,96,1024]{3,2,1,0:T(8,128)(2,1)S(1)}, bf16[2,2,96,1024]{3,2,1,0:T(8,128)(2,1)S(1)}, u32[]{:S(2)}, u32[]{:S(2)}) %collective-permute-start.3) | collective-permute-done | bytes 786464 | tf_op jit(solution)/shard_map/ppermute | solution.py:400
  41.5 17.8 %collective-permute-done.4.refs_2_ = bf16[2,2,96,1024]{3,2,1,0:T(8,128)(2,1)S(1)} collective-permute-done((bf16[2,2,96,1024]{3,2,1,0:T(8,128)(2,1)S(1)}, bf16[2,2,96,1024]{3,2,1,0:T(8,128)(2,1)S(1)}, u32[]{:S(2)}, u32[]{:S(2)}) %collective-permute-start.4) | collective-permute-done | bytes 786464 | tf_op jit(solution)/shard_map/ppermute | solution.py:400
  59.4 0.0 collective-permute-done.5.refs_3_
  59.4 0.9 copy-done.2
  60.3 0.0 all-to-all-done.own_ref
  60.3 0.8 slice.3
  61.1 1.5 collective-permute-start.6
  62.6 0.0 collective-permute-start
  62.6 1.2 collective-permute-done
  63.8 0.4 collective-permute-done.6.other_ref
  64.2 10.1 %attend.1 = (bf16[16,96,128]{2,1,0:T(8,128)(2,1)S(1)}, f32[16,96,128]{2,1,0:T(8,128)S(1)}, bf16[16,96,128]{2,1,0:T(8,128)(2,1)S(1)}) custom-call(s32[1]{0:T(128)} %bitcast.core_ref, s32[4]{0:T(128)S(1)} %fusion.tiles_ref, bf16[16,192,128]{2,1,0:T(8,128)(2,1)S(1)} %all-to-all-done.own_ref, bf16[16,96,128]{2,1,0:T(8,128)(2,1)S(1)} %collective-permute-done.6.other_ref), custom_call_target="tpu_custom_call" | custom-call | tf_op jit(solution)/shard_map/attend/pallas_call | solution.py:205
  74.2 0.2 collective-permute-start.7
  74.5 1.6 collective-permute-done.7
  76.1 0.1 add_convert_fusion.1
  76.1 0.1 pad_maximum_fusion
  76.2 29.3 %all_to_all.25 = bf16[16,192,128]{2,1,0:T(8,128)(2,1)} all-to-all(bf16[16,192,128]{2,1,0:T(8,128)(2,1)S(1)} %pad_maximum_fusion), channel_id=1, replica_groups=mesh['dp'=16,'ctx'=16] {'ctx'}, dimensions={0} | all-to-all | bytes 1572864 | tf_op jit(solution)/shard_map/all_to_all | solution.py:409
  105.6 6.8 %all-to-all-start.2 = ((bf16[4,2,2,192,128]{4,3,2,1,0:T(8,128)(2,1)}), bf16[4,2,2,192,128]{4,3,2,1,0:T(8,128)(2,1)S(1)}, u32[]{:S(2)}, u32[]{:S(2)}) async-start(bf16[4,2,2,192,128]{4,3,2,1,0:T(8,128)(2,1)} %bitcast.7), calls=%async_computation.2 | async-start | bytes 1572864 | tf_op jit(solution)/shard_map/all_to_all | solution.py:411
  112.4 0.1 pad_add_fusion.place_ref
  112.5 9.9 %all-to-all-done.2.grads_ref = bf16[4,2,2,192,128]{4,3,2,1,0:T(8,128)(2,1)S(1)} async-done(((bf16[4,2,2,192,128]{4,3,2,1,0:T(8,128)(2,1)}), bf16[4,2,2,192,128]{4,3,2,1,0:T(8,128)(2,1)S(1)}, u32[]{:S(2)}, u32[]{:S(2)}) %all-to-all-start.2) | async-done | bytes 786464 | tf_op jit(solution)/shard_map/all_to_all | solution.py:411
  122.4 1.1 copy-done.3
  123.5 3.3 %weight_terms.1 = (bf16[16,64,256]{2,1,0:T(8,128)(2,1)S(1)}, bf16[16,64,256]{2,1,0:T(8,128)(2,1)S(1)}) custom-call(s32[2]{0:T(128)S(1)} %pad_add_fusion.place_ref, bf16[4,2,2,192,128]{4,3,2,1,0:T(8,128)(2,1)S(1)} %all-to-all-done.2.grads_ref, bf16[2,2,96,1024]{3,2,1,0:T(8,128)(2,1)S(1)} %copy-done.1, ...), custom_call_target="tpu_custom_call" | custom-call | tf_op jit(solution)/shard_map/weight_terms/pallas_call | solution.py:268
  126.8 3.3 %collective-permute-start.8 = (bf16[16,64,256]{2,1,0:T(8,128)(2,1)S(1)}, bf16[16,64,256]{2,1,0:T(8,128)(2,1)S(1)}, u32[]{:S(2)}, u32[]{:S(2)}) collective-permute-start(bf16[16,64,256]{2,1,0:T(8,128)(2,1)S(1)} %get-tuple-element.31), channel_id=1, source_target_pairs={{0,16},{16,0},{32,48},{48,32},{64,80},{80,64},{96,112},{112,96},{1... | collective-permute-start | bytes 1572872 | tf_op jit(solution)/shard_map/ppermute | solution.py:417
  130.2 1.5 collective-permute-done.8
  131.7 1.0 add_convert_fusion
  132.7 4.5 %all-to-all-start.3 = ((bf16[16,64,256]{2,1,0:T(8,128)(2,1)}), bf16[16,64,256]{2,1,0:T(8,128)(2,1)S(1)}, u32[]{:S(2)}, u32[]{:S(2)}) async-start(bf16[16,64,256]{2,1,0:T(8,128)(2,1)} %add_convert_fusion), calls=%async_computation.3 | async-start | bytes 1048576 | tf_op jit(solution)/shard_map/all_to_all | solution.py:420
  137.2 1.0 dynamic-slice_bitcast_fusion
  138.2 0.7 collective-permute-start.9
  139.0 0.1 pad_add_fusion.2.place_ref
  139.0 1.3 collective-permute-done.9.arrived_ref
  140.3 2.2 %copy-done = bf16[4,1024,512]{2,1,0:T(8,128)(2,1)S(1)} copy-done((bf16[4,1024,512]{2,1,0:T(8,128)(2,1)S(1)}, bf16[4,1024,512]{2,1,0:T(8,128)(2,1)}, u32[]{:S(2)}) %copy-start) | copy-done | bytes 4194328
  142.5 4.9 %outputs.1 = (bf16[2,96,1024]{2,1,0:T(8,128)(2,1)}, bf16[2,96,1024]{2,1,0:T(8,128)(2,1)}) custom-call(s32[2]{0:T(128)S(1)} %pad_add_fusion.2.place_ref, bf16[8,2,192,128]{3,2,1,0:T(8,128)(2,1)} %bitcast.8.grads_ref, bf16[8,192,128]{2,1,0:T(8,128)(2,1)S(1)} %collective-permute-done.9.arrived_ref, bf16[4,1024,512]{2,1,0:T(8,128)(2,1)S(1)} %copy-done), custom_call_target="tpu_custom_call" | custom-call | flops 805306368 | bytes 7340032 | tf_op jit(solution)/shard_map/outputs/pallas_call | solution.py:359
  147.4 5.4 %all-to-all-done.3 = bf16[16,64,256]{2,1,0:T(8,128)(2,1)S(1)} async-done(((bf16[16,64,256]{2,1,0:T(8,128)(2,1)}), bf16[16,64,256]{2,1,0:T(8,128)(2,1)S(1)}, u32[]{:S(2)}, u32[]{:S(2)}) %all-to-all-start.3) | async-done | bytes 524320 | tf_op jit(solution)/shard_map/all_to_all | solution.py:420
  152.8 0.1 reduce_sum.12
  153.0 17.0 %all_to_all.26 = bf16[16,64,256]{2,1,0:T(8,128)(2,1)} all-to-all(bf16[16,64,256]{2,1,0:T(8,128)(2,1)S(1)} %broadcast_in_dim.3), channel_id=1, replica_groups=mesh['dp'=16,'ctx'=16] {'dp'}, dimensions={0} | all-to-all | bytes 1048576 | tf_op jit(solution)/shard_map/all_to_all | solution.py:428
  169.9 1.9 %spread_heads.1 = bf16[4,64,512]{2,1,0:T(8,128)(2,1)} custom-call(bf16[4,2,2,64,256]{4,3,2,1,0:T(8,128)(2,1)} %bitcast.20), custom_call_target="tpu_custom_call" | custom-call | tf_op jit(solution)/shard_map/spread_heads/pallas_call | solution.py:310
  (10 shorter events, 0.1 us)
Async XLA Ops:
  0.6 4.9 %collective-permute-start.1 = (bf16[2,96,1024]{2,1,0:T(8,128)(2,1)}, bf16[2,96,1024]{2,1,0:T(8,128)(2,1)S(1)}, u32[]{:S(2)}, u32[]{:S(2)}) collective-permute-start(bf16[2,96,1024]{2,1,0:T(8,128)(2,1)} %bitcast.16), channel_id=1, source_target_pairs={{0,16},{16,0},{32,48},{48,32},{64,80},{80,64},{96,112},{112,96},{1... | collective-permute-start | bytes 1179656 | tf_op jit(solution)/shard_map/ppermute | solution.py:390
  4.0 2.1 %collective-permute-start.2 = (bf16[2,96,1024]{2,1,0:T(8,128)(2,1)}, bf16[2,96,1024]{2,1,0:T(8,128)(2,1)S(1)}, u32[]{:S(2)}, u32[]{:S(2)}) collective-permute-start(bf16[2,96,1024]{2,1,0:T(8,128)(2,1)} %bitcast.18), channel_id=1, source_target_pairs={{0,16},{16,0},{32,48},{48,32},{64,80},{80,64},{96,112},{112,96},{1... | collective-permute-start | bytes 1179656 | tf_op jit(solution)/shard_map/ppermute | solution.py:391
  6.1 1.0 copy-start.4
  7.1 1.0 copy-start.5
  12.5 9.3 %copy-start.1 = (bf16[2,2,96,1024]{3,2,1,0:T(8,128)(2,1)S(1)}, bf16[2,2,96,1024]{3,2,1,0:T(8,128)(2,1)}, u32[]{:S(2)}) copy-start(bf16[2,2,96,1024]{3,2,1,0:T(8,128)(2,1)} %get-tuple-element.22.refs_0_) | copy-start | bytes 2359300
  12.5 50.1 %copy-start.6 = (s32[1,4]{1,0:T(1,128)S(1)}, s32[1,4]{1,0:T(1,128)}, u32[]{:S(2)}) copy-start(s32[1,4]{1,0:T(1,128)} %param.5) | copy-start | bytes 52
  12.5 47.8 %all-to-all-start = ((bf16[16,192,128]{2,1,0:T(8,128)(2,1)}), bf16[16,192,128]{2,1,0:T(8,128)(2,1)S(1)}, u32[]{:S(2)}, u32[]{:S(2)}) async-start(bf16[16,192,128]{2,1,0:T(8,128)(2,1)} %bitcast.6), calls=%async_computation | async-start | bytes 1572864 | tf_op jit(solution)/shard_map/all_to_all | solution.py:401
  21.8 19.7 %collective-permute-start.3 = (bf16[2,2,96,1024]{3,2,1,0:T(8,128)(2,1)S(1)}, bf16[2,2,96,1024]{3,2,1,0:T(8,128)(2,1)S(1)}, u32[]{:S(2)}, u32[]{:S(2)}) collective-permute-start(bf16[2,2,96,1024]{3,2,1,0:T(8,128)(2,1)S(1)} %copy-done.1), channel_id=1, source_target_pairs={{0,64},{16,80},{32,96},{48,112},{64,128},{80,144},{96,160},{112,17... | collective-permute-start | bytes 2359304 | tf_op jit(solution)/shard_map/ppermute | solution.py:400
  23.1 36.3 %collective-permute-start.4 = (bf16[2,2,96,1024]{3,2,1,0:T(8,128)(2,1)S(1)}, bf16[2,2,96,1024]{3,2,1,0:T(8,128)(2,1)S(1)}, u32[]{:S(2)}, u32[]{:S(2)}) collective-permute-start(bf16[2,2,96,1024]{3,2,1,0:T(8,128)(2,1)S(1)} %copy-done.1), channel_id=1, source_target_pairs={{0,128},{16,144},{32,160},{48,176},{64,192},{80,208},{96,224},{112... | collective-permute-start | bytes 2359304 | tf_op jit(solution)/shard_map/ppermute | solution.py:400
  25.6 33.8 %collective-permute-start.5 = (bf16[2,2,96,1024]{3,2,1,0:T(8,128)(2,1)S(1)}, bf16[2,2,96,1024]{3,2,1,0:T(8,128)(2,1)S(1)}, u32[]{:S(2)}, u32[]{:S(2)}) collective-permute-start(bf16[2,2,96,1024]{3,2,1,0:T(8,128)(2,1)S(1)} %copy-done.1), channel_id=1, source_target_pairs={{0,192},{16,208},{32,224},{48,240},{64,0},{80,16},{96,32},{112,48}... | collective-permute-start | bytes 2359304 | tf_op jit(solution)/shard_map/ppermute | solution.py:400
  59.4 0.9 copy-start.2
  61.1 3.1 %collective-permute-start.6 = (bf16[16,96,128]{2,1,0:T(8,128)(2,1)}, bf16[16,96,128]{2,1,0:T(8,128)(2,1)S(1)}, u32[]{:S(2)}, u32[]{:S(2)}) collective-permute-start(bf16[16,96,128]{2,1,0:T(8,128)(2,1)} %slice.3), channel_id=1, source_target_pairs={{0,16},{16,0},{32,48},{48,32},{64,80},{80,64},{96,112},{112,96},{1... | collective-permute-start | bytes 1179656 | tf_op jit(solution)/shard_map/ppermute | solution.py:403
  62.6 1.2 collective-permute-start
  74.2 1.8 %collective-permute-start.7 = (bf16[16,96,128]{2,1,0:T(8,128)(2,1)S(1)}, bf16[16,96,128]{2,1,0:T(8,128)(2,1)S(1)}, u32[]{:S(2)}, u32[]{:S(2)}) collective-permute-start(bf16[16,96,128]{2,1,0:T(8,128)(2,1)S(1)} %get-tuple-element.26), channel_id=1, source_target_pairs={{0,16},{16,0},{32,48},{48,32},{64,80},{80,64},{96,112},{112,96},{1... | collective-permute-start | bytes 1179656 | tf_op jit(solution)/shard_map/ppermute | solution.py:407
  105.6 16.8 %all-to-all-start.2 = ((bf16[4,2,2,192,128]{4,3,2,1,0:T(8,128)(2,1)}), bf16[4,2,2,192,128]{4,3,2,1,0:T(8,128)(2,1)S(1)}, u32[]{:S(2)}, u32[]{:S(2)}) async-start(bf16[4,2,2,192,128]{4,3,2,1,0:T(8,128)(2,1)} %bitcast.7), calls=%async_computation.2 | async-start | bytes 1572864 | tf_op jit(solution)/shard_map/all_to_all | solution.py:411
  122.4 1.1 copy-start.3
  126.8 4.9 %collective-permute-start.8 = (bf16[16,64,256]{2,1,0:T(8,128)(2,1)S(1)}, bf16[16,64,256]{2,1,0:T(8,128)(2,1)S(1)}, u32[]{:S(2)}, u32[]{:S(2)}) collective-permute-start(bf16[16,64,256]{2,1,0:T(8,128)(2,1)S(1)} %get-tuple-element.31), channel_id=1, source_target_pairs={{0,16},{16,0},{32,48},{48,32},{64,80},{80,64},{96,112},{112,96},{1... | collective-permute-start | bytes 1572872 | tf_op jit(solution)/shard_map/ppermute | solution.py:417
  132.7 20.1 %all-to-all-start.3 = ((bf16[16,64,256]{2,1,0:T(8,128)(2,1)}), bf16[16,64,256]{2,1,0:T(8,128)(2,1)S(1)}, u32[]{:S(2)}, u32[]{:S(2)}) async-start(bf16[16,64,256]{2,1,0:T(8,128)(2,1)} %add_convert_fusion), calls=%async_computation.3 | async-start | bytes 1048576 | tf_op jit(solution)/shard_map/all_to_all | solution.py:420
  138.2 2.1 %collective-permute-start.9 = (bf16[8,192,128]{2,1,0:T(8,128)(2,1)S(1)}, bf16[8,192,128]{2,1,0:T(8,128)(2,1)S(1)}, u32[]{:S(2)}, u32[]{:S(2)}) collective-permute-start(bf16[8,192,128]{2,1,0:T(8,128)(2,1)S(1)} %dynamic-slice_bitcast_fusion), channel_id=1, source_target_pairs={{0,16},{16,0},{32,48},{48,32},{64,80},{80,64},{96,112},{112,96},{1... | collective-permute-start | bytes 1179656 | tf_op jit(solution)/shard_map/ppermute | solution.py:421
  140.3 2.2 %copy-start = (bf16[4,1024,512]{2,1,0:T(8,128)(2,1)S(1)}, bf16[4,1024,512]{2,1,0:T(8,128)(2,1)}, u32[]{:S(2)}) copy-start(bf16[4,1024,512]{2,1,0:T(8,128)(2,1)} %weights_ref.3) | copy-start | bytes 12582916

commit v5 on v4

--- a/solution.py
+++ b/solution.py
@@ -16,7 +16,6 @@
 KEY_ROWS = TILES * SPAN + CHUNK
 NEGATIVE = -1e30
 VMEM_LIMIT = 48 * 1024 * 1024
-PROJECT_VMEM = 51 * 1024 * 1024
 
 CORE_SWAP = [(i, i ^ 1) for i in range(16)]
 CHIP_LINES = [[4 * x + rest for x in range(4)] for rest in range(4)]
@@ -27,27 +26,22 @@
     return lax.broadcasted_iota(jnp.int32, (rows, 128), 1) < HEAD
 
 
-def project_kernel(
-    place_ref, tokens_ref, other_tokens_ref, upstream_ref, other_upstream_ref, weights_ref,
-    out_ref, line_ref,
-):
-    core = place_ref[0]
-    inputs = jnp.concatenate([tokens_ref[0], other_tokens_ref[0]], axis=0)
-    upstream = jnp.concatenate([upstream_ref[0], other_upstream_ref[0]], axis=0)
+def project_kernel(place_ref, tokens_ref, upstream_ref, weights_ref, *refs):
+    out_ref, line_ref = refs[-2:]
+    inputs = tokens_ref[0]
+    upstream = upstream_ref[0]
 
     @pl.when(pl.program_id(0) == 0)
     def _():
-        line_ref[0, 0] = tokens_ref[0]
-        line_ref[0, 1] = upstream_ref[0]
-        line_ref[1, 0] = other_tokens_ref[0]
-        line_ref[1, 1] = other_upstream_ref[0]
+        line_ref[0, 0] = inputs
+        line_ref[0, 1] = upstream
 
     def product(rows, number):
         return jnp.dot(rows, weights_ref[number], preferred_element_type=jnp.float32)
 
     queries, keys, values = (product(inputs, number) for number in range(3))
     grads = product(upstream, 3)
-    low = low_lanes(2 * SPAN)
+    low = low_lanes(SPAN)
     for half, (first, second) in enumerate(((queries, grads), (keys, values))):
         place = slice(SPAN * half, SPAN * half + SPAN)
         for pair in range(2):
@@ -55,15 +49,12 @@
             two = second[:, 128 * pair : 128 * pair + 128]
             even = jnp.where(low, one, pltpu.roll(two, HEAD, 1)).astype(jnp.bfloat16)
             odd = jnp.where(low, pltpu.roll(one, HEAD, 1), two).astype(jnp.bfloat16)
-            for part in range(2):
-                rows = slice(SPAN * part, SPAN * part + SPAN)
-                sequence = jnp.bitwise_xor(core, part)
-                out_ref[2 * pair, sequence, place, :] = even[rows]
-                out_ref[2 * pair + 1, sequence, place, :] = odd[rows]
-
-
-def project(place, rows, weights):
-    block_spec = pl.BlockSpec((1, SPAN, D), lambda j, place: (place[1], 0, 0))
+            out_ref[2 * pair, 0, place, :] = even
+            out_ref[2 * pair + 1, 0, place, :] = odd
+
+
+def project(place, part, tokens, upstream, weights, *filled):
+    block_spec = pl.BlockSpec((1, SPAN, D), lambda j, place: (place[0], 0, 0))
     return pl.pallas_call(
         project_kernel,
         out_shape=(
@@ -74,17 +65,20 @@
             num_scalar_prefetch=1,
             grid=(2,),
             in_specs=[
-                block_spec, block_spec, block_spec, block_spec,
+                block_spec,
+                block_spec,
                 pl.BlockSpec((4, D, HQ // 2), lambda j, place: (0, 0, j)),
-            ],
+            ]
+            + [pl.BlockSpec(memory_space=pl.ANY)] * len(filled),
             out_specs=(
-                pl.BlockSpec((HEADS // 2, 2, 2 * SPAN, 128), lambda j, place: (j, 0, 0, 0)),
-                pl.BlockSpec((2, 2, SPAN, D), lambda j, place: (0, 0, 0, 0)),
+                pl.BlockSpec((HEADS // 2, 1, 2 * SPAN, 128), lambda j, place: (j, place[1], 0, 0)),
+                pl.BlockSpec((1, 2, SPAN, D), lambda j, place: (part, 0, 0, 0)),
             ),
         ),
-        compiler_params=pltpu.CompilerParams(vmem_limit_bytes=PROJECT_VMEM),
+        input_output_aliases={4 + i: i for i in range(len(filled))},
+        compiler_params=pltpu.CompilerParams(vmem_limit_bytes=VMEM_LIMIT),
         name="project",
-    )(place, *rows, weights)
+    )(place, tokens, upstream, weights, *filled)
 
 
 def attend_kernel(
@@ -391,23 +385,27 @@
     other_upstream = lax.ppermute(upstream, "dp", CORE_SWAP)
     other_tiles = lax.ppermute(sweep_tiles, "dp", CORE_SWAP)
     core_number = core.astype(jnp.int32).reshape(1)
+    filled = project(
+        jnp.stack([block, core]).astype(jnp.int32), 0, rows, upstream, weights
+    )
     packed, line = project(
-        jnp.stack([core, block]).astype(jnp.int32),
-        (rows, other_rows, upstream, other_upstream),
-        weights,
+        jnp.stack([block, 1 - core]).astype(jnp.int32),
+        1, other_rows, other_upstream, weights, *filled,
     )
     packed = packed.reshape(RANKS, 2 * SPAN, 128)
     shifted = [lax.ppermute(line, "dp", shift) for shift in X_SHIFTS]
     own = lax.all_to_all(packed, "ctx", 0, 0)
-    own, *shifted = lax.optimization_barrier((own, *shifted))
+    near, far, back_near = shifted
+    own, near, back_near = lax.optimization_barrier((own, near, back_near))
     other = lax.ppermute(own[:, SPAN:], "dp", CORE_SWAP)
-    lines = [line, *shifted]
     tiles = jnp.where(odd == core, sweep_tiles, other_tiles).reshape(-1)
     query_part, own_grad, other_grad = attend(core_number, tiles, own, other)
     arrived = lax.ppermute(other_grad, "dp", CORE_SWAP)
     key_part = (own_grad + arrived.astype(jnp.float32)).astype(jnp.bfloat16)
     back = lax.all_to_all(jnp.concatenate([query_part, key_part], axis=1), "ctx", 0, 0)
+    back, far = lax.optimization_barrier((back, far))
     grads = back.reshape(HEADS, 2, 2 * SPAN, 128)
+    lines = [line, near, far, back_near]
     line_grads = lax.all_to_all(
         back.reshape(4, 2, 2, 2 * SPAN, 128), "dp", 0, 0, axis_index_groups=CHIP_LINES
     )

time: 172 us -> 159 us (0.924)
  blocking collectives: 46.3 us -> 17.2 us
  starting transfers between devices: 34.8 us -> 43.8 us
  Pallas kernels: 24.6 us -> 27.9 us
    all_to_all x1 -> x0, blocking collectives: 29.3 us -> none  [per_device(): lax.all_to_all(jnp.concatenate([query_part, key_part], axis=1), 'ctx', 0, 0)]
    all_to_all x0 -> x1, starting transfers between devices: none -> 6.91 us  [per_device(): lax.all_to_all(jnp.concatenate([query_part, key_part], axis=1), 'ctx', 0, 0)]
    pallas_call x1 -> x2, Pallas kernels: 4.41 us -> 8.06 us  [project(): pl.pallas_call(project_kernel, out_shape=(jax.ShapeDtypeStruct((HEADS, 2,...]
    all_to_all x1, starting transfers between devices: 4.47 us -> 6.99 us  [per_device(): terms = lax.all_to_all(terms, 'ctx', 0, 0)]
    ppermute x3, waiting for transfers between devices: 32.7 us -> 34.5 us  [per_device(): shifted = [lax.ppermute(line, 'dp', shift) for shift in X_SHIFTS]]
    unnamed x14 -> x12, local copies, waits for them, and re-layouts: 6.24 us -> 6.2 us
  transfers between devices with their start and end apart: 13 -> 14, of which waited for: 11 -> 10; matrix products, arithmetic and copies ran while one was open for 1% -> 1% of each run, Pallas kernels for 3% -> 6%
where the time goes in v5:
time: 159 us; the launch traced here: 158 us
  waiting for transfers between devices  57.5 us (36%)
  starting transfers between devices  43.8 us (28%)
  Pallas kernels  27.9 us (18%)
  blocking collectives  17.2 us (11%)
  local copies, waits for them, and re-layouts  8.05 us (5%)
  other arithmetic  2.49 us (2%)
    ppermute x3, waiting for transfers between devices, per_device(): shifted = [lax.ppermute(line, 'dp', shift) for shift in X_SHIFTS]  34.5 us
    all_to_all x1, blocking collectives, per_device(): parts = lax.all_to_all(jnp.broadcast_to(rows, (16, 64, 256)), 'dp', 0, 0)  17.2 us
    all_to_all x1, waiting for transfers between devices, per_device(): lax.all_to_all(back.reshape(4, 2, 2, 2 * SPAN, 128), 'dp', 0, 0, axis_ind...  10.1 us
    pallas_call x1, Pallas kernels, attend(): pl.pallas_call(attend_kernel, out_shape=(jax.ShapeDtypeStruct(block, jnp....  9.78 us
    all_to_all x1, starting transfers between devices, per_device(): own = lax.all_to_all(packed, 'ctx', 0, 0)  9.32 us
    pallas_call x2, Pallas kernels, project(): pl.pallas_call(project_kernel, out_shape=(jax.ShapeDtypeStruct((HEADS, 2,...  8.06 us
    all_to_all x1, starting transfers between devices, per_device(): terms = lax.all_to_all(terms, 'ctx', 0, 0)  6.99 us
    all_to_all x1, starting transfers between devices, per_device(): lax.all_to_all(jnp.concatenate([query_part, key_part], axis=1), 'ctx', 0, 0)  6.91 us
  transfers between devices with their start and end apart: 14, of which 10 were waited for; matrix products, arithmetic and copies ran while one was open for 1% of the time, Pallas kernels for 6%

profile of v5, /device:TPU:1, one launch (start us, length us, event | category | flops | bytes accessed | tf_op | source)
XLA Modules:
  0.0 157.8 jit_solution(15009569788375103861)
XLA Ops:
  0.6 3.3 %collective-permute-start.1 = (bf16[2,96,1024]{2,1,0:T(8,128)(2,1)}, bf16[2,96,1024]{2,1,0:T(8,128)(2,1)S(1)}, u32[]{:S(2)}, u32[]{:S(2)}) collective-permute-start(bf16[2,96,1024]{2,1,0:T(8,128)(2,1)} %bitcast.17), channel_id=1, source_target_pairs={{0,16},{16,0},{32,48},{48,32},{64,80},{80,64},{96,112},{112,96},{1... | collective-permute-start | bytes 1179656 | tf_op jit(solution)/shard_map/ppermute | solution.py:384
  4.0 0.1 collective-permute-start.2
  4.1 0.1 pad_add_fusion.2.place_ref
  4.1 1.0 copy-done.3
  5.1 1.0 copy-done.4
  6.1 4.0 %project.2 = (bf16[8,2,192,128]{3,2,1,0:T(8,128)(2,1)}, bf16[2,2,96,1024]{3,2,1,0:T(8,128)(2,1)S(1)}) custom-call(s32[2]{0:T(128)S(1)} %pad_add_fusion.2.place_ref, bf16[2,96,1024]{2,1,0:T(8,128)(2,1)S(1)} %bitcast.18, bf16[2,96,1024]{2,1,0:T(8,128)(2,1)S(1)} %bitcast.20, bf16[4,1024,512]{2,1,0:T(8,128)(2,1)} %weights_ref.5), custom_call_target="tpu_custom_call" | custom-call | tf_op jit(solution)/shard_map/project/pallas_call | solution.py:58
  10.2 0.1 pad_add_fusion.1.place_ref
  10.2 0.0 collective-permute-done.2.upstream_ref
  10.2 4.0 %project.3 = (bf16[8,2,192,128]{3,2,1,0:T(8,128)(2,1)}, bf16[2,2,96,1024]{3,2,1,0:T(8,128)(2,1)S(1)}) custom-call(s32[2]{0:T(128)S(1)} %pad_add_fusion.1.place_ref, bf16[2,96,1024]{2,1,0:T(8,128)(2,1)S(1)} %collective-permute-done.1.tokens_ref, ...), custom_call_target="tpu_custom_call", output_to_operand_aliasing={{0}: (4, {}), {1}: (5, {})} | custom-call | tf_op jit(solution)/shard_map/project/pallas_call | solution.py:58
  14.3 9.3 %all-to-all-start = ((bf16[16,192,128]{2,1,0:T(8,128)(2,1)}), bf16[16,192,128]{2,1,0:T(8,128)(2,1)S(1)}, u32[]{:S(2)}, u32[]{:S(2)}) async-start(bf16[16,192,128]{2,1,0:T(8,128)(2,1)} %bitcast.7), calls=%async_computation | async-start | bytes 1572864 | tf_op jit(solution)/shard_map/all_to_all | solution.py:397
  23.6 1.3 collective-permute-start.3
  24.9 1.5 collective-permute-start.4
  26.4 16.9 %collective-permute-done.3.refs_1_ = bf16[2,2,96,1024]{3,2,1,0:T(8,128)(2,1)S(1)} collective-permute-done((bf16[2,2,96,1024]{3,2,1,0:T(8,128)(2,1)S(1)}, bf16[2,2,96,1024]{3,2,1,0:T(8,128)(2,1)S(1)}, u32[]{:S(2)}, u32[]{:S(2)}) %collective-permute-start.3) | collective-permute-done | bytes 786464 | tf_op jit(solution)/shard_map/ppermute | solution.py:396
  43.3 0.0 collective-permute-done.4.refs_3_
  43.3 1.7 %all-to-all-done.own_ref = bf16[16,192,128]{2,1,0:T(8,128)(2,1)S(1)} async-done(((bf16[16,192,128]{2,1,0:T(8,128)(2,1)}), bf16[16,192,128]{2,1,0:T(8,128)(2,1)S(1)}, u32[]{:S(2)}, u32[]{:S(2)}) %all-to-all-start) | async-done | bytes 786464 | tf_op jit(solution)/shard_map/all_to_all | solution.py:397
  45.0 0.8 slice.3
  45.8 2.0 %collective-permute-start.5 = (bf16[16,96,128]{2,1,0:T(8,128)(2,1)}, bf16[16,96,128]{2,1,0:T(8,128)(2,1)S(1)}, u32[]{:S(2)}, u32[]{:S(2)}) collective-permute-start(bf16[16,96,128]{2,1,0:T(8,128)(2,1)} %slice.3), channel_id=1, source_target_pairs={{0,16},{16,0},{32,48},{48,32},{64,80},{80,64},{96,112},{112,96},{1... | collective-permute-start | bytes 1179656 | tf_op jit(solution)/shard_map/ppermute | solution.py:400
  47.7 0.0 collective-permute-start
  47.8 1.2 collective-permute-done
  48.9 0.4 collective-permute-done.5.other_ref
  49.3 9.8 %attend.1 = (bf16[16,96,128]{2,1,0:T(8,128)(2,1)S(1)}, f32[16,96,128]{2,1,0:T(8,128)S(1)}, bf16[16,96,128]{2,1,0:T(8,128)(2,1)S(1)}) custom-call(s32[1]{0:T(128)} %bitcast.core_ref, s32[4]{0:T(128)S(1)} %fusion.tiles_ref, bf16[16,192,128]{2,1,0:T(8,128)(2,1)S(1)} %all-to-all-done.own_ref, bf16[16,96,128]{2,1,0:T(8,128)(2,1)S(1)} %collective-permute-done.5.other_ref), custom_call_target="tpu_custom_call" | custom-call | tf_op jit(solution)/shard_map/attend/pallas_call | solution.py:199
  59.1 0.5 collective-permute-start.6
  59.6 1.4 collective-permute-done.6
  60.9 0.1 add_convert_fusion.1
  61.0 1.0 pad_maximum_fusion
  62.0 6.9 %all-to-all-start.1 = ((bf16[16,192,128]{2,1,0:T(8,128)(2,1)}), bf16[16,192,128]{2,1,0:T(8,128)(2,1)}, u32[]{:S(2)}, u32[]{:S(2)}) async-start(bf16[16,192,128]{2,1,0:T(8,128)(2,1)} %pad_maximum_fusion), calls=%async_computation.1 | async-start | bytes 1572864 | tf_op jit(solution)/shard_map/all_to_all | solution.py:405
  68.9 2.5 %collective-permute-start.7 = (bf16[2,2,96,1024]{3,2,1,0:T(8,128)(2,1)S(1)}, bf16[2,2,96,1024]{3,2,1,0:T(8,128)(2,1)S(1)}, u32[]{:S(2)}, u32[]{:S(2)}) collective-permute-start(bf16[2,2,96,1024]{3,2,1,0:T(8,128)(2,1)S(1)} %get-tuple-element.27.refs_0_), channel_id=1, source_target_pairs={{0,128},{16,144},{32,160},{48,176},{64,192},{80,208},{96,224},{112... | collective-permute-start | bytes 2359304 | tf_op jit(solution)/shard_map/ppermute | solution.py:396
  71.5 17.6 %collective-permute-done.7.refs_2_ = bf16[2,2,96,1024]{3,2,1,0:T(8,128)(2,1)S(1)} collective-permute-done((bf16[2,2,96,1024]{3,2,1,0:T(8,128)(2,1)S(1)}, bf16[2,2,96,1024]{3,2,1,0:T(8,128)(2,1)S(1)}, u32[]{:S(2)}, u32[]{:S(2)}) %collective-permute-start.7) | collective-permute-done | bytes 786464 | tf_op jit(solution)/shard_map/ppermute | solution.py:396
  89.1 0.9 copy-done.1
  90.0 5.6 %all-to-all-start.2 = ((bf16[4,2,2,192,128]{4,3,2,1,0:T(8,128)(2,1)}), bf16[4,2,2,192,128]{4,3,2,1,0:T(8,128)(2,1)S(1)}, u32[]{:S(2)}, u32[]{:S(2)}) async-start(bf16[4,2,2,192,128]{4,3,2,1,0:T(8,128)(2,1)} %bitcast.8), calls=%async_computation.2 | async-start | bytes 1572864 | tf_op jit(solution)/shard_map/all_to_all | solution.py:409
  95.6 0.1 pad_add_fusion.place_ref
  95.6 10.1 %all-to-all-done.2.grads_ref = bf16[4,2,2,192,128]{4,3,2,1,0:T(8,128)(2,1)S(1)} async-done(((bf16[4,2,2,192,128]{4,3,2,1,0:T(8,128)(2,1)}), bf16[4,2,2,192,128]{4,3,2,1,0:T(8,128)(2,1)S(1)}, u32[]{:S(2)}, u32[]{:S(2)}) %all-to-all-start.2) | async-done | bytes 786464 | tf_op jit(solution)/shard_map/all_to_all | solution.py:409
  105.8 1.1 copy-done.2
  106.9 3.3 %weight_terms.1 = (bf16[16,64,256]{2,1,0:T(8,128)(2,1)S(1)}, bf16[16,64,256]{2,1,0:T(8,128)(2,1)S(1)}) custom-call(s32[2]{0:T(128)S(1)} %pad_add_fusion.place_ref, bf16[4,2,2,192,128]{4,3,2,1,0:T(8,128)(2,1)S(1)} %all-to-all-done.2.grads_ref, bf16[2,2,96,1024]{3,2,1,0:T(8,128)(2,1)S(1)} %get-tuple-element.27.refs_0_, ...), custom_call_target="tpu_custom_call" | custom-call | tf_op jit(solution)/shard_map/weight_terms/pallas_call | solution.py:262
  110.2 3.1 %collective-permute-start.8 = (bf16[16,64,256]{2,1,0:T(8,128)(2,1)S(1)}, bf16[16,64,256]{2,1,0:T(8,128)(2,1)S(1)}, u32[]{:S(2)}, u32[]{:S(2)}) collective-permute-start(bf16[16,64,256]{2,1,0:T(8,128)(2,1)S(1)} %get-tuple-element.37), channel_id=1, source_target_pairs={{0,16},{16,0},{32,48},{48,32},{64,80},{80,64},{96,112},{112,96},{1... | collective-permute-start | bytes 1572872 | tf_op jit(solution)/shard_map/ppermute | solution.py:415
  113.4 1.5 collective-permute-done.8
  114.9 1.0 add_convert_fusion
  115.9 7.0 %all-to-all-start.3 = ((bf16[16,64,256]{2,1,0:T(8,128)(2,1)}), bf16[16,64,256]{2,1,0:T(8,128)(2,1)S(1)}, u32[]{:S(2)}, u32[]{:S(2)}) async-start(bf16[16,64,256]{2,1,0:T(8,128)(2,1)} %add_convert_fusion), calls=%async_computation.3 | async-start | bytes 1048576 | tf_op jit(solution)/shard_map/all_to_all | solution.py:418
  122.9 1.0 dynamic-slice_bitcast_fusion
  123.9 0.7 collective-permute-start.9
  124.7 0.1 pad_add_fusion.3.place_ref
  124.8 1.3 collective-permute-done.9.arrived_ref
  126.0 2.2 %copy-done = bf16[4,1024,512]{2,1,0:T(8,128)(2,1)S(1)} copy-done((bf16[4,1024,512]{2,1,0:T(8,128)(2,1)S(1)}, bf16[4,1024,512]{2,1,0:T(8,128)(2,1)}, u32[]{:S(2)}) %copy-start) | copy-done | bytes 4194328
  128.2 4.9 %outputs.1 = (bf16[2,96,1024]{2,1,0:T(8,128)(2,1)}, bf16[2,96,1024]{2,1,0:T(8,128)(2,1)}) custom-call(s32[2]{0:T(128)S(1)} %pad_add_fusion.3.place_ref, bf16[8,2,192,128]{3,2,1,0:T(8,128)(2,1)} %bitcast.9.grads_ref, bf16[8,192,128]{2,1,0:T(8,128)(2,1)S(1)} %collective-permute-done.9.arrived_ref, bf16[4,1024,512]{2,1,0:T(8,128)(2,1)S(1)} %copy-done), custom_call_target="tpu_custom_call" | custom-call | flops 805306368 | bytes 7340032 | tf_op jit(solution)/shard_map/outputs/pallas_call | solution.py:353
  133.1 5.4 %all-to-all-done.3 = bf16[16,64,256]{2,1,0:T(8,128)(2,1)S(1)} async-done(((bf16[16,64,256]{2,1,0:T(8,128)(2,1)}), bf16[16,64,256]{2,1,0:T(8,128)(2,1)S(1)}, u32[]{:S(2)}, u32[]{:S(2)}) %all-to-all-start.3) | async-done | bytes 524320 | tf_op jit(solution)/shard_map/all_to_all | solution.py:418
  138.5 0.1 reduce_sum.12
  138.6 17.2 %all_to_all.25 = bf16[16,64,256]{2,1,0:T(8,128)(2,1)} all-to-all(bf16[16,64,256]{2,1,0:T(8,128)(2,1)S(1)} %broadcast_in_dim.3), channel_id=1, replica_groups=mesh['dp'=16,'ctx'=16] {'dp'}, dimensions={0} | all-to-all | bytes 1048576 | tf_op jit(solution)/shard_map/all_to_all | solution.py:426
  155.9 1.9 %spread_heads.1 = bf16[4,64,512]{2,1,0:T(8,128)(2,1)} custom-call(bf16[4,2,2,64,256]{4,3,2,1,0:T(8,128)(2,1)} %bitcast.21), custom_call_target="tpu_custom_call" | custom-call | tf_op jit(solution)/shard_map/spread_heads/pallas_call | solution.py:304
  (11 shorter events, 0.1 us)
Async XLA Ops:
  0.6 9.6 %collective-permute-start.1 = (bf16[2,96,1024]{2,1,0:T(8,128)(2,1)}, bf16[2,96,1024]{2,1,0:T(8,128)(2,1)S(1)}, u32[]{:S(2)}, u32[]{:S(2)}) collective-permute-start(bf16[2,96,1024]{2,1,0:T(8,128)(2,1)} %bitcast.17), channel_id=1, source_target_pairs={{0,16},{16,0},{32,48},{48,32},{64,80},{80,64},{96,112},{112,96},{1... | collective-permute-start | bytes 1179656 | tf_op jit(solution)/shard_map/ppermute | solution.py:384
  4.0 6.3 %collective-permute-start.2 = (bf16[2,96,1024]{2,1,0:T(8,128)(2,1)}, bf16[2,96,1024]{2,1,0:T(8,128)(2,1)S(1)}, u32[]{:S(2)}, u32[]{:S(2)}) collective-permute-start(bf16[2,96,1024]{2,1,0:T(8,128)(2,1)} %bitcast.19), channel_id=1, source_target_pairs={{0,16},{16,0},{32,48},{48,32},{64,80},{80,64},{96,112},{112,96},{1... | collective-permute-start | bytes 1179656 | tf_op jit(solution)/shard_map/ppermute | solution.py:385
  4.1 1.0 copy-start.3
  5.1 1.0 copy-start.4
  14.3 33.5 %copy-start.5 = (s32[1,4]{1,0:T(1,128)S(1)}, s32[1,4]{1,0:T(1,128)}, u32[]{:S(2)}) copy-start(s32[1,4]{1,0:T(1,128)} %param.5) | copy-start | bytes 52
  14.3 30.7 %all-to-all-start = ((bf16[16,192,128]{2,1,0:T(8,128)(2,1)}), bf16[16,192,128]{2,1,0:T(8,128)(2,1)S(1)}, u32[]{:S(2)}, u32[]{:S(2)}) async-start(bf16[16,192,128]{2,1,0:T(8,128)(2,1)} %bitcast.7), calls=%async_computation | async-start | bytes 1572864 | tf_op jit(solution)/shard_map/all_to_all | solution.py:397
  23.6 19.7 %collective-permute-start.3 = (bf16[2,2,96,1024]{3,2,1,0:T(8,128)(2,1)S(1)}, bf16[2,2,96,1024]{3,2,1,0:T(8,128)(2,1)S(1)}, u32[]{:S(2)}, u32[]{:S(2)}) collective-permute-start(bf16[2,2,96,1024]{3,2,1,0:T(8,128)(2,1)S(1)} %get-tuple-element.27.refs_0_), channel_id=1, source_target_pairs={{0,64},{16,80},{32,96},{48,112},{64,128},{80,144},{96,160},{112,17... | collective-permute-start | bytes 2359304 | tf_op jit(solution)/shard_map/ppermute | solution.py:396
  24.9 18.4 %collective-permute-start.4 = (bf16[2,2,96,1024]{3,2,1,0:T(8,128)(2,1)S(1)}, bf16[2,2,96,1024]{3,2,1,0:T(8,128)(2,1)S(1)}, u32[]{:S(2)}, u32[]{:S(2)}) collective-permute-start(bf16[2,2,96,1024]{3,2,1,0:T(8,128)(2,1)S(1)} %get-tuple-element.27.refs_0_), channel_id=1, source_target_pairs={{0,192},{16,208},{32,224},{48,240},{64,0},{80,16},{96,32},{112,48}... | collective-permute-start | bytes 2359304 | tf_op jit(solution)/shard_map/ppermute | solution.py:396
  45.8 3.5 %collective-permute-start.5 = (bf16[16,96,128]{2,1,0:T(8,128)(2,1)}, bf16[16,96,128]{2,1,0:T(8,128)(2,1)S(1)}, u32[]{:S(2)}, u32[]{:S(2)}) collective-permute-start(bf16[16,96,128]{2,1,0:T(8,128)(2,1)} %slice.3), channel_id=1, source_target_pairs={{0,16},{16,0},{32,48},{48,32},{64,80},{80,64},{96,112},{112,96},{1... | collective-permute-start | bytes 1179656 | tf_op jit(solution)/shard_map/ppermute | solution.py:400
  47.7 1.2 collective-permute-start
  59.1 1.8 %collective-permute-start.6 = (bf16[16,96,128]{2,1,0:T(8,128)(2,1)S(1)}, bf16[16,96,128]{2,1,0:T(8,128)(2,1)S(1)}, u32[]{:S(2)}, u32[]{:S(2)}) collective-permute-start(bf16[16,96,128]{2,1,0:T(8,128)(2,1)S(1)} %get-tuple-element.31), channel_id=1, source_target_pairs={{0,16},{16,0},{32,48},{48,32},{64,80},{80,64},{96,112},{112,96},{1... | collective-permute-start | bytes 1179656 | tf_op jit(solution)/shard_map/ppermute | solution.py:403
  62.0 27.9 %all-to-all-start.1 = ((bf16[16,192,128]{2,1,0:T(8,128)(2,1)}), bf16[16,192,128]{2,1,0:T(8,128)(2,1)}, u32[]{:S(2)}, u32[]{:S(2)}) async-start(bf16[16,192,128]{2,1,0:T(8,128)(2,1)} %pad_maximum_fusion), calls=%async_computation.1 | async-start | bytes 1572864 | tf_op jit(solution)/shard_map/all_to_all | solution.py:405
  68.9 20.1 %collective-permute-start.7 = (bf16[2,2,96,1024]{3,2,1,0:T(8,128)(2,1)S(1)}, bf16[2,2,96,1024]{3,2,1,0:T(8,128)(2,1)S(1)}, u32[]{:S(2)}, u32[]{:S(2)}) collective-permute-start(bf16[2,2,96,1024]{3,2,1,0:T(8,128)(2,1)S(1)} %get-tuple-element.27.refs_0_), channel_id=1, source_target_pairs={{0,128},{16,144},{32,160},{48,176},{64,192},{80,208},{96,224},{112... | collective-permute-start | bytes 2359304 | tf_op jit(solution)/shard_map/ppermute | solution.py:396
  89.1 0.9 copy-start.1
  90.0 15.8 %all-to-all-start.2 = ((bf16[4,2,2,192,128]{4,3,2,1,0:T(8,128)(2,1)}), bf16[4,2,2,192,128]{4,3,2,1,0:T(8,128)(2,1)S(1)}, u32[]{:S(2)}, u32[]{:S(2)}) async-start(bf16[4,2,2,192,128]{4,3,2,1,0:T(8,128)(2,1)} %bitcast.8), calls=%async_computation.2 | async-start | bytes 1572864 | tf_op jit(solution)/shard_map/all_to_all | solution.py:409
  105.8 1.1 copy-start.2
  110.2 4.7 %collective-permute-start.8 = (bf16[16,64,256]{2,1,0:T(8,128)(2,1)S(1)}, bf16[16,64,256]{2,1,0:T(8,128)(2,1)S(1)}, u32[]{:S(2)}, u32[]{:S(2)}) collective-permute-start(bf16[16,64,256]{2,1,0:T(8,128)(2,1)S(1)} %get-tuple-element.37), channel_id=1, source_target_pairs={{0,16},{16,0},{32,48},{48,32},{64,80},{80,64},{96,112},{112,96},{1... | collective-permute-start | bytes 1572872 | tf_op jit(solution)/shard_map/ppermute | solution.py:415
  115.9 22.6 %all-to-all-start.3 = ((bf16[16,64,256]{2,1,0:T(8,128)(2,1)}), bf16[16,64,256]{2,1,0:T(8,128)(2,1)S(1)}, u32[]{:S(2)}, u32[]{:S(2)}) async-start(bf16[16,64,256]{2,1,0:T(8,128)(2,1)} %add_convert_fusion), calls=%async_computation.3 | async-start | bytes 1048576 | tf_op jit(solution)/shard_map/all_to_all | solution.py:418
  123.9 2.1 %collective-permute-start.9 = (bf16[8,192,128]{2,1,0:T(8,128)(2,1)S(1)}, bf16[8,192,128]{2,1,0:T(8,128)(2,1)S(1)}, u32[]{:S(2)}, u32[]{:S(2)}) collective-permute-start(bf16[8,192,128]{2,1,0:T(8,128)(2,1)S(1)} %dynamic-slice_bitcast_fusion), channel_id=1, source_target_pairs={{0,16},{16,0},{32,48},{48,32},{64,80},{80,64},{96,112},{112,96},{1... | collective-permute-start | bytes 1179656 | tf_op jit(solution)/shard_map/ppermute | solution.py:419
  126.0 2.2 %copy-start = (bf16[4,1024,512]{2,1,0:T(8,128)(2,1)S(1)}, bf16[4,1024,512]{2,1,0:T(8,128)(2,1)}, u32[]{:S(2)}) copy-start(bf16[4,1024,512]{2,1,0:T(8,128)(2,1)} %weights_ref.5) | copy-start | bytes 12582916

commit v6 on v5

--- a/solution.py
+++ b/solution.py
@@ -15,7 +15,8 @@
 CHUNK = 256
 KEY_ROWS = TILES * SPAN + CHUNK
 NEGATIVE = -1e30
-VMEM_LIMIT = 48 * 1024 * 1024
+SMALL_VMEM = 24 * 1024 * 1024
+STAGE_VMEM = 47 * 1024 * 1024
 
 CORE_SWAP = [(i, i ^ 1) for i in range(16)]
 CHIP_LINES = [[4 * x + rest for x in range(4)] for rest in range(4)]
@@ -26,59 +27,73 @@
     return lax.broadcasted_iota(jnp.int32, (rows, 128), 1) < HEAD
 
 
-def project_kernel(place_ref, tokens_ref, upstream_ref, weights_ref, *refs):
-    out_ref, line_ref = refs[-2:]
-    inputs = tokens_ref[0]
-    upstream = upstream_ref[0]
-
-    @pl.when(pl.program_id(0) == 0)
-    def _():
-        line_ref[0, 0] = inputs
-        line_ref[0, 1] = upstream
-
-    def product(rows, number):
-        return jnp.dot(rows, weights_ref[number], preferred_element_type=jnp.float32)
-
-    queries, keys, values = (product(inputs, number) for number in range(3))
-    grads = product(upstream, 3)
-    low = low_lanes(SPAN)
-    for half, (first, second) in enumerate(((queries, grads), (keys, values))):
-        place = slice(SPAN * half, SPAN * half + SPAN)
-        for pair in range(2):
-            one = first[:, 128 * pair : 128 * pair + 128]
-            two = second[:, 128 * pair : 128 * pair + 128]
-            even = jnp.where(low, one, pltpu.roll(two, HEAD, 1)).astype(jnp.bfloat16)
-            odd = jnp.where(low, pltpu.roll(one, HEAD, 1), two).astype(jnp.bfloat16)
-            out_ref[2 * pair, 0, place, :] = even
-            out_ref[2 * pair + 1, 0, place, :] = odd
-
-
-def project(place, part, tokens, upstream, weights, *filled):
-    block_spec = pl.BlockSpec((1, SPAN, D), lambda j, place: (place[0], 0, 0))
+def stage_kernel(weights_ref, held_ref, sem):
+    copy = pltpu.make_async_copy(weights_ref, held_ref, sem)
+    copy.start()
+    copy.wait()
+
+
+def stage(weights):
+    return pl.pallas_call(
+        stage_kernel,
+        out_shape=jax.ShapeDtypeStruct(weights.shape, weights.dtype),
+        in_specs=[pl.BlockSpec(memory_space=pl.ANY)],
+        out_specs=pl.BlockSpec(memory_space=pltpu.VMEM),
+        scratch_shapes=[pltpu.SemaphoreType.DMA],
+        compiler_params=pltpu.CompilerParams(vmem_limit_bytes=STAGE_VMEM),
+        name="stage",
+    )(weights)
+
+
+def project_kernel(place_ref, mine_ref, other_ref, weights_ref, out_ref, line_ref):
+    core, block = place_ref[0], place_ref[1]
+    inputs, upstream = (
+        jnp.concatenate([mine_ref[kind, block], other_ref[kind, block]], axis=0)
+        for kind in range(2)
+    )
+    for part in range(2):
+        rows = slice(SPAN * part, SPAN * part + SPAN)
+        line_ref[part, 0] = inputs[rows]
+        line_ref[part, 1] = upstream[rows]
+    low = low_lanes(2 * SPAN)
+    for quarter in range(2):
+        columns = slice(256 * quarter, 256 * quarter + 256)
+
+        def product(rows, number):
+            return jnp.dot(
+                rows, weights_ref[number, :, columns], preferred_element_type=jnp.float32
+            )
+
+        queries, keys, values = (product(inputs, number) for number in range(3))
+        grads = product(upstream, 3)
+        for half, (first, second) in enumerate(((queries, grads), (keys, values))):
+            place = slice(SPAN * half, SPAN * half + SPAN)
+            for pair in range(2):
+                one = first[:, 128 * pair : 128 * pair + 128]
+                two = second[:, 128 * pair : 128 * pair + 128]
+                even = jnp.where(low, one, pltpu.roll(two, HEAD, 1)).astype(jnp.bfloat16)
+                odd = jnp.where(low, pltpu.roll(one, HEAD, 1), two).astype(jnp.bfloat16)
+                head = 4 * quarter + 2 * pair
+                for part in range(2):
+                    rows = slice(SPAN * part, SPAN * part + SPAN)
+                    sequence = jnp.bitwise_xor(core, part)
+                    out_ref[head, sequence, place, :] = even[rows]
+                    out_ref[head + 1, sequence, place, :] = odd[rows]
+
+
+def project(place, mine, other, weights):
+    vmem = pl.BlockSpec(memory_space=pltpu.VMEM)
     return pl.pallas_call(
         project_kernel,
         out_shape=(
             jax.ShapeDtypeStruct((HEADS, 2, 2 * SPAN, 128), jnp.bfloat16),
             jax.ShapeDtypeStruct((2, 2, SPAN, D), jnp.bfloat16),
         ),
-        grid_spec=pltpu.PrefetchScalarGridSpec(
-            num_scalar_prefetch=1,
-            grid=(2,),
-            in_specs=[
-                block_spec,
-                block_spec,
-                pl.BlockSpec((4, D, HQ // 2), lambda j, place: (0, 0, j)),
-            ]
-            + [pl.BlockSpec(memory_space=pl.ANY)] * len(filled),
-            out_specs=(
-                pl.BlockSpec((HEADS // 2, 1, 2 * SPAN, 128), lambda j, place: (j, place[1], 0, 0)),
-                pl.BlockSpec((1, 2, SPAN, D), lambda j, place: (part, 0, 0, 0)),
-            ),
-        ),
-        input_output_aliases={4 + i: i for i in range(len(filled))},
-        compiler_params=pltpu.CompilerParams(vmem_limit_bytes=VMEM_LIMIT),
+        in_specs=[pl.BlockSpec(memory_space=pltpu.SMEM), vmem, vmem, vmem],
+        out_specs=(vmem, vmem),
+        compiler_params=pltpu.CompilerParams(vmem_limit_bytes=SMALL_VMEM),
         name="project",
-    )(place, tokens, upstream, weights, *filled)
+    )(place, mine, other, weights)
 
 
 def attend_kernel(
@@ -192,7 +207,7 @@
         other_grad_ref[rank] = grad_ref[tile_rows(TILES - 1 - tile), :].astype(jnp.bfloat16)
 
 
-def attend(core, tiles, own, other):
+def attend(core, tiles, own, other_keys):
     smem = pl.BlockSpec(memory_space=pltpu.SMEM)
     vmem = pl.BlockSpec(memory_space=pltpu.VMEM)
     block = (RANKS, SPAN, 128)
@@ -211,9 +226,9 @@
             pltpu.VMEM((2 * SPAN, 7 * CHUNK), jnp.float32),
             pltpu.VMEM((2 * SPAN, 7 * CHUNK), jnp.float32),
         ],
-        compiler_params=pltpu.CompilerParams(vmem_limit_bytes=VMEM_LIMIT),
+        compiler_params=pltpu.CompilerParams(vmem_limit_bytes=SMALL_VMEM),
         name="attend",
-    )(core, tiles, own, other)
+    )(core, tiles, own, other_keys)
 
 
 def weight_kernel(place_ref, grads_ref, *refs):
@@ -272,7 +287,7 @@
             out_specs=(out_spec, out_spec),
             scratch_shapes=[pltpu.VMEM((8 * SPAN, 512), jnp.bfloat16)],
         ),
-        compiler_params=pltpu.CompilerParams(vmem_limit_bytes=VMEM_LIMIT),
+        compiler_params=pltpu.CompilerParams(vmem_limit_bytes=SMALL_VMEM),
         name="weight_terms",
     )(place, grads, *lines)
 
@@ -364,7 +379,7 @@
             out_specs=(out_spec, out_spec),
             scratch_shapes=[pltpu.VMEM((4, 2 * SPAN, HQ), jnp.bfloat16)],
         ),
-        compiler_params=pltpu.CompilerParams(vmem_limit_bytes=VMEM_LIMIT),
+        compiler_params=pltpu.CompilerParams(vmem_limit_bytes=SMALL_VMEM),
         cost_estimate=pl.CostEstimate(
             flops=8 * 2 * SPAN * D * HQ, bytes_accessed=7 * 1024 * 1024, transcendentals=0
         ),
@@ -379,27 +394,22 @@
     odd = rank % 2
     block = jnp.bitwise_xor(core, odd)
 
-    rows = tokens.reshape(2, SPAN, D)
-    upstream = cotangent.reshape(2, SPAN, D)
-    other_rows = lax.ppermute(rows, "dp", CORE_SWAP)
-    other_upstream = lax.ppermute(upstream, "dp", CORE_SWAP)
+    mine = jnp.stack([rows.reshape(2, SPAN, D) for rows in (tokens, cotangent)])
+    other = lax.ppermute(mine, "dp", CORE_SWAP)
     other_tiles = lax.ppermute(sweep_tiles, "dp", CORE_SWAP)
     core_number = core.astype(jnp.int32).reshape(1)
-    filled = project(
-        jnp.stack([block, core]).astype(jnp.int32), 0, rows, upstream, weights
-    )
     packed, line = project(
-        jnp.stack([block, 1 - core]).astype(jnp.int32),
-        1, other_rows, other_upstream, weights, *filled,
-    )
+        jnp.stack([core, block]).astype(jnp.int32), mine, other, stage(weights)
+    )
+    packed, other_tiles = lax.optimization_barrier((packed, other_tiles))
     packed = packed.reshape(RANKS, 2 * SPAN, 128)
     shifted = [lax.ppermute(line, "dp", shift) for shift in X_SHIFTS]
     own = lax.all_to_all(packed, "ctx", 0, 0)
     near, far, back_near = shifted
     own, near, back_near = lax.optimization_barrier((own, near, back_near))
-    other = lax.ppermute(own[:, SPAN:], "dp", CORE_SWAP)
+    other_keys = lax.ppermute(own[:, SPAN:], "dp", CORE_SWAP)
     tiles = jnp.where(odd == core, sweep_tiles, other_tiles).reshape(-1)
-    query_part, own_grad, other_grad = attend(core_number, tiles, own, other)
+    query_part, own_grad, other_grad = attend(core_number, tiles, own, other_keys)
     arrived = lax.ppermute(other_grad, "dp", CORE_SWAP)
     key_part = (own_grad + arrived.astype(jnp.float32)).astype(jnp.bfloat16)
     back = lax.all_to_all(jnp.concatenate([query_part, key_part], axis=1), "ctx", 0, 0)

time: 159 us -> 159 us (level)
  waiting for transfers between devices: 57.5 us -> 63.2 us
  starting transfers between devices: 43.8 us -> 39.3 us
  local copies, waits for them, and re-layouts: 8.05 us -> 10.2 us
  Pallas kernels: 27.9 us -> 25.8 us
  blocking collectives: 17.2 us -> 15.3 us
    pallas_call x2 -> x1, Pallas kernels: 8.06 us -> 2.55 us  [project(): pl.pallas_call(project_kernel, out_shape=(jax.ShapeDtypeStruct((HEADS, 2,...]
    pallas_call x0 -> x1, Pallas kernels: none -> 2.2 us  [stage(): pl.pallas_call(stage_kernel, out_shape=jax.ShapeDtypeStruct(weights.shape...]
    all_to_all x1, waiting for transfers between devices: 0.01 us -> 2.15 us  [per_device(): lax.all_to_all(jnp.concatenate([query_part, key_part], axis=1), 'ctx', 0, 0)]
    unnamed x12, local copies, waits for them, and re-layouts: 6.2 us -> 8.34 us
    all_to_all x1, starting transfers between devices: 5.62 us -> 3.49 us  [per_device(): lax.all_to_all(back.reshape(4, 2, 2, 2 * SPAN, 128), 'dp', 0, 0, axis_ind...]
    all_to_all x1, blocking collectives: 17.2 us -> 15.3 us  [per_device(): parts = lax.all_to_all(jnp.broadcast_to(rows, (16, 64, 256)), 'dp', 0, 0)]
    all_to_all x1, waiting for transfers between devices: 5.4 us -> 7.11 us  [per_device(): terms = lax.all_to_all(terms, 'ctx', 0, 0)]
    ppermute x3 -> x2, starting transfers between devices: 5.39 us -> 5.37 us  [the longest x1 3.33 us: per_device(): other = lax.ppermute(mine, 'dp', CORE_SWAP)]
  transfers between devices with their start and end apart: 14 -> 13, of which waited for: 10 -> 10; matrix products, arithmetic and copies ran while one was open for 1% -> 1% of each run, Pallas kernels for 6% -> 6%
where the time goes in v6:
time: 159 us; the launch traced here: 158 us
  waiting for transfers between devices  63.2 us (40%)
  starting transfers between devices  39.3 us (25%)
  Pallas kernels  25.8 us (16%)
  blocking collectives  15.3 us (10%)
  local copies, waits for them, and re-layouts  10.2 us (6%)
  other arithmetic  3.57 us (2%)
    ppermute x3, waiting for transfers between devices, per_device(): shifted = [lax.ppermute(line, 'dp', shift) for shift in X_SHIFTS]  36 us
    all_to_all x1, blocking collectives, per_device(): parts = lax.all_to_all(jnp.broadcast_to(rows, (16, 64, 256)), 'dp', 0, 0)  15.3 us
    pallas_call x1, Pallas kernels, attend(): pl.pallas_call(attend_kernel, out_shape=(jax.ShapeDtypeStruct(block, jnp....  11 us
    all_to_all x1, waiting for transfers between devices, per_device(): lax.all_to_all(back.reshape(4, 2, 2, 2 * SPAN, 128), 'dp', 0, 0, axis_ind...  10.2 us
    all_to_all x1, starting transfers between devices, per_device(): own = lax.all_to_all(packed, 'ctx', 0, 0)  9.19 us
    unnamed x12, local copies, waits for them, and re-layouts  8.34 us
    all_to_all x1, waiting for transfers between devices, per_device(): terms = lax.all_to_all(terms, 'ctx', 0, 0)  7.11 us
    all_to_all x1, starting transfers between devices, per_device(): lax.all_to_all(jnp.concatenate([query_part, key_part], axis=1), 'ctx', 0, 0)  6.82 us
  transfers between devices with their start and end apart: 13, of which 10 were waited for; matrix products, arithmetic and copies ran while one was open for 1% of the time, Pallas kernels for 6%

profile of v6, /device:TPU:1, one launch (start us, length us, event | category | flops | bytes accessed | tf_op | source)
XLA Modules:
  0.0 158.2 jit_solution(9221046358197177740)
XLA Ops:
  0.6 1.2 pad_maximum_fusion.mine_ref
  1.8 3.3 %collective-permute-start = (bf16[2,2,96,1024]{3,2,1,0:T(8,128)(2,1)S(1)}, bf16[2,2,96,1024]{3,2,1,0:T(8,128)(2,1)S(1)}, u32[]{:S(2)}, u32[]{:S(2)}) collective-permute-start(bf16[2,2,96,1024]{3,2,1,0:T(8,128)(2,1)S(1)} %pad_maximum_fusion.mine_ref), channel_id=1, source_target_pairs={{0,16},{16,0},{32,48},{48,32},{64,80},{80,64},{96,112},{112,96},{1... | collective-permute-start | bytes 2359304 | tf_op jit(solution)/shard_map/ppermute | solution.py:398
  5.2 0.1 collective-permute-start.1
  5.3 2.2 %stage.1.weights_ref = bf16[4,1024,512]{2,1,0:T(8,128)(2,1)S(1)} custom-call(bf16[4,1024,512]{2,1,0:T(8,128)(2,1)} %weights_ref.3), custom_call_target="tpu_custom_call" | custom-call | tf_op jit(solution)/shard_map/stage/pallas_call | solution.py:37
  7.5 1.9 %copy-done.1 = bf16[4,1024,512]{2,1,0:T(8,128)(2,1)} copy-done((bf16[4,1024,512]{2,1,0:T(8,128)(2,1)}, bf16[4,1024,512]{2,1,0:T(8,128)(2,1)S(1)}, u32[]{:S(2)}) %copy-start.1) | copy-done | bytes 4194328
  9.4 0.1 pad_add_fusion.1.place_ref
  9.5 0.0 collective-permute-done.other_ref
  9.5 2.2 %copy-done.2 = bf16[4,1024,512]{2,1,0:T(8,128)(2,1)S(1)} copy-done((bf16[4,1024,512]{2,1,0:T(8,128)(2,1)S(1)}, bf16[4,1024,512]{2,1,0:T(8,128)(2,1)}, u32[]{:S(2)}) %copy-start.2) | copy-done | bytes 4194328
  11.7 2.5 %project.1 = (bf16[8,2,192,128]{3,2,1,0:T(8,128)(2,1)}, bf16[2,2,96,1024]{3,2,1,0:T(8,128)(2,1)S(1)}) custom-call(s32[2]{0:T(128)S(1)} %pad_add_fusion.1.place_ref, bf16[2,2,96,1024]{3,2,1,0:T(8,128)(2,1)S(1)} %pad_maximum_fusion.mine_ref, bf16[2,2,96,1024]{3,2,1,0:T(8,128)(2,1)S(1)} %collective-permute-done.other_ref, bf16[4,1024,512]{2,1,0:T(8,128)(2,1)S(1)} %copy-done.2), custom_call_target="tpu_custom_call" | custom-call | tf_op jit(solution)/shard_map/project/pallas_call | solution.py:86
  14.2 0.0 collective-permute-done.1
  14.2 9.2 %all-to-all-start = ((bf16[16,192,128]{2,1,0:T(8,128)(2,1)}), bf16[16,192,128]{2,1,0:T(8,128)(2,1)S(1)}, u32[]{:S(2)}, u32[]{:S(2)}) async-start(bf16[16,192,128]{2,1,0:T(8,128)(2,1)} %bitcast.6), calls=%async_computation | async-start | bytes 1572864 | tf_op jit(solution)/shard_map/all_to_all | solution.py:407
  23.4 1.3 collective-permute-start.2
  24.7 1.5 collective-permute-start.3
  26.2 16.9 %collective-permute-done.2.refs_1_ = bf16[2,2,96,1024]{3,2,1,0:T(8,128)(2,1)S(1)} collective-permute-done((bf16[2,2,96,1024]{3,2,1,0:T(8,128)(2,1)S(1)}, bf16[2,2,96,1024]{3,2,1,0:T(8,128)(2,1)S(1)}, u32[]{:S(2)}, u32[]{:S(2)}) %collective-permute-start.2) | collective-permute-done | bytes 786464 | tf_op jit(solution)/shard_map/ppermute | solution.py:406
  43.1 0.0 collective-permute-done.3.refs_3_
  43.1 1.7 %all-to-all-done.own_ref = bf16[16,192,128]{2,1,0:T(8,128)(2,1)S(1)} async-done(((bf16[16,192,128]{2,1,0:T(8,128)(2,1)}), bf16[16,192,128]{2,1,0:T(8,128)(2,1)S(1)}, u32[]{:S(2)}, u32[]{:S(2)}) %all-to-all-start) | async-done | bytes 786464 | tf_op jit(solution)/shard_map/all_to_all | solution.py:407
  44.9 0.8 slice.3
  45.6 2.0 %collective-permute-start.4 = (bf16[16,96,128]{2,1,0:T(8,128)(2,1)}, bf16[16,96,128]{2,1,0:T(8,128)(2,1)S(1)}, u32[]{:S(2)}, u32[]{:S(2)}) collective-permute-start(bf16[16,96,128]{2,1,0:T(8,128)(2,1)} %slice.3), channel_id=1, source_target_pairs={{0,16},{16,0},{32,48},{48,32},{64,80},{80,64},{96,112},{112,96},{1... | collective-permute-start | bytes 1179656 | tf_op jit(solution)/shard_map/ppermute | solution.py:410
  47.7 1.6 collective-permute-done.4.other_ref
  49.2 11.0 %attend.1 = (bf16[16,96,128]{2,1,0:T(8,128)(2,1)S(1)}, f32[16,96,128]{2,1,0:T(8,128)S(1)}, bf16[16,96,128]{2,1,0:T(8,128)(2,1)S(1)}) custom-call(s32[1]{0:T(128)} %bitcast.core_ref, s32[4]{0:T(128)S(1)} %fusion.tiles_ref, bf16[16,192,128]{2,1,0:T(8,128)(2,1)S(1)} %all-to-all-done.own_ref, bf16[16,96,128]{2,1,0:T(8,128)(2,1)S(1)} %collective-permute-done.4.other_ref), custom_call_target="tpu_custom_call" | custom-call | tf_op jit(solution)/shard_map/attend/pallas_call | solution.py:214
  60.2 0.1 collective-permute-start.5
  60.3 1.7 %collective-permute-done.5 = bf16[16,96,128]{2,1,0:T(8,128)(2,1)S(1)} collective-permute-done((bf16[16,96,128]{2,1,0:T(8,128)(2,1)S(1)}, bf16[16,96,128]{2,1,0:T(8,128)(2,1)S(1)}, u32[]{:S(2)}, u32[]{:S(2)}) %collective-permute-start.5) | collective-permute-done | bytes 393248 | tf_op jit(solution)/shard_map/ppermute | solution.py:413
  62.0 0.1 add_convert_fusion.1
  62.1 1.0 pad_maximum_fusion.1
  63.1 6.8 %all-to-all-start.1 = ((bf16[16,192,128]{2,1,0:T(8,128)(2,1)}), bf16[16,192,128]{2,1,0:T(8,128)(2,1)}, u32[]{:S(2)}, u32[]{:S(2)}) async-start(bf16[16,192,128]{2,1,0:T(8,128)(2,1)} %pad_maximum_fusion.1), calls=%async_computation.1 | async-start | bytes 1572864 | tf_op jit(solution)/shard_map/all_to_all | solution.py:415
  70.0 1.3 collective-permute-start.6
  71.3 19.0 %collective-permute-done.6.refs_2_ = bf16[2,2,96,1024]{3,2,1,0:T(8,128)(2,1)S(1)} collective-permute-done((bf16[2,2,96,1024]{3,2,1,0:T(8,128)(2,1)S(1)}, bf16[2,2,96,1024]{3,2,1,0:T(8,128)(2,1)S(1)}, u32[]{:S(2)}, u32[]{:S(2)}) %collective-permute-start.6) | collective-permute-done | bytes 786464 | tf_op jit(solution)/shard_map/ppermute | solution.py:406
  90.3 0.9 copy-done.3
  91.2 2.2 %all-to-all-done.1 = bf16[16,192,128]{2,1,0:T(8,128)(2,1)} async-done(((bf16[16,192,128]{2,1,0:T(8,128)(2,1)}), bf16[16,192,128]{2,1,0:T(8,128)(2,1)}, u32[]{:S(2)}, u32[]{:S(2)}) %all-to-all-start.1) | async-done | bytes 786464 | tf_op jit(solution)/shard_map/all_to_all | solution.py:415
  93.4 3.5 %all-to-all-start.2 = ((bf16[4,2,2,192,128]{4,3,2,1,0:T(8,128)(2,1)}), bf16[4,2,2,192,128]{4,3,2,1,0:T(8,128)(2,1)S(1)}, u32[]{:S(2)}, u32[]{:S(2)}) async-start(bf16[4,2,2,192,128]{4,3,2,1,0:T(8,128)(2,1)} %bitcast.7), calls=%async_computation.2 | async-start | bytes 1572864 | tf_op jit(solution)/shard_map/all_to_all | solution.py:419
  96.9 0.1 pad_add_fusion.place_ref
  97.0 10.2 %all-to-all-done.2.grads_ref = bf16[4,2,2,192,128]{4,3,2,1,0:T(8,128)(2,1)S(1)} async-done(((bf16[4,2,2,192,128]{4,3,2,1,0:T(8,128)(2,1)}), bf16[4,2,2,192,128]{4,3,2,1,0:T(8,128)(2,1)S(1)}, u32[]{:S(2)}, u32[]{:S(2)}) %all-to-all-start.2) | async-done | bytes 786464 | tf_op jit(solution)/shard_map/all_to_all | solution.py:419
  107.1 1.1 copy-done.4
  108.3 3.3 %weight_terms.1 = (bf16[16,64,256]{2,1,0:T(8,128)(2,1)S(1)}, bf16[16,64,256]{2,1,0:T(8,128)(2,1)S(1)}) custom-call(s32[2]{0:T(128)S(1)} %pad_add_fusion.place_ref, bf16[4,2,2,192,128]{4,3,2,1,0:T(8,128)(2,1)S(1)} %all-to-all-done.2.grads_ref, bf16[2,2,96,1024]{3,2,1,0:T(8,128)(2,1)S(1)} %get-tuple-element.27.refs_0_, ...), custom_call_target="tpu_custom_call" | custom-call | tf_op jit(solution)/shard_map/weight_terms/pallas_call | solution.py:277
  111.6 3.0 %collective-permute-start.7 = (bf16[16,64,256]{2,1,0:T(8,128)(2,1)S(1)}, bf16[16,64,256]{2,1,0:T(8,128)(2,1)S(1)}, u32[]{:S(2)}, u32[]{:S(2)}) collective-permute-start(bf16[16,64,256]{2,1,0:T(8,128)(2,1)S(1)} %get-tuple-element.37), channel_id=1, source_target_pairs={{0,16},{16,0},{32,48},{48,32},{64,80},{80,64},{96,112},{112,96},{1... | collective-permute-start | bytes 1572872 | tf_op jit(solution)/shard_map/ppermute | solution.py:425
  114.6 1.5 collective-permute-done.7
  116.2 1.0 add_convert_fusion
  117.1 6.4 %all-to-all-start.3 = ((bf16[16,64,256]{2,1,0:T(8,128)(2,1)}), bf16[16,64,256]{2,1,0:T(8,128)(2,1)S(1)}, u32[]{:S(2)}, u32[]{:S(2)}) async-start(bf16[16,64,256]{2,1,0:T(8,128)(2,1)} %add_convert_fusion), calls=%async_computation.3 | async-start | bytes 1048576 | tf_op jit(solution)/shard_map/all_to_all | solution.py:428
  123.5 1.0 dynamic-slice_bitcast_fusion
  124.6 0.7 collective-permute-start.8
  125.3 0.1 pad_add_fusion.2.place_ref
  125.4 1.3 collective-permute-done.8.arrived_ref
  126.6 2.2 %copy-done = bf16[4,1024,512]{2,1,0:T(8,128)(2,1)S(1)} copy-done((bf16[4,1024,512]{2,1,0:T(8,128)(2,1)S(1)}, bf16[4,1024,512]{2,1,0:T(8,128)(2,1)}, u32[]{:S(2)}) %copy-start) | copy-done | bytes 4194328
  128.8 4.9 %outputs.1 = (bf16[2,96,1024]{2,1,0:T(8,128)(2,1)}, bf16[2,96,1024]{2,1,0:T(8,128)(2,1)}) custom-call(s32[2]{0:T(128)S(1)} %pad_add_fusion.2.place_ref, bf16[8,2,192,128]{3,2,1,0:T(8,128)(2,1)} %bitcast.8.grads_ref, bf16[8,192,128]{2,1,0:T(8,128)(2,1)S(1)} %collective-permute-done.8.arrived_ref, bf16[4,1024,512]{2,1,0:T(8,128)(2,1)S(1)} %copy-done), custom_call_target="tpu_custom_call" | custom-call | flops 805306368 | bytes 7340032 | tf_op jit(solution)/shard_map/outputs/pallas_call | solution.py:368
  133.7 7.1 %all-to-all-done.3 = bf16[16,64,256]{2,1,0:T(8,128)(2,1)S(1)} async-done(((bf16[16,64,256]{2,1,0:T(8,128)(2,1)}), bf16[16,64,256]{2,1,0:T(8,128)(2,1)S(1)}, u32[]{:S(2)}, u32[]{:S(2)}) %all-to-all-start.3) | async-done | bytes 524320 | tf_op jit(solution)/shard_map/all_to_all | solution.py:428
  140.8 0.1 reduce_sum.12
  141.0 15.3 %all_to_all.25 = bf16[16,64,256]{2,1,0:T(8,128)(2,1)} all-to-all(bf16[16,64,256]{2,1,0:T(8,128)(2,1)S(1)} %broadcast_in_dim.3), channel_id=1, replica_groups=mesh['dp'=16,'ctx'=16] {'dp'}, dimensions={0} | all-to-all | bytes 1048576 | tf_op jit(solution)/shard_map/all_to_all | solution.py:436
  156.3 1.9 %spread_heads.1 = bf16[4,64,512]{2,1,0:T(8,128)(2,1)} custom-call(bf16[4,2,2,64,256]{4,3,2,1,0:T(8,128)(2,1)} %bitcast.16), custom_call_target="tpu_custom_call" | custom-call | tf_op jit(solution)/shard_map/spread_heads/pallas_call | solution.py:319
  (9 shorter events, 0.1 us)
Async XLA Ops:
  0.6 4.5 %copy-start.5 = (s32[1,4]{1,0:T(1,128)S(1)}, s32[1,4]{1,0:T(1,128)}, u32[]{:S(2)}) copy-start(s32[1,4]{1,0:T(1,128)} %param.5) | copy-start | bytes 52
  1.8 7.7 %collective-permute-start = (bf16[2,2,96,1024]{3,2,1,0:T(8,128)(2,1)S(1)}, bf16[2,2,96,1024]{3,2,1,0:T(8,128)(2,1)S(1)}, u32[]{:S(2)}, u32[]{:S(2)}) collective-permute-start(bf16[2,2,96,1024]{3,2,1,0:T(8,128)(2,1)S(1)} %pad_maximum_fusion.mine_ref), channel_id=1, source_target_pairs={{0,16},{16,0},{32,48},{48,32},{64,80},{80,64},{96,112},{112,96},{1... | collective-permute-start | bytes 2359304 | tf_op jit(solution)/shard_map/ppermute | solution.py:398
  5.2 9.1 %collective-permute-start.1 = (s32[1,4]{1,0:T(1,128)S(1)}, s32[1,4]{1,0:T(1,128)S(1)}, u32[]{:S(2)}, u32[]{:S(2)}) collective-permute-start(s32[1,4]{1,0:T(1,128)S(1)} %copy-done.5), channel_id=1, source_target_pairs={{0,16},{16,0},{32,48},{48,32},{64,80},{80,64},{96,112},{112,96},{1... | collective-permute-start | bytes 56 | tf_op jit(solution)/shard_map/ppermute | solution.py:399
  7.5 1.9 %copy-start.1 = (bf16[4,1024,512]{2,1,0:T(8,128)(2,1)}, bf16[4,1024,512]{2,1,0:T(8,128)(2,1)S(1)}, u32[]{:S(2)}) copy-start(bf16[4,1024,512]{2,1,0:T(8,128)(2,1)S(1)} %stage.1.weights_ref) | copy-start | bytes 12582916
  9.5 2.2 %copy-start.2 = (bf16[4,1024,512]{2,1,0:T(8,128)(2,1)S(1)}, bf16[4,1024,512]{2,1,0:T(8,128)(2,1)}, u32[]{:S(2)}) copy-start(bf16[4,1024,512]{2,1,0:T(8,128)(2,1)} %copy-done.1) | copy-start | bytes 12582916
  14.2 30.6 %all-to-all-start = ((bf16[16,192,128]{2,1,0:T(8,128)(2,1)}), bf16[16,192,128]{2,1,0:T(8,128)(2,1)S(1)}, u32[]{:S(2)}, u32[]{:S(2)}) async-start(bf16[16,192,128]{2,1,0:T(8,128)(2,1)} %bitcast.6), calls=%async_computation | async-start | bytes 1572864 | tf_op jit(solution)/shard_map/all_to_all | solution.py:407
  23.4 19.7 %collective-permute-start.2 = (bf16[2,2,96,1024]{3,2,1,0:T(8,128)(2,1)S(1)}, bf16[2,2,96,1024]{3,2,1,0:T(8,128)(2,1)S(1)}, u32[]{:S(2)}, u32[]{:S(2)}) collective-permute-start(bf16[2,2,96,1024]{3,2,1,0:T(8,128)(2,1)S(1)} %get-tuple-element.27.refs_0_), channel_id=1, source_target_pairs={{0,64},{16,80},{32,96},{48,112},{64,128},{80,144},{96,160},{112,17... | collective-permute-start | bytes 2359304 | tf_op jit(solution)/shard_map/ppermute | solution.py:406
  24.7 18.4 %collective-permute-start.3 = (bf16[2,2,96,1024]{3,2,1,0:T(8,128)(2,1)S(1)}, bf16[2,2,96,1024]{3,2,1,0:T(8,128)(2,1)S(1)}, u32[]{:S(2)}, u32[]{:S(2)}) collective-permute-start(bf16[2,2,96,1024]{3,2,1,0:T(8,128)(2,1)S(1)} %get-tuple-element.27.refs_0_), channel_id=1, source_target_pairs={{0,192},{16,208},{32,224},{48,240},{64,0},{80,16},{96,32},{112,48}... | collective-permute-start | bytes 2359304 | tf_op jit(solution)/shard_map/ppermute | solution.py:406
  45.6 3.6 %collective-permute-start.4 = (bf16[16,96,128]{2,1,0:T(8,128)(2,1)}, bf16[16,96,128]{2,1,0:T(8,128)(2,1)S(1)}, u32[]{:S(2)}, u32[]{:S(2)}) collective-permute-start(bf16[16,96,128]{2,1,0:T(8,128)(2,1)} %slice.3), channel_id=1, source_target_pairs={{0,16},{16,0},{32,48},{48,32},{64,80},{80,64},{96,112},{112,96},{1... | collective-permute-start | bytes 1179656 | tf_op jit(solution)/shard_map/ppermute | solution.py:410
  60.2 1.8 %collective-permute-start.5 = (bf16[16,96,128]{2,1,0:T(8,128)(2,1)S(1)}, bf16[16,96,128]{2,1,0:T(8,128)(2,1)S(1)}, u32[]{:S(2)}, u32[]{:S(2)}) collective-permute-start(bf16[16,96,128]{2,1,0:T(8,128)(2,1)S(1)} %get-tuple-element.31), channel_id=1, source_target_pairs={{0,16},{16,0},{32,48},{48,32},{64,80},{80,64},{96,112},{112,96},{1... | collective-permute-start | bytes 1179656 | tf_op jit(solution)/shard_map/ppermute | solution.py:413
  63.1 30.3 %all-to-all-start.1 = ((bf16[16,192,128]{2,1,0:T(8,128)(2,1)}), bf16[16,192,128]{2,1,0:T(8,128)(2,1)}, u32[]{:S(2)}, u32[]{:S(2)}) async-start(bf16[16,192,128]{2,1,0:T(8,128)(2,1)} %pad_maximum_fusion.1), calls=%async_computation.1 | async-start | bytes 1572864 | tf_op jit(solution)/shard_map/all_to_all | solution.py:415
  70.0 20.4 %collective-permute-start.6 = (bf16[2,2,96,1024]{3,2,1,0:T(8,128)(2,1)S(1)}, bf16[2,2,96,1024]{3,2,1,0:T(8,128)(2,1)S(1)}, u32[]{:S(2)}, u32[]{:S(2)}) collective-permute-start(bf16[2,2,96,1024]{3,2,1,0:T(8,128)(2,1)S(1)} %get-tuple-element.27.refs_0_), channel_id=1, source_target_pairs={{0,128},{16,144},{32,160},{48,176},{64,192},{80,208},{96,224},{112... | collective-permute-start | bytes 2359304 | tf_op jit(solution)/shard_map/ppermute | solution.py:406
  90.3 0.9 copy-start.3
  93.4 13.7 %all-to-all-start.2 = ((bf16[4,2,2,192,128]{4,3,2,1,0:T(8,128)(2,1)}), bf16[4,2,2,192,128]{4,3,2,1,0:T(8,128)(2,1)S(1)}, u32[]{:S(2)}, u32[]{:S(2)}) async-start(bf16[4,2,2,192,128]{4,3,2,1,0:T(8,128)(2,1)} %bitcast.7), calls=%async_computation.2 | async-start | bytes 1572864 | tf_op jit(solution)/shard_map/all_to_all | solution.py:419
  107.1 1.1 copy-start.4
  111.6 4.6 %collective-permute-start.7 = (bf16[16,64,256]{2,1,0:T(8,128)(2,1)S(1)}, bf16[16,64,256]{2,1,0:T(8,128)(2,1)S(1)}, u32[]{:S(2)}, u32[]{:S(2)}) collective-permute-start(bf16[16,64,256]{2,1,0:T(8,128)(2,1)S(1)} %get-tuple-element.37), channel_id=1, source_target_pairs={{0,16},{16,0},{32,48},{48,32},{64,80},{80,64},{96,112},{112,96},{1... | collective-permute-start | bytes 1572872 | tf_op jit(solution)/shard_map/ppermute | solution.py:425
  117.1 23.7 %all-to-all-start.3 = ((bf16[16,64,256]{2,1,0:T(8,128)(2,1)}), bf16[16,64,256]{2,1,0:T(8,128)(2,1)S(1)}, u32[]{:S(2)}, u32[]{:S(2)}) async-start(bf16[16,64,256]{2,1,0:T(8,128)(2,1)} %add_convert_fusion), calls=%async_computation.3 | async-start | bytes 1048576 | tf_op jit(solution)/shard_map/all_to_all | solution.py:428
  124.6 2.1 %collective-permute-start.8 = (bf16[8,192,128]{2,1,0:T(8,128)(2,1)S(1)}, bf16[8,192,128]{2,1,0:T(8,128)(2,1)S(1)}, u32[]{:S(2)}, u32[]{:S(2)}) collective-permute-start(bf16[8,192,128]{2,1,0:T(8,128)(2,1)S(1)} %dynamic-slice_bitcast_fusion), channel_id=1, source_target_pairs={{0,16},{16,0},{32,48},{48,32},{64,80},{80,64},{96,112},{112,96},{1... | collective-permute-start | bytes 1179656 | tf_op jit(solution)/shard_map/ppermute | solution.py:429
  126.6 2.2 %copy-start = (bf16[4,1024,512]{2,1,0:T(8,128)(2,1)S(1)}, bf16[4,1024,512]{2,1,0:T(8,128)(2,1)}, u32[]{:S(2)}) copy-start(bf16[4,1024,512]{2,1,0:T(8,128)(2,1)} %weights_ref.3) | copy-start | bytes 12582916

commit v7 on v5

--- a/solution.py
+++ b/solution.py
@@ -15,7 +15,8 @@
 CHUNK = 256
 KEY_ROWS = TILES * SPAN + CHUNK
 NEGATIVE = -1e30
-VMEM_LIMIT = 48 * 1024 * 1024
+SMALL_VMEM = 24 * 1024 * 1024
+PROJECT_VMEM = 60 * 1024 * 1024
 
 CORE_SWAP = [(i, i ^ 1) for i in range(16)]
 CHIP_LINES = [[4 * x + rest for x in range(4)] for rest in range(4)]
@@ -26,59 +27,56 @@
     return lax.broadcasted_iota(jnp.int32, (rows, 128), 1) < HEAD
 
 
-def project_kernel(place_ref, tokens_ref, upstream_ref, weights_ref, *refs):
-    out_ref, line_ref = refs[-2:]
-    inputs = tokens_ref[0]
-    upstream = upstream_ref[0]
-
-    @pl.when(pl.program_id(0) == 0)
-    def _():
-        line_ref[0, 0] = inputs
-        line_ref[0, 1] = upstream
+def project_kernel(place_ref, tokens_ref, upstream_ref, weights_ref, keep_ref, give_ref):
+    keep_first = place_ref[1] == 0
+    inputs = tokens_ref[...].reshape(2 * SPAN, D)
+    upstream = upstream_ref[...].reshape(2 * SPAN, D)
 
     def product(rows, number):
         return jnp.dot(rows, weights_ref[number], preferred_element_type=jnp.float32)
 
     queries, keys, values = (product(inputs, number) for number in range(3))
     grads = product(upstream, 3)
-    low = low_lanes(SPAN)
+    low = low_lanes(2 * SPAN)
     for half, (first, second) in enumerate(((queries, grads), (keys, values))):
         place = slice(SPAN * half, SPAN * half + SPAN)
         for pair in range(2):
             one = first[:, 128 * pair : 128 * pair + 128]
             two = second[:, 128 * pair : 128 * pair + 128]
-            even = jnp.where(low, one, pltpu.roll(two, HEAD, 1)).astype(jnp.bfloat16)
-            odd = jnp.where(low, pltpu.roll(one, HEAD, 1), two).astype(jnp.bfloat16)
-            out_ref[2 * pair, 0, place, :] = even
-            out_ref[2 * pair + 1, 0, place, :] = odd
-
-
-def project(place, part, tokens, upstream, weights, *filled):
-    block_spec = pl.BlockSpec((1, SPAN, D), lambda j, place: (place[0], 0, 0))
+            even = jnp.where(low, one, pltpu.roll(two, HEAD, 1))
+            odd = jnp.where(low, pltpu.roll(one, HEAD, 1), two)
+            for head, rows in ((2 * pair, even), (2 * pair + 1, odd)):
+                zero, other = rows[:SPAN], rows[SPAN:]
+                keep_ref[head, 0, place, :] = jnp.where(keep_first, zero, other).astype(
+                    jnp.bfloat16
+                )
+                give_ref[head, place, :] = jnp.where(keep_first, other, zero).astype(jnp.bfloat16)
+
+
+def project(place, tokens, upstream, weights):
+    rows_spec = pl.BlockSpec((2, SPAN, D), lambda j, place: (0, 0, 0))
     return pl.pallas_call(
         project_kernel,
         out_shape=(
             jax.ShapeDtypeStruct((HEADS, 2, 2 * SPAN, 128), jnp.bfloat16),
-            jax.ShapeDtypeStruct((2, 2, SPAN, D), jnp.bfloat16),
+            jax.ShapeDtypeStruct((HEADS, 2 * SPAN, 128), jnp.bfloat16),
         ),
         grid_spec=pltpu.PrefetchScalarGridSpec(
             num_scalar_prefetch=1,
             grid=(2,),
             in_specs=[
-                block_spec,
-                block_spec,
+                rows_spec,
+                rows_spec,
                 pl.BlockSpec((4, D, HQ // 2), lambda j, place: (0, 0, j)),
-            ]
-            + [pl.BlockSpec(memory_space=pl.ANY)] * len(filled),
+            ],
             out_specs=(
-                pl.BlockSpec((HEADS // 2, 1, 2 * SPAN, 128), lambda j, place: (j, place[1], 0, 0)),
-                pl.BlockSpec((1, 2, SPAN, D), lambda j, place: (part, 0, 0, 0)),
+                pl.BlockSpec((HEADS // 2, 1, 2 * SPAN, 128), lambda j, place: (j, place[0], 0, 0)),
+                pl.BlockSpec((HEADS // 2, 2 * SPAN, 128), lambda j, place: (j, 0, 0)),
             ),
         ),
-        input_output_aliases={4 + i: i for i in range(len(filled))},
-        compiler_params=pltpu.CompilerParams(vmem_limit_bytes=VMEM_LIMIT),
+        compiler_params=pltpu.CompilerParams(vmem_limit_bytes=PROJECT_VMEM),
         name="project",
-    )(place, tokens, upstream, weights, *filled)
+    )(place, tokens, upstream, weights)
 
 
 def attend_kernel(
@@ -192,7 +190,7 @@
         other_grad_ref[rank] = grad_ref[tile_rows(TILES - 1 - tile), :].astype(jnp.bfloat16)
 
 
-def attend(core, tiles, own, other):
+def attend(core, tiles, own, other_keys):
     smem = pl.BlockSpec(memory_space=pltpu.SMEM)
     vmem = pl.BlockSpec(memory_space=pltpu.VMEM)
     block = (RANKS, SPAN, 128)
@@ -211,9 +209,9 @@
             pltpu.VMEM((2 * SPAN, 7 * CHUNK), jnp.float32),
             pltpu.VMEM((2 * SPAN, 7 * CHUNK), jnp.float32),
         ],
-        compiler_params=pltpu.CompilerParams(vmem_limit_bytes=VMEM_LIMIT),
+        compiler_params=pltpu.CompilerParams(vmem_limit_bytes=SMALL_VMEM),
         name="attend",
-    )(core, tiles, own, other)
+    )(core, tiles, own, other_keys)
 
 
 def weight_kernel(place_ref, grads_ref, *refs):
@@ -272,7 +270,7 @@
             out_specs=(out_spec, out_spec),
             scratch_shapes=[pltpu.VMEM((8 * SPAN, 512), jnp.bfloat16)],
         ),
-        compiler_params=pltpu.CompilerParams(vmem_limit_bytes=VMEM_LIMIT),
+        compiler_params=pltpu.CompilerParams(vmem_limit_bytes=SMALL_VMEM),
         name="weight_terms",
     )(place, grads, *lines)
 
@@ -364,7 +362,7 @@
             out_specs=(out_spec, out_spec),
             scratch_shapes=[pltpu.VMEM((4, 2 * SPAN, HQ), jnp.bfloat16)],
         ),
-        compiler_params=pltpu.CompilerParams(vmem_limit_bytes=VMEM_LIMIT),
+        compiler_params=pltpu.CompilerParams(vmem_limit_bytes=SMALL_VMEM),
         cost_estimate=pl.CostEstimate(
             flops=8 * 2 * SPAN * D * HQ, bytes_accessed=7 * 1024 * 1024, transcendentals=0
         ),
@@ -381,25 +379,29 @@
 
     rows = tokens.reshape(2, SPAN, D)
     upstream = cotangent.reshape(2, SPAN, D)
-    other_rows = lax.ppermute(rows, "dp", CORE_SWAP)
-    other_upstream = lax.ppermute(upstream, "dp", CORE_SWAP)
     other_tiles = lax.ppermute(sweep_tiles, "dp", CORE_SWAP)
     core_number = core.astype(jnp.int32).reshape(1)
-    filled = project(
-        jnp.stack([block, core]).astype(jnp.int32), 0, rows, upstream, weights
-    )
-    packed, line = project(
-        jnp.stack([block, 1 - core]).astype(jnp.int32),
-        1, other_rows, other_upstream, weights, *filled,
-    )
+    packed, give = project(
+        jnp.stack([core, block]).astype(jnp.int32), rows, upstream, weights
+    )
+    given = lax.ppermute(give, "dp", CORE_SWAP)
+    packed = lax.dynamic_update_index_in_dim(packed, given, 1 - core, 1)
+
+    def chosen(number):
+        return jnp.stack(
+            [lax.dynamic_index_in_dim(x, number, 0, keepdims=False) for x in (rows, upstream)]
+        )
+
+    line = jnp.stack([chosen(block), lax.ppermute(chosen(1 - block), "dp", CORE_SWAP)])
+    packed, other_tiles = lax.optimization_barrier((packed, other_tiles))
     packed = packed.reshape(RANKS, 2 * SPAN, 128)
     shifted = [lax.ppermute(line, "dp", shift) for shift in X_SHIFTS]
     own = lax.all_to_all(packed, "ctx", 0, 0)
     near, far, back_near = shifted
     own, near, back_near = lax.optimization_barrier((own, near, back_near))
-    other = lax.ppermute(own[:, SPAN:], "dp", CORE_SWAP)
+    other_keys = lax.ppermute(own[:, SPAN:], "dp", CORE_SWAP)
     tiles = jnp.where(odd == core, sweep_tiles, other_tiles).reshape(-1)
-    query_part, own_grad, other_grad = attend(core_number, tiles, own, other)
+    query_part, own_grad, other_grad = attend(core_number, tiles, own, other_keys)
     arrived = lax.ppermute(other_grad, "dp", CORE_SWAP)
     key_part = (own_grad + arrived.astype(jnp.float32)).astype(jnp.bfloat16)
     back = lax.all_to_all(jnp.concatenate([query_part, key_part], axis=1), "ctx", 0, 0)

time: 159 us -> 159 us (level)
  starting transfers between devices: 43.8 us -> 47.5 us
  Pallas kernels: 27.9 us -> 24.6 us
    ppermute x1 -> x2, starting transfers between devices: 3.12 us -> 9.45 us  [per_device(): given = lax.ppermute(give, 'dp', CORE_SWAP)]
    ppermute x3 -> x2, starting transfers between devices: 5.39 us -> 1.94 us  [the longest x1 1.2 us: per_device(): other_keys = lax.ppermute(own[:, SPAN:], 'dp', CORE_SWAP)]
    pallas_call x2 -> x1, Pallas kernels: 8.06 us -> 4.7 us  [project(): pl.pallas_call(project_kernel, out_shape=(jax.ShapeDtypeStruct((HEADS, 2,...]
    ppermute x3 -> x2, waiting for transfers between devices: 0.39 us -> 2.86 us  [the longest x1 1.56 us: per_device(): other_keys = lax.ppermute(own[:, SPAN:], 'dp', CORE_SWAP)]
    all_to_all x1, starting transfers between devices: 6.91 us -> 9.37 us  [per_device(): lax.all_to_all(jnp.concatenate([query_part, key_part], axis=1), 'ctx', 0, 0)]
    unnamed x12, local copies, waits for them, and re-layouts: 6.2 us -> 4.22 us
    all_to_all x1, waiting for transfers between devices: 10.1 us -> 8.26 us  [per_device(): lax.all_to_all(back.reshape(4, 2, 2, 2 * SPAN, 128), 'dp', 0, 0, axis_ind...]
    all_to_all x1, waiting for transfers between devices: 1.72 us -> 0.01 us  [per_device(): own = lax.all_to_all(packed, 'ctx', 0, 0)]
  transfers between devices with their start and end apart: 14 -> 14, of which waited for: 10 -> 10; matrix products, arithmetic and copies ran while one was open for 1% -> 1% of each run, Pallas kernels for 6% -> 3%
where the time goes in v7:
time: 159 us; the launch traced here: 157 us
  waiting for transfers between devices  57.4 us (36%)
  starting transfers between devices  47.5 us (30%)
  Pallas kernels  24.6 us (15%)
  blocking collectives  17.2 us (11%)
  local copies, waits for them, and re-layouts  6.95 us (4%)
  other arithmetic  3.06 us (2%)
    ppermute x3, waiting for transfers between devices, per_device(): shifted = [lax.ppermute(line, 'dp', shift) for shift in X_SHIFTS]  35.4 us
    all_to_all x1, blocking collectives, per_device(): parts = lax.all_to_all(jnp.broadcast_to(rows, (16, 64, 256)), 'dp', 0, 0)  17.2 us
    pallas_call x1, Pallas kernels, attend(): pl.pallas_call(attend_kernel, out_shape=(jax.ShapeDtypeStruct(block, jnp....  9.77 us
    ppermute x2, starting transfers between devices, per_device(): given = lax.ppermute(give, 'dp', CORE_SWAP)  9.45 us
    all_to_all x1, starting transfers between devices, per_device(): lax.all_to_all(jnp.concatenate([query_part, key_part], axis=1), 'ctx', 0, 0)  9.37 us
    all_to_all x1, starting transfers between devices, per_device(): own = lax.all_to_all(packed, 'ctx', 0, 0)  9.19 us
    all_to_all x1, waiting for transfers between devices, per_device(): lax.all_to_all(back.reshape(4, 2, 2, 2 * SPAN, 128), 'dp', 0, 0, axis_ind...  8.26 us
    all_to_all x1, starting transfers between devices, per_device(): terms = lax.all_to_all(terms, 'ctx', 0, 0)  6.99 us
  transfers between devices with their start and end apart: 14, of which 10 were waited for; matrix products, arithmetic and copies ran while one was open for 1% of the time, Pallas kernels for 3%

profile of v7, /device:TPU:1, one launch (start us, length us, event | category | flops | bytes accessed | tf_op | source)
XLA Modules:
  0.0 157.4 jit_solution(5145281721231038820)
XLA Ops:
  0.7 0.6 pad_add_fusion.1.place_ref
  1.2 4.7 %project.1 = (bf16[8,2,192,128]{3,2,1,0:T(8,128)(2,1)}, bf16[8,192,128]{2,1,0:T(8,128)(2,1)}) custom-call(s32[2]{0:T(128)} %pad_add_fusion.1.place_ref, bf16[2,96,1024]{2,1,0:T(8,128)(2,1)} %bitcast.32, bf16[2,96,1024]{2,1,0:T(8,128)(2,1)} %bitcast.33, bf16[4,1024,512]{2,1,0:T(8,128)(2,1)} %weights_ref.3), custom_call_target="tpu_custom_call" | custom-call | tf_op jit(solution)/shard_map/project/pallas_call | solution.py:58
  5.9 3.3 %collective-permute-start = (bf16[8,192,128]{2,1,0:T(8,128)(2,1)}, bf16[8,192,128]{2,1,0:T(8,128)(2,1)S(1)}, u32[]{:S(2)}, u32[]{:S(2)}) collective-permute-start(bf16[8,192,128]{2,1,0:T(8,128)(2,1)} %get-tuple-element.25), channel_id=1, source_target_pairs={{0,16},{16,0},{32,48},{48,32},{64,80},{80,64},{96,112},{112,96},{1... | collective-permute-start | bytes 1179656 | tf_op jit(solution)/shard_map/ppermute | solution.py:387
  9.3 0.1 collective-permute-start.1
  9.4 1.4 collective-permute-done
  10.8 0.8 bitcast_dynamic-update-slice_fusion
  11.6 0.0 collective-permute-done.1
  11.6 9.2 %all-to-all-start = ((bf16[16,192,128]{2,1,0:T(8,128)(2,1)}), bf16[16,192,128]{2,1,0:T(8,128)(2,1)S(1)}, u32[]{:S(2)}, u32[]{:S(2)}) async-start(bf16[16,192,128]{2,1,0:T(8,128)(2,1)} %bitcast.34), calls=%async_computation | async-start | bytes 1572864 | tf_op jit(solution)/shard_map/all_to_all | solution.py:399
  20.9 0.1 dynamic-slice_bitcast_fusion.3
  21.0 0.7 collective-permute-start.2
  21.8 1.3 collective-permute-done.2
  23.1 0.1 pad_maximum_fusion.refs_0_
  23.1 1.3 collective-permute-start.3
  24.4 1.5 collective-permute-start.4
  25.9 17.3 %collective-permute-done.3.refs_1_ = bf16[2,2,96,1024]{3,2,1,0:T(8,128)(2,1)S(1)} collective-permute-done((bf16[2,2,96,1024]{3,2,1,0:T(8,128)(2,1)S(1)}, bf16[2,2,96,1024]{3,2,1,0:T(8,128)(2,1)S(1)}, u32[]{:S(2)}, u32[]{:S(2)}) %collective-permute-start.3) | collective-permute-done | bytes 786464 | tf_op jit(solution)/shard_map/ppermute | solution.py:398
  43.2 0.0 collective-permute-done.4.refs_3_
  43.2 0.0 all-to-all-done.own_ref
  43.2 0.8 slice.3
  44.0 1.2 collective-permute-start.5
  45.2 1.6 collective-permute-done.5.other_ref
  46.7 9.8 %attend.1 = (bf16[16,96,128]{2,1,0:T(8,128)(2,1)S(1)}, f32[16,96,128]{2,1,0:T(8,128)S(1)}, bf16[16,96,128]{2,1,0:T(8,128)(2,1)S(1)}) custom-call(s32[1]{0:T(128)} %bitcast.core_ref, s32[4]{0:T(128)S(1)} %fusion.tiles_ref, bf16[16,192,128]{2,1,0:T(8,128)(2,1)S(1)} %all-to-all-done.own_ref, bf16[16,96,128]{2,1,0:T(8,128)(2,1)S(1)} %collective-permute-done.5.other_ref), custom_call_target="tpu_custom_call" | custom-call | tf_op jit(solution)/shard_map/attend/pallas_call | solution.py:197
  56.5 1.0 collective-permute-start.6
  57.6 1.3 collective-permute-done.6
  58.9 0.1 add_convert_fusion.1
  59.0 1.0 pad_maximum_fusion.1
  60.0 9.4 %all-to-all-start.1 = ((bf16[16,192,128]{2,1,0:T(8,128)(2,1)}), bf16[16,192,128]{2,1,0:T(8,128)(2,1)}, u32[]{:S(2)}, u32[]{:S(2)}) async-start(bf16[16,192,128]{2,1,0:T(8,128)(2,1)} %pad_maximum_fusion.1), calls=%async_computation.1 | async-start | bytes 1572864 | tf_op jit(solution)/shard_map/all_to_all | solution.py:407
  69.4 2.0 %collective-permute-start.7 = (bf16[2,2,96,1024]{3,2,1,0:T(8,128)(2,1)S(1)}, bf16[2,2,96,1024]{3,2,1,0:T(8,128)(2,1)S(1)}, u32[]{:S(2)}, u32[]{:S(2)}) collective-permute-start(bf16[2,2,96,1024]{3,2,1,0:T(8,128)(2,1)S(1)} %pad_maximum_fusion.refs_0_), channel_id=1, source_target_pairs={{0,128},{16,144},{32,160},{48,176},{64,192},{80,208},{96,224},{112... | collective-permute-start | bytes 2359304 | tf_op jit(solution)/shard_map/ppermute | solution.py:398
  71.4 18.1 %collective-permute-done.7.refs_2_ = bf16[2,2,96,1024]{3,2,1,0:T(8,128)(2,1)S(1)} collective-permute-done((bf16[2,2,96,1024]{3,2,1,0:T(8,128)(2,1)S(1)}, bf16[2,2,96,1024]{3,2,1,0:T(8,128)(2,1)S(1)}, u32[]{:S(2)}, u32[]{:S(2)}) %collective-permute-start.7) | collective-permute-done | bytes 786464 | tf_op jit(solution)/shard_map/ppermute | solution.py:398
  89.4 0.9 copy-done.1
  90.3 4.0 %all-to-all-start.2 = ((bf16[4,2,2,192,128]{4,3,2,1,0:T(8,128)(2,1)}), bf16[4,2,2,192,128]{4,3,2,1,0:T(8,128)(2,1)S(1)}, u32[]{:S(2)}, u32[]{:S(2)}) async-start(bf16[4,2,2,192,128]{4,3,2,1,0:T(8,128)(2,1)} %bitcast.15), calls=%async_computation.2 | async-start | bytes 1572864 | tf_op jit(solution)/shard_map/all_to_all | solution.py:411
  94.3 0.1 pad_add_fusion.place_ref
  94.3 8.3 %all-to-all-done.2.grads_ref = bf16[4,2,2,192,128]{4,3,2,1,0:T(8,128)(2,1)S(1)} async-done(((bf16[4,2,2,192,128]{4,3,2,1,0:T(8,128)(2,1)}), bf16[4,2,2,192,128]{4,3,2,1,0:T(8,128)(2,1)S(1)}, u32[]{:S(2)}, u32[]{:S(2)}) %all-to-all-start.2) | async-done | bytes 786464 | tf_op jit(solution)/shard_map/all_to_all | solution.py:411
  102.6 1.1 copy-done.2
  103.7 3.3 %weight_terms.1 = (bf16[16,64,256]{2,1,0:T(8,128)(2,1)S(1)}, bf16[16,64,256]{2,1,0:T(8,128)(2,1)S(1)}) custom-call(s32[2]{0:T(128)S(1)} %pad_add_fusion.place_ref, bf16[4,2,2,192,128]{4,3,2,1,0:T(8,128)(2,1)S(1)} %all-to-all-done.2.grads_ref, bf16[2,2,96,1024]{3,2,1,0:T(8,128)(2,1)S(1)} %pad_maximum_fusion.refs_0_, ...), custom_call_target="tpu_custom_call" | custom-call | tf_op jit(solution)/shard_map/weight_terms/pallas_call | solution.py:260
  107.1 6.1 %collective-permute-start.8 = (bf16[16,64,256]{2,1,0:T(8,128)(2,1)S(1)}, bf16[16,64,256]{2,1,0:T(8,128)(2,1)S(1)}, u32[]{:S(2)}, u32[]{:S(2)}) collective-permute-start(bf16[16,64,256]{2,1,0:T(8,128)(2,1)S(1)} %get-tuple-element.37), channel_id=1, source_target_pairs={{0,16},{16,0},{32,48},{48,32},{64,80},{80,64},{96,112},{112,96},{1... | collective-permute-start | bytes 1572872 | tf_op jit(solution)/shard_map/ppermute | solution.py:417
  113.2 1.5 collective-permute-done.8
  114.7 1.0 add_convert_fusion
  115.7 7.0 %all-to-all-start.3 = ((bf16[16,64,256]{2,1,0:T(8,128)(2,1)}), bf16[16,64,256]{2,1,0:T(8,128)(2,1)S(1)}, u32[]{:S(2)}, u32[]{:S(2)}) async-start(bf16[16,64,256]{2,1,0:T(8,128)(2,1)} %add_convert_fusion), calls=%async_computation.3 | async-start | bytes 1048576 | tf_op jit(solution)/shard_map/all_to_all | solution.py:420
  122.7 1.0 dynamic-slice_bitcast_fusion
  123.7 0.7 collective-permute-start.9
  124.5 0.1 pad_add_fusion.2.place_ref
  124.6 1.3 collective-permute-done.9.arrived_ref
  125.8 2.2 %copy-done = bf16[4,1024,512]{2,1,0:T(8,128)(2,1)S(1)} copy-done((bf16[4,1024,512]{2,1,0:T(8,128)(2,1)S(1)}, bf16[4,1024,512]{2,1,0:T(8,128)(2,1)}, u32[]{:S(2)}) %copy-start) | copy-done | bytes 4194328
  128.0 4.9 %outputs.1 = (bf16[2,96,1024]{2,1,0:T(8,128)(2,1)}, bf16[2,96,1024]{2,1,0:T(8,128)(2,1)}) custom-call(s32[2]{0:T(128)S(1)} %pad_add_fusion.2.place_ref, bf16[8,2,192,128]{3,2,1,0:T(8,128)(2,1)} %bitcast.16.grads_ref, bf16[8,192,128]{2,1,0:T(8,128)(2,1)S(1)} %collective-permute-done.9.arrived_ref, bf16[4,1024,512]{2,1,0:T(8,128)(2,1)S(1)} %copy-done), custom_call_target="tpu_custom_call" | custom-call | flops 805306368 | bytes 7340032 | tf_op jit(solution)/shard_map/outputs/pallas_call | solution.py:351
  132.9 5.3 %all-to-all-done.3 = bf16[16,64,256]{2,1,0:T(8,128)(2,1)S(1)} async-done(((bf16[16,64,256]{2,1,0:T(8,128)(2,1)}), bf16[16,64,256]{2,1,0:T(8,128)(2,1)S(1)}, u32[]{:S(2)}, u32[]{:S(2)}) %all-to-all-start.3) | async-done | bytes 524320 | tf_op jit(solution)/shard_map/all_to_all | solution.py:420
  138.2 0.1 reduce_sum.12
  138.3 17.2 %all_to_all.25 = bf16[16,64,256]{2,1,0:T(8,128)(2,1)} all-to-all(bf16[16,64,256]{2,1,0:T(8,128)(2,1)S(1)} %broadcast_in_dim.8), channel_id=1, replica_groups=mesh['dp'=16,'ctx'=16] {'dp'}, dimensions={0} | all-to-all | bytes 1048576 | tf_op jit(solution)/shard_map/all_to_all | solution.py:428
  155.5 1.9 %spread_heads.1 = bf16[4,64,512]{2,1,0:T(8,128)(2,1)} custom-call(bf16[4,2,2,64,256]{4,3,2,1,0:T(8,128)(2,1)} %bitcast.31), custom_call_target="tpu_custom_call" | custom-call | tf_op jit(solution)/shard_map/spread_heads/pallas_call | solution.py:302
  (14 shorter events, 0.1 us)
Async XLA Ops:
  1.2 8.0 %copy-start.5 = (s32[1,4]{1,0:T(1,128)S(1)}, s32[1,4]{1,0:T(1,128)}, u32[]{:S(2)}) copy-start(s32[1,4]{1,0:T(1,128)} %param.5) | copy-start | bytes 52
  5.9 14.9 %copy-start.3 = (bf16[1,1,2,96,1024]{4,3,2,1,0:T(8,128)(2,1)S(1)}, bf16[1,1,2,96,1024]{4,3,2,1,0:T(8,128)(2,1)}, u32[]{:S(2)}) copy-start(bf16[1,1,2,96,1024]{4,3,2,1,0:T(8,128)(2,1)} %param.4) | copy-start | bytes 1179652
  5.9 14.9 %copy-start.4 = (bf16[1,1,2,96,1024]{4,3,2,1,0:T(8,128)(2,1)S(1)}, bf16[1,1,2,96,1024]{4,3,2,1,0:T(8,128)(2,1)}, u32[]{:S(2)}) copy-start(bf16[1,1,2,96,1024]{4,3,2,1,0:T(8,128)(2,1)} %param.7) | copy-start | bytes 1179652
  5.9 4.9 %collective-permute-start = (bf16[8,192,128]{2,1,0:T(8,128)(2,1)}, bf16[8,192,128]{2,1,0:T(8,128)(2,1)S(1)}, u32[]{:S(2)}, u32[]{:S(2)}) collective-permute-start(bf16[8,192,128]{2,1,0:T(8,128)(2,1)} %get-tuple-element.25), channel_id=1, source_target_pairs={{0,16},{16,0},{32,48},{48,32},{64,80},{80,64},{96,112},{112,96},{1... | collective-permute-start | bytes 1179656 | tf_op jit(solution)/shard_map/ppermute | solution.py:387
  9.3 2.4 %collective-permute-start.1 = (s32[1,4]{1,0:T(1,128)S(1)}, s32[1,4]{1,0:T(1,128)S(1)}, u32[]{:S(2)}, u32[]{:S(2)}) collective-permute-start(s32[1,4]{1,0:T(1,128)S(1)} %copy-done.5), channel_id=1, source_target_pairs={{0,16},{16,0},{32,48},{48,32},{64,80},{80,64},{96,112},{112,96},{1... | collective-permute-start | bytes 56 | tf_op jit(solution)/shard_map/ppermute | solution.py:382
  11.6 31.5 %all-to-all-start = ((bf16[16,192,128]{2,1,0:T(8,128)(2,1)}), bf16[16,192,128]{2,1,0:T(8,128)(2,1)S(1)}, u32[]{:S(2)}, u32[]{:S(2)}) async-start(bf16[16,192,128]{2,1,0:T(8,128)(2,1)} %bitcast.34), calls=%async_computation | async-start | bytes 1572864 | tf_op jit(solution)/shard_map/all_to_all | solution.py:399
  21.0 2.1 %collective-permute-start.2 = (bf16[2,96,1024]{2,1,0:T(8,128)(2,1)S(1)}, bf16[2,96,1024]{2,1,0:T(8,128)(2,1)S(1)}, u32[]{:S(2)}, u32[]{:S(2)}) collective-permute-start(bf16[2,96,1024]{2,1,0:T(8,128)(2,1)S(1)} %pad_maximum_fusion.2), channel_id=1, source_target_pairs={{0,16},{16,0},{32,48},{48,32},{64,80},{80,64},{96,112},{112,96},{1... | collective-permute-start | bytes 1179656 | tf_op jit(solution)/shard_map/ppermute | solution.py:395
  23.1 20.0 %collective-permute-start.3 = (bf16[2,2,96,1024]{3,2,1,0:T(8,128)(2,1)S(1)}, bf16[2,2,96,1024]{3,2,1,0:T(8,128)(2,1)S(1)}, u32[]{:S(2)}, u32[]{:S(2)}) collective-permute-start(bf16[2,2,96,1024]{3,2,1,0:T(8,128)(2,1)S(1)} %pad_maximum_fusion.refs_0_), channel_id=1, source_target_pairs={{0,64},{16,80},{32,96},{48,112},{64,128},{80,144},{96,160},{112,17... | collective-permute-start | bytes 2359304 | tf_op jit(solution)/shard_map/ppermute | solution.py:398
  24.4 18.8 %collective-permute-start.4 = (bf16[2,2,96,1024]{3,2,1,0:T(8,128)(2,1)S(1)}, bf16[2,2,96,1024]{3,2,1,0:T(8,128)(2,1)S(1)}, u32[]{:S(2)}, u32[]{:S(2)}) collective-permute-start(bf16[2,2,96,1024]{3,2,1,0:T(8,128)(2,1)S(1)} %pad_maximum_fusion.refs_0_), channel_id=1, source_target_pairs={{0,192},{16,208},{32,224},{48,240},{64,0},{80,16},{96,32},{112,48}... | collective-permute-start | bytes 2359304 | tf_op jit(solution)/shard_map/ppermute | solution.py:398
  44.0 2.8 %collective-permute-start.5 = (bf16[16,96,128]{2,1,0:T(8,128)(2,1)}, bf16[16,96,128]{2,1,0:T(8,128)(2,1)S(1)}, u32[]{:S(2)}, u32[]{:S(2)}) collective-permute-start(bf16[16,96,128]{2,1,0:T(8,128)(2,1)} %slice.3), channel_id=1, source_target_pairs={{0,16},{16,0},{32,48},{48,32},{64,80},{80,64},{96,112},{112,96},{1... | collective-permute-start | bytes 1179656 | tf_op jit(solution)/shard_map/ppermute | solution.py:402
  56.5 2.4 %collective-permute-start.6 = (bf16[16,96,128]{2,1,0:T(8,128)(2,1)S(1)}, bf16[16,96,128]{2,1,0:T(8,128)(2,1)S(1)}, u32[]{:S(2)}, u32[]{:S(2)}) collective-permute-start(bf16[16,96,128]{2,1,0:T(8,128)(2,1)S(1)} %get-tuple-element.31), channel_id=1, source_target_pairs={{0,16},{16,0},{32,48},{48,32},{64,80},{80,64},{96,112},{112,96},{1... | collective-permute-start | bytes 1179656 | tf_op jit(solution)/shard_map/ppermute | solution.py:405
  60.0 30.3 %all-to-all-start.1 = ((bf16[16,192,128]{2,1,0:T(8,128)(2,1)}), bf16[16,192,128]{2,1,0:T(8,128)(2,1)}, u32[]{:S(2)}, u32[]{:S(2)}) async-start(bf16[16,192,128]{2,1,0:T(8,128)(2,1)} %pad_maximum_fusion.1), calls=%async_computation.1 | async-start | bytes 1572864 | tf_op jit(solution)/shard_map/all_to_all | solution.py:407
  69.4 20.0 %collective-permute-start.7 = (bf16[2,2,96,1024]{3,2,1,0:T(8,128)(2,1)S(1)}, bf16[2,2,96,1024]{3,2,1,0:T(8,128)(2,1)S(1)}, u32[]{:S(2)}, u32[]{:S(2)}) collective-permute-start(bf16[2,2,96,1024]{3,2,1,0:T(8,128)(2,1)S(1)} %pad_maximum_fusion.refs_0_), channel_id=1, source_target_pairs={{0,128},{16,144},{32,160},{48,176},{64,192},{80,208},{96,224},{112... | collective-permute-start | bytes 2359304 | tf_op jit(solution)/shard_map/ppermute | solution.py:398
  89.4 0.9 copy-start.1
  90.3 12.3 %all-to-all-start.2 = ((bf16[4,2,2,192,128]{4,3,2,1,0:T(8,128)(2,1)}), bf16[4,2,2,192,128]{4,3,2,1,0:T(8,128)(2,1)S(1)}, u32[]{:S(2)}, u32[]{:S(2)}) async-start(bf16[4,2,2,192,128]{4,3,2,1,0:T(8,128)(2,1)} %bitcast.15), calls=%async_computation.2 | async-start | bytes 1572864 | tf_op jit(solution)/shard_map/all_to_all | solution.py:411
  102.6 1.1 copy-start.2
  107.1 7.7 %collective-permute-start.8 = (bf16[16,64,256]{2,1,0:T(8,128)(2,1)S(1)}, bf16[16,64,256]{2,1,0:T(8,128)(2,1)S(1)}, u32[]{:S(2)}, u32[]{:S(2)}) collective-permute-start(bf16[16,64,256]{2,1,0:T(8,128)(2,1)S(1)} %get-tuple-element.37), channel_id=1, source_target_pairs={{0,16},{16,0},{32,48},{48,32},{64,80},{80,64},{96,112},{112,96},{1... | collective-permute-start | bytes 1572872 | tf_op jit(solution)/shard_map/ppermute | solution.py:417
  115.7 22.5 %all-to-all-start.3 = ((bf16[16,64,256]{2,1,0:T(8,128)(2,1)}), bf16[16,64,256]{2,1,0:T(8,128)(2,1)S(1)}, u32[]{:S(2)}, u32[]{:S(2)}) async-start(bf16[16,64,256]{2,1,0:T(8,128)(2,1)} %add_convert_fusion), calls=%async_computation.3 | async-start | bytes 1048576 | tf_op jit(solution)/shard_map/all_to_all | solution.py:420
  123.7 2.1 %collective-permute-start.9 = (bf16[8,192,128]{2,1,0:T(8,128)(2,1)S(1)}, bf16[8,192,128]{2,1,0:T(8,128)(2,1)S(1)}, u32[]{:S(2)}, u32[]{:S(2)}) collective-permute-start(bf16[8,192,128]{2,1,0:T(8,128)(2,1)S(1)} %dynamic-slice_bitcast_fusion), channel_id=1, source_target_pairs={{0,16},{16,0},{32,48},{48,32},{64,80},{80,64},{96,112},{112,96},{1... | collective-permute-start | bytes 1179656 | tf_op jit(solution)/shard_map/ppermute | solution.py:421
  125.8 2.2 %copy-start = (bf16[4,1024,512]{2,1,0:T(8,128)(2,1)S(1)}, bf16[4,1024,512]{2,1,0:T(8,128)(2,1)}, u32[]{:S(2)}) copy-start(bf16[4,1024,512]{2,1,0:T(8,128)(2,1)} %weights_ref.3) | copy-start | bytes 12582916

commit v8 on v7

--- a/solution.py
+++ b/solution.py
@@ -210,12 +210,17 @@
             pltpu.VMEM((2 * SPAN, 7 * CHUNK), jnp.float32),
         ],
         compiler_params=pltpu.CompilerParams(vmem_limit_bytes=SMALL_VMEM),
+        cost_estimate=pl.CostEstimate(
+            flops=12_000_000_000, bytes_accessed=4 * 1024 * 1024, transcendentals=0
+        ),
         name="attend",
     )(core, tiles, own, other_keys)
 
 
-def weight_kernel(place_ref, grads_ref, *refs):
-    line_refs, (keep_ref, give_ref, held_ref) = refs[:4], refs[4:]
+def weight_kernel(
+    place_ref, grads_ref, own_ref, near_ref, back_ref, far_tokens_ref, far_upstream_ref,
+    keep_ref, give_ref, held_ref,
+):
     core, column = place_ref[0], place_ref[1]
 
     @pl.when(pl.program_id(0) == 0)
@@ -233,7 +238,9 @@
                         ]
 
     def product(kind, columns):
-        rows = jnp.concatenate([ref[part, kind] for ref in line_refs for part in range(2)], axis=0)
+        far_ref = (far_tokens_ref, far_upstream_ref)[kind]
+        lines = (own_ref[kind], near_ref[kind], far_ref[...], back_ref[kind])
+        rows = jnp.concatenate([line.reshape(2 * SPAN, D // 4) for line in lines], axis=0)
         return lax.dot_general(
             rows, held_ref[:, :columns], (((0,), (0,)), ((), ())), preferred_element_type=jnp.float32
         )
@@ -256,6 +263,7 @@
 def weight_terms(place, grads, lines):
     shape = jax.ShapeDtypeStruct((RANKS, 64, 256), jnp.bfloat16)
     line_spec = pl.BlockSpec((2, 2, SPAN, D // 4), lambda j, place: (0, 0, 0, j))
+    half_spec = pl.BlockSpec((2, SPAN, D // 4), lambda j, place: (0, 0, j))
     out_spec = pl.BlockSpec((4, 64, 256), lambda j, place: (j, 0, 0))
     return pl.pallas_call(
         weight_kernel,
@@ -265,7 +273,7 @@
             grid=(4,),
             in_specs=[
                 pl.BlockSpec((4, 2, 2, 2 * SPAN, 128), lambda j, place: (0, 0, 0, 0, 0)),
-                line_spec, line_spec, line_spec, line_spec,
+                line_spec, line_spec, line_spec, half_spec, half_spec,
             ],
             out_specs=(out_spec, out_spec),
             scratch_shapes=[pltpu.VMEM((8 * SPAN, 512), jnp.bfloat16)],
@@ -392,22 +400,23 @@
             [lax.dynamic_index_in_dim(x, number, 0, keepdims=False) for x in (rows, upstream)]
         )
 
-    line = jnp.stack([chosen(block), lax.ppermute(chosen(1 - block), "dp", CORE_SWAP)])
+    line = jnp.stack([chosen(block), lax.ppermute(chosen(1 - block), "dp", CORE_SWAP)], axis=1)
     packed, other_tiles = lax.optimization_barrier((packed, other_tiles))
     packed = packed.reshape(RANKS, 2 * SPAN, 128)
-    shifted = [lax.ppermute(line, "dp", shift) for shift in X_SHIFTS]
+    near, back_near = (lax.ppermute(line, "dp", X_SHIFTS[i]) for i in (0, 2))
+    far_tokens, far_upstream = (lax.ppermute(half, "dp", X_SHIFTS[1]) for half in line)
     own = lax.all_to_all(packed, "ctx", 0, 0)
-    near, far, back_near = shifted
-    own, near, back_near = lax.optimization_barrier((own, near, back_near))
+    own, far_tokens = lax.optimization_barrier((own, far_tokens))
     other_keys = lax.ppermute(own[:, SPAN:], "dp", CORE_SWAP)
     tiles = jnp.where(odd == core, sweep_tiles, other_tiles).reshape(-1)
     query_part, own_grad, other_grad = attend(core_number, tiles, own, other_keys)
     arrived = lax.ppermute(other_grad, "dp", CORE_SWAP)
     key_part = (own_grad + arrived.astype(jnp.float32)).astype(jnp.bfloat16)
+    key_part, near, back_near = lax.optimization_barrier((key_part, near, back_near))
     back = lax.all_to_all(jnp.concatenate([query_part, key_part], axis=1), "ctx", 0, 0)
-    back, far = lax.optimization_barrier((back, far))
+    back, far_upstream = lax.optimization_barrier((back, far_upstream))
     grads = back.reshape(HEADS, 2, 2 * SPAN, 128)
-    lines = [line, near, far, back_near]
+    lines = [line, near, back_near, far_tokens, far_upstream]
     line_grads = lax.all_to_all(
         back.reshape(4, 2, 2, 2 * SPAN, 128), "dp", 0, 0, axis_index_groups=CHIP_LINES
     )

time: 159 us -> 157 us (0.987)
  starting transfers between devices: 47.5 us -> 44.3 us
    ppermute x3 -> x4, waiting for transfers between devices: 35.4 us -> 23.5 us  [the longest x2 18.1 us: per_device(): lax.ppermute(half, 'dp', X_SHIFTS[1])]
    all_to_all x1, waiting for transfers between devices: 0.01 us -> 7.1 us  [per_device(): lax.all_to_all(jnp.concatenate([query_part, key_part], axis=1), 'ctx', 0, 0)]
    all_to_all x1, waiting for transfers between devices: 0.01 us -> 6.54 us  [per_device(): own = lax.all_to_all(packed, 'ctx', 0, 0)]
    all_to_all x1, starting transfers between devices: 9.37 us -> 4.72 us  [per_device(): lax.all_to_all(jnp.concatenate([query_part, key_part], axis=1), 'ctx', 0, 0)]
    ppermute x3 -> x4, starting transfers between devices: 4.71 us -> 7.81 us  [the longest x2 4.95 us: per_device(): lax.ppermute(half, 'dp', X_SHIFTS[1])]
    ppermute x2, starting transfers between devices: 9.45 us -> 7.56 us  [per_device(): given = lax.ppermute(give, 'dp', CORE_SWAP)]
    unnamed x12 -> x14, local copies, waits for them, and re-layouts: 4.22 us -> 3.94 us
  transfers between devices with their start and end apart: 14 -> 15, of which waited for: 10 -> 12; matrix products, arithmetic and copies ran while one was open for 1% -> 2% of each run, Pallas kernels for 3% -> 10%
where the time goes in v8:
time: 157 us; the launch traced here: 156 us
  waiting for transfers between devices  58.2 us (37%)
  starting transfers between devices  44.3 us (28%)
  Pallas kernels  25.1 us (16%)
  blocking collectives  17.3 us (11%)
  local copies, waits for them, and re-layouts  6.67 us (4%)
  other arithmetic  3.86 us (2%)
    ppermute x2, waiting for transfers between devices, per_device(): lax.ppermute(half, 'dp', X_SHIFTS[1])  18.1 us
    all_to_all x1, blocking collectives, per_device(): parts = lax.all_to_all(jnp.broadcast_to(rows, (16, 64, 256)), 'dp', 0, 0)  17.3 us
    pallas_call x1, Pallas kernels, attend(): pl.pallas_call(attend_kernel, out_shape=(jax.ShapeDtypeStruct(block, jnp....  10.2 us
    all_to_all x1, starting transfers between devices, per_device(): own = lax.all_to_all(packed, 'ctx', 0, 0)  9.19 us
    all_to_all x1, waiting for transfers between devices, per_device(): lax.all_to_all(back.reshape(4, 2, 2, 2 * SPAN, 128), 'dp', 0, 0, axis_ind...  9.02 us
    ppermute x2, starting transfers between devices, per_device(): given = lax.ppermute(give, 'dp', CORE_SWAP)  7.56 us
    all_to_all x1, starting transfers between devices, per_device(): terms = lax.all_to_all(terms, 'ctx', 0, 0)  7.37 us
    all_to_all x1, waiting for transfers between devices, per_device(): lax.all_to_all(jnp.concatenate([query_part, key_part], axis=1), 'ctx', 0, 0)  7.1 us
  transfers between devices with their start and end apart: 15, of which 12 were waited for; matrix products, arithmetic and copies ran while one was open for 2% of the time, Pallas kernels for 10%

profile of v8, /device:TPU:1, one launch (start us, length us, event | category | flops | bytes accessed | tf_op | source)
XLA Modules:
  0.0 156.2 jit_solution(11396950240802168216)
XLA Ops:
  0.7 0.6 pad_add_fusion.1.place_ref
  1.2 4.7 %project.1 = (bf16[8,2,192,128]{3,2,1,0:T(8,128)(2,1)}, bf16[8,192,128]{2,1,0:T(8,128)(2,1)}) custom-call(s32[2]{0:T(128)} %pad_add_fusion.1.place_ref, bf16[2,96,1024]{2,1,0:T(8,128)(2,1)} %bitcast.36, bf16[2,96,1024]{2,1,0:T(8,128)(2,1)} %bitcast.37, bf16[4,1024,512]{2,1,0:T(8,128)(2,1)} %weights_ref.3), custom_call_target="tpu_custom_call" | custom-call | tf_op jit(solution)/shard_map/project/pallas_call | solution.py:58
  5.9 3.3 %collective-permute-start = (bf16[8,192,128]{2,1,0:T(8,128)(2,1)}, bf16[8,192,128]{2,1,0:T(8,128)(2,1)S(1)}, u32[]{:S(2)}, u32[]{:S(2)}) collective-permute-start(bf16[8,192,128]{2,1,0:T(8,128)(2,1)} %get-tuple-element.27), channel_id=1, source_target_pairs={{0,16},{16,0},{32,48},{48,32},{64,80},{80,64},{96,112},{112,96},{1... | collective-permute-start | bytes 1179656 | tf_op jit(solution)/shard_map/ppermute | solution.py:395
  9.3 0.1 collective-permute-start.1
  9.4 1.4 collective-permute-done
  10.8 0.8 bitcast_dynamic-update-slice_fusion
  11.6 9.2 %all-to-all-start = ((bf16[16,192,128]{2,1,0:T(8,128)(2,1)}), bf16[16,192,128]{2,1,0:T(8,128)(2,1)S(1)}, u32[]{:S(2)}, u32[]{:S(2)}) async-start(bf16[16,192,128]{2,1,0:T(8,128)(2,1)} %bitcast.40), calls=%async_computation | async-start | bytes 1572864 | tf_op jit(solution)/shard_map/all_to_all | solution.py:408
  21.0 0.7 collective-permute-start.2
  21.8 1.3 collective-permute-done.2
  23.1 0.8 fusion.3
  23.9 2.7 %collective-permute-start.3 = (bf16[2,96,1024]{2,1,0:T(8,128)(2,1)S(1)}, bf16[2,96,1024]{2,1,0:T(8,128)(2,1)S(1)}, u32[]{:S(2)}, u32[]{:S(2)}) collective-permute-start(bf16[2,96,1024]{2,1,0:T(8,128)(2,1)S(1)} %get-tuple-element.50), channel_id=1, source_target_pairs={{0,128},{16,144},{32,160},{48,176},{64,192},{80,208},{96,224},{112... | collective-permute-start | bytes 1179656 | tf_op jit(solution)/shard_map/ppermute | solution.py:407
  26.6 9.1 %collective-permute-done.3.far_tokens_ref = bf16[2,96,1024]{2,1,0:T(8,128)(2,1)S(1)} collective-permute-done((bf16[2,96,1024]{2,1,0:T(8,128)(2,1)S(1)}, bf16[2,96,1024]{2,1,0:T(8,128)(2,1)S(1)}, u32[]{:S(2)}, u32[]{:S(2)}) %collective-permute-start.3) | collective-permute-done | bytes 393248 | tf_op jit(solution)/shard_map/ppermute | solution.py:407
  35.7 6.5 %all-to-all-done.own_ref = bf16[16,192,128]{2,1,0:T(8,128)(2,1)S(1)} async-done(((bf16[16,192,128]{2,1,0:T(8,128)(2,1)}), bf16[16,192,128]{2,1,0:T(8,128)(2,1)S(1)}, u32[]{:S(2)}, u32[]{:S(2)}) %all-to-all-start) | async-done | bytes 786464 | tf_op jit(solution)/shard_map/all_to_all | solution.py:408
  42.3 0.8 slice.3
  43.0 1.9 %collective-permute-start.4 = (bf16[16,96,128]{2,1,0:T(8,128)(2,1)}, bf16[16,96,128]{2,1,0:T(8,128)(2,1)}, u32[]{:S(2)}, u32[]{:S(2)}) collective-permute-start(bf16[16,96,128]{2,1,0:T(8,128)(2,1)} %slice.3), channel_id=1, source_target_pairs={{0,16},{16,0},{32,48},{48,32},{64,80},{80,64},{96,112},{112,96},{1... | collective-permute-start | bytes 1179656 | tf_op jit(solution)/shard_map/ppermute | solution.py:410
  45.0 0.1 pad_maximum_fusion.own_ref
  45.1 1.3 collective-permute-start.6
  46.4 1.6 %collective-permute-start.7 = (bf16[2,2,96,1024]{3,2,1,0:T(8,128)(2,1)S(1)}, bf16[2,2,96,1024]{3,2,1,0:T(8,128)(2,1)S(1)}, u32[]{:S(2)}, u32[]{:S(2)}) collective-permute-start(bf16[2,2,96,1024]{3,2,1,0:T(8,128)(2,1)S(1)} %pad_maximum_fusion.own_ref), channel_id=1, source_target_pairs={{0,192},{16,208},{32,224},{48,240},{64,0},{80,16},{96,32},{112,48}... | collective-permute-start | bytes 2359304 | tf_op jit(solution)/shard_map/ppermute | solution.py:406
  47.9 10.2 %attend.1 = (bf16[16,96,128]{2,1,0:T(8,128)(2,1)S(1)}, f32[16,96,128]{2,1,0:T(8,128)S(1)}, bf16[16,96,128]{2,1,0:T(8,128)(2,1)S(1)}) custom-call(s32[1]{0:T(128)} %bitcast.core_ref, s32[4]{0:T(128)S(1)} %fusion.4.tiles_ref, bf16[16,192,128]{2,1,0:T(8,128)(2,1)S(1)} %all-to-all-done.own_ref, bf16[16,96,128]{2,1,0:T(8,128)(2,1)} %collective-permute-done.4.other_ref), custom_call_target="tpu_custom_call" | custom-call | flops 12000000000 | bytes 4194304 | tf_op jit(solution)/shard_map/attend/pallas_call | solution.py:197
  58.2 0.6 collective-permute-start.5
  58.7 1.3 collective-permute-done.5
  60.1 0.1 add_convert_fusion.1
  60.2 5.4 %collective-permute-done.6.near_ref = bf16[2,2,96,1024]{3,2,1,0:T(8,128)(2,1)S(1)} collective-permute-done((bf16[2,2,96,1024]{3,2,1,0:T(8,128)(2,1)S(1)}, bf16[2,2,96,1024]{3,2,1,0:T(8,128)(2,1)S(1)}, u32[]{:S(2)}, u32[]{:S(2)}) %collective-permute-start.6) | collective-permute-done | bytes 786464 | tf_op jit(solution)/shard_map/ppermute | solution.py:406
  65.5 1.0 pad_maximum_fusion.1
  66.5 4.7 %all-to-all-start.1 = ((bf16[16,192,128]{2,1,0:T(8,128)(2,1)}), bf16[16,192,128]{2,1,0:T(8,128)(2,1)}, u32[]{:S(2)}, u32[]{:S(2)}) async-start(bf16[16,192,128]{2,1,0:T(8,128)(2,1)} %pad_maximum_fusion.1), calls=%async_computation.1 | async-start | bytes 1572864 | tf_op jit(solution)/shard_map/all_to_all | solution.py:416
  71.3 2.2 %collective-permute-start.8 = (bf16[2,96,1024]{2,1,0:T(8,128)(2,1)S(1)}, bf16[2,96,1024]{2,1,0:T(8,128)(2,1)S(1)}, u32[]{:S(2)}, u32[]{:S(2)}) collective-permute-start(bf16[2,96,1024]{2,1,0:T(8,128)(2,1)S(1)} %copy-done.5), channel_id=1, source_target_pairs={{0,128},{16,144},{32,160},{48,176},{64,192},{80,208},{96,224},{112... | collective-permute-start | bytes 1179656 | tf_op jit(solution)/shard_map/ppermute | solution.py:407
  73.5 9.0 %collective-permute-done.8.far_upstream_ref = bf16[2,96,1024]{2,1,0:T(8,128)(2,1)S(1)} collective-permute-done((bf16[2,96,1024]{2,1,0:T(8,128)(2,1)S(1)}, bf16[2,96,1024]{2,1,0:T(8,128)(2,1)S(1)}, u32[]{:S(2)}, u32[]{:S(2)}) %collective-permute-start.8) | collective-permute-done | bytes 393248 | tf_op jit(solution)/shard_map/ppermute | solution.py:407
  82.5 0.7 copy-done.1
  83.3 7.1 %all-to-all-done.1 = bf16[16,192,128]{2,1,0:T(8,128)(2,1)} async-done(((bf16[16,192,128]{2,1,0:T(8,128)(2,1)}), bf16[16,192,128]{2,1,0:T(8,128)(2,1)}, u32[]{:S(2)}, u32[]{:S(2)}) %all-to-all-start.1) | async-done | bytes 786464 | tf_op jit(solution)/shard_map/all_to_all | solution.py:416
  90.4 3.5 %all-to-all-start.2 = ((bf16[4,2,2,192,128]{4,3,2,1,0:T(8,128)(2,1)}), bf16[4,2,2,192,128]{4,3,2,1,0:T(8,128)(2,1)S(1)}, u32[]{:S(2)}, u32[]{:S(2)}) async-start(bf16[4,2,2,192,128]{4,3,2,1,0:T(8,128)(2,1)} %bitcast.17), calls=%async_computation.2 | async-start | bytes 1572864 | tf_op jit(solution)/shard_map/all_to_all | solution.py:420
  93.9 0.1 pad_add_fusion.place_ref
  94.0 9.0 %all-to-all-done.2.grads_ref = bf16[4,2,2,192,128]{4,3,2,1,0:T(8,128)(2,1)S(1)} async-done(((bf16[4,2,2,192,128]{4,3,2,1,0:T(8,128)(2,1)}), bf16[4,2,2,192,128]{4,3,2,1,0:T(8,128)(2,1)S(1)}, u32[]{:S(2)}, u32[]{:S(2)}) %all-to-all-start.2) | async-done | bytes 786464 | tf_op jit(solution)/shard_map/all_to_all | solution.py:420
  103.0 1.0 copy-done.2
  104.0 3.4 %weight_terms.1 = (bf16[16,64,256]{2,1,0:T(8,128)(2,1)S(1)}, bf16[16,64,256]{2,1,0:T(8,128)(2,1)S(1)}) custom-call(s32[2]{0:T(128)S(1)} %pad_add_fusion.place_ref, bf16[4,2,2,192,128]{4,3,2,1,0:T(8,128)(2,1)S(1)} %all-to-all-done.2.grads_ref, bf16[2,2,96,1024]{3,2,1,0:T(8,128)(2,1)S(1)} %pad_maximum_fusion.own_ref, ...), custom_call_target="tpu_custom_call" | custom-call | tf_op jit(solution)/shard_map/weight_terms/pallas_call | solution.py:268
  107.4 4.2 %collective-permute-start.9 = (bf16[16,64,256]{2,1,0:T(8,128)(2,1)S(1)}, bf16[16,64,256]{2,1,0:T(8,128)(2,1)S(1)}, u32[]{:S(2)}, u32[]{:S(2)}) collective-permute-start(bf16[16,64,256]{2,1,0:T(8,128)(2,1)S(1)} %get-tuple-element.41), channel_id=1, source_target_pairs={{0,16},{16,0},{32,48},{48,32},{64,80},{80,64},{96,112},{112,96},{1... | collective-permute-start | bytes 1572872 | tf_op jit(solution)/shard_map/ppermute | solution.py:426
  111.6 1.5 collective-permute-done.9
  113.1 1.0 add_convert_fusion
  114.1 7.4 %all-to-all-start.3 = ((bf16[16,64,256]{2,1,0:T(8,128)(2,1)}), bf16[16,64,256]{2,1,0:T(8,128)(2,1)S(1)}, u32[]{:S(2)}, u32[]{:S(2)}) async-start(bf16[16,64,256]{2,1,0:T(8,128)(2,1)} %add_convert_fusion), calls=%async_computation.3 | async-start | bytes 1048576 | tf_op jit(solution)/shard_map/all_to_all | solution.py:429
  121.5 1.0 dynamic-slice_bitcast_fusion
  122.5 0.7 collective-permute-start.10
  123.3 0.1 pad_add_fusion.2.place_ref
  123.4 1.3 collective-permute-done.10.arrived_ref
  124.6 2.2 %copy-done = bf16[4,1024,512]{2,1,0:T(8,128)(2,1)S(1)} copy-done((bf16[4,1024,512]{2,1,0:T(8,128)(2,1)S(1)}, bf16[4,1024,512]{2,1,0:T(8,128)(2,1)}, u32[]{:S(2)}) %copy-start) | copy-done | bytes 4194328
  126.8 4.9 %outputs.1 = (bf16[2,96,1024]{2,1,0:T(8,128)(2,1)}, bf16[2,96,1024]{2,1,0:T(8,128)(2,1)}) custom-call(s32[2]{0:T(128)S(1)} %pad_add_fusion.2.place_ref, bf16[8,2,192,128]{3,2,1,0:T(8,128)(2,1)} %bitcast.18.grads_ref, bf16[8,192,128]{2,1,0:T(8,128)(2,1)S(1)} %collective-permute-done.10.arrived_ref, bf16[4,1024,512]{2,1,0:T(8,128)(2,1)S(1)} %copy-done), custom_call_target="tpu_custom_call" | custom-call | flops 805306368 | bytes 7340032 | tf_op jit(solution)/shard_map/outputs/pallas_call | solution.py:359
  131.7 5.2 %all-to-all-done.3 = bf16[16,64,256]{2,1,0:T(8,128)(2,1)S(1)} async-done(((bf16[16,64,256]{2,1,0:T(8,128)(2,1)}), bf16[16,64,256]{2,1,0:T(8,128)(2,1)S(1)}, u32[]{:S(2)}, u32[]{:S(2)}) %all-to-all-start.3) | async-done | bytes 524320 | tf_op jit(solution)/shard_map/all_to_all | solution.py:429
  136.9 0.1 reduce_sum.12
  137.0 17.3 %all_to_all.25 = bf16[16,64,256]{2,1,0:T(8,128)(2,1)} all-to-all(bf16[16,64,256]{2,1,0:T(8,128)(2,1)S(1)} %broadcast_in_dim.8), channel_id=1, replica_groups=mesh['dp'=16,'ctx'=16] {'dp'}, dimensions={0} | all-to-all | bytes 1048576 | tf_op jit(solution)/shard_map/all_to_all | solution.py:437
  154.3 1.9 %spread_heads.1 = bf16[4,64,512]{2,1,0:T(8,128)(2,1)} custom-call(bf16[4,2,2,64,256]{4,3,2,1,0:T(8,128)(2,1)} %bitcast.35), custom_call_target="tpu_custom_call" | custom-call | tf_op jit(solution)/shard_map/spread_heads/pallas_call | solution.py:310
  (19 shorter events, 0.2 us)
Async XLA Ops:
  1.2 8.0 %copy-start.6 = (s32[1,4]{1,0:T(1,128)S(1)}, s32[1,4]{1,0:T(1,128)}, u32[]{:S(2)}) copy-start(s32[1,4]{1,0:T(1,128)} %param.5) | copy-start | bytes 52
  5.9 14.9 %copy-start.3 = (bf16[1,1,2,96,1024]{4,3,2,1,0:T(8,128)(2,1)S(1)}, bf16[1,1,2,96,1024]{4,3,2,1,0:T(8,128)(2,1)}, u32[]{:S(2)}) copy-start(bf16[1,1,2,96,1024]{4,3,2,1,0:T(8,128)(2,1)} %param.4) | copy-start | bytes 1179652
  5.9 14.9 %copy-start.4 = (bf16[1,1,2,96,1024]{4,3,2,1,0:T(8,128)(2,1)S(1)}, bf16[1,1,2,96,1024]{4,3,2,1,0:T(8,128)(2,1)}, u32[]{:S(2)}) copy-start(bf16[1,1,2,96,1024]{4,3,2,1,0:T(8,128)(2,1)} %param.7) | copy-start | bytes 1179652
  5.9 4.9 %collective-permute-start = (bf16[8,192,128]{2,1,0:T(8,128)(2,1)}, bf16[8,192,128]{2,1,0:T(8,128)(2,1)S(1)}, u32[]{:S(2)}, u32[]{:S(2)}) collective-permute-start(bf16[8,192,128]{2,1,0:T(8,128)(2,1)} %get-tuple-element.27), channel_id=1, source_target_pairs={{0,16},{16,0},{32,48},{48,32},{64,80},{80,64},{96,112},{112,96},{1... | collective-permute-start | bytes 1179656 | tf_op jit(solution)/shard_map/ppermute | solution.py:395
  9.3 2.4 %collective-permute-start.1 = (s32[1,4]{1,0:T(1,128)S(1)}, s32[1,4]{1,0:T(1,128)S(1)}, u32[]{:S(2)}, u32[]{:S(2)}) collective-permute-start(s32[1,4]{1,0:T(1,128)S(1)} %copy-done.6), channel_id=1, source_target_pairs={{0,16},{16,0},{32,48},{48,32},{64,80},{80,64},{96,112},{112,96},{1... | collective-permute-start | bytes 56 | tf_op jit(solution)/shard_map/ppermute | solution.py:390
  11.6 30.6 %all-to-all-start = ((bf16[16,192,128]{2,1,0:T(8,128)(2,1)}), bf16[16,192,128]{2,1,0:T(8,128)(2,1)S(1)}, u32[]{:S(2)}, u32[]{:S(2)}) async-start(bf16[16,192,128]{2,1,0:T(8,128)(2,1)} %bitcast.40), calls=%async_computation | async-start | bytes 1572864 | tf_op jit(solution)/shard_map/all_to_all | solution.py:408
  21.0 2.1 %collective-permute-start.2 = (bf16[2,96,1024]{2,1,0:T(8,128)(2,1)S(1)}, bf16[2,96,1024]{2,1,0:T(8,128)(2,1)S(1)}, u32[]{:S(2)}, u32[]{:S(2)}) collective-permute-start(bf16[2,96,1024]{2,1,0:T(8,128)(2,1)S(1)} %pad_maximum_fusion.2), channel_id=1, source_target_pairs={{0,16},{16,0},{32,48},{48,32},{64,80},{80,64},{96,112},{112,96},{1... | collective-permute-start | bytes 1179656 | tf_op jit(solution)/shard_map/ppermute | solution.py:403
  23.9 11.8 %collective-permute-start.3 = (bf16[2,96,1024]{2,1,0:T(8,128)(2,1)S(1)}, bf16[2,96,1024]{2,1,0:T(8,128)(2,1)S(1)}, u32[]{:S(2)}, u32[]{:S(2)}) collective-permute-start(bf16[2,96,1024]{2,1,0:T(8,128)(2,1)S(1)} %get-tuple-element.50), channel_id=1, source_target_pairs={{0,128},{16,144},{32,160},{48,176},{64,192},{80,208},{96,224},{112... | collective-permute-start | bytes 1179656 | tf_op jit(solution)/shard_map/ppermute | solution.py:407
  43.0 4.9 %collective-permute-start.4 = (bf16[16,96,128]{2,1,0:T(8,128)(2,1)}, bf16[16,96,128]{2,1,0:T(8,128)(2,1)}, u32[]{:S(2)}, u32[]{:S(2)}) collective-permute-start(bf16[16,96,128]{2,1,0:T(8,128)(2,1)} %slice.3), channel_id=1, source_target_pairs={{0,16},{16,0},{32,48},{48,32},{64,80},{80,64},{96,112},{112,96},{1... | collective-permute-start | bytes 1179656 | tf_op jit(solution)/shard_map/ppermute | solution.py:410
  45.1 20.5 %collective-permute-start.6 = (bf16[2,2,96,1024]{3,2,1,0:T(8,128)(2,1)S(1)}, bf16[2,2,96,1024]{3,2,1,0:T(8,128)(2,1)S(1)}, u32[]{:S(2)}, u32[]{:S(2)}) collective-permute-start(bf16[2,2,96,1024]{3,2,1,0:T(8,128)(2,1)S(1)} %pad_maximum_fusion.own_ref), channel_id=1, source_target_pairs={{0,64},{16,80},{32,96},{48,112},{64,128},{80,144},{96,160},{112,17... | collective-permute-start | bytes 2359304 | tf_op jit(solution)/shard_map/ppermute | solution.py:406
  46.4 19.2 %collective-permute-start.7 = (bf16[2,2,96,1024]{3,2,1,0:T(8,128)(2,1)S(1)}, bf16[2,2,96,1024]{3,2,1,0:T(8,128)(2,1)S(1)}, u32[]{:S(2)}, u32[]{:S(2)}) collective-permute-start(bf16[2,2,96,1024]{3,2,1,0:T(8,128)(2,1)S(1)} %pad_maximum_fusion.own_ref), channel_id=1, source_target_pairs={{0,192},{16,208},{32,224},{48,240},{64,0},{80,16},{96,32},{112,48}... | collective-permute-start | bytes 2359304 | tf_op jit(solution)/shard_map/ppermute | solution.py:406
  58.2 1.9 %collective-permute-start.5 = (bf16[16,96,128]{2,1,0:T(8,128)(2,1)S(1)}, bf16[16,96,128]{2,1,0:T(8,128)(2,1)S(1)}, u32[]{:S(2)}, u32[]{:S(2)}) collective-permute-start(bf16[16,96,128]{2,1,0:T(8,128)(2,1)S(1)} %get-tuple-element.33), channel_id=1, source_target_pairs={{0,16},{16,0},{32,48},{48,32},{64,80},{80,64},{96,112},{112,96},{1... | collective-permute-start | bytes 1179656 | tf_op jit(solution)/shard_map/ppermute | solution.py:413
  65.5 5.8 %copy-start.5 = (bf16[2,96,1024]{2,1,0:T(8,128)(2,1)S(1)}, bf16[2,96,1024]{2,1,0:T(8,128)(2,1)}, u32[]{:S(2)}) copy-start(bf16[2,96,1024]{2,1,0:T(8,128)(2,1)} %get-tuple-element.49) | copy-start | bytes 1179652
  66.5 23.8 %all-to-all-start.1 = ((bf16[16,192,128]{2,1,0:T(8,128)(2,1)}), bf16[16,192,128]{2,1,0:T(8,128)(2,1)}, u32[]{:S(2)}, u32[]{:S(2)}) async-start(bf16[16,192,128]{2,1,0:T(8,128)(2,1)} %pad_maximum_fusion.1), calls=%async_computation.1 | async-start | bytes 1572864 | tf_op jit(solution)/shard_map/all_to_all | solution.py:416
  71.3 11.2 %collective-permute-start.8 = (bf16[2,96,1024]{2,1,0:T(8,128)(2,1)S(1)}, bf16[2,96,1024]{2,1,0:T(8,128)(2,1)S(1)}, u32[]{:S(2)}, u32[]{:S(2)}) collective-permute-start(bf16[2,96,1024]{2,1,0:T(8,128)(2,1)S(1)} %copy-done.5), channel_id=1, source_target_pairs={{0,128},{16,144},{32,160},{48,176},{64,192},{80,208},{96,224},{112... | collective-permute-start | bytes 1179656 | tf_op jit(solution)/shard_map/ppermute | solution.py:407
  82.5 0.7 copy-start.1
  90.4 12.6 %all-to-all-start.2 = ((bf16[4,2,2,192,128]{4,3,2,1,0:T(8,128)(2,1)}), bf16[4,2,2,192,128]{4,3,2,1,0:T(8,128)(2,1)S(1)}, u32[]{:S(2)}, u32[]{:S(2)}) async-start(bf16[4,2,2,192,128]{4,3,2,1,0:T(8,128)(2,1)} %bitcast.17), calls=%async_computation.2 | async-start | bytes 1572864 | tf_op jit(solution)/shard_map/all_to_all | solution.py:420
  103.0 1.0 copy-start.2
  107.4 5.8 %collective-permute-start.9 = (bf16[16,64,256]{2,1,0:T(8,128)(2,1)S(1)}, bf16[16,64,256]{2,1,0:T(8,128)(2,1)S(1)}, u32[]{:S(2)}, u32[]{:S(2)}) collective-permute-start(bf16[16,64,256]{2,1,0:T(8,128)(2,1)S(1)} %get-tuple-element.41), channel_id=1, source_target_pairs={{0,16},{16,0},{32,48},{48,32},{64,80},{80,64},{96,112},{112,96},{1... | collective-permute-start | bytes 1572872 | tf_op jit(solution)/shard_map/ppermute | solution.py:426
  114.1 22.8 %all-to-all-start.3 = ((bf16[16,64,256]{2,1,0:T(8,128)(2,1)}), bf16[16,64,256]{2,1,0:T(8,128)(2,1)S(1)}, u32[]{:S(2)}, u32[]{:S(2)}) async-start(bf16[16,64,256]{2,1,0:T(8,128)(2,1)} %add_convert_fusion), calls=%async_computation.3 | async-start | bytes 1048576 | tf_op jit(solution)/shard_map/all_to_all | solution.py:429
  122.5 2.1 %collective-permute-start.10 = (bf16[8,192,128]{2,1,0:T(8,128)(2,1)S(1)}, bf16[8,192,128]{2,1,0:T(8,128)(2,1)S(1)}, u32[]{:S(2)}, u32[]{:S(2)}) collective-permute-start(bf16[8,192,128]{2,1,0:T(8,128)(2,1)S(1)} %dynamic-slice_bitcast_fusion), channel_id=1, source_target_pairs={{0,16},{16,0},{32,48},{48,32},{64,80},{80,64},{96,112},{112,96},{1... | collective-permute-start | bytes 1179656 | tf_op jit(solution)/shard_map/ppermute | solution.py:430
  124.6 2.2 %copy-start = (bf16[4,1024,512]{2,1,0:T(8,128)(2,1)S(1)}, bf16[4,1024,512]{2,1,0:T(8,128)(2,1)}, u32[]{:S(2)}) copy-start(bf16[4,1024,512]{2,1,0:T(8,128)(2,1)} %weights_ref.3) | copy-start | bytes 12582916

commit v9 on v7

--- a/solution.py
+++ b/solution.py
@@ -210,12 +210,15 @@
             pltpu.VMEM((2 * SPAN, 7 * CHUNK), jnp.float32),
         ],
         compiler_params=pltpu.CompilerParams(vmem_limit_bytes=SMALL_VMEM),
+        cost_estimate=pl.CostEstimate(
+            flops=12_000_000_000, bytes_accessed=4 * 1024 * 1024, transcendentals=0
+        ),
         name="attend",
     )(core, tiles, own, other_keys)
 
 
 def weight_kernel(place_ref, grads_ref, *refs):
-    line_refs, (keep_ref, give_ref, held_ref) = refs[:4], refs[4:]
+    line_refs, (keep_ref, give_ref, held_ref) = refs[:8], refs[8:]
     core, column = place_ref[0], place_ref[1]
 
     @pl.when(pl.program_id(0) == 0)
@@ -233,7 +236,9 @@
                         ]
 
     def product(kind, columns):
-        rows = jnp.concatenate([ref[part, kind] for ref in line_refs for part in range(2)], axis=0)
+        rows = jnp.concatenate(
+            [ref[...].reshape(2 * SPAN, D // 4) for ref in line_refs[kind::2]], axis=0
+        )
         return lax.dot_general(
             rows, held_ref[:, :columns], (((0,), (0,)), ((), ())), preferred_element_type=jnp.float32
         )
@@ -255,7 +260,7 @@
 
 def weight_terms(place, grads, lines):
     shape = jax.ShapeDtypeStruct((RANKS, 64, 256), jnp.bfloat16)
-    line_spec = pl.BlockSpec((2, 2, SPAN, D // 4), lambda j, place: (0, 0, 0, j))
+    line_spec = pl.BlockSpec((2, SPAN, D // 4), lambda j, place: (0, 0, j))
     out_spec = pl.BlockSpec((4, 64, 256), lambda j, place: (j, 0, 0))
     return pl.pallas_call(
         weight_kernel,
@@ -265,7 +270,7 @@
             grid=(4,),
             in_specs=[
                 pl.BlockSpec((4, 2, 2, 2 * SPAN, 128), lambda j, place: (0, 0, 0, 0, 0)),
-                line_spec, line_spec, line_spec, line_spec,
+                *[line_spec] * 8,
             ],
             out_specs=(out_spec, out_spec),
             scratch_shapes=[pltpu.VMEM((8 * SPAN, 512), jnp.bfloat16)],
@@ -387,27 +392,32 @@
     given = lax.ppermute(give, "dp", CORE_SWAP)
     packed = lax.dynamic_update_index_in_dim(packed, given, 1 - core, 1)
 
-    def chosen(number):
-        return jnp.stack(
-            [lax.dynamic_index_in_dim(x, number, 0, keepdims=False) for x in (rows, upstream)]
-        )
-
-    line = jnp.stack([chosen(block), lax.ppermute(chosen(1 - block), "dp", CORE_SWAP)])
+    def chosen(x, number):
+        return lax.dynamic_index_in_dim(x, number, 0, keepdims=False)
+
+    arrived = lax.ppermute(
+        jnp.stack([chosen(x, 1 - block) for x in (rows, upstream)]), "dp", CORE_SWAP
+    )
+    own_line = [
+        jnp.stack([chosen(x, block), arrived[kind]]) for kind, x in enumerate((rows, upstream))
+    ]
     packed, other_tiles = lax.optimization_barrier((packed, other_tiles))
     packed = packed.reshape(RANKS, 2 * SPAN, 128)
-    shifted = [lax.ppermute(line, "dp", shift) for shift in X_SHIFTS]
+    near, far, back_near = (
+        [lax.ppermute(half, "dp", shift) for half in own_line] for shift in X_SHIFTS
+    )
     own = lax.all_to_all(packed, "ctx", 0, 0)
-    near, far, back_near = shifted
-    own, near, back_near = lax.optimization_barrier((own, near, back_near))
+    own, near, back_near, own_line = lax.optimization_barrier((own, near, back_near, own_line))
     other_keys = lax.ppermute(own[:, SPAN:], "dp", CORE_SWAP)
     tiles = jnp.where(odd == core, sweep_tiles, other_tiles).reshape(-1)
     query_part, own_grad, other_grad = attend(core_number, tiles, own, other_keys)
+    other_grad, far[0] = lax.optimization_barrier((other_grad, far[0]))
     arrived = lax.ppermute(other_grad, "dp", CORE_SWAP)
     key_part = (own_grad + arrived.astype(jnp.float32)).astype(jnp.bfloat16)
     back = lax.all_to_all(jnp.concatenate([query_part, key_part], axis=1), "ctx", 0, 0)
-    back, far = lax.optimization_barrier((back, far))
+    back, far[1] = lax.optimization_barrier((back, far[1]))
     grads = back.reshape(HEADS, 2, 2 * SPAN, 128)
-    lines = [line, near, far, back_near]
+    lines = [*own_line, *near, *far, *back_near]
     line_grads = lax.all_to_all(
         back.reshape(4, 2, 2, 2 * SPAN, 128), "dp", 0, 0, axis_index_groups=CHIP_LINES
     )

time: 159 us -> 158 us (level)
    all_to_all x1, waiting for transfers between devices: 0.01 us -> 9.05 us  [per_device(): lax.all_to_all(jnp.concatenate([query_part, key_part], axis=1), 'ctx', 0, 0)]
    ppermute x4 -> x7, waiting for transfers between devices: 36.7 us -> 28.2 us  [the longest x6 26.9 us: per_device(): lax.ppermute(half, 'dp', shift)]
    ppermute x4 -> x7, starting transfers between devices: 5.45 us -> 8.05 us  [the longest x6 7.26 us: per_device(): lax.ppermute(half, 'dp', shift)]
    ppermute x2, starting transfers between devices: 9.45 us -> 6.85 us  [per_device(): given = lax.ppermute(give, 'dp', CORE_SWAP)]
  transfers between devices with their start and end apart: 14 -> 17, of which waited for: 10 -> 14; matrix products, arithmetic and copies ran while one was open for 1% -> 1% of each run, Pallas kernels for 3% -> 10%
where the time goes in v9:
time: 158 us
  waiting for transfers between devices  58.8 us (37%)
  starting transfers between devices  46.6 us (29%)
  Pallas kernels  25.2 us (16%)
  blocking collectives  16.4 us (10%)
  local copies, waits for them, and re-layouts  6.7 us (4%)
  other arithmetic  3.06 us (2%)
    ppermute x6, waiting for transfers between devices, per_device(): lax.ppermute(half, 'dp', shift)  26.9 us
    all_to_all x1, blocking collectives, per_device(): parts = lax.all_to_all(jnp.broadcast_to(rows, (16, 64, 256)), 'dp', 0, 0)  16.4 us
    pallas_call x1, Pallas kernels, attend(): pl.pallas_call(attend_kernel, out_shape=(jax.ShapeDtypeStruct(block, jnp....  10.2 us
    all_to_all x1, waiting for transfers between devices, per_device(): lax.all_to_all(back.reshape(4, 2, 2, 2 * SPAN, 128), 'dp', 0, 0, axis_ind...  9.73 us
    all_to_all x1, starting transfers between devices, per_device(): lax.all_to_all(jnp.concatenate([query_part, key_part], axis=1), 'ctx', 0, 0)  9.38 us
    all_to_all x1, starting transfers between devices, per_device(): own = lax.all_to_all(packed, 'ctx', 0, 0)  9.19 us
    all_to_all x1, waiting for transfers between devices, per_device(): lax.all_to_all(jnp.concatenate([query_part, key_part], axis=1), 'ctx', 0, 0)  9.05 us
    ppermute x6, starting transfers between devices, per_device(): lax.ppermute(half, 'dp', shift)  7.26 us
  transfers between devices with their start and end apart: 17, of which 14 were waited for; matrix products, arithmetic and copies ran while one was open for 1% of the time, Pallas kernels for 10%

profile of v9, /device:TPU:1, one launch (start us, length us, event | category | flops | bytes accessed | tf_op | source)
XLA Modules:
  0.0 157.5 jit_solution(7071825447213491191)
XLA Ops:
  0.7 0.6 pad_add_fusion.1.place_ref
  1.3 4.7 %project.1 = (bf16[8,2,192,128]{3,2,1,0:T(8,128)(2,1)}, bf16[8,192,128]{2,1,0:T(8,128)(2,1)}) custom-call(s32[2]{0:T(128)} %pad_add_fusion.1.place_ref, bf16[2,96,1024]{2,1,0:T(8,128)(2,1)} %bitcast.29, bf16[2,96,1024]{2,1,0:T(8,128)(2,1)} %bitcast.30, bf16[4,1024,512]{2,1,0:T(8,128)(2,1)} %weights_ref.3), custom_call_target="tpu_custom_call" | custom-call | tf_op jit(solution)/shard_map/project/pallas_call | solution.py:58
  6.0 3.3 %collective-permute-start = (bf16[8,192,128]{2,1,0:T(8,128)(2,1)}, bf16[8,192,128]{2,1,0:T(8,128)(2,1)S(1)}, u32[]{:S(2)}, u32[]{:S(2)}) collective-permute-start(bf16[8,192,128]{2,1,0:T(8,128)(2,1)} %get-tuple-element.31), channel_id=1, source_target_pairs={{0,16},{16,0},{32,48},{48,32},{64,80},{80,64},{96,112},{112,96},{1... | collective-permute-start | bytes 1179656 | tf_op jit(solution)/shard_map/ppermute | solution.py:392
  9.3 0.1 collective-permute-start.1
  9.4 1.4 collective-permute-done
  10.9 0.8 bitcast_dynamic-update-slice_fusion
  11.7 9.2 %all-to-all-start = ((bf16[16,192,128]{2,1,0:T(8,128)(2,1)}), bf16[16,192,128]{2,1,0:T(8,128)(2,1)S(1)}, u32[]{:S(2)}, u32[]{:S(2)}) async-start(bf16[16,192,128]{2,1,0:T(8,128)(2,1)} %bitcast.31), calls=%async_computation | async-start | bytes 1572864 | tf_op jit(solution)/shard_map/all_to_all | solution.py:409
  21.0 0.8 collective-permute-start.2
  21.8 1.3 collective-permute-done.2
  23.2 1.3 collective-permute-start.3
  24.6 1.3 collective-permute-start.4
  25.9 1.5 collective-permute-start.5
  27.3 0.3 collective-permute-start.6
  27.6 7.3 %collective-permute-done.3.refs_2_ = bf16[2,96,1024]{2,1,0:T(8,128)(2,1)S(1)} collective-permute-done((bf16[2,96,1024]{2,1,0:T(8,128)(2,1)S(1)}, bf16[2,96,1024]{2,1,0:T(8,128)(2,1)S(1)}, u32[]{:S(2)}, u32[]{:S(2)}) %collective-permute-start.3) | collective-permute-done | bytes 393248 | tf_op jit(solution)/shard_map/ppermute | solution.py:407
  34.9 8.4 %collective-permute-done.4.refs_3_ = bf16[2,96,1024]{2,1,0:T(8,128)(2,1)S(1)} collective-permute-done((bf16[2,96,1024]{2,1,0:T(8,128)(2,1)S(1)}, bf16[2,96,1024]{2,1,0:T(8,128)(2,1)S(1)}, u32[]{:S(2)}, u32[]{:S(2)}) %collective-permute-start.4) | collective-permute-done | bytes 393248 | tf_op jit(solution)/shard_map/ppermute | solution.py:407
  43.3 0.7 collective-permute-done.6.refs_7_
  44.0 0.8 slice.11
  44.7 1.8 %collective-permute-start.7 = (bf16[16,96,128]{2,1,0:T(8,128)(2,1)}, bf16[16,96,128]{2,1,0:T(8,128)(2,1)}, u32[]{:S(2)}, u32[]{:S(2)}) collective-permute-start(bf16[16,96,128]{2,1,0:T(8,128)(2,1)} %slice.11), channel_id=1, source_target_pairs={{0,16},{16,0},{32,48},{48,32},{64,80},{80,64},{96,112},{112,96},{1... | collective-permute-start | bytes 1179656 | tf_op jit(solution)/shard_map/ppermute | solution.py:411
  46.6 1.4 collective-permute-start.8
  48.0 0.2 collective-permute-done.7.other_ref
  48.3 10.2 %attend.1 = (bf16[16,96,128]{2,1,0:T(8,128)(2,1)S(1)}, f32[16,96,128]{2,1,0:T(8,128)S(1)}, bf16[16,96,128]{2,1,0:T(8,128)(2,1)S(1)}) custom-call(s32[1]{0:T(128)} %bitcast.core_ref, s32[4]{0:T(128)S(1)} %fusion.tiles_ref, bf16[16,192,128]{2,1,0:T(8,128)(2,1)S(1)} %all-to-all-done.own_ref, bf16[16,96,128]{2,1,0:T(8,128)(2,1)} %collective-permute-done.7.other_ref), custom_call_target="tpu_custom_call" | custom-call | flops 12000000000 | bytes 4194304 | tf_op jit(solution)/shard_map/attend/pallas_call | solution.py:197
  58.5 0.3 collective-permute-done.8.refs_4_
  58.8 0.8 collective-permute-start.9
  59.6 1.3 collective-permute-done.9
  61.0 0.1 add_convert_fusion.1
  61.1 1.0 pad_maximum_fusion
  62.1 9.4 %all-to-all-start.1 = ((bf16[16,192,128]{2,1,0:T(8,128)(2,1)}), bf16[16,192,128]{2,1,0:T(8,128)(2,1)}, u32[]{:S(2)}, u32[]{:S(2)}) async-start(bf16[16,192,128]{2,1,0:T(8,128)(2,1)} %pad_maximum_fusion), calls=%async_computation.1 | async-start | bytes 1572864 | tf_op jit(solution)/shard_map/all_to_all | solution.py:417
  71.5 1.5 collective-permute-start.10
  73.0 10.2 %collective-permute-done.10.refs_5_ = bf16[2,96,1024]{2,1,0:T(8,128)(2,1)S(1)} collective-permute-done((bf16[2,96,1024]{2,1,0:T(8,128)(2,1)S(1)}, bf16[2,96,1024]{2,1,0:T(8,128)(2,1)S(1)}, u32[]{:S(2)}, u32[]{:S(2)}) %collective-permute-start.10) | collective-permute-done | bytes 393248 | tf_op jit(solution)/shard_map/ppermute | solution.py:407
  83.2 0.7 copy-done.1
  83.9 9.0 %all-to-all-done.1 = bf16[16,192,128]{2,1,0:T(8,128)(2,1)} async-done(((bf16[16,192,128]{2,1,0:T(8,128)(2,1)}), bf16[16,192,128]{2,1,0:T(8,128)(2,1)}, u32[]{:S(2)}, u32[]{:S(2)}) %all-to-all-start.1) | async-done | bytes 786464 | tf_op jit(solution)/shard_map/all_to_all | solution.py:417
  93.0 3.9 %all-to-all-start.2 = ((bf16[4,2,2,192,128]{4,3,2,1,0:T(8,128)(2,1)}), bf16[4,2,2,192,128]{4,3,2,1,0:T(8,128)(2,1)S(1)}, u32[]{:S(2)}, u32[]{:S(2)}) async-start(bf16[4,2,2,192,128]{4,3,2,1,0:T(8,128)(2,1)} %bitcast.13), calls=%async_computation.2 | async-start | bytes 1572864 | tf_op jit(solution)/shard_map/all_to_all | solution.py:421
  97.0 9.7 %all-to-all-done.2.grads_ref = bf16[4,2,2,192,128]{4,3,2,1,0:T(8,128)(2,1)S(1)} async-done(((bf16[4,2,2,192,128]{4,3,2,1,0:T(8,128)(2,1)}), bf16[4,2,2,192,128]{4,3,2,1,0:T(8,128)(2,1)S(1)}, u32[]{:S(2)}, u32[]{:S(2)}) %all-to-all-start.2) | async-done | bytes 786464 | tf_op jit(solution)/shard_map/all_to_all | solution.py:421
  106.7 1.0 copy-done.2
  107.7 3.4 %weight_terms.1 = (bf16[16,64,256]{2,1,0:T(8,128)(2,1)S(1)}, bf16[16,64,256]{2,1,0:T(8,128)(2,1)S(1)}) custom-call(s32[2]{0:T(128)S(1)} %pad_add_fusion.place_ref, bf16[4,2,2,192,128]{4,3,2,1,0:T(8,128)(2,1)S(1)} %all-to-all-done.2.grads_ref, bf16[2,96,1024]{2,1,0:T(8,128)(2,1)S(1)} %pad_maximum_fusion.2.refs_0_, ...), custom_call_target="tpu_custom_call" | custom-call | tf_op jit(solution)/shard_map/weight_terms/pallas_call | solution.py:265
  111.2 3.5 %collective-permute-start.11 = (bf16[16,64,256]{2,1,0:T(8,128)(2,1)S(1)}, bf16[16,64,256]{2,1,0:T(8,128)(2,1)S(1)}, u32[]{:S(2)}, u32[]{:S(2)}) collective-permute-start(bf16[16,64,256]{2,1,0:T(8,128)(2,1)S(1)} %get-tuple-element.49), channel_id=1, source_target_pairs={{0,16},{16,0},{32,48},{48,32},{64,80},{80,64},{96,112},{112,96},{1... | collective-permute-start | bytes 1572872 | tf_op jit(solution)/shard_map/ppermute | solution.py:427
  114.7 1.5 collective-permute-done.11
  116.2 1.0 add_convert_fusion
  117.2 5.7 %all-to-all-start.3 = ((bf16[16,64,256]{2,1,0:T(8,128)(2,1)}), bf16[16,64,256]{2,1,0:T(8,128)(2,1)S(1)}, u32[]{:S(2)}, u32[]{:S(2)}) async-start(bf16[16,64,256]{2,1,0:T(8,128)(2,1)} %add_convert_fusion), calls=%async_computation.3 | async-start | bytes 1048576 | tf_op jit(solution)/shard_map/all_to_all | solution.py:430
  122.9 1.0 dynamic-slice_bitcast_fusion
  123.9 0.7 collective-permute-start.12
  124.7 1.3 collective-permute-done.12.arrived_ref
  126.0 2.2 %copy-done = bf16[4,1024,512]{2,1,0:T(8,128)(2,1)S(1)} copy-done((bf16[4,1024,512]{2,1,0:T(8,128)(2,1)S(1)}, bf16[4,1024,512]{2,1,0:T(8,128)(2,1)}, u32[]{:S(2)}) %copy-start) | copy-done | bytes 4194328
  128.2 4.9 %outputs.1 = (bf16[2,96,1024]{2,1,0:T(8,128)(2,1)}, bf16[2,96,1024]{2,1,0:T(8,128)(2,1)}) custom-call(s32[2]{0:T(128)S(1)} %pad_add_fusion.2.place_ref, bf16[8,2,192,128]{3,2,1,0:T(8,128)(2,1)} %bitcast.14.grads_ref, bf16[8,192,128]{2,1,0:T(8,128)(2,1)S(1)} %collective-permute-done.12.arrived_ref, bf16[4,1024,512]{2,1,0:T(8,128)(2,1)S(1)} %copy-done), custom_call_target="tpu_custom_call" | custom-call | flops 805306368 | bytes 7340032 | tf_op jit(solution)/shard_map/outputs/pallas_call | solution.py:356
  133.1 6.0 %all-to-all-done.3 = bf16[16,64,256]{2,1,0:T(8,128)(2,1)S(1)} async-done(((bf16[16,64,256]{2,1,0:T(8,128)(2,1)}), bf16[16,64,256]{2,1,0:T(8,128)(2,1)S(1)}, u32[]{:S(2)}, u32[]{:S(2)}) %all-to-all-start.3) | async-done | bytes 524320 | tf_op jit(solution)/shard_map/all_to_all | solution.py:430
  139.1 0.1 reduce_sum.12
  139.2 16.4 %all_to_all.25 = bf16[16,64,256]{2,1,0:T(8,128)(2,1)} all-to-all(bf16[16,64,256]{2,1,0:T(8,128)(2,1)S(1)} %broadcast_in_dim.8), channel_id=1, replica_groups=mesh['dp'=16,'ctx'=16] {'dp'}, dimensions={0} | all-to-all | bytes 1048576 | tf_op jit(solution)/shard_map/all_to_all | solution.py:438
  155.6 1.9 %spread_heads.1 = bf16[4,64,512]{2,1,0:T(8,128)(2,1)} custom-call(bf16[4,2,2,64,256]{4,3,2,1,0:T(8,128)(2,1)} %bitcast.28), custom_call_target="tpu_custom_call" | custom-call | tf_op jit(solution)/shard_map/spread_heads/pallas_call | solution.py:307
  (21 shorter events, 0.4 us)
Async XLA Ops:
  1.3 8.0 %copy-start.5 = (s32[1,4]{1,0:T(1,128)S(1)}, s32[1,4]{1,0:T(1,128)}, u32[]{:S(2)}) copy-start(s32[1,4]{1,0:T(1,128)} %param.5) | copy-start | bytes 52
  6.0 14.9 %copy-start.3 = (bf16[1,1,2,96,1024]{4,3,2,1,0:T(8,128)(2,1)S(1)}, bf16[1,1,2,96,1024]{4,3,2,1,0:T(8,128)(2,1)}, u32[]{:S(2)}) copy-start(bf16[1,1,2,96,1024]{4,3,2,1,0:T(8,128)(2,1)} %param.4) | copy-start | bytes 1179652
  6.0 14.9 %copy-start.4 = (bf16[1,1,2,96,1024]{4,3,2,1,0:T(8,128)(2,1)S(1)}, bf16[1,1,2,96,1024]{4,3,2,1,0:T(8,128)(2,1)}, u32[]{:S(2)}) copy-start(bf16[1,1,2,96,1024]{4,3,2,1,0:T(8,128)(2,1)} %param.7) | copy-start | bytes 1179652
  6.0 4.9 %collective-permute-start = (bf16[8,192,128]{2,1,0:T(8,128)(2,1)}, bf16[8,192,128]{2,1,0:T(8,128)(2,1)S(1)}, u32[]{:S(2)}, u32[]{:S(2)}) collective-permute-start(bf16[8,192,128]{2,1,0:T(8,128)(2,1)} %get-tuple-element.31), channel_id=1, source_target_pairs={{0,16},{16,0},{32,48},{48,32},{64,80},{80,64},{96,112},{112,96},{1... | collective-permute-start | bytes 1179656 | tf_op jit(solution)/shard_map/ppermute | solution.py:392
  9.3 2.4 %collective-permute-start.1 = (s32[1,4]{1,0:T(1,128)S(1)}, s32[1,4]{1,0:T(1,128)S(1)}, u32[]{:S(2)}, u32[]{:S(2)}) collective-permute-start(s32[1,4]{1,0:T(1,128)S(1)} %copy-done.5), channel_id=1, source_target_pairs={{0,16},{16,0},{32,48},{48,32},{64,80},{80,64},{96,112},{112,96},{1... | collective-permute-start | bytes 56 | tf_op jit(solution)/shard_map/ppermute | solution.py:387
  11.7 32.3 %all-to-all-start = ((bf16[16,192,128]{2,1,0:T(8,128)(2,1)}), bf16[16,192,128]{2,1,0:T(8,128)(2,1)S(1)}, u32[]{:S(2)}, u32[]{:S(2)}) async-start(bf16[16,192,128]{2,1,0:T(8,128)(2,1)} %bitcast.31), calls=%async_computation | async-start | bytes 1572864 | tf_op jit(solution)/shard_map/all_to_all | solution.py:409
  21.0 2.1 %collective-permute-start.2 = (bf16[2,96,1024]{2,1,0:T(8,128)(2,1)S(1)}, bf16[2,96,1024]{2,1,0:T(8,128)(2,1)S(1)}, u32[]{:S(2)}, u32[]{:S(2)}) collective-permute-start(bf16[2,96,1024]{2,1,0:T(8,128)(2,1)S(1)} %pad_maximum_fusion.1), channel_id=1, source_target_pairs={{0,16},{16,0},{32,48},{48,32},{64,80},{80,64},{96,112},{112,96},{1... | collective-permute-start | bytes 1179656 | tf_op jit(solution)/shard_map/ppermute | solution.py:398
  23.2 11.6 %collective-permute-start.3 = (bf16[2,96,1024]{2,1,0:T(8,128)(2,1)S(1)}, bf16[2,96,1024]{2,1,0:T(8,128)(2,1)S(1)}, u32[]{:S(2)}, u32[]{:S(2)}) collective-permute-start(bf16[2,96,1024]{2,1,0:T(8,128)(2,1)S(1)} %pad_maximum_fusion.2.refs_0_), channel_id=1, source_target_pairs={{0,64},{16,80},{32,96},{48,112},{64,128},{80,144},{96,160},{112,17... | collective-permute-start | bytes 1179656 | tf_op jit(solution)/shard_map/ppermute | solution.py:407
  24.6 18.7 %collective-permute-start.4 = (bf16[2,96,1024]{2,1,0:T(8,128)(2,1)S(1)}, bf16[2,96,1024]{2,1,0:T(8,128)(2,1)S(1)}, u32[]{:S(2)}, u32[]{:S(2)}) collective-permute-start(bf16[2,96,1024]{2,1,0:T(8,128)(2,1)S(1)} %pad_maximum_fusion.3.refs_1_), channel_id=1, source_target_pairs={{0,64},{16,80},{32,96},{48,112},{64,128},{80,144},{96,160},{112,17... | collective-permute-start | bytes 1179656 | tf_op jit(solution)/shard_map/ppermute | solution.py:407
  25.9 17.4 %collective-permute-start.5 = (bf16[2,96,1024]{2,1,0:T(8,128)(2,1)S(1)}, bf16[2,96,1024]{2,1,0:T(8,128)(2,1)S(1)}, u32[]{:S(2)}, u32[]{:S(2)}) collective-permute-start(bf16[2,96,1024]{2,1,0:T(8,128)(2,1)S(1)} %pad_maximum_fusion.2.refs_0_), channel_id=1, source_target_pairs={{0,192},{16,208},{32,224},{48,240},{64,0},{80,16},{96,32},{112,48}... | collective-permute-start | bytes 1179656 | tf_op jit(solution)/shard_map/ppermute | solution.py:407
  27.3 16.6 %collective-permute-start.6 = (bf16[2,96,1024]{2,1,0:T(8,128)(2,1)S(1)}, bf16[2,96,1024]{2,1,0:T(8,128)(2,1)S(1)}, u32[]{:S(2)}, u32[]{:S(2)}) collective-permute-start(bf16[2,96,1024]{2,1,0:T(8,128)(2,1)S(1)} %pad_maximum_fusion.3.refs_1_), channel_id=1, source_target_pairs={{0,192},{16,208},{32,224},{48,240},{64,0},{80,16},{96,32},{112,48}... | collective-permute-start | bytes 1179656 | tf_op jit(solution)/shard_map/ppermute | solution.py:407
  44.7 3.5 %collective-permute-start.7 = (bf16[16,96,128]{2,1,0:T(8,128)(2,1)}, bf16[16,96,128]{2,1,0:T(8,128)(2,1)}, u32[]{:S(2)}, u32[]{:S(2)}) collective-permute-start(bf16[16,96,128]{2,1,0:T(8,128)(2,1)} %slice.11), channel_id=1, source_target_pairs={{0,16},{16,0},{32,48},{48,32},{64,80},{80,64},{96,112},{112,96},{1... | collective-permute-start | bytes 1179656 | tf_op jit(solution)/shard_map/ppermute | solution.py:411
  46.6 12.3 %collective-permute-start.8 = (bf16[2,96,1024]{2,1,0:T(8,128)(2,1)S(1)}, bf16[2,96,1024]{2,1,0:T(8,128)(2,1)S(1)}, u32[]{:S(2)}, u32[]{:S(2)}) collective-permute-start(bf16[2,96,1024]{2,1,0:T(8,128)(2,1)S(1)} %pad_maximum_fusion.2.refs_0_), channel_id=1, source_target_pairs={{0,128},{16,144},{32,160},{48,176},{64,192},{80,208},{96,224},{112... | collective-permute-start | bytes 1179656 | tf_op jit(solution)/shard_map/ppermute | solution.py:407
  58.8 2.1 %collective-permute-start.9 = (bf16[16,96,128]{2,1,0:T(8,128)(2,1)S(1)}, bf16[16,96,128]{2,1,0:T(8,128)(2,1)S(1)}, u32[]{:S(2)}, u32[]{:S(2)}) collective-permute-start(bf16[16,96,128]{2,1,0:T(8,128)(2,1)S(1)} %get-tuple-element.38), channel_id=1, source_target_pairs={{0,16},{16,0},{32,48},{48,32},{64,80},{80,64},{96,112},{112,96},{1... | collective-permute-start | bytes 1179656 | tf_op jit(solution)/shard_map/ppermute | solution.py:415
  62.1 30.9 %all-to-all-start.1 = ((bf16[16,192,128]{2,1,0:T(8,128)(2,1)}), bf16[16,192,128]{2,1,0:T(8,128)(2,1)}, u32[]{:S(2)}, u32[]{:S(2)}) async-start(bf16[16,192,128]{2,1,0:T(8,128)(2,1)} %pad_maximum_fusion), calls=%async_computation.1 | async-start | bytes 1572864 | tf_op jit(solution)/shard_map/all_to_all | solution.py:417
  71.5 11.7 %collective-permute-start.10 = (bf16[2,96,1024]{2,1,0:T(8,128)(2,1)S(1)}, bf16[2,96,1024]{2,1,0:T(8,128)(2,1)S(1)}, u32[]{:S(2)}, u32[]{:S(2)}) collective-permute-start(bf16[2,96,1024]{2,1,0:T(8,128)(2,1)S(1)} %pad_maximum_fusion.3.refs_1_), channel_id=1, source_target_pairs={{0,128},{16,144},{32,160},{48,176},{64,192},{80,208},{96,224},{112... | collective-permute-start | bytes 1179656 | tf_op jit(solution)/shard_map/ppermute | solution.py:407
  83.2 0.7 copy-start.1
  93.0 13.8 %all-to-all-start.2 = ((bf16[4,2,2,192,128]{4,3,2,1,0:T(8,128)(2,1)}), bf16[4,2,2,192,128]{4,3,2,1,0:T(8,128)(2,1)S(1)}, u32[]{:S(2)}, u32[]{:S(2)}) async-start(bf16[4,2,2,192,128]{4,3,2,1,0:T(8,128)(2,1)} %bitcast.13), calls=%async_computation.2 | async-start | bytes 1572864 | tf_op jit(solution)/shard_map/all_to_all | solution.py:421
  106.7 1.0 copy-start.2
  111.2 5.1 %collective-permute-start.11 = (bf16[16,64,256]{2,1,0:T(8,128)(2,1)S(1)}, bf16[16,64,256]{2,1,0:T(8,128)(2,1)S(1)}, u32[]{:S(2)}, u32[]{:S(2)}) collective-permute-start(bf16[16,64,256]{2,1,0:T(8,128)(2,1)S(1)} %get-tuple-element.49), channel_id=1, source_target_pairs={{0,16},{16,0},{32,48},{48,32},{64,80},{80,64},{96,112},{112,96},{1... | collective-permute-start | bytes 1572872 | tf_op jit(solution)/shard_map/ppermute | solution.py:427
  117.2 21.9 %all-to-all-start.3 = ((bf16[16,64,256]{2,1,0:T(8,128)(2,1)}), bf16[16,64,256]{2,1,0:T(8,128)(2,1)S(1)}, u32[]{:S(2)}, u32[]{:S(2)}) async-start(bf16[16,64,256]{2,1,0:T(8,128)(2,1)} %add_convert_fusion), calls=%async_computation.3 | async-start | bytes 1048576 | tf_op jit(solution)/shard_map/all_to_all | solution.py:430
  123.9 2.1 %collective-permute-start.12 = (bf16[8,192,128]{2,1,0:T(8,128)(2,1)S(1)}, bf16[8,192,128]{2,1,0:T(8,128)(2,1)S(1)}, u32[]{:S(2)}, u32[]{:S(2)}) collective-permute-start(bf16[8,192,128]{2,1,0:T(8,128)(2,1)S(1)} %dynamic-slice_bitcast_fusion), channel_id=1, source_target_pairs={{0,16},{16,0},{32,48},{48,32},{64,80},{80,64},{96,112},{112,96},{1... | collective-permute-start | bytes 1179656 | tf_op jit(solution)/shard_map/ppermute | solution.py:431
  126.0 2.2 %copy-start = (bf16[4,1024,512]{2,1,0:T(8,128)(2,1)S(1)}, bf16[4,1024,512]{2,1,0:T(8,128)(2,1)}, u32[]{:S(2)}) copy-start(bf16[4,1024,512]{2,1,0:T(8,128)(2,1)} %weights_ref.3) | copy-start | bytes 12582916

commit v10 on v9

--- a/solution.py
+++ b/solution.py
@@ -217,8 +217,38 @@
     )(core, tiles, own, other_keys)
 
 
-def weight_kernel(place_ref, grads_ref, *refs):
-    line_refs, (keep_ref, give_ref, held_ref) = refs[:8], refs[8:]
+def repack_kernel(back_ref, out_ref):
+    low = low_lanes(SPAN)
+    for sequence in range(2):
+        for half, (lower, upper) in enumerate(((0, 3), (1, 2))):
+            place = slice(SPAN * half, SPAN * half + SPAN)
+            for pair in range(HEADS // 2):
+                columns = slice(128 * pair, 128 * pair + 128)
+                one = back_ref[2 * pair, sequence, place, :].astype(jnp.float32)
+                two = back_ref[2 * pair + 1, sequence, place, :].astype(jnp.float32)
+                out_ref[lower, sequence, :, columns] = jnp.where(
+                    low, one, pltpu.roll(two, HEAD, 1)
+                ).astype(jnp.bfloat16)
+                out_ref[upper, sequence, :, columns] = jnp.where(
+                    low, pltpu.roll(one, HEAD, 1), two
+                ).astype(jnp.bfloat16)
+
+
+def repack(back):
+    vmem = pl.BlockSpec(memory_space=pltpu.VMEM)
+    return pl.pallas_call(
+        repack_kernel,
+        out_shape=jax.ShapeDtypeStruct((4, 2, SPAN, HQ), jnp.bfloat16),
+        in_specs=[vmem],
+        out_specs=vmem,
+        compiler_params=pltpu.CompilerParams(vmem_limit_bytes=SMALL_VMEM),
+        name="repack",
+    )(back)
+
+
+def weight_kernel(
+    place_ref, grads_ref, own_ref, near_ref, far_ref, back_ref, keep_ref, give_ref, held_ref
+):
     core, column = place_ref[0], place_ref[1]
 
     @pl.when(pl.program_id(0) == 0)
@@ -226,36 +256,22 @@
         for shift in range(4):
             chip = jnp.bitwise_and(column + 4 - shift, 3)
             for part in range(2):
-                sequence = jnp.bitwise_xor(core, part)
                 first = (2 * shift + part) * SPAN
-                for head in range(2):
-                    for half in range(2):
-                        lanes = 128 * (2 * half + head)
-                        held_ref[first : first + SPAN, lanes : lanes + 128] = grads_ref[
-                            chip, head, sequence, SPAN * half : SPAN * half + SPAN, :
-                        ]
-
-    def product(kind, columns):
-        rows = jnp.concatenate(
-            [ref[...].reshape(2 * SPAN, D // 4) for ref in line_refs[kind::2]], axis=0
-        )
-        return lax.dot_general(
-            rows, held_ref[:, :columns], (((0,), (0,)), ((), ())), preferred_element_type=jnp.float32
-        )
-
-    by_tokens = product(0, 512)
-    by_upstream = product(1, 256)
-    low = low_lanes(D // 4)
-    firsts = [
-        jnp.where(low, by_tokens[:, 128 * i : 128 * i + 128], by_upstream[:, 128 * i : 128 * i + 128])
-        for i in range(2)
-    ]
-    seconds = [by_tokens[:, 256:384], by_tokens[:, 384:]]
-    for lanes, (zero, one) in ((slice(0, 128), firsts), (slice(128, 256), seconds)):
-        kept = jnp.where(core == 0, zero, one).astype(jnp.bfloat16)
-        given = jnp.where(core == 0, one, zero).astype(jnp.bfloat16)
-        keep_ref[:, :, lanes] = kept.reshape(4, 64, 128)
-        give_ref[:, :, lanes] = given.reshape(4, 64, 128)
+                held_ref[first : first + SPAN, :] = grads_ref[chip, jnp.bitwise_xor(core, part)]
+
+    rows = jnp.concatenate(
+        [
+            ref[...].reshape(2 * SPAN, D // 4)
+            for ref in (own_ref, near_ref, far_ref, back_ref)
+        ],
+        axis=0,
+    )
+    result = lax.dot_general(
+        rows, held_ref[...], (((0,), (0,)), ((), ())), preferred_element_type=jnp.float32
+    )
+    zero, one = result[:, :256], result[:, 256:]
+    keep_ref[...] = jnp.where(core == 0, zero, one).astype(jnp.bfloat16).reshape(4, 64, 256)
+    give_ref[...] = jnp.where(core == 0, one, zero).astype(jnp.bfloat16).reshape(4, 64, 256)
 
 
 def weight_terms(place, grads, lines):
@@ -269,11 +285,11 @@
             num_scalar_prefetch=1,
             grid=(4,),
             in_specs=[
-                pl.BlockSpec((4, 2, 2, 2 * SPAN, 128), lambda j, place: (0, 0, 0, 0, 0)),
-                *[line_spec] * 8,
+                pl.BlockSpec((4, 2, SPAN, HQ), lambda j, place: (0, 0, 0, 0)),
+                *[line_spec] * 4,
             ],
             out_specs=(out_spec, out_spec),
-            scratch_shapes=[pltpu.VMEM((8 * SPAN, 512), jnp.bfloat16)],
+            scratch_shapes=[pltpu.VMEM((8 * SPAN, HQ), jnp.bfloat16)],
         ),
         compiler_params=pltpu.CompilerParams(vmem_limit_bytes=SMALL_VMEM),
         name="weight_terms",
@@ -281,33 +297,22 @@
 
 
 def spread_kernel(parts_ref, out_ref):
-    low = low_lanes(64)
     factor = float(16 * RANKS * 2 * SPAN) ** -0.5
     for column in range(4):
-        columns = slice(128 * column, 128 * column + 128)
-        for half, (lower, upper) in enumerate(((0, 3), (1, 2))):
-            lanes = slice(128 * half, 128 * half + 128)
-            one, two = (
-                factor
-                * (
-                    parts_ref[column, 0, core, :, lanes].astype(jnp.float32)
-                    + parts_ref[column, 1, core, :, lanes].astype(jnp.float32)
-                )
-                for core in range(2)
-            )
-            out_ref[lower, :, columns] = jnp.where(low, one, pltpu.roll(two, HEAD, 1)).astype(
+        for core in range(2):
+            total = parts_ref[column, 0, core].astype(jnp.float32) + parts_ref[
+                column, 1, core
+            ].astype(jnp.float32)
+            out_ref[column, :, 256 * core : 256 * core + 256] = (total * factor).astype(
                 jnp.bfloat16
             )
-            out_ref[upper, :, columns] = jnp.where(low, pltpu.roll(one, HEAD, 1), two).astype(
-                jnp.bfloat16
-            )
-
-
-def spread_heads(parts):
+
+
+def spread(parts):
     return pl.pallas_call(
         spread_kernel,
         out_shape=jax.ShapeDtypeStruct((4, 64, HQ), jnp.bfloat16),
-        name="spread_heads",
+        name="spread",
     )(parts)
 
 
@@ -316,37 +321,23 @@
 
     @pl.when(pl.program_id(0) == 0)
     def _():
-        low = low_lanes(SPAN)
         for block in range(2):
-            holder = jnp.bitwise_xor(odd, block)
-            rows = slice(SPAN * block, SPAN * block + SPAN)
-            for half in range(2):
-                place = slice(SPAN * half, SPAN * half + SPAN)
-                for pair in range(HEADS // 2):
-                    columns = slice(128 * pair, 128 * pair + 128)
-                    one, two = (
-                        jnp.where(
-                            holder == core,
-                            grads_ref[head, 0, place, :].astype(jnp.float32),
-                            arrived_ref[head, place, :].astype(jnp.float32),
-                        )
-                        for head in (2 * pair, 2 * pair + 1)
-                    )
-                    held_ref[2 * half, rows, columns] = jnp.where(
-                        low, one, pltpu.roll(two, HEAD, 1)
-                    ).astype(jnp.bfloat16)
-                    held_ref[2 * half + 1, rows, columns] = jnp.where(
-                        low, pltpu.roll(one, HEAD, 1), two
-                    ).astype(jnp.bfloat16)
-
-    def product(number, weight):
+            mine = jnp.bitwise_xor(odd, block) == core
+            for number in range(4):
+                held_ref[number, SPAN * block : SPAN * block + SPAN, :] = jnp.where(
+                    mine,
+                    grads_ref[number, 0].astype(jnp.float32),
+                    arrived_ref[number].astype(jnp.float32),
+                ).astype(jnp.bfloat16)
+
+    def product(number):
         return lax.dot_general(
-            held_ref[number], weights_ref[weight], (((1,), (1,)), ((), ())),
+            held_ref[number], weights_ref[number], (((1,), (1,)), ((), ())),
             preferred_element_type=jnp.float32,
         )
 
-    out_ref[...] = product(1, 3).astype(jnp.bfloat16).reshape(2, SPAN, D // 4)
-    input_grad = product(0, 0) + product(2, 1) + product(3, 2)
+    out_ref[...] = product(3).astype(jnp.bfloat16).reshape(2, SPAN, D // 4)
+    input_grad = product(0) + product(1) + product(2)
     input_grad_ref[...] = input_grad.astype(jnp.bfloat16).reshape(2, SPAN, D // 4)
 
 
@@ -360,8 +351,8 @@
             num_scalar_prefetch=1,
             grid=(4,),
             in_specs=[
-                pl.BlockSpec((HEADS, 1, 2 * SPAN, 128), lambda j, place: (0, place[0], 0, 0)),
-                pl.BlockSpec((HEADS, 2 * SPAN, 128), lambda j, place: (0, 0, 0)),
+                pl.BlockSpec((4, 1, SPAN, HQ), lambda j, place: (0, place[0], 0, 0)),
+                pl.BlockSpec((4, SPAN, HQ), lambda j, place: (0, 0, 0)),
                 pl.BlockSpec((4, D // 4, HQ), lambda j, place: (0, j, 0)),
             ],
             out_specs=(out_spec, out_spec),
@@ -403,26 +394,25 @@
     ]
     packed, other_tiles = lax.optimization_barrier((packed, other_tiles))
     packed = packed.reshape(RANKS, 2 * SPAN, 128)
+    line, *lines = (
+        jnp.where((column + shift) % 4 == 3, own_line[1], own_line[0]) for shift in range(4)
+    )
     near, far, back_near = (
-        [lax.ppermute(half, "dp", shift) for half in own_line] for shift in X_SHIFTS
+        lax.ppermute(rows, "dp", shift) for rows, shift in zip(lines, X_SHIFTS)
     )
     own = lax.all_to_all(packed, "ctx", 0, 0)
-    own, near, back_near, own_line = lax.optimization_barrier((own, near, back_near, own_line))
+    own, near, back_near = lax.optimization_barrier((own, near, back_near))
     other_keys = lax.ppermute(own[:, SPAN:], "dp", CORE_SWAP)
     tiles = jnp.where(odd == core, sweep_tiles, other_tiles).reshape(-1)
     query_part, own_grad, other_grad = attend(core_number, tiles, own, other_keys)
-    other_grad, far[0] = lax.optimization_barrier((other_grad, far[0]))
     arrived = lax.ppermute(other_grad, "dp", CORE_SWAP)
     key_part = (own_grad + arrived.astype(jnp.float32)).astype(jnp.bfloat16)
     back = lax.all_to_all(jnp.concatenate([query_part, key_part], axis=1), "ctx", 0, 0)
-    back, far[1] = lax.optimization_barrier((back, far[1]))
-    grads = back.reshape(HEADS, 2, 2 * SPAN, 128)
-    lines = [*own_line, *near, *far, *back_near]
-    line_grads = lax.all_to_all(
-        back.reshape(4, 2, 2, 2 * SPAN, 128), "dp", 0, 0, axis_index_groups=CHIP_LINES
-    )
+    grads = repack(back.reshape(HEADS, 2, 2 * SPAN, 128))
+    grads, far = lax.optimization_barrier((grads, far))
+    line_grads = lax.all_to_all(grads, "dp", 0, 0, axis_index_groups=CHIP_LINES)
     keep, give = weight_terms(
-        jnp.stack([core, column]).astype(jnp.int32), line_grads, lines
+        jnp.stack([core, column]).astype(jnp.int32), line_grads, (line, near, far, back_near)
     )
     given = lax.ppermute(give, "dp", CORE_SWAP)
     terms = (keep.astype(jnp.float32) + given.astype(jnp.float32)).astype(jnp.bfloat16)
@@ -436,7 +426,7 @@
     terms, attn_out, input_grad = lax.optimization_barrier((terms, attn_out, input_grad))
     rows = jnp.sum(terms.astype(jnp.float32), axis=0).astype(jnp.bfloat16)
     parts = lax.all_to_all(jnp.broadcast_to(rows, (16, 64, 256)), "dp", 0, 0)
-    weight_grads = spread_heads(parts.reshape(4, 2, 2, 64, 256))
+    weight_grads = spread(parts.reshape(4, 2, 2, 64, 256))
     return (attn_out.reshape(tokens.shape), input_grad.reshape(tokens.shape), weight_grads)
 
 

time: 158 us -> 149 us (0.943)
  starting transfers between devices: 46.6 us -> 37.8 us
  local copies, waits for them, and re-layouts: 6.7 us -> 4.22 us
  waiting for transfers between devices: 58.8 us -> 60.4 us
    ppermute x6 -> x3, waiting for transfers between devices: 26.9 us -> 11.2 us  [per_device(): lax.ppermute(rows, 'dp', shift)]
    all_to_all x1, waiting for transfers between devices: 9.05 us -> 20.3 us  [per_device(): lax.all_to_all(jnp.concatenate([query_part, key_part], axis=1), 'ctx', 0, 0)]
    all_to_all x1, waiting for transfers between devices: 0.01 us -> 5.22 us  [per_device(): own = lax.all_to_all(packed, 'ctx', 0, 0)]
    all_to_all x1, starting transfers between devices: 9.38 us -> 4.64 us  [per_device(): lax.all_to_all(jnp.concatenate([query_part, key_part], axis=1), 'ctx', 0, 0)]
    ppermute x6 -> x3, starting transfers between devices: 7.26 us -> 5.29 us  [per_device(): lax.ppermute(rows, 'dp', shift)]
    unnamed x12 -> x8, local copies, waits for them, and re-layouts: 3.94 us -> 2.2 us
  transfers between devices with their start and end apart: 17 -> 14, of which waited for: 14 -> 12; matrix products, arithmetic and copies ran while one was open for 1% -> 2% of each run, Pallas kernels for 10% -> 4%
where the time goes in v10:
time: 149 us
  waiting for transfers between devices  60.4 us (41%)
  starting transfers between devices  37.8 us (25%)
  Pallas kernels  25.2 us (17%)
  blocking collectives  17.2 us (12%)
  local copies, waits for them, and re-layouts  4.22 us (3%)
  other arithmetic  3.05 us (2%)
    all_to_all x1, waiting for transfers between devices, per_device(): lax.all_to_all(jnp.concatenate([query_part, key_part], axis=1), 'ctx', 0, 0)  20.3 us
    all_to_all x1, blocking collectives, per_device(): parts = lax.all_to_all(jnp.broadcast_to(rows, (16, 64, 256)), 'dp', 0, 0)  17.2 us
    ppermute x3, waiting for transfers between devices, per_device(): lax.ppermute(rows, 'dp', shift)  11.2 us
    pallas_call x1, Pallas kernels, attend(): pl.pallas_call(attend_kernel, out_shape=(jax.ShapeDtypeStruct(block, jnp....  10.3 us
    all_to_all x1, waiting for transfers between devices, per_device(): line_grads = lax.all_to_all(grads, 'dp', 0, 0, axis_index_groups=CHIP_LINES)  9.59 us
    all_to_all x1, starting transfers between devices, per_device(): own = lax.all_to_all(packed, 'ctx', 0, 0)  9.19 us
    ppermute x2, starting transfers between devices, per_device(): given = lax.ppermute(give, 'dp', CORE_SWAP)  6.95 us
    all_to_all x1, waiting for transfers between devices, per_device(): terms = lax.all_to_all(terms, 'ctx', 0, 0)  5.36 us
  transfers between devices with their start and end apart: 14, of which 12 were waited for; matrix products, arithmetic and copies ran while one was open for 2% of the time, Pallas kernels for 4%

profile of v10, /device:TPU:1, one launch (start us, length us, event | category | flops | bytes accessed | tf_op | source)
XLA Modules:
  0.0 148.7 jit_solution(5859141921503617925)
XLA Ops:
  0.7 0.6 pad_add_fusion.1.place_ref
  1.2 4.7 %project.1 = (bf16[8,2,192,128]{3,2,1,0:T(8,128)(2,1)}, bf16[8,192,128]{2,1,0:T(8,128)(2,1)}) custom-call(s32[2]{0:T(128)} %pad_add_fusion.1.place_ref, bf16[2,96,1024]{2,1,0:T(8,128)(2,1)} %bitcast.29, bf16[2,96,1024]{2,1,0:T(8,128)(2,1)} %bitcast.30, bf16[4,1024,512]{2,1,0:T(8,128)(2,1)} %weights_ref.3), custom_call_target="tpu_custom_call" | custom-call | tf_op jit(solution)/shard_map/project/pallas_call | solution.py:58
  5.9 3.3 %collective-permute-start = (bf16[8,192,128]{2,1,0:T(8,128)(2,1)}, bf16[8,192,128]{2,1,0:T(8,128)(2,1)S(1)}, u32[]{:S(2)}, u32[]{:S(2)}) collective-permute-start(bf16[8,192,128]{2,1,0:T(8,128)(2,1)} %get-tuple-element.25), channel_id=1, source_target_pairs={{0,16},{16,0},{32,48},{48,32},{64,80},{80,64},{96,112},{112,96},{1... | collective-permute-start | bytes 1179656 | tf_op jit(solution)/shard_map/ppermute | solution.py:383
  9.3 0.1 collective-permute-start.1
  9.4 1.4 collective-permute-done
  10.8 0.8 bitcast_dynamic-update-slice_fusion
  11.6 0.0 collective-permute-done.1
  11.6 9.2 %all-to-all-start = ((bf16[16,192,128]{2,1,0:T(8,128)(2,1)}), bf16[16,192,128]{2,1,0:T(8,128)(2,1)S(1)}, u32[]{:S(2)}, u32[]{:S(2)}) async-start(bf16[16,192,128]{2,1,0:T(8,128)(2,1)} %bitcast.31), calls=%async_computation | async-start | bytes 1572864 | tf_op jit(solution)/shard_map/all_to_all | solution.py:403
  20.9 0.1 dynamic-slice_bitcast_fusion.1
  21.0 0.7 collective-permute-start.2
  21.7 1.3 collective-permute-done.2
  23.1 0.1 broadcast_select_fusion.3
  23.2 0.1 broadcast_select_fusion
  23.3 2.6 %collective-permute-start.4 = (bf16[2,96,1024]{2,1,0:T(8,128)(2,1)S(1)}, bf16[2,96,1024]{2,1,0:T(8,128)(2,1)S(1)}, u32[]{:S(2)}, u32[]{:S(2)}) collective-permute-start(bf16[2,96,1024]{2,1,0:T(8,128)(2,1)S(1)} %get-tuple-element.46), channel_id=1, source_target_pairs={{0,192},{16,208},{32,224},{48,240},{64,0},{80,16},{96,32},{112,48}... | collective-permute-start | bytes 1179656 | tf_op jit(solution)/shard_map/ppermute | solution.py:401
  25.8 0.0 collective-permute-start.3
  25.8 8.1 %collective-permute-done.4.back_ref = bf16[2,96,1024]{2,1,0:T(8,128)(2,1)S(1)} collective-permute-done((bf16[2,96,1024]{2,1,0:T(8,128)(2,1)S(1)}, bf16[2,96,1024]{2,1,0:T(8,128)(2,1)S(1)}, u32[]{:S(2)}, u32[]{:S(2)}) %collective-permute-start.4) | collective-permute-done | bytes 393248 | tf_op jit(solution)/shard_map/ppermute | solution.py:401
  34.0 3.1 %collective-permute-done.3.near_ref = bf16[2,96,1024]{2,1,0:T(8,128)(2,1)S(1)} collective-permute-done((bf16[2,96,1024]{2,1,0:T(8,128)(2,1)S(1)}, bf16[2,96,1024]{2,1,0:T(8,128)(2,1)S(1)}, u32[]{:S(2)}, u32[]{:S(2)}) %collective-permute-start.3) | collective-permute-done | bytes 393248 | tf_op jit(solution)/shard_map/ppermute | solution.py:401
  37.1 5.2 %all-to-all-done.own_ref = bf16[16,192,128]{2,1,0:T(8,128)(2,1)S(1)} async-done(((bf16[16,192,128]{2,1,0:T(8,128)(2,1)}), bf16[16,192,128]{2,1,0:T(8,128)(2,1)S(1)}, u32[]{:S(2)}, u32[]{:S(2)}) %all-to-all-start) | async-done | bytes 786464 | tf_op jit(solution)/shard_map/all_to_all | solution.py:403
  42.3 2.2 %collective-permute-start.5 = (bf16[16,96,128]{2,1,0:T(8,128)(2,1)S(1)}, bf16[16,96,128]{2,1,0:T(8,128)(2,1)S(1)}, u32[]{:S(2)}, u32[]{:S(2)}) collective-permute-start(bf16[16,96,128]{2,1,0:T(8,128)(2,1)S(1)} %slice.11), channel_id=1, source_target_pairs={{0,16},{16,0},{32,48},{48,32},{64,80},{80,64},{96,112},{112,96},{1... | collective-permute-start | bytes 1179656 | tf_op jit(solution)/shard_map/ppermute | solution.py:405
  44.5 1.3 collective-permute-done.5.other_ref
  45.9 10.3 %attend.1 = (bf16[16,96,128]{2,1,0:T(8,128)(2,1)S(1)}, f32[16,96,128]{2,1,0:T(8,128)S(1)}, bf16[16,96,128]{2,1,0:T(8,128)(2,1)S(1)}) custom-call(s32[1]{0:T(128)} %bitcast.core_ref, s32[4]{0:T(128)S(1)} %fusion.tiles_ref, bf16[16,192,128]{2,1,0:T(8,128)(2,1)S(1)} %all-to-all-done.own_ref, bf16[16,96,128]{2,1,0:T(8,128)(2,1)S(1)} %collective-permute-done.5.other_ref), custom_call_target="tpu_custom_call" | custom-call | flops 12000000000 | bytes 4194304 | tf_op jit(solution)/shard_map/attend/pallas_call | solution.py:197
  56.1 0.1 collective-permute-start.6
  56.2 1.7 %collective-permute-done.6 = bf16[16,96,128]{2,1,0:T(8,128)(2,1)S(1)} collective-permute-done((bf16[16,96,128]{2,1,0:T(8,128)(2,1)S(1)}, bf16[16,96,128]{2,1,0:T(8,128)(2,1)S(1)}, u32[]{:S(2)}, u32[]{:S(2)}) %collective-permute-start.6) | collective-permute-done | bytes 393248 | tf_op jit(solution)/shard_map/ppermute | solution.py:408
  57.9 0.1 add_convert_fusion.1
  58.0 1.0 pad_maximum_fusion
  59.0 4.6 %all-to-all-start.1 = ((bf16[16,192,128]{2,1,0:T(8,128)(2,1)}), bf16[16,192,128]{2,1,0:T(8,128)(2,1)S(1)}, u32[]{:S(2)}, u32[]{:S(2)}) async-start(bf16[16,192,128]{2,1,0:T(8,128)(2,1)} %pad_maximum_fusion), calls=%async_computation.1 | async-start | bytes 1572864 | tf_op jit(solution)/shard_map/all_to_all | solution.py:410
  63.6 2.7 %collective-permute-start.7 = (bf16[2,96,1024]{2,1,0:T(8,128)(2,1)S(1)}, bf16[2,96,1024]{2,1,0:T(8,128)(2,1)S(1)}, u32[]{:S(2)}, u32[]{:S(2)}) collective-permute-start(bf16[2,96,1024]{2,1,0:T(8,128)(2,1)S(1)} %get-tuple-element.47), channel_id=1, source_target_pairs={{0,128},{16,144},{32,160},{48,176},{64,192},{80,208},{96,224},{112... | collective-permute-start | bytes 1179656 | tf_op jit(solution)/shard_map/ppermute | solution.py:401
  66.4 20.3 %all-to-all-done.1 = bf16[16,192,128]{2,1,0:T(8,128)(2,1)S(1)} async-done(((bf16[16,192,128]{2,1,0:T(8,128)(2,1)}), bf16[16,192,128]{2,1,0:T(8,128)(2,1)S(1)}, u32[]{:S(2)}, u32[]{:S(2)}) %all-to-all-start.1) | async-done | bytes 786464 | tf_op jit(solution)/shard_map/all_to_all | solution.py:410
  86.7 1.2 repack.1.grads_ref
  87.9 0.0 collective-permute-done.7.far_ref
  87.9 3.5 %all-to-all-start.2 = ((bf16[4,2,96,512]{3,2,1,0:T(8,128)(2,1)}), bf16[4,2,96,512]{3,2,1,0:T(8,128)(2,1)S(1)}, u32[]{:S(2)}, u32[]{:S(2)}) async-start(bf16[4,2,96,512]{3,2,1,0:T(8,128)(2,1)} %repack.1.grads_ref), calls=%async_computation.2 | async-start | bytes 1572864 | tf_op jit(solution)/shard_map/all_to_all | solution.py:413
  91.4 0.1 pad_add_fusion.place_ref
  91.5 9.6 %all-to-all-done.2.grads_ref = bf16[4,2,96,512]{3,2,1,0:T(8,128)(2,1)S(1)} async-done(((bf16[4,2,96,512]{3,2,1,0:T(8,128)(2,1)}), bf16[4,2,96,512]{3,2,1,0:T(8,128)(2,1)S(1)}, u32[]{:S(2)}, u32[]{:S(2)}) %all-to-all-start.2) | async-done | bytes 786464 | tf_op jit(solution)/shard_map/all_to_all | solution.py:413
  101.1 2.5 %weight_terms.1 = (bf16[16,64,256]{2,1,0:T(8,128)(2,1)S(1)}, bf16[16,64,256]{2,1,0:T(8,128)(2,1)S(1)}) custom-call(s32[2]{0:T(128)S(1)} %pad_add_fusion.place_ref, bf16[4,2,96,512]{3,2,1,0:T(8,128)(2,1)S(1)} %all-to-all-done.2.grads_ref, bf16[2,96,1024]{2,1,0:T(8,128)(2,1)S(1)} %get-tuple-element.45.own_ref, ...), custom_call_target="tpu_custom_call" | custom-call | tf_op jit(solution)/shard_map/weight_terms/pallas_call | solution.py:281
  103.6 3.6 %collective-permute-start.8 = (bf16[16,64,256]{2,1,0:T(8,128)(2,1)S(1)}, bf16[16,64,256]{2,1,0:T(8,128)(2,1)S(1)}, u32[]{:S(2)}, u32[]{:S(2)}) collective-permute-start(bf16[16,64,256]{2,1,0:T(8,128)(2,1)S(1)} %get-tuple-element.37), channel_id=1, source_target_pairs={{0,16},{16,0},{32,48},{48,32},{64,80},{80,64},{96,112},{112,96},{1... | collective-permute-start | bytes 1572872 | tf_op jit(solution)/shard_map/ppermute | solution.py:417
  107.2 1.5 %collective-permute-done.8 = bf16[16,64,256]{2,1,0:T(8,128)(2,1)S(1)} collective-permute-done((bf16[16,64,256]{2,1,0:T(8,128)(2,1)S(1)}, bf16[16,64,256]{2,1,0:T(8,128)(2,1)S(1)}, u32[]{:S(2)}, u32[]{:S(2)}) %collective-permute-start.8) | collective-permute-done | bytes 524320 | tf_op jit(solution)/shard_map/ppermute | solution.py:417
  108.7 1.0 add_convert_fusion
  109.7 4.3 %all-to-all-start.3 = ((bf16[16,64,256]{2,1,0:T(8,128)(2,1)}), bf16[16,64,256]{2,1,0:T(8,128)(2,1)S(1)}, u32[]{:S(2)}, u32[]{:S(2)}) async-start(bf16[16,64,256]{2,1,0:T(8,128)(2,1)} %add_convert_fusion), calls=%async_computation.3 | async-start | bytes 1048576 | tf_op jit(solution)/shard_map/all_to_all | solution.py:420
  114.1 1.0 dynamic-slice_bitcast_fusion
  115.1 0.7 collective-permute-start.9
  115.9 0.1 pad_add_fusion.2.place_ref
  115.9 1.3 collective-permute-done.9.arrived_ref
  117.2 2.2 %copy-done = bf16[4,1024,512]{2,1,0:T(8,128)(2,1)S(1)} copy-done((bf16[4,1024,512]{2,1,0:T(8,128)(2,1)S(1)}, bf16[4,1024,512]{2,1,0:T(8,128)(2,1)}, u32[]{:S(2)}) %copy-start) | copy-done | bytes 4194328
  119.4 4.7 %outputs.1 = (bf16[2,96,1024]{2,1,0:T(8,128)(2,1)}, bf16[2,96,1024]{2,1,0:T(8,128)(2,1)}) custom-call(s32[2]{0:T(128)S(1)} %pad_add_fusion.2.place_ref, bf16[4,2,96,512]{3,2,1,0:T(8,128)(2,1)} %repack.1.grads_ref, bf16[4,96,512]{2,1,0:T(8,128)(2,1)S(1)} %collective-permute-done.9.arrived_ref, bf16[4,1024,512]{2,1,0:T(8,128)(2,1)S(1)} %copy-done), custom_call_target="tpu_custom_call" | custom-call | flops 805306368 | bytes 7340032 | tf_op jit(solution)/shard_map/outputs/pallas_call | solution.py:347
  124.1 5.4 %all-to-all-done.3 = bf16[16,64,256]{2,1,0:T(8,128)(2,1)S(1)} async-done(((bf16[16,64,256]{2,1,0:T(8,128)(2,1)}), bf16[16,64,256]{2,1,0:T(8,128)(2,1)S(1)}, u32[]{:S(2)}, u32[]{:S(2)}) %all-to-all-start.3) | async-done | bytes 524320 | tf_op jit(solution)/shard_map/all_to_all | solution.py:420
  129.5 0.1 reduce_sum.12
  129.6 17.2 %all_to_all.25 = bf16[16,64,256]{2,1,0:T(8,128)(2,1)} all-to-all(bf16[16,64,256]{2,1,0:T(8,128)(2,1)S(1)} %broadcast_in_dim.8), channel_id=1, replica_groups=mesh['dp'=16,'ctx'=16] {'dp'}, dimensions={0} | all-to-all | bytes 1048576 | tf_op jit(solution)/shard_map/all_to_all | solution.py:428
  146.8 1.8 %spread.1 = bf16[4,64,512]{2,1,0:T(8,128)(2,1)} custom-call(bf16[4,2,2,64,256]{4,3,2,1,0:T(8,128)(2,1)} %bitcast.28), custom_call_target="tpu_custom_call" | custom-call | tf_op jit(solution)/shard_map/spread/pallas_call | solution.py:312
  (12 shorter events, 0.2 us)
Async XLA Ops:
  1.2 8.0 %copy-start.3 = (s32[1,4]{1,0:T(1,128)S(1)}, s32[1,4]{1,0:T(1,128)}, u32[]{:S(2)}) copy-start(s32[1,4]{1,0:T(1,128)} %param.5) | copy-start | bytes 52
  5.9 14.9 %copy-start.1 = (bf16[1,1,2,96,1024]{4,3,2,1,0:T(8,128)(2,1)S(1)}, bf16[1,1,2,96,1024]{4,3,2,1,0:T(8,128)(2,1)}, u32[]{:S(2)}) copy-start(bf16[1,1,2,96,1024]{4,3,2,1,0:T(8,128)(2,1)} %param.4) | copy-start | bytes 1179652
  5.9 14.9 %copy-start.2 = (bf16[1,1,2,96,1024]{4,3,2,1,0:T(8,128)(2,1)S(1)}, bf16[1,1,2,96,1024]{4,3,2,1,0:T(8,128)(2,1)}, u32[]{:S(2)}) copy-start(bf16[1,1,2,96,1024]{4,3,2,1,0:T(8,128)(2,1)} %param.7) | copy-start | bytes 1179652
  5.9 4.9 %collective-permute-start = (bf16[8,192,128]{2,1,0:T(8,128)(2,1)}, bf16[8,192,128]{2,1,0:T(8,128)(2,1)S(1)}, u32[]{:S(2)}, u32[]{:S(2)}) collective-permute-start(bf16[8,192,128]{2,1,0:T(8,128)(2,1)} %get-tuple-element.25), channel_id=1, source_target_pairs={{0,16},{16,0},{32,48},{48,32},{64,80},{80,64},{96,112},{112,96},{1... | collective-permute-start | bytes 1179656 | tf_op jit(solution)/shard_map/ppermute | solution.py:383
  9.3 2.4 %collective-permute-start.1 = (s32[1,4]{1,0:T(1,128)S(1)}, s32[1,4]{1,0:T(1,128)S(1)}, u32[]{:S(2)}, u32[]{:S(2)}) collective-permute-start(s32[1,4]{1,0:T(1,128)S(1)} %copy-done.3), channel_id=1, source_target_pairs={{0,16},{16,0},{32,48},{48,32},{64,80},{80,64},{96,112},{112,96},{1... | collective-permute-start | bytes 56 | tf_op jit(solution)/shard_map/ppermute | solution.py:378
  11.6 30.6 %all-to-all-start = ((bf16[16,192,128]{2,1,0:T(8,128)(2,1)}), bf16[16,192,128]{2,1,0:T(8,128)(2,1)S(1)}, u32[]{:S(2)}, u32[]{:S(2)}) async-start(bf16[16,192,128]{2,1,0:T(8,128)(2,1)} %bitcast.31), calls=%async_computation | async-start | bytes 1572864 | tf_op jit(solution)/shard_map/all_to_all | solution.py:403
  21.0 2.1 %collective-permute-start.2 = (bf16[2,96,1024]{2,1,0:T(8,128)(2,1)S(1)}, bf16[2,96,1024]{2,1,0:T(8,128)(2,1)S(1)}, u32[]{:S(2)}, u32[]{:S(2)}) collective-permute-start(bf16[2,96,1024]{2,1,0:T(8,128)(2,1)S(1)} %pad_maximum_fusion.1), channel_id=1, source_target_pairs={{0,16},{16,0},{32,48},{48,32},{64,80},{80,64},{96,112},{112,96},{1... | collective-permute-start | bytes 1179656 | tf_op jit(solution)/shard_map/ppermute | solution.py:389
  23.3 10.7 %collective-permute-start.4 = (bf16[2,96,1024]{2,1,0:T(8,128)(2,1)S(1)}, bf16[2,96,1024]{2,1,0:T(8,128)(2,1)S(1)}, u32[]{:S(2)}, u32[]{:S(2)}) collective-permute-start(bf16[2,96,1024]{2,1,0:T(8,128)(2,1)S(1)} %get-tuple-element.46), channel_id=1, source_target_pairs={{0,192},{16,208},{32,224},{48,240},{64,0},{80,16},{96,32},{112,48}... | collective-permute-start | bytes 1179656 | tf_op jit(solution)/shard_map/ppermute | solution.py:401
  25.8 11.2 %collective-permute-start.3 = (bf16[2,96,1024]{2,1,0:T(8,128)(2,1)S(1)}, bf16[2,96,1024]{2,1,0:T(8,128)(2,1)S(1)}, u32[]{:S(2)}, u32[]{:S(2)}) collective-permute-start(bf16[2,96,1024]{2,1,0:T(8,128)(2,1)S(1)} %broadcast_select_fusion.3), channel_id=1, source_target_pairs={{0,64},{16,80},{32,96},{48,112},{64,128},{80,144},{96,160},{112,17... | collective-permute-start | bytes 1179656 | tf_op jit(solution)/shard_map/ppermute | solution.py:401
  42.3 3.6 %collective-permute-start.5 = (bf16[16,96,128]{2,1,0:T(8,128)(2,1)S(1)}, bf16[16,96,128]{2,1,0:T(8,128)(2,1)S(1)}, u32[]{:S(2)}, u32[]{:S(2)}) collective-permute-start(bf16[16,96,128]{2,1,0:T(8,128)(2,1)S(1)} %slice.11), channel_id=1, source_target_pairs={{0,16},{16,0},{32,48},{48,32},{64,80},{80,64},{96,112},{112,96},{1... | collective-permute-start | bytes 1179656 | tf_op jit(solution)/shard_map/ppermute | solution.py:405
  56.1 1.8 %collective-permute-start.6 = (bf16[16,96,128]{2,1,0:T(8,128)(2,1)S(1)}, bf16[16,96,128]{2,1,0:T(8,128)(2,1)S(1)}, u32[]{:S(2)}, u32[]{:S(2)}) collective-permute-start(bf16[16,96,128]{2,1,0:T(8,128)(2,1)S(1)} %get-tuple-element.31), channel_id=1, source_target_pairs={{0,16},{16,0},{32,48},{48,32},{64,80},{80,64},{96,112},{112,96},{1... | collective-permute-start | bytes 1179656 | tf_op jit(solution)/shard_map/ppermute | solution.py:408
  59.0 27.7 %all-to-all-start.1 = ((bf16[16,192,128]{2,1,0:T(8,128)(2,1)}), bf16[16,192,128]{2,1,0:T(8,128)(2,1)S(1)}, u32[]{:S(2)}, u32[]{:S(2)}) async-start(bf16[16,192,128]{2,1,0:T(8,128)(2,1)} %pad_maximum_fusion), calls=%async_computation.1 | async-start | bytes 1572864 | tf_op jit(solution)/shard_map/all_to_all | solution.py:410
  63.6 24.3 %collective-permute-start.7 = (bf16[2,96,1024]{2,1,0:T(8,128)(2,1)S(1)}, bf16[2,96,1024]{2,1,0:T(8,128)(2,1)S(1)}, u32[]{:S(2)}, u32[]{:S(2)}) collective-permute-start(bf16[2,96,1024]{2,1,0:T(8,128)(2,1)S(1)} %get-tuple-element.47), channel_id=1, source_target_pairs={{0,128},{16,144},{32,160},{48,176},{64,192},{80,208},{96,224},{112... | collective-permute-start | bytes 1179656 | tf_op jit(solution)/shard_map/ppermute | solution.py:401
  87.9 13.2 %all-to-all-start.2 = ((bf16[4,2,96,512]{3,2,1,0:T(8,128)(2,1)}), bf16[4,2,96,512]{3,2,1,0:T(8,128)(2,1)S(1)}, u32[]{:S(2)}, u32[]{:S(2)}) async-start(bf16[4,2,96,512]{3,2,1,0:T(8,128)(2,1)} %repack.1.grads_ref), calls=%async_computation.2 | async-start | bytes 1572864 | tf_op jit(solution)/shard_map/all_to_all | solution.py:413
  103.6 5.2 %collective-permute-start.8 = (bf16[16,64,256]{2,1,0:T(8,128)(2,1)S(1)}, bf16[16,64,256]{2,1,0:T(8,128)(2,1)S(1)}, u32[]{:S(2)}, u32[]{:S(2)}) collective-permute-start(bf16[16,64,256]{2,1,0:T(8,128)(2,1)S(1)} %get-tuple-element.37), channel_id=1, source_target_pairs={{0,16},{16,0},{32,48},{48,32},{64,80},{80,64},{96,112},{112,96},{1... | collective-permute-start | bytes 1572872 | tf_op jit(solution)/shard_map/ppermute | solution.py:417
  109.7 19.7 %all-to-all-start.3 = ((bf16[16,64,256]{2,1,0:T(8,128)(2,1)}), bf16[16,64,256]{2,1,0:T(8,128)(2,1)S(1)}, u32[]{:S(2)}, u32[]{:S(2)}) async-start(bf16[16,64,256]{2,1,0:T(8,128)(2,1)} %add_convert_fusion), calls=%async_computation.3 | async-start | bytes 1048576 | tf_op jit(solution)/shard_map/all_to_all | solution.py:420
  115.1 2.1 %collective-permute-start.9 = (bf16[4,96,512]{2,1,0:T(8,128)(2,1)S(1)}, bf16[4,96,512]{2,1,0:T(8,128)(2,1)S(1)}, u32[]{:S(2)}, u32[]{:S(2)}) collective-permute-start(bf16[4,96,512]{2,1,0:T(8,128)(2,1)S(1)} %dynamic-slice_bitcast_fusion), channel_id=1, source_target_pairs={{0,16},{16,0},{32,48},{48,32},{64,80},{80,64},{96,112},{112,96},{1... | collective-permute-start | bytes 1179656 | tf_op jit(solution)/shard_map/ppermute | solution.py:421
  117.2 2.2 %copy-start = (bf16[4,1024,512]{2,1,0:T(8,128)(2,1)S(1)}, bf16[4,1024,512]{2,1,0:T(8,128)(2,1)}, u32[]{:S(2)}) copy-start(bf16[4,1024,512]{2,1,0:T(8,128)(2,1)} %weights_ref.3) | copy-start | bytes 12582916

commit v11 on v10

--- a/solution.py
+++ b/solution.py
@@ -19,7 +19,6 @@
 PROJECT_VMEM = 60 * 1024 * 1024
 
 CORE_SWAP = [(i, i ^ 1) for i in range(16)]
-CHIP_LINES = [[4 * x + rest for x in range(4)] for rest in range(4)]
 X_SHIFTS = [[(i, (i + 4 * shift) % 16) for i in range(16)] for shift in range(1, 4)]
 
 
@@ -217,7 +216,7 @@
     )(core, tiles, own, other_keys)
 
 
-def repack_kernel(back_ref, out_ref):
+def repack_kernel(column_ref, back_ref, out_ref, *shift_refs):
     low = low_lanes(SPAN)
     for sequence in range(2):
         for half, (lower, upper) in enumerate(((0, 3), (1, 2))):
@@ -232,40 +231,37 @@
                 out_ref[upper, sequence, :, columns] = jnp.where(
                     low, pltpu.roll(one, HEAD, 1), two
                 ).astype(jnp.bfloat16)
-
-
-def repack(back):
+    for shift, ref in enumerate(shift_refs):
+        ref[...] = out_ref[jnp.bitwise_and(column_ref[0] + shift, 3)]
+
+
+def repack(column, back):
     vmem = pl.BlockSpec(memory_space=pltpu.VMEM)
     return pl.pallas_call(
         repack_kernel,
-        out_shape=jax.ShapeDtypeStruct((4, 2, SPAN, HQ), jnp.bfloat16),
-        in_specs=[vmem],
-        out_specs=vmem,
+        out_shape=(
+            jax.ShapeDtypeStruct((4, 2, SPAN, HQ), jnp.bfloat16),
+            *[jax.ShapeDtypeStruct((2, SPAN, HQ), jnp.bfloat16)] * 4,
+        ),
+        in_specs=[pl.BlockSpec(memory_space=pltpu.SMEM), vmem],
+        out_specs=(vmem,) * 5,
         compiler_params=pltpu.CompilerParams(vmem_limit_bytes=SMALL_VMEM),
         name="repack",
-    )(back)
-
-
-def weight_kernel(
-    place_ref, grads_ref, own_ref, near_ref, far_ref, back_ref, keep_ref, give_ref, held_ref
-):
-    core, column = place_ref[0], place_ref[1]
+    )(column, back)
+
+
+def weight_kernel(core_ref, *refs):
+    grad_refs, line_refs, (keep_ref, give_ref, held_ref) = refs[:4], refs[4:8], refs[8:]
+    core = core_ref[0]
 
     @pl.when(pl.program_id(0) == 0)
     def _():
         for shift in range(4):
-            chip = jnp.bitwise_and(column + 4 - shift, 3)
             for part in range(2):
                 first = (2 * shift + part) * SPAN
-                held_ref[first : first + SPAN, :] = grads_ref[chip, jnp.bitwise_xor(core, part)]
-
-    rows = jnp.concatenate(
-        [
-            ref[...].reshape(2 * SPAN, D // 4)
-            for ref in (own_ref, near_ref, far_ref, back_ref)
-        ],
-        axis=0,
-    )
+                held_ref[first : first + SPAN, :] = grad_refs[shift][jnp.bitwise_xor(core, part)]
+
+    rows = jnp.concatenate([ref[...].reshape(2 * SPAN, D // 4) for ref in line_refs], axis=0)
     result = lax.dot_general(
         rows, held_ref[...], (((0,), (0,)), ((), ())), preferred_element_type=jnp.float32
     )
@@ -274,10 +270,11 @@
     give_ref[...] = jnp.where(core == 0, one, zero).astype(jnp.bfloat16).reshape(4, 64, 256)
 
 
-def weight_terms(place, grads, lines):
+def weight_terms(core, grads, lines):
     shape = jax.ShapeDtypeStruct((RANKS, 64, 256), jnp.bfloat16)
-    line_spec = pl.BlockSpec((2, SPAN, D // 4), lambda j, place: (0, 0, j))
-    out_spec = pl.BlockSpec((4, 64, 256), lambda j, place: (j, 0, 0))
+    grad_spec = pl.BlockSpec((2, SPAN, HQ), lambda j, core: (0, 0, 0))
+    line_spec = pl.BlockSpec((2, SPAN, D // 4), lambda j, core: (0, 0, j))
+    out_spec = pl.BlockSpec((4, 64, 256), lambda j, core: (j, 0, 0))
     return pl.pallas_call(
         weight_kernel,
         out_shape=(shape, shape),
@@ -285,7 +282,7 @@
             num_scalar_prefetch=1,
             grid=(4,),
             in_specs=[
-                pl.BlockSpec((4, 2, SPAN, HQ), lambda j, place: (0, 0, 0, 0)),
+                *[grad_spec] * 4,
                 *[line_spec] * 4,
             ],
             out_specs=(out_spec, out_spec),
@@ -293,7 +290,7 @@
         ),
         compiler_params=pltpu.CompilerParams(vmem_limit_bytes=SMALL_VMEM),
         name="weight_terms",
-    )(place, grads, *lines)
+    )(core, *grads, *lines)
 
 
 def spread_kernel(parts_ref, out_ref):
@@ -408,12 +405,12 @@
     arrived = lax.ppermute(other_grad, "dp", CORE_SWAP)
     key_part = (own_grad + arrived.astype(jnp.float32)).astype(jnp.bfloat16)
     back = lax.all_to_all(jnp.concatenate([query_part, key_part], axis=1), "ctx", 0, 0)
-    grads = repack(back.reshape(HEADS, 2, 2 * SPAN, 128))
-    grads, far = lax.optimization_barrier((grads, far))
-    line_grads = lax.all_to_all(grads, "dp", 0, 0, axis_index_groups=CHIP_LINES)
-    keep, give = weight_terms(
-        jnp.stack([core, column]).astype(jnp.int32), line_grads, (line, near, far, back_near)
-    )
+    grads, *pieces = repack(
+        column.astype(jnp.int32).reshape(1), back.reshape(HEADS, 2, 2 * SPAN, 128)
+    )
+    pieces, far = lax.optimization_barrier((pieces, far))
+    pieces = [pieces[0]] + [lax.ppermute(x, "dp", y) for x, y in zip(pieces[1:], X_SHIFTS)]
+    keep, give = weight_terms(core_number, pieces, (line, near, far, back_near))
     given = lax.ppermute(give, "dp", CORE_SWAP)
     terms = (keep.astype(jnp.float32) + given.astype(jnp.float32)).astype(jnp.bfloat16)
     terms, own_grads = lax.optimization_barrier((terms, grads))

time: 149 us -> 146 us (0.980)
  starting transfers between devices: 37.8 us -> 41.9 us
  Pallas kernels: 25.2 us -> 22.7 us
  waiting for transfers between devices: 60.4 us -> 58.3 us
  blocking collectives: 17.2 us -> 15.6 us
    all_to_all x1 -> x0, waiting for transfers between devices: 9.59 us -> none  [per_device(): line_grads = lax.all_to_all(grads, 'dp', 0, 0, axis_index_groups=CHIP_LINES)]
    ppermute x0 -> x3, starting transfers between devices: none -> 7.42 us  [per_device(): lax.ppermute(x, 'dp', y)]
    ppermute x0 -> x3, waiting for transfers between devices: none -> 6.86 us  [per_device(): lax.ppermute(x, 'dp', y)]
    all_to_all x1, waiting for transfers between devices: 5.36 us -> 9.29 us  [per_device(): terms = lax.all_to_all(terms, 'ctx', 0, 0)]
    all_to_all x1 -> x0, starting transfers between devices: 3.49 us -> none  [per_device(): line_grads = lax.all_to_all(grads, 'dp', 0, 0, axis_index_groups=CHIP_LINES)]
    all_to_all x1, waiting for transfers between devices: 20.3 us -> 17.1 us  [per_device(): lax.all_to_all(jnp.concatenate([query_part, key_part], axis=1), 'ctx', 0, 0)]
    all_to_all x1, blocking collectives: 17.2 us -> 15.6 us  [per_device(): parts = lax.all_to_all(jnp.broadcast_to(rows, (16, 64, 256)), 'dp', 0, 0)]
  transfers between devices with their start and end apart: 14 -> 16, of which waited for: 12 -> 13; matrix products, arithmetic and copies ran while one was open for 2% -> 1% of each run, Pallas kernels for 4% -> 3%
where the time goes in v11:
time: 146 us
  waiting for transfers between devices  58.3 us (40%)
  starting transfers between devices  41.9 us (29%)
  Pallas kernels  22.7 us (16%)
  blocking collectives  15.6 us (11%)
  local copies, waits for them, and re-layouts  3.23 us (2%)
  other arithmetic  2.95 us (2%)
    all_to_all x1, waiting for transfers between devices, per_device(): lax.all_to_all(jnp.concatenate([query_part, key_part], axis=1), 'ctx', 0, 0)  17.1 us
    all_to_all x1, blocking collectives, per_device(): parts = lax.all_to_all(jnp.broadcast_to(rows, (16, 64, 256)), 'dp', 0, 0)  15.6 us
    ppermute x3, waiting for transfers between devices, per_device(): lax.ppermute(rows, 'dp', shift)  11.2 us
    pallas_call x1, Pallas kernels, attend(): pl.pallas_call(attend_kernel, out_shape=(jax.ShapeDtypeStruct(block, jnp....  10 us
    all_to_all x1, waiting for transfers between devices, per_device(): terms = lax.all_to_all(terms, 'ctx', 0, 0)  9.29 us
    all_to_all x1, starting transfers between devices, per_device(): own = lax.all_to_all(packed, 'ctx', 0, 0)  9.19 us
    ppermute x3, starting transfers between devices, per_device(): lax.ppermute(x, 'dp', y)  7.42 us
    ppermute x3, waiting for transfers between devices, per_device(): lax.ppermute(x, 'dp', y)  6.86 us
  transfers between devices with their start and end apart: 16, of which 13 were waited for; matrix products, arithmetic and copies ran while one was open for 1% of the time, Pallas kernels for 3%

profile of v11, /device:TPU:1, one launch (start us, length us, event | category | flops | bytes accessed | tf_op | source)
XLA Modules:
  0.0 145.5 jit_solution(4599028078829495713)
XLA Ops:
  0.7 0.6 pad_add_fusion.place_ref
  1.2 4.7 %project.1 = (bf16[8,2,192,128]{3,2,1,0:T(8,128)(2,1)}, bf16[8,192,128]{2,1,0:T(8,128)(2,1)}) custom-call(s32[2]{0:T(128)} %pad_add_fusion.place_ref, bf16[2,96,1024]{2,1,0:T(8,128)(2,1)} %bitcast.29, bf16[2,96,1024]{2,1,0:T(8,128)(2,1)} %bitcast.30, bf16[4,1024,512]{2,1,0:T(8,128)(2,1)} %weights_ref.3), custom_call_target="tpu_custom_call" | custom-call | tf_op jit(solution)/shard_map/project/pallas_call | solution.py:57
  5.9 3.3 %collective-permute-start = (bf16[8,192,128]{2,1,0:T(8,128)(2,1)}, bf16[8,192,128]{2,1,0:T(8,128)(2,1)S(1)}, u32[]{:S(2)}, u32[]{:S(2)}) collective-permute-start(bf16[8,192,128]{2,1,0:T(8,128)(2,1)} %get-tuple-element.33), channel_id=1, source_target_pairs={{0,16},{16,0},{32,48},{48,32},{64,80},{80,64},{96,112},{112,96},{1... | collective-permute-start | bytes 1179656 | tf_op jit(solution)/shard_map/ppermute | solution.py:380
  9.3 0.1 collective-permute-start.1
  9.4 1.4 collective-permute-done
  10.8 0.8 bitcast_dynamic-update-slice_fusion
  11.7 0.0 collective-permute-done.1
  11.7 9.2 %all-to-all-start = ((bf16[16,192,128]{2,1,0:T(8,128)(2,1)}), bf16[16,192,128]{2,1,0:T(8,128)(2,1)S(1)}, u32[]{:S(2)}, u32[]{:S(2)}) async-start(bf16[16,192,128]{2,1,0:T(8,128)(2,1)} %bitcast.31), calls=%async_computation | async-start | bytes 1572864 | tf_op jit(solution)/shard_map/all_to_all | solution.py:400
  20.9 0.1 dynamic-slice_bitcast_fusion.1
  21.0 0.7 collective-permute-start.2
  21.7 1.3 collective-permute-done.2
  23.1 0.1 broadcast_select_fusion.3
  23.2 0.1 broadcast_select_fusion
  23.3 2.6 %collective-permute-start.4 = (bf16[2,96,1024]{2,1,0:T(8,128)(2,1)S(1)}, bf16[2,96,1024]{2,1,0:T(8,128)(2,1)S(1)}, u32[]{:S(2)}, u32[]{:S(2)}) collective-permute-start(bf16[2,96,1024]{2,1,0:T(8,128)(2,1)S(1)} %get-tuple-element.62), channel_id=1, source_target_pairs={{0,192},{16,208},{32,224},{48,240},{64,0},{80,16},{96,32},{112,48}... | collective-permute-start | bytes 1179656 | tf_op jit(solution)/shard_map/ppermute | solution.py:398
  25.8 0.0 collective-permute-start.3
  25.8 8.1 %collective-permute-done.4.refs_7_ = bf16[2,96,1024]{2,1,0:T(8,128)(2,1)S(1)} collective-permute-done((bf16[2,96,1024]{2,1,0:T(8,128)(2,1)S(1)}, bf16[2,96,1024]{2,1,0:T(8,128)(2,1)S(1)}, u32[]{:S(2)}, u32[]{:S(2)}) %collective-permute-start.4) | collective-permute-done | bytes 393248 | tf_op jit(solution)/shard_map/ppermute | solution.py:398
  34.0 3.1 %collective-permute-done.3.refs_5_ = bf16[2,96,1024]{2,1,0:T(8,128)(2,1)S(1)} collective-permute-done((bf16[2,96,1024]{2,1,0:T(8,128)(2,1)S(1)}, bf16[2,96,1024]{2,1,0:T(8,128)(2,1)S(1)}, u32[]{:S(2)}, u32[]{:S(2)}) %collective-permute-start.3) | collective-permute-done | bytes 393248 | tf_op jit(solution)/shard_map/ppermute | solution.py:398
  37.1 5.2 %all-to-all-done.own_ref = bf16[16,192,128]{2,1,0:T(8,128)(2,1)S(1)} async-done(((bf16[16,192,128]{2,1,0:T(8,128)(2,1)}), bf16[16,192,128]{2,1,0:T(8,128)(2,1)S(1)}, u32[]{:S(2)}, u32[]{:S(2)}) %all-to-all-start) | async-done | bytes 786464 | tf_op jit(solution)/shard_map/all_to_all | solution.py:400
  42.3 2.2 %collective-permute-start.5 = (bf16[16,96,128]{2,1,0:T(8,128)(2,1)S(1)}, bf16[16,96,128]{2,1,0:T(8,128)(2,1)S(1)}, u32[]{:S(2)}, u32[]{:S(2)}) collective-permute-start(bf16[16,96,128]{2,1,0:T(8,128)(2,1)S(1)} %slice.11), channel_id=1, source_target_pairs={{0,16},{16,0},{32,48},{48,32},{64,80},{80,64},{96,112},{112,96},{1... | collective-permute-start | bytes 1179656 | tf_op jit(solution)/shard_map/ppermute | solution.py:402
  44.5 1.3 collective-permute-done.5.other_ref
  45.9 10.0 %attend.1 = (bf16[16,96,128]{2,1,0:T(8,128)(2,1)S(1)}, f32[16,96,128]{2,1,0:T(8,128)S(1)}, bf16[16,96,128]{2,1,0:T(8,128)(2,1)S(1)}) custom-call(s32[1]{0:T(128)} %bitcast.core_ref, s32[4]{0:T(128)S(1)} %fusion.tiles_ref, bf16[16,192,128]{2,1,0:T(8,128)(2,1)S(1)} %all-to-all-done.own_ref, bf16[16,96,128]{2,1,0:T(8,128)(2,1)S(1)} %collective-permute-done.5.other_ref), custom_call_target="tpu_custom_call" | custom-call | flops 12000000000 | bytes 4194304 | tf_op jit(solution)/shard_map/attend/pallas_call | solution.py:196
  55.9 0.2 collective-permute-start.6
  56.1 1.6 %collective-permute-done.6 = bf16[16,96,128]{2,1,0:T(8,128)(2,1)S(1)} collective-permute-done((bf16[16,96,128]{2,1,0:T(8,128)(2,1)S(1)}, bf16[16,96,128]{2,1,0:T(8,128)(2,1)S(1)}, u32[]{:S(2)}, u32[]{:S(2)}) %collective-permute-start.6) | collective-permute-done | bytes 393248 | tf_op jit(solution)/shard_map/ppermute | solution.py:405
  57.7 0.1 add_convert_fusion.1
  57.8 1.0 pad_maximum_fusion
  58.8 4.7 %all-to-all-start.1 = ((bf16[16,192,128]{2,1,0:T(8,128)(2,1)}), bf16[16,192,128]{2,1,0:T(8,128)(2,1)S(1)}, u32[]{:S(2)}, u32[]{:S(2)}) async-start(bf16[16,192,128]{2,1,0:T(8,128)(2,1)} %pad_maximum_fusion), calls=%async_computation.1 | async-start | bytes 1572864 | tf_op jit(solution)/shard_map/all_to_all | solution.py:407
  63.5 3.2 %collective-permute-start.7 = (bf16[2,96,1024]{2,1,0:T(8,128)(2,1)S(1)}, bf16[2,96,1024]{2,1,0:T(8,128)(2,1)S(1)}, u32[]{:S(2)}, u32[]{:S(2)}) collective-permute-start(bf16[2,96,1024]{2,1,0:T(8,128)(2,1)S(1)} %get-tuple-element.63), channel_id=1, source_target_pairs={{0,128},{16,144},{32,160},{48,176},{64,192},{80,208},{96,224},{112... | collective-permute-start | bytes 1179656 | tf_op jit(solution)/shard_map/ppermute | solution.py:398
  66.6 17.1 %all-to-all-done.1 = bf16[16,192,128]{2,1,0:T(8,128)(2,1)S(1)} async-done(((bf16[16,192,128]{2,1,0:T(8,128)(2,1)}), bf16[16,192,128]{2,1,0:T(8,128)(2,1)S(1)}, u32[]{:S(2)}, u32[]{:S(2)}) %all-to-all-start.1) | async-done | bytes 786464 | tf_op jit(solution)/shard_map/all_to_all | solution.py:407
  83.8 0.4 repack.1
  84.2 0.0 collective-permute-done.7.refs_6_
  84.2 3.4 %collective-permute-start.8 = (bf16[2,96,512]{2,1,0:T(8,128)(2,1)S(1)}, bf16[2,96,512]{2,1,0:T(8,128)(2,1)S(1)}, u32[]{:S(2)}, u32[]{:S(2)}) collective-permute-start(bf16[2,96,512]{2,1,0:T(8,128)(2,1)S(1)} %get-tuple-element.45), channel_id=1, source_target_pairs={{0,64},{16,80},{32,96},{48,112},{64,128},{80,144},{96,160},{112,17... | collective-permute-start | bytes 589832 | tf_op jit(solution)/shard_map/ppermute | solution.py:412
  87.6 4.0 %collective-permute-start.9 = (bf16[2,96,512]{2,1,0:T(8,128)(2,1)S(1)}, bf16[2,96,512]{2,1,0:T(8,128)(2,1)S(1)}, u32[]{:S(2)}, u32[]{:S(2)}) collective-permute-start(bf16[2,96,512]{2,1,0:T(8,128)(2,1)S(1)} %get-tuple-element.46), channel_id=1, source_target_pairs={{0,128},{16,144},{32,160},{48,176},{64,192},{80,208},{96,224},{112... | collective-permute-start | bytes 589832 | tf_op jit(solution)/shard_map/ppermute | solution.py:412
  91.6 1.9 %collective-permute-done.8.refs_1_ = bf16[2,96,512]{2,1,0:T(8,128)(2,1)S(1)} collective-permute-done((bf16[2,96,512]{2,1,0:T(8,128)(2,1)S(1)}, bf16[2,96,512]{2,1,0:T(8,128)(2,1)S(1)}, u32[]{:S(2)}, u32[]{:S(2)}) %collective-permute-start.8) | collective-permute-done | bytes 196640 | tf_op jit(solution)/shard_map/ppermute | solution.py:412
  93.5 5.0 %collective-permute-done.9.refs_2_ = bf16[2,96,512]{2,1,0:T(8,128)(2,1)S(1)} collective-permute-done((bf16[2,96,512]{2,1,0:T(8,128)(2,1)S(1)}, bf16[2,96,512]{2,1,0:T(8,128)(2,1)S(1)}, u32[]{:S(2)}, u32[]{:S(2)}) %collective-permute-start.9) | collective-permute-done | bytes 196640 | tf_op jit(solution)/shard_map/ppermute | solution.py:412
  98.5 1.9 %weight_terms.1 = (bf16[16,64,256]{2,1,0:T(8,128)(2,1)S(1)}, bf16[16,64,256]{2,1,0:T(8,128)(2,1)S(1)}) custom-call(s32[1]{0:T(128)} %bitcast.core_ref, bf16[2,96,512]{2,1,0:T(8,128)(2,1)S(1)} %get-tuple-element.44.refs_0_, bf16[2,96,512]{2,1,0:T(8,128)(2,1)S(1)} %collective-permute-done.8.refs_1_, bf16[2,96,512]{2,1,0:T(8,128)(2,1)S(1)} %collective-permute-done.9.refs_2_, ...), custom_call_target="tpu_custom_call" | custom-call | tf_op jit(solution)/shard_map/weight_terms/pallas_call | solution.py:278
  100.4 3.3 %collective-permute-start.11 = (bf16[16,64,256]{2,1,0:T(8,128)(2,1)S(1)}, bf16[16,64,256]{2,1,0:T(8,128)(2,1)S(1)}, u32[]{:S(2)}, u32[]{:S(2)}) collective-permute-start(bf16[16,64,256]{2,1,0:T(8,128)(2,1)S(1)} %get-tuple-element.52), channel_id=1, source_target_pairs={{0,16},{16,0},{32,48},{48,32},{64,80},{80,64},{96,112},{112,96},{1... | collective-permute-start | bytes 1572872 | tf_op jit(solution)/shard_map/ppermute | solution.py:414
  103.7 1.5 %collective-permute-done.11 = bf16[16,64,256]{2,1,0:T(8,128)(2,1)S(1)} collective-permute-done((bf16[16,64,256]{2,1,0:T(8,128)(2,1)S(1)}, bf16[16,64,256]{2,1,0:T(8,128)(2,1)S(1)}, u32[]{:S(2)}, u32[]{:S(2)}) %collective-permute-start.11) | collective-permute-done | bytes 524320 | tf_op jit(solution)/shard_map/ppermute | solution.py:414
  105.3 1.0 add_convert_fusion
  106.2 4.3 %all-to-all-start.2 = ((bf16[16,64,256]{2,1,0:T(8,128)(2,1)}), bf16[16,64,256]{2,1,0:T(8,128)(2,1)S(1)}, u32[]{:S(2)}, u32[]{:S(2)}) async-start(bf16[16,64,256]{2,1,0:T(8,128)(2,1)} %add_convert_fusion), calls=%async_computation.2 | async-start | bytes 1048576 | tf_op jit(solution)/shard_map/all_to_all | solution.py:417
  110.5 0.7 collective-permute-start.12
  111.3 0.1 pad_add_fusion.1.place_ref
  111.3 1.3 collective-permute-done.12.arrived_ref
  112.6 2.2 %copy-done = bf16[4,1024,512]{2,1,0:T(8,128)(2,1)S(1)} copy-done((bf16[4,1024,512]{2,1,0:T(8,128)(2,1)S(1)}, bf16[4,1024,512]{2,1,0:T(8,128)(2,1)}, u32[]{:S(2)}) %copy-start) | copy-done | bytes 4194328
  114.8 3.8 %outputs.1 = (bf16[2,96,1024]{2,1,0:T(8,128)(2,1)}, bf16[2,96,1024]{2,1,0:T(8,128)(2,1)}) custom-call(s32[2]{0:T(128)S(1)} %pad_add_fusion.1.place_ref, bf16[4,2,96,512]{3,2,1,0:T(8,128)(2,1)S(1)} %get-tuple-element.55.grads_ref, bf16[4,96,512]{2,1,0:T(8,128)(2,1)S(1)} %collective-permute-done.12.arrived_ref, bf16[4,1024,512]{2,1,0:T(8,128)(2,1)S(1)} %copy-done), custom_call_target="tpu_custom_call" | custom-call | flops 805306368 | bytes 7340032 | tf_op jit(solution)/shard_map/outputs/pallas_call | solution.py:344
  118.6 9.3 %all-to-all-done.2 = bf16[16,64,256]{2,1,0:T(8,128)(2,1)S(1)} async-done(((bf16[16,64,256]{2,1,0:T(8,128)(2,1)}), bf16[16,64,256]{2,1,0:T(8,128)(2,1)S(1)}, u32[]{:S(2)}, u32[]{:S(2)}) %all-to-all-start.2) | async-done | bytes 524320 | tf_op jit(solution)/shard_map/all_to_all | solution.py:417
  127.9 0.1 reduce_sum.12
  128.0 15.6 %all_to_all.20 = bf16[16,64,256]{2,1,0:T(8,128)(2,1)} all-to-all(bf16[16,64,256]{2,1,0:T(8,128)(2,1)S(1)} %broadcast_in_dim.8), channel_id=1, replica_groups=mesh['dp'=16,'ctx'=16] {'dp'}, dimensions={0} | all-to-all | bytes 1048576 | tf_op jit(solution)/shard_map/all_to_all | solution.py:425
  143.7 1.8 %spread.1 = bf16[4,64,512]{2,1,0:T(8,128)(2,1)} custom-call(bf16[4,2,2,64,256]{4,3,2,1,0:T(8,128)(2,1)} %bitcast.28), custom_call_target="tpu_custom_call" | custom-call | tf_op jit(solution)/shard_map/spread/pallas_call | solution.py:309
  (15 shorter events, 0.2 us)
Async XLA Ops:
  1.2 8.0 %copy-start.3 = (s32[1,4]{1,0:T(1,128)S(1)}, s32[1,4]{1,0:T(1,128)}, u32[]{:S(2)}) copy-start(s32[1,4]{1,0:T(1,128)} %param.5) | copy-start | bytes 52
  5.9 14.9 %copy-start.1 = (bf16[1,1,2,96,1024]{4,3,2,1,0:T(8,128)(2,1)S(1)}, bf16[1,1,2,96,1024]{4,3,2,1,0:T(8,128)(2,1)}, u32[]{:S(2)}) copy-start(bf16[1,1,2,96,1024]{4,3,2,1,0:T(8,128)(2,1)} %param.4) | copy-start | bytes 1179652
  5.9 14.9 %copy-start.2 = (bf16[1,1,2,96,1024]{4,3,2,1,0:T(8,128)(2,1)S(1)}, bf16[1,1,2,96,1024]{4,3,2,1,0:T(8,128)(2,1)}, u32[]{:S(2)}) copy-start(bf16[1,1,2,96,1024]{4,3,2,1,0:T(8,128)(2,1)} %param.7) | copy-start | bytes 1179652
  5.9 4.9 %collective-permute-start = (bf16[8,192,128]{2,1,0:T(8,128)(2,1)}, bf16[8,192,128]{2,1,0:T(8,128)(2,1)S(1)}, u32[]{:S(2)}, u32[]{:S(2)}) collective-permute-start(bf16[8,192,128]{2,1,0:T(8,128)(2,1)} %get-tuple-element.33), channel_id=1, source_target_pairs={{0,16},{16,0},{32,48},{48,32},{64,80},{80,64},{96,112},{112,96},{1... | collective-permute-start | bytes 1179656 | tf_op jit(solution)/shard_map/ppermute | solution.py:380
  9.3 2.4 %collective-permute-start.1 = (s32[1,4]{1,0:T(1,128)S(1)}, s32[1,4]{1,0:T(1,128)S(1)}, u32[]{:S(2)}, u32[]{:S(2)}) collective-permute-start(s32[1,4]{1,0:T(1,128)S(1)} %copy-done.3), channel_id=1, source_target_pairs={{0,16},{16,0},{32,48},{48,32},{64,80},{80,64},{96,112},{112,96},{1... | collective-permute-start | bytes 56 | tf_op jit(solution)/shard_map/ppermute | solution.py:375
  11.7 30.6 %all-to-all-start = ((bf16[16,192,128]{2,1,0:T(8,128)(2,1)}), bf16[16,192,128]{2,1,0:T(8,128)(2,1)S(1)}, u32[]{:S(2)}, u32[]{:S(2)}) async-start(bf16[16,192,128]{2,1,0:T(8,128)(2,1)} %bitcast.31), calls=%async_computation | async-start | bytes 1572864 | tf_op jit(solution)/shard_map/all_to_all | solution.py:400
  21.0 2.1 %collective-permute-start.2 = (bf16[2,96,1024]{2,1,0:T(8,128)(2,1)S(1)}, bf16[2,96,1024]{2,1,0:T(8,128)(2,1)S(1)}, u32[]{:S(2)}, u32[]{:S(2)}) collective-permute-start(bf16[2,96,1024]{2,1,0:T(8,128)(2,1)S(1)} %pad_maximum_fusion.1), channel_id=1, source_target_pairs={{0,16},{16,0},{32,48},{48,32},{64,80},{80,64},{96,112},{112,96},{1... | collective-permute-start | bytes 1179656 | tf_op jit(solution)/shard_map/ppermute | solution.py:386
  23.3 10.7 %collective-permute-start.4 = (bf16[2,96,1024]{2,1,0:T(8,128)(2,1)S(1)}, bf16[2,96,1024]{2,1,0:T(8,128)(2,1)S(1)}, u32[]{:S(2)}, u32[]{:S(2)}) collective-permute-start(bf16[2,96,1024]{2,1,0:T(8,128)(2,1)S(1)} %get-tuple-element.62), channel_id=1, source_target_pairs={{0,192},{16,208},{32,224},{48,240},{64,0},{80,16},{96,32},{112,48}... | collective-permute-start | bytes 1179656 | tf_op jit(solution)/shard_map/ppermute | solution.py:398
  25.8 11.2 %collective-permute-start.3 = (bf16[2,96,1024]{2,1,0:T(8,128)(2,1)S(1)}, bf16[2,96,1024]{2,1,0:T(8,128)(2,1)S(1)}, u32[]{:S(2)}, u32[]{:S(2)}) collective-permute-start(bf16[2,96,1024]{2,1,0:T(8,128)(2,1)S(1)} %broadcast_select_fusion.3), channel_id=1, source_target_pairs={{0,64},{16,80},{32,96},{48,112},{64,128},{80,144},{96,160},{112,17... | collective-permute-start | bytes 1179656 | tf_op jit(solution)/shard_map/ppermute | solution.py:398
  42.3 3.6 %collective-permute-start.5 = (bf16[16,96,128]{2,1,0:T(8,128)(2,1)S(1)}, bf16[16,96,128]{2,1,0:T(8,128)(2,1)S(1)}, u32[]{:S(2)}, u32[]{:S(2)}) collective-permute-start(bf16[16,96,128]{2,1,0:T(8,128)(2,1)S(1)} %slice.11), channel_id=1, source_target_pairs={{0,16},{16,0},{32,48},{48,32},{64,80},{80,64},{96,112},{112,96},{1... | collective-permute-start | bytes 1179656 | tf_op jit(solution)/shard_map/ppermute | solution.py:402
  55.9 1.8 %collective-permute-start.6 = (bf16[16,96,128]{2,1,0:T(8,128)(2,1)S(1)}, bf16[16,96,128]{2,1,0:T(8,128)(2,1)S(1)}, u32[]{:S(2)}, u32[]{:S(2)}) collective-permute-start(bf16[16,96,128]{2,1,0:T(8,128)(2,1)S(1)} %get-tuple-element.39), channel_id=1, source_target_pairs={{0,16},{16,0},{32,48},{48,32},{64,80},{80,64},{96,112},{112,96},{1... | collective-permute-start | bytes 1179656 | tf_op jit(solution)/shard_map/ppermute | solution.py:405
  58.8 25.0 %all-to-all-start.1 = ((bf16[16,192,128]{2,1,0:T(8,128)(2,1)}), bf16[16,192,128]{2,1,0:T(8,128)(2,1)S(1)}, u32[]{:S(2)}, u32[]{:S(2)}) async-start(bf16[16,192,128]{2,1,0:T(8,128)(2,1)} %pad_maximum_fusion), calls=%async_computation.1 | async-start | bytes 1572864 | tf_op jit(solution)/shard_map/all_to_all | solution.py:407
  63.5 20.7 %collective-permute-start.7 = (bf16[2,96,1024]{2,1,0:T(8,128)(2,1)S(1)}, bf16[2,96,1024]{2,1,0:T(8,128)(2,1)S(1)}, u32[]{:S(2)}, u32[]{:S(2)}) collective-permute-start(bf16[2,96,1024]{2,1,0:T(8,128)(2,1)S(1)} %get-tuple-element.63), channel_id=1, source_target_pairs={{0,128},{16,144},{32,160},{48,176},{64,192},{80,208},{96,224},{112... | collective-permute-start | bytes 1179656 | tf_op jit(solution)/shard_map/ppermute | solution.py:398
  84.2 9.3 %collective-permute-start.8 = (bf16[2,96,512]{2,1,0:T(8,128)(2,1)S(1)}, bf16[2,96,512]{2,1,0:T(8,128)(2,1)S(1)}, u32[]{:S(2)}, u32[]{:S(2)}) collective-permute-start(bf16[2,96,512]{2,1,0:T(8,128)(2,1)S(1)} %get-tuple-element.45), channel_id=1, source_target_pairs={{0,64},{16,80},{32,96},{48,112},{64,128},{80,144},{96,160},{112,17... | collective-permute-start | bytes 589832 | tf_op jit(solution)/shard_map/ppermute | solution.py:412
  87.6 10.9 %collective-permute-start.9 = (bf16[2,96,512]{2,1,0:T(8,128)(2,1)S(1)}, bf16[2,96,512]{2,1,0:T(8,128)(2,1)S(1)}, u32[]{:S(2)}, u32[]{:S(2)}) collective-permute-start(bf16[2,96,512]{2,1,0:T(8,128)(2,1)S(1)} %get-tuple-element.46), channel_id=1, source_target_pairs={{0,128},{16,144},{32,160},{48,176},{64,192},{80,208},{96,224},{112... | collective-permute-start | bytes 589832 | tf_op jit(solution)/shard_map/ppermute | solution.py:412
  91.6 6.9 %collective-permute-start.10 = (bf16[2,96,512]{2,1,0:T(8,128)(2,1)S(1)}, bf16[2,96,512]{2,1,0:T(8,128)(2,1)S(1)}, u32[]{:S(2)}, u32[]{:S(2)}) collective-permute-start(bf16[2,96,512]{2,1,0:T(8,128)(2,1)S(1)} %get-tuple-element.47), channel_id=1, source_target_pairs={{0,192},{16,208},{32,224},{48,240},{64,0},{80,16},{96,32},{112,48}... | collective-permute-start | bytes 589832 | tf_op jit(solution)/shard_map/ppermute | solution.py:412
  100.4 4.8 %collective-permute-start.11 = (bf16[16,64,256]{2,1,0:T(8,128)(2,1)S(1)}, bf16[16,64,256]{2,1,0:T(8,128)(2,1)S(1)}, u32[]{:S(2)}, u32[]{:S(2)}) collective-permute-start(bf16[16,64,256]{2,1,0:T(8,128)(2,1)S(1)} %get-tuple-element.52), channel_id=1, source_target_pairs={{0,16},{16,0},{32,48},{48,32},{64,80},{80,64},{96,112},{112,96},{1... | collective-permute-start | bytes 1572872 | tf_op jit(solution)/shard_map/ppermute | solution.py:414
  106.2 21.7 %all-to-all-start.2 = ((bf16[16,64,256]{2,1,0:T(8,128)(2,1)}), bf16[16,64,256]{2,1,0:T(8,128)(2,1)S(1)}, u32[]{:S(2)}, u32[]{:S(2)}) async-start(bf16[16,64,256]{2,1,0:T(8,128)(2,1)} %add_convert_fusion), calls=%async_computation.2 | async-start | bytes 1048576 | tf_op jit(solution)/shard_map/all_to_all | solution.py:417
  110.5 2.1 %collective-permute-start.12 = (bf16[4,96,512]{2,1,0:T(8,128)(2,1)S(1)}, bf16[4,96,512]{2,1,0:T(8,128)(2,1)S(1)}, u32[]{:S(2)}, u32[]{:S(2)}) collective-permute-start(bf16[4,96,512]{2,1,0:T(8,128)(2,1)S(1)} %dynamic-slice_bitcast_fusion), channel_id=1, source_target_pairs={{0,16},{16,0},{32,48},{48,32},{64,80},{80,64},{96,112},{112,96},{1... | collective-permute-start | bytes 1179656 | tf_op jit(solution)/shard_map/ppermute | solution.py:418
  112.6 2.2 %copy-start = (bf16[4,1024,512]{2,1,0:T(8,128)(2,1)S(1)}, bf16[4,1024,512]{2,1,0:T(8,128)(2,1)}, u32[]{:S(2)}) copy-start(bf16[4,1024,512]{2,1,0:T(8,128)(2,1)} %weights_ref.3) | copy-start | bytes 12582916

commit v12 on v11

--- a/solution.py
+++ b/solution.py
@@ -19,6 +19,7 @@
 PROJECT_VMEM = 60 * 1024 * 1024
 
 CORE_SWAP = [(i, i ^ 1) for i in range(16)]
+Z_SWAP = [(i, i ^ 2) for i in range(16)]
 X_SHIFTS = [[(i, (i + 4 * shift) % 16) for i in range(16)] for shift in range(1, 4)]
 
 
@@ -293,24 +294,22 @@
     )(core, *grads, *lines)
 
 
-def spread_kernel(parts_ref, out_ref):
-    factor = float(16 * RANKS * 2 * SPAN) ** -0.5
-    for column in range(4):
-        for core in range(2):
-            total = parts_ref[column, 0, core].astype(jnp.float32) + parts_ref[
-                column, 1, core
-            ].astype(jnp.float32)
-            out_ref[column, :, 256 * core : 256 * core + 256] = (total * factor).astype(
-                jnp.bfloat16
-            )
-
-
-def spread(parts):
-    return pl.pallas_call(
-        spread_kernel,
+def place_kernel(column_ref, *refs):
+    out_ref = refs[4]
+    for shift in range(4):
+        out_ref[jnp.bitwise_and(column_ref[0] + 4 - shift, 3)] = refs[shift][...]
+
+
+def place_weights(column, parts):
+    vmem = pl.BlockSpec(memory_space=pltpu.VMEM)
+    return pl.pallas_call(
+        place_kernel,
         out_shape=jax.ShapeDtypeStruct((4, 64, HQ), jnp.bfloat16),
-        name="spread",
-    )(parts)
+        in_specs=[pl.BlockSpec(memory_space=pltpu.SMEM), vmem, vmem, vmem, vmem],
+        out_specs=vmem,
+        compiler_params=pltpu.CompilerParams(vmem_limit_bytes=SMALL_VMEM),
+        name="place_weights",
+    )(column, *parts)
 
 
 def output_kernel(place_ref, grads_ref, arrived_ref, weights_ref, out_ref, input_grad_ref, held_ref):
@@ -421,9 +420,17 @@
     place = jnp.stack([core, odd]).astype(jnp.int32)
     attn_out, input_grad = outputs(place, own_grads, swapped, weights)
     terms, attn_out, input_grad = lax.optimization_barrier((terms, attn_out, input_grad))
-    rows = jnp.sum(terms.astype(jnp.float32), axis=0).astype(jnp.bfloat16)
-    parts = lax.all_to_all(jnp.broadcast_to(rows, (16, 64, 256)), "dp", 0, 0)
-    weight_grads = spread(parts.reshape(4, 2, 2, 64, 256))
+    rows = lax.reduce_precision(jnp.sum(terms.astype(jnp.float32), axis=0), 8, 7)
+    other_rows = lax.ppermute(rows.astype(jnp.bfloat16), "dp", Z_SWAP)
+    factor = float(16 * RANKS * 2 * SPAN) ** -0.5
+    total = ((rows + other_rows.astype(jnp.float32)) * factor).astype(jnp.bfloat16)
+    other_total = lax.ppermute(total, "dp", CORE_SWAP)
+    first = core == 0
+    part = jnp.concatenate(
+        [jnp.where(first, total, other_total), jnp.where(first, other_total, total)], axis=1
+    )
+    parts = [part] + [lax.ppermute(part, "dp", shift) for shift in X_SHIFTS]
+    weight_grads = place_weights(column.astype(jnp.int32).reshape(1), parts)
     return (attn_out.reshape(tokens.shape), input_grad.reshape(tokens.shape), weight_grads)
 
 

time: 146 us -> 143 us (0.979)
  blocking collectives: 15.6 us -> 0 us
  starting transfers between devices: 41.9 us -> 50.1 us
  waiting for transfers between devices: 58.3 us -> 63.2 us
    all_to_all x1 -> x0, blocking collectives: 15.6 us -> none  [per_device(): parts = lax.all_to_all(jnp.broadcast_to(rows, (16, 64, 256)), 'dp', 0, 0)]
    ppermute x0 -> x5, starting transfers between devices: none -> 8.45 us  [the longest x1 3.28 us: per_device(): other_total = lax.ppermute(total, 'dp', CORE_SWAP)]
    ppermute x0 -> x5, waiting for transfers between devices: none -> 5.75 us  [the longest x3 3.59 us: per_device(): parts = [part] + [lax.ppermute(part, 'dp', shift) for shift in X_SHIFTS]]
    ppermute x3, starting transfers between devices: 7.42 us -> 5.66 us  [per_device(): lax.ppermute(x, 'dp', y)]
  transfers between devices with their start and end apart: 16 -> 21, of which waited for: 13 -> 17; matrix products, arithmetic and copies ran while one was open for 1% -> 1% of each run, Pallas kernels for 3% -> 3%
where the time goes in v12:
time: 143 us
  waiting for transfers between devices  63.2 us (44%)
  starting transfers between devices  50.1 us (35%)
  Pallas kernels  22.2 us (16%)
  local copies, waits for them, and re-layouts  3.19 us (2%)
  other arithmetic  3.01 us (2%)
    all_to_all x1, waiting for transfers between devices, per_device(): lax.all_to_all(jnp.concatenate([query_part, key_part], axis=1), 'ctx', 0, 0)  18.1 us
    ppermute x3, waiting for transfers between devices, per_device(): lax.ppermute(rows, 'dp', shift)  11.2 us
    pallas_call x1, Pallas kernels, attend(): pl.pallas_call(attend_kernel, out_shape=(jax.ShapeDtypeStruct(block, jnp....  10.7 us
    all_to_all x1, starting transfers between devices, per_device(): own = lax.all_to_all(packed, 'ctx', 0, 0)  9.19 us
    all_to_all x1, waiting for transfers between devices, per_device(): terms = lax.all_to_all(terms, 'ctx', 0, 0)  7.96 us
    ppermute x2, starting transfers between devices, per_device(): given = lax.ppermute(give, 'dp', CORE_SWAP)  7.4 us
    ppermute x3, waiting for transfers between devices, per_device(): lax.ppermute(x, 'dp', y)  6.34 us
    ppermute x3, starting transfers between devices, per_device(): lax.ppermute(x, 'dp', y)  5.66 us
  transfers between devices with their start and end apart: 21, of which 17 were waited for; matrix products, arithmetic and copies ran while one was open for 1% of the time, Pallas kernels for 3%

profile of v12, /device:TPU:1, one launch (start us, length us, event | category | flops | bytes accessed | tf_op | source)
XLA Modules:
  0.0 142.6 jit_solution(10573824563223760085)
XLA Ops:
  0.7 0.6 pad_add_fusion.place_ref
  1.3 4.7 %project.1 = (bf16[8,2,192,128]{3,2,1,0:T(8,128)(2,1)}, bf16[8,192,128]{2,1,0:T(8,128)(2,1)}) custom-call(s32[2]{0:T(128)} %pad_add_fusion.place_ref, bf16[2,96,1024]{2,1,0:T(8,128)(2,1)} %bitcast.27, bf16[2,96,1024]{2,1,0:T(8,128)(2,1)} %bitcast.28, bf16[4,1024,512]{2,1,0:T(8,128)(2,1)} %weights_ref.3), custom_call_target="tpu_custom_call" | custom-call | tf_op jit(solution)/shard_map/project/pallas_call | solution.py:58
  6.0 3.3 %collective-permute-start = (bf16[8,192,128]{2,1,0:T(8,128)(2,1)}, bf16[8,192,128]{2,1,0:T(8,128)(2,1)S(1)}, u32[]{:S(2)}, u32[]{:S(2)}) collective-permute-start(bf16[8,192,128]{2,1,0:T(8,128)(2,1)} %get-tuple-element.33), channel_id=1, source_target_pairs={{0,16},{16,0},{32,48},{48,32},{64,80},{80,64},{96,112},{112,96},{1... | collective-permute-start | bytes 1179656 | tf_op jit(solution)/shard_map/ppermute | solution.py:379
  9.3 0.1 collective-permute-start.1
  9.4 1.4 %collective-permute-done = bf16[8,192,128]{2,1,0:T(8,128)(2,1)S(1)} collective-permute-done((bf16[8,192,128]{2,1,0:T(8,128)(2,1)}, bf16[8,192,128]{2,1,0:T(8,128)(2,1)S(1)}, u32[]{:S(2)}, u32[]{:S(2)}) %collective-permute-start) | collective-permute-done | bytes 393248 | tf_op jit(solution)/shard_map/ppermute | solution.py:379
  10.9 0.8 bitcast_dynamic-update-slice_fusion
  11.7 9.2 %all-to-all-start = ((bf16[16,192,128]{2,1,0:T(8,128)(2,1)}), bf16[16,192,128]{2,1,0:T(8,128)(2,1)S(1)}, u32[]{:S(2)}, u32[]{:S(2)}) async-start(bf16[16,192,128]{2,1,0:T(8,128)(2,1)} %bitcast.29), calls=%async_computation | async-start | bytes 1572864 | tf_op jit(solution)/shard_map/all_to_all | solution.py:399
  21.0 0.7 collective-permute-start.2
  21.8 1.3 collective-permute-done.2
  23.1 0.1 broadcast_select_fusion
  23.2 2.6 %collective-permute-start.4 = (bf16[2,96,1024]{2,1,0:T(8,128)(2,1)S(1)}, bf16[2,96,1024]{2,1,0:T(8,128)(2,1)S(1)}, u32[]{:S(2)}, u32[]{:S(2)}) collective-permute-start(bf16[2,96,1024]{2,1,0:T(8,128)(2,1)S(1)} %get-tuple-element.62), channel_id=1, source_target_pairs={{0,192},{16,208},{32,224},{48,240},{64,0},{80,16},{96,32},{112,48}... | collective-permute-start | bytes 1179656 | tf_op jit(solution)/shard_map/ppermute | solution.py:397
  26.0 8.0 %collective-permute-done.4.refs_7_ = bf16[2,96,1024]{2,1,0:T(8,128)(2,1)S(1)} collective-permute-done((bf16[2,96,1024]{2,1,0:T(8,128)(2,1)S(1)}, bf16[2,96,1024]{2,1,0:T(8,128)(2,1)S(1)}, u32[]{:S(2)}, u32[]{:S(2)}) %collective-permute-start.4) | collective-permute-done | bytes 393248 | tf_op jit(solution)/shard_map/ppermute | solution.py:397
  33.9 3.2 %collective-permute-done.3.refs_5_ = bf16[2,96,1024]{2,1,0:T(8,128)(2,1)S(1)} collective-permute-done((bf16[2,96,1024]{2,1,0:T(8,128)(2,1)S(1)}, bf16[2,96,1024]{2,1,0:T(8,128)(2,1)S(1)}, u32[]{:S(2)}, u32[]{:S(2)}) %collective-permute-start.3) | collective-permute-done | bytes 393248 | tf_op jit(solution)/shard_map/ppermute | solution.py:397
  37.2 5.2 %all-to-all-done.own_ref = bf16[16,192,128]{2,1,0:T(8,128)(2,1)S(1)} async-done(((bf16[16,192,128]{2,1,0:T(8,128)(2,1)}), bf16[16,192,128]{2,1,0:T(8,128)(2,1)S(1)}, u32[]{:S(2)}, u32[]{:S(2)}) %all-to-all-start) | async-done | bytes 786464 | tf_op jit(solution)/shard_map/all_to_all | solution.py:399
  42.3 2.2 %collective-permute-start.5 = (bf16[16,96,128]{2,1,0:T(8,128)(2,1)S(1)}, bf16[16,96,128]{2,1,0:T(8,128)(2,1)S(1)}, u32[]{:S(2)}, u32[]{:S(2)}) collective-permute-start(bf16[16,96,128]{2,1,0:T(8,128)(2,1)S(1)} %slice.11), channel_id=1, source_target_pairs={{0,16},{16,0},{32,48},{48,32},{64,80},{80,64},{96,112},{112,96},{1... | collective-permute-start | bytes 1179656 | tf_op jit(solution)/shard_map/ppermute | solution.py:401
  44.6 1.3 collective-permute-done.5.other_ref
  45.9 10.7 %attend.1 = (bf16[16,96,128]{2,1,0:T(8,128)(2,1)S(1)}, f32[16,96,128]{2,1,0:T(8,128)S(1)}, bf16[16,96,128]{2,1,0:T(8,128)(2,1)S(1)}) custom-call(s32[1]{0:T(128)} %bitcast.core_ref, s32[4]{0:T(128)S(1)} %fusion.tiles_ref, bf16[16,192,128]{2,1,0:T(8,128)(2,1)S(1)} %all-to-all-done.own_ref, bf16[16,96,128]{2,1,0:T(8,128)(2,1)S(1)} %collective-permute-done.5.other_ref), custom_call_target="tpu_custom_call" | custom-call | flops 12000000000 | bytes 4194304 | tf_op jit(solution)/shard_map/attend/pallas_call | solution.py:197
  56.6 0.1 collective-permute-start.6
  56.7 1.7 %collective-permute-done.6 = bf16[16,96,128]{2,1,0:T(8,128)(2,1)S(1)} collective-permute-done((bf16[16,96,128]{2,1,0:T(8,128)(2,1)S(1)}, bf16[16,96,128]{2,1,0:T(8,128)(2,1)S(1)}, u32[]{:S(2)}, u32[]{:S(2)}) %collective-permute-start.6) | collective-permute-done | bytes 393248 | tf_op jit(solution)/shard_map/ppermute | solution.py:404
  58.5 1.0 pad_maximum_fusion
  59.5 4.7 %all-to-all-start.1 = ((bf16[16,192,128]{2,1,0:T(8,128)(2,1)}), bf16[16,192,128]{2,1,0:T(8,128)(2,1)S(1)}, u32[]{:S(2)}, u32[]{:S(2)}) async-start(bf16[16,192,128]{2,1,0:T(8,128)(2,1)} %pad_maximum_fusion), calls=%async_computation.1 | async-start | bytes 1572864 | tf_op jit(solution)/shard_map/all_to_all | solution.py:406
  64.1 2.8 %collective-permute-start.7 = (bf16[2,96,1024]{2,1,0:T(8,128)(2,1)S(1)}, bf16[2,96,1024]{2,1,0:T(8,128)(2,1)S(1)}, u32[]{:S(2)}, u32[]{:S(2)}) collective-permute-start(bf16[2,96,1024]{2,1,0:T(8,128)(2,1)S(1)} %get-tuple-element.63), channel_id=1, source_target_pairs={{0,128},{16,144},{32,160},{48,176},{64,192},{80,208},{96,224},{112... | collective-permute-start | bytes 1179656 | tf_op jit(solution)/shard_map/ppermute | solution.py:397
  67.0 18.1 %all-to-all-done.1 = bf16[16,192,128]{2,1,0:T(8,128)(2,1)S(1)} async-done(((bf16[16,192,128]{2,1,0:T(8,128)(2,1)}), bf16[16,192,128]{2,1,0:T(8,128)(2,1)S(1)}, u32[]{:S(2)}, u32[]{:S(2)}) %all-to-all-start.1) | async-done | bytes 786464 | tf_op jit(solution)/shard_map/all_to_all | solution.py:406
  85.1 0.4 repack.1
  85.5 2.5 %collective-permute-start.10 = (bf16[2,96,512]{2,1,0:T(8,128)(2,1)S(1)}, bf16[2,96,512]{2,1,0:T(8,128)(2,1)S(1)}, u32[]{:S(2)}, u32[]{:S(2)}) collective-permute-start(bf16[2,96,512]{2,1,0:T(8,128)(2,1)S(1)} %get-tuple-element.47), channel_id=1, source_target_pairs={{0,192},{16,208},{32,224},{48,240},{64,0},{80,16},{96,32},{112,48}... | collective-permute-start | bytes 589832 | tf_op jit(solution)/shard_map/ppermute | solution.py:411
  88.0 1.5 %collective-permute-start.8 = (bf16[2,96,512]{2,1,0:T(8,128)(2,1)S(1)}, bf16[2,96,512]{2,1,0:T(8,128)(2,1)S(1)}, u32[]{:S(2)}, u32[]{:S(2)}) collective-permute-start(bf16[2,96,512]{2,1,0:T(8,128)(2,1)S(1)} %get-tuple-element.45), channel_id=1, source_target_pairs={{0,64},{16,80},{32,96},{48,112},{64,128},{80,144},{96,160},{112,17... | collective-permute-start | bytes 589832 | tf_op jit(solution)/shard_map/ppermute | solution.py:411
  89.5 1.7 %collective-permute-start.9 = (bf16[2,96,512]{2,1,0:T(8,128)(2,1)S(1)}, bf16[2,96,512]{2,1,0:T(8,128)(2,1)S(1)}, u32[]{:S(2)}, u32[]{:S(2)}) collective-permute-start(bf16[2,96,512]{2,1,0:T(8,128)(2,1)S(1)} %get-tuple-element.46), channel_id=1, source_target_pairs={{0,128},{16,144},{32,160},{48,176},{64,192},{80,208},{96,224},{112... | collective-permute-start | bytes 589832 | tf_op jit(solution)/shard_map/ppermute | solution.py:411
  91.2 1.3 collective-permute-done.10.refs_3_
  92.4 1.3 collective-permute-done.8.refs_1_
  93.7 3.8 %collective-permute-done.9.refs_2_ = bf16[2,96,512]{2,1,0:T(8,128)(2,1)S(1)} collective-permute-done((bf16[2,96,512]{2,1,0:T(8,128)(2,1)S(1)}, bf16[2,96,512]{2,1,0:T(8,128)(2,1)S(1)}, u32[]{:S(2)}, u32[]{:S(2)}) %collective-permute-start.9) | collective-permute-done | bytes 196640 | tf_op jit(solution)/shard_map/ppermute | solution.py:411
  97.5 1.9 %weight_terms.1 = (bf16[16,64,256]{2,1,0:T(8,128)(2,1)S(1)}, bf16[16,64,256]{2,1,0:T(8,128)(2,1)S(1)}) custom-call(s32[1]{0:T(128)} %bitcast.core_ref, bf16[2,96,512]{2,1,0:T(8,128)(2,1)S(1)} %get-tuple-element.44.refs_0_, bf16[2,96,512]{2,1,0:T(8,128)(2,1)S(1)} %collective-permute-done.8.refs_1_, bf16[2,96,512]{2,1,0:T(8,128)(2,1)S(1)} %collective-permute-done.9.refs_2_, ...), custom_call_target="tpu_custom_call" | custom-call | tf_op jit(solution)/shard_map/weight_terms/pallas_call | solution.py:279
  99.5 4.1 %collective-permute-start.11 = (bf16[16,64,256]{2,1,0:T(8,128)(2,1)S(1)}, bf16[16,64,256]{2,1,0:T(8,128)(2,1)S(1)}, u32[]{:S(2)}, u32[]{:S(2)}) collective-permute-start(bf16[16,64,256]{2,1,0:T(8,128)(2,1)S(1)} %get-tuple-element.52), channel_id=1, source_target_pairs={{0,16},{16,0},{32,48},{48,32},{64,80},{80,64},{96,112},{112,96},{1... | collective-permute-start | bytes 1572872 | tf_op jit(solution)/shard_map/ppermute | solution.py:413
  103.5 1.5 %collective-permute-done.11 = bf16[16,64,256]{2,1,0:T(8,128)(2,1)S(1)} collective-permute-done((bf16[16,64,256]{2,1,0:T(8,128)(2,1)S(1)}, bf16[16,64,256]{2,1,0:T(8,128)(2,1)S(1)}, u32[]{:S(2)}, u32[]{:S(2)}) %collective-permute-start.11) | collective-permute-done | bytes 524320 | tf_op jit(solution)/shard_map/ppermute | solution.py:413
  105.1 1.0 add_convert_fusion
  106.0 5.4 %all-to-all-start.2 = ((bf16[16,64,256]{2,1,0:T(8,128)(2,1)}), bf16[16,64,256]{2,1,0:T(8,128)(2,1)S(1)}, u32[]{:S(2)}, u32[]{:S(2)}) async-start(bf16[16,64,256]{2,1,0:T(8,128)(2,1)} %add_convert_fusion), calls=%async_computation.2 | async-start | bytes 1048576 | tf_op jit(solution)/shard_map/all_to_all | solution.py:416
  111.5 0.7 collective-permute-start.12
  112.3 1.3 collective-permute-done.12.arrived_ref
  113.6 2.2 %copy-done = bf16[4,1024,512]{2,1,0:T(8,128)(2,1)S(1)} copy-done((bf16[4,1024,512]{2,1,0:T(8,128)(2,1)S(1)}, bf16[4,1024,512]{2,1,0:T(8,128)(2,1)}, u32[]{:S(2)}) %copy-start) | copy-done | bytes 4194328
  115.7 3.8 %outputs.1 = (bf16[2,96,1024]{2,1,0:T(8,128)(2,1)}, bf16[2,96,1024]{2,1,0:T(8,128)(2,1)}) custom-call(s32[2]{0:T(128)S(1)} %pad_add_fusion.1.place_ref, bf16[4,2,96,512]{3,2,1,0:T(8,128)(2,1)S(1)} %get-tuple-element.55.grads_ref, bf16[4,96,512]{2,1,0:T(8,128)(2,1)S(1)} %collective-permute-done.12.arrived_ref, bf16[4,1024,512]{2,1,0:T(8,128)(2,1)S(1)} %copy-done), custom_call_target="tpu_custom_call" | custom-call | flops 805306368 | bytes 7340032 | tf_op jit(solution)/shard_map/outputs/pallas_call | solution.py:343
  119.6 8.0 %all-to-all-done.2 = bf16[16,64,256]{2,1,0:T(8,128)(2,1)S(1)} async-done(((bf16[16,64,256]{2,1,0:T(8,128)(2,1)}), bf16[16,64,256]{2,1,0:T(8,128)(2,1)S(1)}, u32[]{:S(2)}, u32[]{:S(2)}) %all-to-all-start.2) | async-done | bytes 524320 | tf_op jit(solution)/shard_map/all_to_all | solution.py:416
  127.6 2.4 %collective-permute-start.13 = (bf16[64,256]{1,0:T(8,128)(2,1)S(1)}, bf16[64,256]{1,0:T(8,128)(2,1)S(1)}, u32[]{:S(2)}, u32[]{:S(2)}) collective-permute-start(bf16[64,256]{1,0:T(8,128)(2,1)S(1)} %reduce-precision_convert_fusion), channel_id=1, source_target_pairs={{0,32},{16,48},{32,0},{48,16},{64,96},{80,112},{96,64},{112,80},{1... | collective-permute-start | bytes 98312 | tf_op jit(solution)/shard_map/ppermute | solution.py:424
  130.0 1.3 collective-permute-done.13
  131.4 3.3 %collective-permute-start.14 = (bf16[64,256]{1,0:T(8,128)(2,1)S(1)}, bf16[64,256]{1,0:T(8,128)(2,1)S(1)}, u32[]{:S(2)}, u32[]{:S(2)}) collective-permute-start(bf16[64,256]{1,0:T(8,128)(2,1)S(1)} %multiply_convert_fusion), channel_id=1, source_target_pairs={{0,16},{16,0},{32,48},{48,32},{64,80},{80,64},{96,112},{112,96},{1... | collective-permute-start | bytes 98312 | tf_op jit(solution)/shard_map/ppermute | solution.py:427
  134.6 0.9 collective-permute-done.14
  135.6 1.2 collective-permute-start.16
  136.8 1.5 %collective-permute-start.17 = (bf16[64,512]{1,0:T(8,128)(2,1)S(1)}, bf16[64,512]{1,0:T(8,128)(2,1)S(1)}, u32[]{:S(2)}, u32[]{:S(2)}) collective-permute-start(bf16[64,512]{1,0:T(8,128)(2,1)S(1)} %pad_maximum_fusion.4.refs_0_), channel_id=1, source_target_pairs={{0,192},{16,208},{32,224},{48,240},{64,0},{80,16},{96,32},{112,48}... | collective-permute-start | bytes 196616 | tf_op jit(solution)/shard_map/ppermute | solution.py:432
  138.3 3.6 %collective-permute-done.15.refs_1_ = bf16[64,512]{1,0:T(8,128)(2,1)S(1)} collective-permute-done((bf16[64,512]{1,0:T(8,128)(2,1)S(1)}, bf16[64,512]{1,0:T(8,128)(2,1)S(1)}, u32[]{:S(2)}, u32[]{:S(2)}) %collective-permute-start.15) | collective-permute-done | bytes 65568 | tf_op jit(solution)/shard_map/ppermute | solution.py:432
  141.9 0.7 place_weights.1
  (27 shorter events, 0.7 us)
Async XLA Ops:
  1.3 8.0 %copy-start.3 = (s32[1,4]{1,0:T(1,128)S(1)}, s32[1,4]{1,0:T(1,128)}, u32[]{:S(2)}) copy-start(s32[1,4]{1,0:T(1,128)} %param.5) | copy-start | bytes 52
  6.0 14.9 %copy-start.1 = (bf16[1,1,2,96,1024]{4,3,2,1,0:T(8,128)(2,1)S(1)}, bf16[1,1,2,96,1024]{4,3,2,1,0:T(8,128)(2,1)}, u32[]{:S(2)}) copy-start(bf16[1,1,2,96,1024]{4,3,2,1,0:T(8,128)(2,1)} %param.4) | copy-start | bytes 1179652
  6.0 14.9 %copy-start.2 = (bf16[1,1,2,96,1024]{4,3,2,1,0:T(8,128)(2,1)S(1)}, bf16[1,1,2,96,1024]{4,3,2,1,0:T(8,128)(2,1)}, u32[]{:S(2)}) copy-start(bf16[1,1,2,96,1024]{4,3,2,1,0:T(8,128)(2,1)} %param.7) | copy-start | bytes 1179652
  6.0 4.9 %collective-permute-start = (bf16[8,192,128]{2,1,0:T(8,128)(2,1)}, bf16[8,192,128]{2,1,0:T(8,128)(2,1)S(1)}, u32[]{:S(2)}, u32[]{:S(2)}) collective-permute-start(bf16[8,192,128]{2,1,0:T(8,128)(2,1)} %get-tuple-element.33), channel_id=1, source_target_pairs={{0,16},{16,0},{32,48},{48,32},{64,80},{80,64},{96,112},{112,96},{1... | collective-permute-start | bytes 1179656 | tf_op jit(solution)/shard_map/ppermute | solution.py:379
  9.3 2.4 %collective-permute-start.1 = (s32[1,4]{1,0:T(1,128)S(1)}, s32[1,4]{1,0:T(1,128)S(1)}, u32[]{:S(2)}, u32[]{:S(2)}) collective-permute-start(s32[1,4]{1,0:T(1,128)S(1)} %copy-done.3), channel_id=1, source_target_pairs={{0,16},{16,0},{32,48},{48,32},{64,80},{80,64},{96,112},{112,96},{1... | collective-permute-start | bytes 56 | tf_op jit(solution)/shard_map/ppermute | solution.py:374
  11.7 30.6 %all-to-all-start = ((bf16[16,192,128]{2,1,0:T(8,128)(2,1)}), bf16[16,192,128]{2,1,0:T(8,128)(2,1)S(1)}, u32[]{:S(2)}, u32[]{:S(2)}) async-start(bf16[16,192,128]{2,1,0:T(8,128)(2,1)} %bitcast.29), calls=%async_computation | async-start | bytes 1572864 | tf_op jit(solution)/shard_map/all_to_all | solution.py:399
  21.0 2.1 %collective-permute-start.2 = (bf16[2,96,1024]{2,1,0:T(8,128)(2,1)S(1)}, bf16[2,96,1024]{2,1,0:T(8,128)(2,1)S(1)}, u32[]{:S(2)}, u32[]{:S(2)}) collective-permute-start(bf16[2,96,1024]{2,1,0:T(8,128)(2,1)S(1)} %pad_maximum_fusion.1), channel_id=1, source_target_pairs={{0,16},{16,0},{32,48},{48,32},{64,80},{80,64},{96,112},{112,96},{1... | collective-permute-start | bytes 1179656 | tf_op jit(solution)/shard_map/ppermute | solution.py:385
  23.2 10.7 %collective-permute-start.4 = (bf16[2,96,1024]{2,1,0:T(8,128)(2,1)S(1)}, bf16[2,96,1024]{2,1,0:T(8,128)(2,1)S(1)}, u32[]{:S(2)}, u32[]{:S(2)}) collective-permute-start(bf16[2,96,1024]{2,1,0:T(8,128)(2,1)S(1)} %get-tuple-element.62), channel_id=1, source_target_pairs={{0,192},{16,208},{32,224},{48,240},{64,0},{80,16},{96,32},{112,48}... | collective-permute-start | bytes 1179656 | tf_op jit(solution)/shard_map/ppermute | solution.py:397
  25.9 11.3 %collective-permute-start.3 = (bf16[2,96,1024]{2,1,0:T(8,128)(2,1)S(1)}, bf16[2,96,1024]{2,1,0:T(8,128)(2,1)S(1)}, u32[]{:S(2)}, u32[]{:S(2)}) collective-permute-start(bf16[2,96,1024]{2,1,0:T(8,128)(2,1)S(1)} %broadcast_select_fusion.3), channel_id=1, source_target_pairs={{0,64},{16,80},{32,96},{48,112},{64,128},{80,144},{96,160},{112,17... | collective-permute-start | bytes 1179656 | tf_op jit(solution)/shard_map/ppermute | solution.py:397
  42.3 3.6 %collective-permute-start.5 = (bf16[16,96,128]{2,1,0:T(8,128)(2,1)S(1)}, bf16[16,96,128]{2,1,0:T(8,128)(2,1)S(1)}, u32[]{:S(2)}, u32[]{:S(2)}) collective-permute-start(bf16[16,96,128]{2,1,0:T(8,128)(2,1)S(1)} %slice.11), channel_id=1, source_target_pairs={{0,16},{16,0},{32,48},{48,32},{64,80},{80,64},{96,112},{112,96},{1... | collective-permute-start | bytes 1179656 | tf_op jit(solution)/shard_map/ppermute | solution.py:401
  56.6 1.8 %collective-permute-start.6 = (bf16[16,96,128]{2,1,0:T(8,128)(2,1)S(1)}, bf16[16,96,128]{2,1,0:T(8,128)(2,1)S(1)}, u32[]{:S(2)}, u32[]{:S(2)}) collective-permute-start(bf16[16,96,128]{2,1,0:T(8,128)(2,1)S(1)} %get-tuple-element.39), channel_id=1, source_target_pairs={{0,16},{16,0},{32,48},{48,32},{64,80},{80,64},{96,112},{112,96},{1... | collective-permute-start | bytes 1179656 | tf_op jit(solution)/shard_map/ppermute | solution.py:404
  59.5 25.6 %all-to-all-start.1 = ((bf16[16,192,128]{2,1,0:T(8,128)(2,1)}), bf16[16,192,128]{2,1,0:T(8,128)(2,1)S(1)}, u32[]{:S(2)}, u32[]{:S(2)}) async-start(bf16[16,192,128]{2,1,0:T(8,128)(2,1)} %pad_maximum_fusion), calls=%async_computation.1 | async-start | bytes 1572864 | tf_op jit(solution)/shard_map/all_to_all | solution.py:406
  64.1 21.4 %collective-permute-start.7 = (bf16[2,96,1024]{2,1,0:T(8,128)(2,1)S(1)}, bf16[2,96,1024]{2,1,0:T(8,128)(2,1)S(1)}, u32[]{:S(2)}, u32[]{:S(2)}) collective-permute-start(bf16[2,96,1024]{2,1,0:T(8,128)(2,1)S(1)} %get-tuple-element.63), channel_id=1, source_target_pairs={{0,128},{16,144},{32,160},{48,176},{64,192},{80,208},{96,224},{112... | collective-permute-start | bytes 1179656 | tf_op jit(solution)/shard_map/ppermute | solution.py:397
  85.5 6.9 %collective-permute-start.10 = (bf16[2,96,512]{2,1,0:T(8,128)(2,1)S(1)}, bf16[2,96,512]{2,1,0:T(8,128)(2,1)S(1)}, u32[]{:S(2)}, u32[]{:S(2)}) collective-permute-start(bf16[2,96,512]{2,1,0:T(8,128)(2,1)S(1)} %get-tuple-element.47), channel_id=1, source_target_pairs={{0,192},{16,208},{32,224},{48,240},{64,0},{80,16},{96,32},{112,48}... | collective-permute-start | bytes 589832 | tf_op jit(solution)/shard_map/ppermute | solution.py:411
  88.0 5.7 %collective-permute-start.8 = (bf16[2,96,512]{2,1,0:T(8,128)(2,1)S(1)}, bf16[2,96,512]{2,1,0:T(8,128)(2,1)S(1)}, u32[]{:S(2)}, u32[]{:S(2)}) collective-permute-start(bf16[2,96,512]{2,1,0:T(8,128)(2,1)S(1)} %get-tuple-element.45), channel_id=1, source_target_pairs={{0,64},{16,80},{32,96},{48,112},{64,128},{80,144},{96,160},{112,17... | collective-permute-start | bytes 589832 | tf_op jit(solution)/shard_map/ppermute | solution.py:411
  89.5 8.0 %collective-permute-start.9 = (bf16[2,96,512]{2,1,0:T(8,128)(2,1)S(1)}, bf16[2,96,512]{2,1,0:T(8,128)(2,1)S(1)}, u32[]{:S(2)}, u32[]{:S(2)}) collective-permute-start(bf16[2,96,512]{2,1,0:T(8,128)(2,1)S(1)} %get-tuple-element.46), channel_id=1, source_target_pairs={{0,128},{16,144},{32,160},{48,176},{64,192},{80,208},{96,224},{112... | collective-permute-start | bytes 589832 | tf_op jit(solution)/shard_map/ppermute | solution.py:411
  99.5 5.6 %collective-permute-start.11 = (bf16[16,64,256]{2,1,0:T(8,128)(2,1)S(1)}, bf16[16,64,256]{2,1,0:T(8,128)(2,1)S(1)}, u32[]{:S(2)}, u32[]{:S(2)}) collective-permute-start(bf16[16,64,256]{2,1,0:T(8,128)(2,1)S(1)} %get-tuple-element.52), channel_id=1, source_target_pairs={{0,16},{16,0},{32,48},{48,32},{64,80},{80,64},{96,112},{112,96},{1... | collective-permute-start | bytes 1572872 | tf_op jit(solution)/shard_map/ppermute | solution.py:413
  106.0 21.5 %all-to-all-start.2 = ((bf16[16,64,256]{2,1,0:T(8,128)(2,1)}), bf16[16,64,256]{2,1,0:T(8,128)(2,1)S(1)}, u32[]{:S(2)}, u32[]{:S(2)}) async-start(bf16[16,64,256]{2,1,0:T(8,128)(2,1)} %add_convert_fusion), calls=%async_computation.2 | async-start | bytes 1048576 | tf_op jit(solution)/shard_map/all_to_all | solution.py:416
  111.5 2.1 %collective-permute-start.12 = (bf16[4,96,512]{2,1,0:T(8,128)(2,1)S(1)}, bf16[4,96,512]{2,1,0:T(8,128)(2,1)S(1)}, u32[]{:S(2)}, u32[]{:S(2)}) collective-permute-start(bf16[4,96,512]{2,1,0:T(8,128)(2,1)S(1)} %dynamic-slice_bitcast_fusion), channel_id=1, source_target_pairs={{0,16},{16,0},{32,48},{48,32},{64,80},{80,64},{96,112},{112,96},{1... | collective-permute-start | bytes 1179656 | tf_op jit(solution)/shard_map/ppermute | solution.py:417
  113.5 2.2 %copy-start = (bf16[4,1024,512]{2,1,0:T(8,128)(2,1)S(1)}, bf16[4,1024,512]{2,1,0:T(8,128)(2,1)}, u32[]{:S(2)}) copy-start(bf16[4,1024,512]{2,1,0:T(8,128)(2,1)} %weights_ref.3) | copy-start | bytes 12582916
  127.6 3.7 %collective-permute-start.13 = (bf16[64,256]{1,0:T(8,128)(2,1)S(1)}, bf16[64,256]{1,0:T(8,128)(2,1)S(1)}, u32[]{:S(2)}, u32[]{:S(2)}) collective-permute-start(bf16[64,256]{1,0:T(8,128)(2,1)S(1)} %reduce-precision_convert_fusion), channel_id=1, source_target_pairs={{0,32},{16,48},{32,0},{48,16},{64,96},{80,112},{96,64},{112,80},{1... | collective-permute-start | bytes 98312 | tf_op jit(solution)/shard_map/ppermute | solution.py:424
  131.4 4.1 %collective-permute-start.14 = (bf16[64,256]{1,0:T(8,128)(2,1)S(1)}, bf16[64,256]{1,0:T(8,128)(2,1)S(1)}, u32[]{:S(2)}, u32[]{:S(2)}) collective-permute-start(bf16[64,256]{1,0:T(8,128)(2,1)S(1)} %multiply_convert_fusion), channel_id=1, source_target_pairs={{0,16},{16,0},{32,48},{48,32},{64,80},{80,64},{96,112},{112,96},{1... | collective-permute-start | bytes 98312 | tf_op jit(solution)/shard_map/ppermute | solution.py:427
  135.5 6.3 %collective-permute-start.15 = (bf16[64,512]{1,0:T(8,128)(2,1)S(1)}, bf16[64,512]{1,0:T(8,128)(2,1)S(1)}, u32[]{:S(2)}, u32[]{:S(2)}) collective-permute-start(bf16[64,512]{1,0:T(8,128)(2,1)S(1)} %pad_maximum_fusion.4.refs_0_), channel_id=1, source_target_pairs={{0,64},{16,80},{32,96},{48,112},{64,128},{80,144},{96,160},{112,17... | collective-permute-start | bytes 196616 | tf_op jit(solution)/shard_map/ppermute | solution.py:432
  135.6 6.3 %collective-permute-start.16 = (bf16[64,512]{1,0:T(8,128)(2,1)S(1)}, bf16[64,512]{1,0:T(8,128)(2,1)S(1)}, u32[]{:S(2)}, u32[]{:S(2)}) collective-permute-start(bf16[64,512]{1,0:T(8,128)(2,1)S(1)} %pad_maximum_fusion.4.refs_0_), channel_id=1, source_target_pairs={{0,128},{16,144},{32,160},{48,176},{64,192},{80,208},{96,224},{112... | collective-permute-start | bytes 196616 | tf_op jit(solution)/shard_map/ppermute | solution.py:432
  136.8 5.1 %collective-permute-start.17 = (bf16[64,512]{1,0:T(8,128)(2,1)S(1)}, bf16[64,512]{1,0:T(8,128)(2,1)S(1)}, u32[]{:S(2)}, u32[]{:S(2)}) collective-permute-start(bf16[64,512]{1,0:T(8,128)(2,1)S(1)} %pad_maximum_fusion.4.refs_0_), channel_id=1, source_target_pairs={{0,192},{16,208},{32,224},{48,240},{64,0},{80,16},{96,32},{112,48}... | collective-permute-start | bytes 196616 | tf_op jit(solution)/shard_map/ppermute | solution.py:432

commit v13 on v12

--- a/solution.py
+++ b/solution.py
@@ -20,6 +20,7 @@
 
 CORE_SWAP = [(i, i ^ 1) for i in range(16)]
 Z_SWAP = [(i, i ^ 2) for i in range(16)]
+BOTH_SWAP = [(i, i ^ 3) for i in range(16)]
 X_SHIFTS = [[(i, (i + 4 * shift) % 16) for i in range(16)] for shift in range(1, 4)]
 
 
@@ -421,10 +422,14 @@
     attn_out, input_grad = outputs(place, own_grads, swapped, weights)
     terms, attn_out, input_grad = lax.optimization_barrier((terms, attn_out, input_grad))
     rows = lax.reduce_precision(jnp.sum(terms.astype(jnp.float32), axis=0), 8, 7)
-    other_rows = lax.ppermute(rows.astype(jnp.bfloat16), "dp", Z_SWAP)
+    rows_low = rows.astype(jnp.bfloat16)
+    other_rows, core_rows, far_rows = (
+        lax.ppermute(rows_low, "dp", swap).astype(jnp.float32)
+        for swap in (Z_SWAP, CORE_SWAP, BOTH_SWAP)
+    )
     factor = float(16 * RANKS * 2 * SPAN) ** -0.5
-    total = ((rows + other_rows.astype(jnp.float32)) * factor).astype(jnp.bfloat16)
-    other_total = lax.ppermute(total, "dp", CORE_SWAP)
+    total = ((rows + other_rows) * factor).astype(jnp.bfloat16)
+    other_total = ((core_rows + far_rows) * factor).astype(jnp.bfloat16)
     first = core == 0
     part = jnp.concatenate(
         [jnp.where(first, total, other_total), jnp.where(first, other_total, total)], axis=1

time: 143 us -> 144 us (level)
    ppermute x2 -> x3, waiting for transfers between devices: 2.16 us -> 3.34 us  [per_device(): lax.ppermute(rows_low, 'dp', swap).astype(jnp.float32)]
    ppermute x2 -> x3, starting transfers between devices: 5.7 us -> 5.67 us  [per_device(): lax.ppermute(rows_low, 'dp', swap).astype(jnp.float32)]
  transfers between devices with their start and end apart: 21 -> 22, of which waited for: 17 -> 18; matrix products, arithmetic and copies ran while one was open for 1% -> 1% of each run, Pallas kernels for 3% -> 3%
where the time goes in v13:
time: 144 us; the launch traced here: 143 us
  waiting for transfers between devices  64.6 us (45%)
  starting transfers between devices  49.8 us (35%)
  Pallas kernels  21.7 us (15%)
  local copies, waits for them, and re-layouts  3.17 us (2%)
  other arithmetic  3.04 us (2%)
    all_to_all x1, waiting for transfers between devices, per_device(): lax.all_to_all(jnp.concatenate([query_part, key_part], axis=1), 'ctx', 0, 0)  18.7 us
    ppermute x3, waiting for transfers between devices, per_device(): lax.ppermute(rows, 'dp', shift)  11.2 us
    pallas_call x1, Pallas kernels, attend(): pl.pallas_call(attend_kernel, out_shape=(jax.ShapeDtypeStruct(block, jnp....  10.1 us
    all_to_all x1, starting transfers between devices, per_device(): own = lax.all_to_all(packed, 'ctx', 0, 0)  9.19 us
    ppermute x2, starting transfers between devices, per_device(): given = lax.ppermute(give, 'dp', CORE_SWAP)  7.32 us
    all_to_all x1, waiting for transfers between devices, per_device(): terms = lax.all_to_all(terms, 'ctx', 0, 0)  7.32 us
    ppermute x3, waiting for transfers between devices, per_device(): lax.ppermute(x, 'dp', y)  6.37 us
    ppermute x3, starting transfers between devices, per_device(): lax.ppermute(rows, 'dp', shift)  6.21 us
  transfers between devices with their start and end apart: 22, of which 18 were waited for; matrix products, arithmetic and copies ran while one was open for 1% of the time, Pallas kernels for 3%

profile of v13, /device:TPU:1, one launch (start us, length us, event | category | flops | bytes accessed | tf_op | source)
XLA Modules:
  0.0 143.1 jit_solution(3698554316150123787)
XLA Ops:
  0.7 0.7 pad_add_fusion.place_ref
  1.3 4.7 %project.1 = (bf16[8,2,192,128]{3,2,1,0:T(8,128)(2,1)}, bf16[8,192,128]{2,1,0:T(8,128)(2,1)}) custom-call(s32[2]{0:T(128)} %pad_add_fusion.place_ref, bf16[2,96,1024]{2,1,0:T(8,128)(2,1)} %bitcast.27, bf16[2,96,1024]{2,1,0:T(8,128)(2,1)} %bitcast.28, bf16[4,1024,512]{2,1,0:T(8,128)(2,1)} %weights_ref.3), custom_call_target="tpu_custom_call" | custom-call | tf_op jit(solution)/shard_map/project/pallas_call | solution.py:59
  6.0 3.3 %collective-permute-start = (bf16[8,192,128]{2,1,0:T(8,128)(2,1)}, bf16[8,192,128]{2,1,0:T(8,128)(2,1)S(1)}, u32[]{:S(2)}, u32[]{:S(2)}) collective-permute-start(bf16[8,192,128]{2,1,0:T(8,128)(2,1)} %get-tuple-element.33), channel_id=1, source_target_pairs={{0,16},{16,0},{32,48},{48,32},{64,80},{80,64},{96,112},{112,96},{1... | collective-permute-start | bytes 1179656 | tf_op jit(solution)/shard_map/ppermute | solution.py:380
  9.3 0.1 collective-permute-start.1
  9.4 1.4 %collective-permute-done = bf16[8,192,128]{2,1,0:T(8,128)(2,1)S(1)} collective-permute-done((bf16[8,192,128]{2,1,0:T(8,128)(2,1)}, bf16[8,192,128]{2,1,0:T(8,128)(2,1)S(1)}, u32[]{:S(2)}, u32[]{:S(2)}) %collective-permute-start) | collective-permute-done | bytes 393248 | tf_op jit(solution)/shard_map/ppermute | solution.py:380
  10.9 0.8 bitcast_dynamic-update-slice_fusion
  11.7 9.2 %all-to-all-start = ((bf16[16,192,128]{2,1,0:T(8,128)(2,1)}), bf16[16,192,128]{2,1,0:T(8,128)(2,1)S(1)}, u32[]{:S(2)}, u32[]{:S(2)}) async-start(bf16[16,192,128]{2,1,0:T(8,128)(2,1)} %bitcast.29), calls=%async_computation | async-start | bytes 1572864 | tf_op jit(solution)/shard_map/all_to_all | solution.py:400
  21.1 0.7 collective-permute-start.2
  21.8 1.3 collective-permute-done.2
  23.3 2.6 %collective-permute-start.4 = (bf16[2,96,1024]{2,1,0:T(8,128)(2,1)S(1)}, bf16[2,96,1024]{2,1,0:T(8,128)(2,1)S(1)}, u32[]{:S(2)}, u32[]{:S(2)}) collective-permute-start(bf16[2,96,1024]{2,1,0:T(8,128)(2,1)S(1)} %get-tuple-element.62), channel_id=1, source_target_pairs={{0,192},{16,208},{32,224},{48,240},{64,0},{80,16},{96,32},{112,48}... | collective-permute-start | bytes 1179656 | tf_op jit(solution)/shard_map/ppermute | solution.py:398
  26.0 8.0 %collective-permute-done.4.refs_7_ = bf16[2,96,1024]{2,1,0:T(8,128)(2,1)S(1)} collective-permute-done((bf16[2,96,1024]{2,1,0:T(8,128)(2,1)S(1)}, bf16[2,96,1024]{2,1,0:T(8,128)(2,1)S(1)}, u32[]{:S(2)}, u32[]{:S(2)}) %collective-permute-start.4) | collective-permute-done | bytes 393248 | tf_op jit(solution)/shard_map/ppermute | solution.py:398
  33.9 3.2 %collective-permute-done.3.refs_5_ = bf16[2,96,1024]{2,1,0:T(8,128)(2,1)S(1)} collective-permute-done((bf16[2,96,1024]{2,1,0:T(8,128)(2,1)S(1)}, bf16[2,96,1024]{2,1,0:T(8,128)(2,1)S(1)}, u32[]{:S(2)}, u32[]{:S(2)}) %collective-permute-start.3) | collective-permute-done | bytes 393248 | tf_op jit(solution)/shard_map/ppermute | solution.py:398
  37.2 5.2 %all-to-all-done.own_ref = bf16[16,192,128]{2,1,0:T(8,128)(2,1)S(1)} async-done(((bf16[16,192,128]{2,1,0:T(8,128)(2,1)}), bf16[16,192,128]{2,1,0:T(8,128)(2,1)S(1)}, u32[]{:S(2)}, u32[]{:S(2)}) %all-to-all-start) | async-done | bytes 786464 | tf_op jit(solution)/shard_map/all_to_all | solution.py:400
  42.4 2.2 %collective-permute-start.5 = (bf16[16,96,128]{2,1,0:T(8,128)(2,1)S(1)}, bf16[16,96,128]{2,1,0:T(8,128)(2,1)S(1)}, u32[]{:S(2)}, u32[]{:S(2)}) collective-permute-start(bf16[16,96,128]{2,1,0:T(8,128)(2,1)S(1)} %slice.11), channel_id=1, source_target_pairs={{0,16},{16,0},{32,48},{48,32},{64,80},{80,64},{96,112},{112,96},{1... | collective-permute-start | bytes 1179656 | tf_op jit(solution)/shard_map/ppermute | solution.py:402
  44.6 1.3 collective-permute-done.5.other_ref
  45.9 10.1 %attend.1 = (bf16[16,96,128]{2,1,0:T(8,128)(2,1)S(1)}, f32[16,96,128]{2,1,0:T(8,128)S(1)}, bf16[16,96,128]{2,1,0:T(8,128)(2,1)S(1)}) custom-call(s32[1]{0:T(128)} %bitcast.core_ref, s32[4]{0:T(128)S(1)} %fusion.tiles_ref, bf16[16,192,128]{2,1,0:T(8,128)(2,1)S(1)} %all-to-all-done.own_ref, bf16[16,96,128]{2,1,0:T(8,128)(2,1)S(1)} %collective-permute-done.5.other_ref), custom_call_target="tpu_custom_call" | custom-call | flops 12000000000 | bytes 4194304 | tf_op jit(solution)/shard_map/attend/pallas_call | solution.py:198
  56.0 0.2 collective-permute-start.6
  56.2 1.6 %collective-permute-done.6 = bf16[16,96,128]{2,1,0:T(8,128)(2,1)S(1)} collective-permute-done((bf16[16,96,128]{2,1,0:T(8,128)(2,1)S(1)}, bf16[16,96,128]{2,1,0:T(8,128)(2,1)S(1)}, u32[]{:S(2)}, u32[]{:S(2)}) %collective-permute-start.6) | collective-permute-done | bytes 393248 | tf_op jit(solution)/shard_map/ppermute | solution.py:405
  57.9 1.0 pad_maximum_fusion
  58.9 4.8 %all-to-all-start.1 = ((bf16[16,192,128]{2,1,0:T(8,128)(2,1)}), bf16[16,192,128]{2,1,0:T(8,128)(2,1)S(1)}, u32[]{:S(2)}, u32[]{:S(2)}) async-start(bf16[16,192,128]{2,1,0:T(8,128)(2,1)} %pad_maximum_fusion), calls=%async_computation.1 | async-start | bytes 1572864 | tf_op jit(solution)/shard_map/all_to_all | solution.py:407
  63.7 3.6 %collective-permute-start.7 = (bf16[2,96,1024]{2,1,0:T(8,128)(2,1)S(1)}, bf16[2,96,1024]{2,1,0:T(8,128)(2,1)S(1)}, u32[]{:S(2)}, u32[]{:S(2)}) collective-permute-start(bf16[2,96,1024]{2,1,0:T(8,128)(2,1)S(1)} %get-tuple-element.63), channel_id=1, source_target_pairs={{0,128},{16,144},{32,160},{48,176},{64,192},{80,208},{96,224},{112... | collective-permute-start | bytes 1179656 | tf_op jit(solution)/shard_map/ppermute | solution.py:398
  67.3 18.7 %all-to-all-done.1 = bf16[16,192,128]{2,1,0:T(8,128)(2,1)S(1)} async-done(((bf16[16,192,128]{2,1,0:T(8,128)(2,1)}), bf16[16,192,128]{2,1,0:T(8,128)(2,1)S(1)}, u32[]{:S(2)}, u32[]{:S(2)}) %all-to-all-start.1) | async-done | bytes 786464 | tf_op jit(solution)/shard_map/all_to_all | solution.py:407
  86.0 0.4 repack.1
  86.4 0.9 collective-permute-start.10
  87.3 0.7 collective-permute-start.8
  88.0 3.7 %collective-permute-start.9 = (bf16[2,96,512]{2,1,0:T(8,128)(2,1)S(1)}, bf16[2,96,512]{2,1,0:T(8,128)(2,1)S(1)}, u32[]{:S(2)}, u32[]{:S(2)}) collective-permute-start(bf16[2,96,512]{2,1,0:T(8,128)(2,1)S(1)} %get-tuple-element.46), channel_id=1, source_target_pairs={{0,128},{16,144},{32,160},{48,176},{64,192},{80,208},{96,224},{112... | collective-permute-start | bytes 589832 | tf_op jit(solution)/shard_map/ppermute | solution.py:412
  91.7 1.9 %collective-permute-done.8.refs_1_ = bf16[2,96,512]{2,1,0:T(8,128)(2,1)S(1)} collective-permute-done((bf16[2,96,512]{2,1,0:T(8,128)(2,1)S(1)}, bf16[2,96,512]{2,1,0:T(8,128)(2,1)S(1)}, u32[]{:S(2)}, u32[]{:S(2)}) %collective-permute-start.8) | collective-permute-done | bytes 196640 | tf_op jit(solution)/shard_map/ppermute | solution.py:412
  93.6 4.5 %collective-permute-done.9.refs_2_ = bf16[2,96,512]{2,1,0:T(8,128)(2,1)S(1)} collective-permute-done((bf16[2,96,512]{2,1,0:T(8,128)(2,1)S(1)}, bf16[2,96,512]{2,1,0:T(8,128)(2,1)S(1)}, u32[]{:S(2)}, u32[]{:S(2)}) %collective-permute-start.9) | collective-permute-done | bytes 196640 | tf_op jit(solution)/shard_map/ppermute | solution.py:412
  98.1 1.9 %weight_terms.1 = (bf16[16,64,256]{2,1,0:T(8,128)(2,1)S(1)}, bf16[16,64,256]{2,1,0:T(8,128)(2,1)S(1)}) custom-call(s32[1]{0:T(128)} %bitcast.core_ref, bf16[2,96,512]{2,1,0:T(8,128)(2,1)S(1)} %get-tuple-element.44.refs_0_, bf16[2,96,512]{2,1,0:T(8,128)(2,1)S(1)} %collective-permute-done.8.refs_1_, bf16[2,96,512]{2,1,0:T(8,128)(2,1)S(1)} %collective-permute-done.9.refs_2_, ...), custom_call_target="tpu_custom_call" | custom-call | tf_op jit(solution)/shard_map/weight_terms/pallas_call | solution.py:280
  100.0 4.0 %collective-permute-start.11 = (bf16[16,64,256]{2,1,0:T(8,128)(2,1)S(1)}, bf16[16,64,256]{2,1,0:T(8,128)(2,1)S(1)}, u32[]{:S(2)}, u32[]{:S(2)}) collective-permute-start(bf16[16,64,256]{2,1,0:T(8,128)(2,1)S(1)} %get-tuple-element.52), channel_id=1, source_target_pairs={{0,16},{16,0},{32,48},{48,32},{64,80},{80,64},{96,112},{112,96},{1... | collective-permute-start | bytes 1572872 | tf_op jit(solution)/shard_map/ppermute | solution.py:414
  104.0 1.5 %collective-permute-done.11 = bf16[16,64,256]{2,1,0:T(8,128)(2,1)S(1)} collective-permute-done((bf16[16,64,256]{2,1,0:T(8,128)(2,1)S(1)}, bf16[16,64,256]{2,1,0:T(8,128)(2,1)S(1)}, u32[]{:S(2)}, u32[]{:S(2)}) %collective-permute-start.11) | collective-permute-done | bytes 524320 | tf_op jit(solution)/shard_map/ppermute | solution.py:414
  105.6 0.9 add_convert_fusion
  106.5 4.6 %all-to-all-start.2 = ((bf16[16,64,256]{2,1,0:T(8,128)(2,1)}), bf16[16,64,256]{2,1,0:T(8,128)(2,1)S(1)}, u32[]{:S(2)}, u32[]{:S(2)}) async-start(bf16[16,64,256]{2,1,0:T(8,128)(2,1)} %add_convert_fusion), calls=%async_computation.2 | async-start | bytes 1048576 | tf_op jit(solution)/shard_map/all_to_all | solution.py:417
  111.2 0.7 collective-permute-start.12
  112.0 1.3 collective-permute-done.12.arrived_ref
  113.3 2.2 %copy-done = bf16[4,1024,512]{2,1,0:T(8,128)(2,1)S(1)} copy-done((bf16[4,1024,512]{2,1,0:T(8,128)(2,1)S(1)}, bf16[4,1024,512]{2,1,0:T(8,128)(2,1)}, u32[]{:S(2)}) %copy-start) | copy-done | bytes 4194328
  115.4 3.8 %outputs.1 = (bf16[2,96,1024]{2,1,0:T(8,128)(2,1)}, bf16[2,96,1024]{2,1,0:T(8,128)(2,1)}) custom-call(s32[2]{0:T(128)S(1)} %pad_add_fusion.1.place_ref, bf16[4,2,96,512]{3,2,1,0:T(8,128)(2,1)S(1)} %get-tuple-element.55.grads_ref, bf16[4,96,512]{2,1,0:T(8,128)(2,1)S(1)} %collective-permute-done.12.arrived_ref, bf16[4,1024,512]{2,1,0:T(8,128)(2,1)S(1)} %copy-done), custom_call_target="tpu_custom_call" | custom-call | flops 805306368 | bytes 7340032 | tf_op jit(solution)/shard_map/outputs/pallas_call | solution.py:344
  119.3 7.3 %all-to-all-done.2 = bf16[16,64,256]{2,1,0:T(8,128)(2,1)S(1)} async-done(((bf16[16,64,256]{2,1,0:T(8,128)(2,1)}), bf16[16,64,256]{2,1,0:T(8,128)(2,1)S(1)}, u32[]{:S(2)}, u32[]{:S(2)}) %all-to-all-start.2) | async-done | bytes 524320 | tf_op jit(solution)/shard_map/all_to_all | solution.py:417
  126.7 4.8 %collective-permute-start.13 = (bf16[64,256]{1,0:T(8,128)(2,1)S(1)}, bf16[64,256]{1,0:T(8,128)(2,1)S(1)}, u32[]{:S(2)}, u32[]{:S(2)}) collective-permute-start(bf16[64,256]{1,0:T(8,128)(2,1)S(1)} %reduce-precision_convert_fusion), channel_id=1, source_target_pairs={{0,32},{16,48},{32,0},{48,16},{64,96},{80,112},{96,64},{112,80},{1... | collective-permute-start | bytes 98312 | tf_op jit(solution)/shard_map/ppermute | solution.py:427
  131.4 0.9 collective-permute-start.14
  132.3 0.4 collective-permute-done.13
  132.7 0.5 collective-permute-done.14
  133.2 2.5 %collective-permute-done.15 = bf16[64,256]{1,0:T(8,128)(2,1)S(1)} collective-permute-done((bf16[64,256]{1,0:T(8,128)(2,1)S(1)}, bf16[64,256]{1,0:T(8,128)(2,1)S(1)}, u32[]{:S(2)}, u32[]{:S(2)}) %collective-permute-start.15) | collective-permute-done | bytes 32800 | tf_op jit(solution)/shard_map/ppermute | solution.py:427
  135.8 1.2 collective-permute-start.17
  137.0 1.5 %collective-permute-start.18 = (bf16[64,512]{1,0:T(8,128)(2,1)S(1)}, bf16[64,512]{1,0:T(8,128)(2,1)S(1)}, u32[]{:S(2)}, u32[]{:S(2)}) collective-permute-start(bf16[64,512]{1,0:T(8,128)(2,1)S(1)} %pad_maximum_fusion.4.refs_0_), channel_id=1, source_target_pairs={{0,192},{16,208},{32,224},{48,240},{64,0},{80,16},{96,32},{112,48}... | collective-permute-start | bytes 196616 | tf_op jit(solution)/shard_map/ppermute | solution.py:437
  138.5 3.7 %collective-permute-done.16.refs_1_ = bf16[64,512]{1,0:T(8,128)(2,1)S(1)} collective-permute-done((bf16[64,512]{1,0:T(8,128)(2,1)S(1)}, bf16[64,512]{1,0:T(8,128)(2,1)S(1)}, u32[]{:S(2)}, u32[]{:S(2)}) %collective-permute-start.16) | collective-permute-done | bytes 65568 | tf_op jit(solution)/shard_map/ppermute | solution.py:437
  142.1 0.2 collective-permute-done.18.refs_3_
  142.4 0.7 place_weights.1
  (28 shorter events, 0.8 us)
Async XLA Ops:
  1.3 8.0 %copy-start.3 = (s32[1,4]{1,0:T(1,128)S(1)}, s32[1,4]{1,0:T(1,128)}, u32[]{:S(2)}) copy-start(s32[1,4]{1,0:T(1,128)} %param.5) | copy-start | bytes 52
  6.0 14.9 %copy-start.1 = (bf16[1,1,2,96,1024]{4,3,2,1,0:T(8,128)(2,1)S(1)}, bf16[1,1,2,96,1024]{4,3,2,1,0:T(8,128)(2,1)}, u32[]{:S(2)}) copy-start(bf16[1,1,2,96,1024]{4,3,2,1,0:T(8,128)(2,1)} %param.4) | copy-start | bytes 1179652
  6.0 14.9 %copy-start.2 = (bf16[1,1,2,96,1024]{4,3,2,1,0:T(8,128)(2,1)S(1)}, bf16[1,1,2,96,1024]{4,3,2,1,0:T(8,128)(2,1)}, u32[]{:S(2)}) copy-start(bf16[1,1,2,96,1024]{4,3,2,1,0:T(8,128)(2,1)} %param.7) | copy-start | bytes 1179652
  6.0 4.9 %collective-permute-start = (bf16[8,192,128]{2,1,0:T(8,128)(2,1)}, bf16[8,192,128]{2,1,0:T(8,128)(2,1)S(1)}, u32[]{:S(2)}, u32[]{:S(2)}) collective-permute-start(bf16[8,192,128]{2,1,0:T(8,128)(2,1)} %get-tuple-element.33), channel_id=1, source_target_pairs={{0,16},{16,0},{32,48},{48,32},{64,80},{80,64},{96,112},{112,96},{1... | collective-permute-start | bytes 1179656 | tf_op jit(solution)/shard_map/ppermute | solution.py:380
  9.3 2.4 %collective-permute-start.1 = (s32[1,4]{1,0:T(1,128)S(1)}, s32[1,4]{1,0:T(1,128)S(1)}, u32[]{:S(2)}, u32[]{:S(2)}) collective-permute-start(s32[1,4]{1,0:T(1,128)S(1)} %copy-done.3), channel_id=1, source_target_pairs={{0,16},{16,0},{32,48},{48,32},{64,80},{80,64},{96,112},{112,96},{1... | collective-permute-start | bytes 56 | tf_op jit(solution)/shard_map/ppermute | solution.py:375
  11.7 30.6 %all-to-all-start = ((bf16[16,192,128]{2,1,0:T(8,128)(2,1)}), bf16[16,192,128]{2,1,0:T(8,128)(2,1)S(1)}, u32[]{:S(2)}, u32[]{:S(2)}) async-start(bf16[16,192,128]{2,1,0:T(8,128)(2,1)} %bitcast.29), calls=%async_computation | async-start | bytes 1572864 | tf_op jit(solution)/shard_map/all_to_all | solution.py:400
  21.1 2.1 %collective-permute-start.2 = (bf16[2,96,1024]{2,1,0:T(8,128)(2,1)S(1)}, bf16[2,96,1024]{2,1,0:T(8,128)(2,1)S(1)}, u32[]{:S(2)}, u32[]{:S(2)}) collective-permute-start(bf16[2,96,1024]{2,1,0:T(8,128)(2,1)S(1)} %pad_maximum_fusion.1), channel_id=1, source_target_pairs={{0,16},{16,0},{32,48},{48,32},{64,80},{80,64},{96,112},{112,96},{1... | collective-permute-start | bytes 1179656 | tf_op jit(solution)/shard_map/ppermute | solution.py:386
  23.3 10.7 %collective-permute-start.4 = (bf16[2,96,1024]{2,1,0:T(8,128)(2,1)S(1)}, bf16[2,96,1024]{2,1,0:T(8,128)(2,1)S(1)}, u32[]{:S(2)}, u32[]{:S(2)}) collective-permute-start(bf16[2,96,1024]{2,1,0:T(8,128)(2,1)S(1)} %get-tuple-element.62), channel_id=1, source_target_pairs={{0,192},{16,208},{32,224},{48,240},{64,0},{80,16},{96,32},{112,48}... | collective-permute-start | bytes 1179656 | tf_op jit(solution)/shard_map/ppermute | solution.py:398
  25.9 11.3 %collective-permute-start.3 = (bf16[2,96,1024]{2,1,0:T(8,128)(2,1)S(1)}, bf16[2,96,1024]{2,1,0:T(8,128)(2,1)S(1)}, u32[]{:S(2)}, u32[]{:S(2)}) collective-permute-start(bf16[2,96,1024]{2,1,0:T(8,128)(2,1)S(1)} %broadcast_select_fusion.3), channel_id=1, source_target_pairs={{0,64},{16,80},{32,96},{48,112},{64,128},{80,144},{96,160},{112,17... | collective-permute-start | bytes 1179656 | tf_op jit(solution)/shard_map/ppermute | solution.py:398
  42.4 3.6 %collective-permute-start.5 = (bf16[16,96,128]{2,1,0:T(8,128)(2,1)S(1)}, bf16[16,96,128]{2,1,0:T(8,128)(2,1)S(1)}, u32[]{:S(2)}, u32[]{:S(2)}) collective-permute-start(bf16[16,96,128]{2,1,0:T(8,128)(2,1)S(1)} %slice.11), channel_id=1, source_target_pairs={{0,16},{16,0},{32,48},{48,32},{64,80},{80,64},{96,112},{112,96},{1... | collective-permute-start | bytes 1179656 | tf_op jit(solution)/shard_map/ppermute | solution.py:402
  56.0 1.8 %collective-permute-start.6 = (bf16[16,96,128]{2,1,0:T(8,128)(2,1)S(1)}, bf16[16,96,128]{2,1,0:T(8,128)(2,1)S(1)}, u32[]{:S(2)}, u32[]{:S(2)}) collective-permute-start(bf16[16,96,128]{2,1,0:T(8,128)(2,1)S(1)} %get-tuple-element.39), channel_id=1, source_target_pairs={{0,16},{16,0},{32,48},{48,32},{64,80},{80,64},{96,112},{112,96},{1... | collective-permute-start | bytes 1179656 | tf_op jit(solution)/shard_map/ppermute | solution.py:405
  58.9 27.1 %all-to-all-start.1 = ((bf16[16,192,128]{2,1,0:T(8,128)(2,1)}), bf16[16,192,128]{2,1,0:T(8,128)(2,1)S(1)}, u32[]{:S(2)}, u32[]{:S(2)}) async-start(bf16[16,192,128]{2,1,0:T(8,128)(2,1)} %pad_maximum_fusion), calls=%async_computation.1 | async-start | bytes 1572864 | tf_op jit(solution)/shard_map/all_to_all | solution.py:407
  63.7 22.7 %collective-permute-start.7 = (bf16[2,96,1024]{2,1,0:T(8,128)(2,1)S(1)}, bf16[2,96,1024]{2,1,0:T(8,128)(2,1)S(1)}, u32[]{:S(2)}, u32[]{:S(2)}) collective-permute-start(bf16[2,96,1024]{2,1,0:T(8,128)(2,1)S(1)} %get-tuple-element.63), channel_id=1, source_target_pairs={{0,128},{16,144},{32,160},{48,176},{64,192},{80,208},{96,224},{112... | collective-permute-start | bytes 1179656 | tf_op jit(solution)/shard_map/ppermute | solution.py:398
  86.4 5.3 %collective-permute-start.10 = (bf16[2,96,512]{2,1,0:T(8,128)(2,1)S(1)}, bf16[2,96,512]{2,1,0:T(8,128)(2,1)S(1)}, u32[]{:S(2)}, u32[]{:S(2)}) collective-permute-start(bf16[2,96,512]{2,1,0:T(8,128)(2,1)S(1)} %get-tuple-element.47), channel_id=1, source_target_pairs={{0,192},{16,208},{32,224},{48,240},{64,0},{80,16},{96,32},{112,48}... | collective-permute-start | bytes 589832 | tf_op jit(solution)/shard_map/ppermute | solution.py:412
  87.3 6.3 %collective-permute-start.8 = (bf16[2,96,512]{2,1,0:T(8,128)(2,1)S(1)}, bf16[2,96,512]{2,1,0:T(8,128)(2,1)S(1)}, u32[]{:S(2)}, u32[]{:S(2)}) collective-permute-start(bf16[2,96,512]{2,1,0:T(8,128)(2,1)S(1)} %get-tuple-element.45), channel_id=1, source_target_pairs={{0,64},{16,80},{32,96},{48,112},{64,128},{80,144},{96,160},{112,17... | collective-permute-start | bytes 589832 | tf_op jit(solution)/shard_map/ppermute | solution.py:412
  88.0 10.1 %collective-permute-start.9 = (bf16[2,96,512]{2,1,0:T(8,128)(2,1)S(1)}, bf16[2,96,512]{2,1,0:T(8,128)(2,1)S(1)}, u32[]{:S(2)}, u32[]{:S(2)}) collective-permute-start(bf16[2,96,512]{2,1,0:T(8,128)(2,1)S(1)} %get-tuple-element.46), channel_id=1, source_target_pairs={{0,128},{16,144},{32,160},{48,176},{64,192},{80,208},{96,224},{112... | collective-permute-start | bytes 589832 | tf_op jit(solution)/shard_map/ppermute | solution.py:412
  100.0 5.5 %collective-permute-start.11 = (bf16[16,64,256]{2,1,0:T(8,128)(2,1)S(1)}, bf16[16,64,256]{2,1,0:T(8,128)(2,1)S(1)}, u32[]{:S(2)}, u32[]{:S(2)}) collective-permute-start(bf16[16,64,256]{2,1,0:T(8,128)(2,1)S(1)} %get-tuple-element.52), channel_id=1, source_target_pairs={{0,16},{16,0},{32,48},{48,32},{64,80},{80,64},{96,112},{112,96},{1... | collective-permute-start | bytes 1572872 | tf_op jit(solution)/shard_map/ppermute | solution.py:414
  106.5 20.1 %all-to-all-start.2 = ((bf16[16,64,256]{2,1,0:T(8,128)(2,1)}), bf16[16,64,256]{2,1,0:T(8,128)(2,1)S(1)}, u32[]{:S(2)}, u32[]{:S(2)}) async-start(bf16[16,64,256]{2,1,0:T(8,128)(2,1)} %add_convert_fusion), calls=%async_computation.2 | async-start | bytes 1048576 | tf_op jit(solution)/shard_map/all_to_all | solution.py:417
  111.2 2.1 %collective-permute-start.12 = (bf16[4,96,512]{2,1,0:T(8,128)(2,1)S(1)}, bf16[4,96,512]{2,1,0:T(8,128)(2,1)S(1)}, u32[]{:S(2)}, u32[]{:S(2)}) collective-permute-start(bf16[4,96,512]{2,1,0:T(8,128)(2,1)S(1)} %dynamic-slice_bitcast_fusion), channel_id=1, source_target_pairs={{0,16},{16,0},{32,48},{48,32},{64,80},{80,64},{96,112},{112,96},{1... | collective-permute-start | bytes 1179656 | tf_op jit(solution)/shard_map/ppermute | solution.py:418
  113.3 2.2 %copy-start = (bf16[4,1024,512]{2,1,0:T(8,128)(2,1)S(1)}, bf16[4,1024,512]{2,1,0:T(8,128)(2,1)}, u32[]{:S(2)}) copy-start(bf16[4,1024,512]{2,1,0:T(8,128)(2,1)} %weights_ref.3) | copy-start | bytes 12582916
  126.7 6.1 %collective-permute-start.13 = (bf16[64,256]{1,0:T(8,128)(2,1)S(1)}, bf16[64,256]{1,0:T(8,128)(2,1)S(1)}, u32[]{:S(2)}, u32[]{:S(2)}) collective-permute-start(bf16[64,256]{1,0:T(8,128)(2,1)S(1)} %reduce-precision_convert_fusion), channel_id=1, source_target_pairs={{0,32},{16,48},{32,0},{48,16},{64,96},{80,112},{96,64},{112,80},{1... | collective-permute-start | bytes 98312 | tf_op jit(solution)/shard_map/ppermute | solution.py:427
  131.4 1.8 %collective-permute-start.14 = (bf16[64,256]{1,0:T(8,128)(2,1)S(1)}, bf16[64,256]{1,0:T(8,128)(2,1)S(1)}, u32[]{:S(2)}, u32[]{:S(2)}) collective-permute-start(bf16[64,256]{1,0:T(8,128)(2,1)S(1)} %reduce-precision_convert_fusion), channel_id=1, source_target_pairs={{0,16},{16,0},{32,48},{48,32},{64,80},{80,64},{96,112},{112,96},{1... | collective-permute-start | bytes 98312 | tf_op jit(solution)/shard_map/ppermute | solution.py:427
  132.3 3.3 %collective-permute-start.15 = (bf16[64,256]{1,0:T(8,128)(2,1)S(1)}, bf16[64,256]{1,0:T(8,128)(2,1)S(1)}, u32[]{:S(2)}, u32[]{:S(2)}) collective-permute-start(bf16[64,256]{1,0:T(8,128)(2,1)S(1)} %reduce-precision_convert_fusion), channel_id=1, source_target_pairs={{0,48},{16,32},{32,16},{48,0},{64,112},{80,96},{96,80},{112,64},{1... | collective-permute-start | bytes 98312 | tf_op jit(solution)/shard_map/ppermute | solution.py:427
  135.7 6.4 %collective-permute-start.16 = (bf16[64,512]{1,0:T(8,128)(2,1)S(1)}, bf16[64,512]{1,0:T(8,128)(2,1)S(1)}, u32[]{:S(2)}, u32[]{:S(2)}) collective-permute-start(bf16[64,512]{1,0:T(8,128)(2,1)S(1)} %pad_maximum_fusion.4.refs_0_), channel_id=1, source_target_pairs={{0,64},{16,80},{32,96},{48,112},{64,128},{80,144},{96,160},{112,17... | collective-permute-start | bytes 196616 | tf_op jit(solution)/shard_map/ppermute | solution.py:437
  135.8 6.3 %collective-permute-start.17 = (bf16[64,512]{1,0:T(8,128)(2,1)S(1)}, bf16[64,512]{1,0:T(8,128)(2,1)S(1)}, u32[]{:S(2)}, u32[]{:S(2)}) collective-permute-start(bf16[64,512]{1,0:T(8,128)(2,1)S(1)} %pad_maximum_fusion.4.refs_0_), channel_id=1, source_target_pairs={{0,128},{16,144},{32,160},{48,176},{64,192},{80,208},{96,224},{112... | collective-permute-start | bytes 196616 | tf_op jit(solution)/shard_map/ppermute | solution.py:437
  137.0 5.4 %collective-permute-start.18 = (bf16[64,512]{1,0:T(8,128)(2,1)S(1)}, bf16[64,512]{1,0:T(8,128)(2,1)S(1)}, u32[]{:S(2)}, u32[]{:S(2)}) collective-permute-start(bf16[64,512]{1,0:T(8,128)(2,1)S(1)} %pad_maximum_fusion.4.refs_0_), channel_id=1, source_target_pairs={{0,192},{16,208},{32,224},{48,240},{64,0},{80,16},{96,32},{112,48}... | collective-permute-start | bytes 196616 | tf_op jit(solution)/shard_map/ppermute | solution.py:437

commit v14 on v12

--- a/solution.py
+++ b/solution.py
@@ -252,23 +252,24 @@
 
 
 def weight_kernel(core_ref, *refs):
-    grad_refs, line_refs, (keep_ref, give_ref, held_ref) = refs[:4], refs[4:8], refs[8:]
+    grad_refs, line_refs, (out_ref, held_ref) = refs[:4], refs[4:8], refs[8:]
     core = core_ref[0]
+    columns = pl.ds(pl.multiple_of(256 * core_ref[1], 256), 256)
 
     @pl.when(pl.program_id(0) == 0)
     def _():
         for shift in range(4):
             for part in range(2):
                 first = (2 * shift + part) * SPAN
-                held_ref[first : first + SPAN, :] = grad_refs[shift][jnp.bitwise_xor(core, part)]
+                held_ref[first : first + SPAN, :] = grad_refs[shift][
+                    jnp.bitwise_xor(core, part), :, columns
+                ]
 
     rows = jnp.concatenate([ref[...].reshape(2 * SPAN, D // 4) for ref in line_refs], axis=0)
     result = lax.dot_general(
         rows, held_ref[...], (((0,), (0,)), ((), ())), preferred_element_type=jnp.float32
     )
-    zero, one = result[:, :256], result[:, 256:]
-    keep_ref[...] = jnp.where(core == 0, zero, one).astype(jnp.bfloat16).reshape(4, 64, 256)
-    give_ref[...] = jnp.where(core == 0, one, zero).astype(jnp.bfloat16).reshape(4, 64, 256)
+    out_ref[...] = result.astype(jnp.bfloat16).reshape(4, 64, 256)
 
 
 def weight_terms(core, grads, lines):
@@ -278,7 +279,7 @@
     out_spec = pl.BlockSpec((4, 64, 256), lambda j, core: (j, 0, 0))
     return pl.pallas_call(
         weight_kernel,
-        out_shape=(shape, shape),
+        out_shape=shape,
         grid_spec=pltpu.PrefetchScalarGridSpec(
             num_scalar_prefetch=1,
             grid=(4,),
@@ -286,10 +287,13 @@
                 *[grad_spec] * 4,
                 *[line_spec] * 4,
             ],
-            out_specs=(out_spec, out_spec),
-            scratch_shapes=[pltpu.VMEM((8 * SPAN, HQ), jnp.bfloat16)],
+            out_specs=out_spec,
+            scratch_shapes=[pltpu.VMEM((8 * SPAN, 256), jnp.bfloat16)],
         ),
         compiler_params=pltpu.CompilerParams(vmem_limit_bytes=SMALL_VMEM),
+        cost_estimate=pl.CostEstimate(
+            flops=2_000_000_000, bytes_accessed=3 * 1024 * 1024, transcendentals=0
+        ),
         name="weight_terms",
     )(core, *grads, *lines)
 
@@ -409,7 +413,11 @@
     )
     pieces, far = lax.optimization_barrier((pieces, far))
     pieces = [pieces[0]] + [lax.ppermute(x, "dp", y) for x, y in zip(pieces[1:], X_SHIFTS)]
-    keep, give = weight_terms(core_number, pieces, (line, near, far, back_near))
+    lines = (line, near, far, back_near)
+    give, keep = (
+        weight_terms(jnp.stack([core, half]).astype(jnp.int32), pieces, lines)
+        for half in (1 - core, core)
+    )
     given = lax.ppermute(give, "dp", CORE_SWAP)
     terms = (keep.astype(jnp.float32) + given.astype(jnp.float32)).astype(jnp.bfloat16)
     terms, own_grads = lax.optimization_barrier((terms, grads))

time: 143 us -> 144 us (level)
  waiting for transfers between devices: 63.2 us -> 68.4 us
  starting transfers between devices: 50.1 us -> 45 us
  Pallas kernels: 22.2 us -> 24.2 us
    all_to_all x1, waiting for transfers between devices: 18.1 us -> 20.7 us  [per_device(): lax.all_to_all(jnp.concatenate([query_part, key_part], axis=1), 'ctx', 0, 0)]
    ppermute x3, starting transfers between devices: 5.66 us -> 3.3 us  [per_device(): lax.ppermute(x, 'dp', y)]
    pallas_call x1 -> x2, Pallas kernels: 1.94 us -> 4.28 us  [weight_terms(): pl.pallas_call(weight_kernel, out_shape=shape, grid_spec=pltpu.PrefetchSc...]
    ppermute x1, starting transfers between devices: 2.43 us -> 0.09 us  [per_device(): other_rows = lax.ppermute(rows.astype(jnp.bfloat16), 'dp', Z_SWAP)]
    all_to_all x1, waiting for transfers between devices: 7.96 us -> 10.1 us  [per_device(): terms = lax.all_to_all(terms, 'ctx', 0, 0)]
    ppermute x2, waiting for transfers between devices: 2.99 us -> 1.45 us  [per_device(): given = lax.ppermute(give, 'dp', CORE_SWAP)]
    ppermute x1, waiting for transfers between devices: 1.3 us -> 2.75 us  [per_device(): other_rows = lax.ppermute(rows.astype(jnp.bfloat16), 'dp', Z_SWAP)]
  transfers between devices with their start and end apart: 21 -> 21, of which waited for: 17 -> 16; matrix products, arithmetic and copies ran while one was open for 1% -> 1% of each run, Pallas kernels for 3% -> 4%
where the time goes in v14:
time: 144 us; the launch traced here: 145 us
  waiting for transfers between devices  68.4 us (48%)
  starting transfers between devices  45 us (31%)
  Pallas kernels  24.2 us (17%)
  local copies, waits for them, and re-layouts  3.23 us (2%)
  other arithmetic  3.15 us (2%)
    all_to_all x1, waiting for transfers between devices, per_device(): lax.all_to_all(jnp.concatenate([query_part, key_part], axis=1), 'ctx', 0, 0)  20.7 us
    ppermute x3, waiting for transfers between devices, per_device(): lax.ppermute(rows, 'dp', shift)  11.2 us
    pallas_call x1, Pallas kernels, attend(): pl.pallas_call(attend_kernel, out_shape=(jax.ShapeDtypeStruct(block, jnp....  10.2 us
    all_to_all x1, waiting for transfers between devices, per_device(): terms = lax.all_to_all(terms, 'ctx', 0, 0)  10.1 us
    all_to_all x1, starting transfers between devices, per_device(): own = lax.all_to_all(packed, 'ctx', 0, 0)  9.19 us
    ppermute x2, starting transfers between devices, per_device(): given = lax.ppermute(give, 'dp', CORE_SWAP)  8.06 us
    ppermute x3, waiting for transfers between devices, per_device(): lax.ppermute(x, 'dp', y)  6.7 us
    all_to_all x1, starting transfers between devices, per_device(): lax.all_to_all(jnp.concatenate([query_part, key_part], axis=1), 'ctx', 0, 0)  5.29 us
  transfers between devices with their start and end apart: 21, of which 16 were waited for; matrix products, arithmetic and copies ran while one was open for 1% of the time, Pallas kernels for 4%

profile of v14, /device:TPU:1, one launch (start us, length us, event | category | flops | bytes accessed | tf_op | source)
XLA Modules:
  0.0 144.8 jit_solution(18330609884342295154)
XLA Ops:
  0.7 0.6 pad_add_fusion.1.place_ref
  1.2 4.7 %project.1 = (bf16[8,2,192,128]{3,2,1,0:T(8,128)(2,1)}, bf16[8,192,128]{2,1,0:T(8,128)(2,1)}) custom-call(s32[2]{0:T(128)} %pad_add_fusion.1.place_ref, bf16[2,96,1024]{2,1,0:T(8,128)(2,1)} %bitcast.28, bf16[2,96,1024]{2,1,0:T(8,128)(2,1)} %bitcast.29, bf16[4,1024,512]{2,1,0:T(8,128)(2,1)} %weights_ref.3), custom_call_target="tpu_custom_call" | custom-call | tf_op jit(solution)/shard_map/project/pallas_call | solution.py:58
  6.0 3.3 %collective-permute-start = (bf16[8,192,128]{2,1,0:T(8,128)(2,1)}, bf16[8,192,128]{2,1,0:T(8,128)(2,1)S(1)}, u32[]{:S(2)}, u32[]{:S(2)}) collective-permute-start(bf16[8,192,128]{2,1,0:T(8,128)(2,1)} %get-tuple-element.31), channel_id=1, source_target_pairs={{0,16},{16,0},{32,48},{48,32},{64,80},{80,64},{96,112},{112,96},{1... | collective-permute-start | bytes 1179656 | tf_op jit(solution)/shard_map/ppermute | solution.py:383
  9.3 0.1 collective-permute-start.1
  9.4 1.4 %collective-permute-done = bf16[8,192,128]{2,1,0:T(8,128)(2,1)S(1)} collective-permute-done((bf16[8,192,128]{2,1,0:T(8,128)(2,1)}, bf16[8,192,128]{2,1,0:T(8,128)(2,1)S(1)}, u32[]{:S(2)}, u32[]{:S(2)}) %collective-permute-start) | collective-permute-done | bytes 393248 | tf_op jit(solution)/shard_map/ppermute | solution.py:383
  10.8 0.9 bitcast_dynamic-update-slice_fusion
  11.7 9.2 %all-to-all-start = ((bf16[16,192,128]{2,1,0:T(8,128)(2,1)}), bf16[16,192,128]{2,1,0:T(8,128)(2,1)S(1)}, u32[]{:S(2)}, u32[]{:S(2)}) async-start(bf16[16,192,128]{2,1,0:T(8,128)(2,1)} %bitcast.30), calls=%async_computation | async-start | bytes 1572864 | tf_op jit(solution)/shard_map/all_to_all | solution.py:403
  21.1 0.7 collective-permute-start.2
  21.7 1.3 collective-permute-done.2
  23.1 0.1 broadcast_select_fusion
  23.2 2.6 %collective-permute-start.4 = (bf16[2,96,1024]{2,1,0:T(8,128)(2,1)S(1)}, bf16[2,96,1024]{2,1,0:T(8,128)(2,1)S(1)}, u32[]{:S(2)}, u32[]{:S(2)}) collective-permute-start(bf16[2,96,1024]{2,1,0:T(8,128)(2,1)S(1)} %get-tuple-element.58), channel_id=1, source_target_pairs={{0,192},{16,208},{32,224},{48,240},{64,0},{80,16},{96,32},{112,48}... | collective-permute-start | bytes 1179656 | tf_op jit(solution)/shard_map/ppermute | solution.py:401
  25.8 0.1 collective-permute-start.3
  25.9 8.0 %collective-permute-done.4.refs_7_ = bf16[2,96,1024]{2,1,0:T(8,128)(2,1)S(1)} collective-permute-done((bf16[2,96,1024]{2,1,0:T(8,128)(2,1)S(1)}, bf16[2,96,1024]{2,1,0:T(8,128)(2,1)S(1)}, u32[]{:S(2)}, u32[]{:S(2)}) %collective-permute-start.4) | collective-permute-done | bytes 393248 | tf_op jit(solution)/shard_map/ppermute | solution.py:401
  33.9 3.2 %collective-permute-done.3.refs_5_ = bf16[2,96,1024]{2,1,0:T(8,128)(2,1)S(1)} collective-permute-done((bf16[2,96,1024]{2,1,0:T(8,128)(2,1)S(1)}, bf16[2,96,1024]{2,1,0:T(8,128)(2,1)S(1)}, u32[]{:S(2)}, u32[]{:S(2)}) %collective-permute-start.3) | collective-permute-done | bytes 393248 | tf_op jit(solution)/shard_map/ppermute | solution.py:401
  37.1 5.2 %all-to-all-done.own_ref = bf16[16,192,128]{2,1,0:T(8,128)(2,1)S(1)} async-done(((bf16[16,192,128]{2,1,0:T(8,128)(2,1)}), bf16[16,192,128]{2,1,0:T(8,128)(2,1)S(1)}, u32[]{:S(2)}, u32[]{:S(2)}) %all-to-all-start) | async-done | bytes 786464 | tf_op jit(solution)/shard_map/all_to_all | solution.py:403
  42.4 2.2 %collective-permute-start.5 = (bf16[16,96,128]{2,1,0:T(8,128)(2,1)S(1)}, bf16[16,96,128]{2,1,0:T(8,128)(2,1)S(1)}, u32[]{:S(2)}, u32[]{:S(2)}) collective-permute-start(bf16[16,96,128]{2,1,0:T(8,128)(2,1)S(1)} %slice.11), channel_id=1, source_target_pairs={{0,16},{16,0},{32,48},{48,32},{64,80},{80,64},{96,112},{112,96},{1... | collective-permute-start | bytes 1179656 | tf_op jit(solution)/shard_map/ppermute | solution.py:405
  44.6 1.3 collective-permute-done.5.other_ref
  45.9 10.2 %attend.1 = (bf16[16,96,128]{2,1,0:T(8,128)(2,1)S(1)}, f32[16,96,128]{2,1,0:T(8,128)S(1)}, bf16[16,96,128]{2,1,0:T(8,128)(2,1)S(1)}) custom-call(s32[1]{0:T(128)} %bitcast.core_ref, s32[4]{0:T(128)S(1)} %fusion.tiles_ref, bf16[16,192,128]{2,1,0:T(8,128)(2,1)S(1)} %all-to-all-done.own_ref, bf16[16,96,128]{2,1,0:T(8,128)(2,1)S(1)} %collective-permute-done.5.other_ref), custom_call_target="tpu_custom_call" | custom-call | flops 12000000000 | bytes 4194304 | tf_op jit(solution)/shard_map/attend/pallas_call | solution.py:197
  56.2 0.1 collective-permute-start.6
  56.3 1.7 %collective-permute-done.6 = bf16[16,96,128]{2,1,0:T(8,128)(2,1)S(1)} collective-permute-done((bf16[16,96,128]{2,1,0:T(8,128)(2,1)S(1)}, bf16[16,96,128]{2,1,0:T(8,128)(2,1)S(1)}, u32[]{:S(2)}, u32[]{:S(2)}) %collective-permute-start.6) | collective-permute-done | bytes 393248 | tf_op jit(solution)/shard_map/ppermute | solution.py:408
  58.1 1.0 pad_maximum_fusion
  59.1 5.3 %all-to-all-start.1 = ((bf16[16,192,128]{2,1,0:T(8,128)(2,1)}), bf16[16,192,128]{2,1,0:T(8,128)(2,1)S(1)}, u32[]{:S(2)}, u32[]{:S(2)}) async-start(bf16[16,192,128]{2,1,0:T(8,128)(2,1)} %pad_maximum_fusion), calls=%async_computation.1 | async-start | bytes 1572864 | tf_op jit(solution)/shard_map/all_to_all | solution.py:410
  64.4 2.3 %collective-permute-start.7 = (bf16[2,96,1024]{2,1,0:T(8,128)(2,1)S(1)}, bf16[2,96,1024]{2,1,0:T(8,128)(2,1)S(1)}, u32[]{:S(2)}, u32[]{:S(2)}) collective-permute-start(bf16[2,96,1024]{2,1,0:T(8,128)(2,1)S(1)} %get-tuple-element.59), channel_id=1, source_target_pairs={{0,128},{16,144},{32,160},{48,176},{64,192},{80,208},{96,224},{112... | collective-permute-start | bytes 1179656 | tf_op jit(solution)/shard_map/ppermute | solution.py:401
  66.7 20.7 %all-to-all-done.1 = bf16[16,192,128]{2,1,0:T(8,128)(2,1)S(1)} async-done(((bf16[16,192,128]{2,1,0:T(8,128)(2,1)}), bf16[16,192,128]{2,1,0:T(8,128)(2,1)S(1)}, u32[]{:S(2)}, u32[]{:S(2)}) %all-to-all-start.1) | async-done | bytes 786464 | tf_op jit(solution)/shard_map/all_to_all | solution.py:410
  87.4 0.4 repack.1
  87.8 1.8 %collective-permute-start.10 = (bf16[2,96,512]{2,1,0:T(8,128)(2,1)S(1)}, bf16[2,96,512]{2,1,0:T(8,128)(2,1)S(1)}, u32[]{:S(2)}, u32[]{:S(2)}) collective-permute-start(bf16[2,96,512]{2,1,0:T(8,128)(2,1)S(1)} %get-tuple-element.45), channel_id=1, source_target_pairs={{0,192},{16,208},{32,224},{48,240},{64,0},{80,16},{96,32},{112,48}... | collective-permute-start | bytes 589832 | tf_op jit(solution)/shard_map/ppermute | solution.py:415
  89.6 1.5 %collective-permute-start.9 = (bf16[2,96,512]{2,1,0:T(8,128)(2,1)S(1)}, bf16[2,96,512]{2,1,0:T(8,128)(2,1)S(1)}, u32[]{:S(2)}, u32[]{:S(2)}) collective-permute-start(bf16[2,96,512]{2,1,0:T(8,128)(2,1)S(1)} %get-tuple-element.44), channel_id=1, source_target_pairs={{0,128},{16,144},{32,160},{48,176},{64,192},{80,208},{96,224},{112... | collective-permute-start | bytes 589832 | tf_op jit(solution)/shard_map/ppermute | solution.py:415
  91.2 1.2 collective-permute-done.10.refs_3_
  92.4 5.3 %collective-permute-done.8.refs_1_ = bf16[2,96,512]{2,1,0:T(8,128)(2,1)S(1)} collective-permute-done((bf16[2,96,512]{2,1,0:T(8,128)(2,1)S(1)}, bf16[2,96,512]{2,1,0:T(8,128)(2,1)S(1)}, u32[]{:S(2)}, u32[]{:S(2)}) %collective-permute-start.8) | collective-permute-done | bytes 196640 | tf_op jit(solution)/shard_map/ppermute | solution.py:415
  97.8 0.1 collective-permute-done.9.refs_2_
  97.9 2.1 %weight_terms.3 = bf16[16,64,256]{2,1,0:T(8,128)(2,1)S(1)} custom-call(s32[2]{0:T(128)S(1)} %pad_add_fusion.2.core_ref, bf16[2,96,512]{2,1,0:T(8,128)(2,1)S(1)} %get-tuple-element.42.refs_0_, bf16[2,96,512]{2,1,0:T(8,128)(2,1)S(1)} %collective-permute-done.8.refs_1_, bf16[2,96,512]{2,1,0:T(8,128)(2,1)S(1)} %collective-permute-done.9.refs_2_, ...), custom_call_target="tpu_custom_call" | custom-call | flops 2000000000 | bytes 3145728 | tf_op jit(solution)/shard_map/weight_terms/pallas_call | solution.py:280
  100.1 4.7 %collective-permute-start.11 = (bf16[16,64,256]{2,1,0:T(8,128)(2,1)S(1)}, bf16[16,64,256]{2,1,0:T(8,128)(2,1)S(1)}, u32[]{:S(2)}, u32[]{:S(2)}) collective-permute-start(bf16[16,64,256]{2,1,0:T(8,128)(2,1)S(1)} %weight_terms.3), channel_id=1, source_target_pairs={{0,16},{16,0},{32,48},{48,32},{64,80},{80,64},{96,112},{112,96},{1... | collective-permute-start | bytes 1572872 | tf_op jit(solution)/shard_map/ppermute | solution.py:421
  104.9 2.1 %weight_terms.2 = bf16[16,64,256]{2,1,0:T(8,128)(2,1)S(1)} custom-call(s32[2]{0:T(128)S(1)} %pad_add_fusion.core_ref, bf16[2,96,512]{2,1,0:T(8,128)(2,1)S(1)} %get-tuple-element.42.refs_0_, bf16[2,96,512]{2,1,0:T(8,128)(2,1)S(1)} %collective-permute-done.8.refs_1_, bf16[2,96,512]{2,1,0:T(8,128)(2,1)S(1)} %collective-permute-done.9.refs_2_, ...), custom_call_target="tpu_custom_call" | custom-call | flops 2000000000 | bytes 3145728 | tf_op jit(solution)/shard_map/weight_terms/pallas_call | solution.py:280
  107.0 1.0 add_convert_fusion
  108.0 4.7 %all-to-all-start.2 = ((bf16[16,64,256]{2,1,0:T(8,128)(2,1)}), bf16[16,64,256]{2,1,0:T(8,128)(2,1)S(1)}, u32[]{:S(2)}, u32[]{:S(2)}) async-start(bf16[16,64,256]{2,1,0:T(8,128)(2,1)} %add_convert_fusion), calls=%async_computation.2 | async-start | bytes 1048576 | tf_op jit(solution)/shard_map/all_to_all | solution.py:424
  112.8 0.4 collective-permute-start.12
  113.2 1.4 collective-permute-done.12.arrived_ref
  114.6 2.2 %copy-done = bf16[4,1024,512]{2,1,0:T(8,128)(2,1)S(1)} copy-done((bf16[4,1024,512]{2,1,0:T(8,128)(2,1)S(1)}, bf16[4,1024,512]{2,1,0:T(8,128)(2,1)}, u32[]{:S(2)}) %copy-start) | copy-done | bytes 4194328
  116.8 3.8 %outputs.1 = (bf16[2,96,1024]{2,1,0:T(8,128)(2,1)}, bf16[2,96,1024]{2,1,0:T(8,128)(2,1)}) custom-call(s32[2]{0:T(128)S(1)} %pad_add_fusion.3.place_ref, bf16[4,2,96,512]{3,2,1,0:T(8,128)(2,1)S(1)} %get-tuple-element.51.grads_ref, bf16[4,96,512]{2,1,0:T(8,128)(2,1)S(1)} %collective-permute-done.12.arrived_ref, bf16[4,1024,512]{2,1,0:T(8,128)(2,1)S(1)} %copy-done), custom_call_target="tpu_custom_call" | custom-call | flops 805306368 | bytes 7340032 | tf_op jit(solution)/shard_map/outputs/pallas_call | solution.py:347
  120.6 10.1 %all-to-all-done.2 = bf16[16,64,256]{2,1,0:T(8,128)(2,1)S(1)} async-done(((bf16[16,64,256]{2,1,0:T(8,128)(2,1)}), bf16[16,64,256]{2,1,0:T(8,128)(2,1)S(1)}, u32[]{:S(2)}, u32[]{:S(2)}) %all-to-all-start.2) | async-done | bytes 524320 | tf_op jit(solution)/shard_map/all_to_all | solution.py:424
  130.8 0.1 collective-permute-start.13
  130.9 2.8 %collective-permute-done.13 = bf16[64,256]{1,0:T(8,128)(2,1)S(1)} collective-permute-done((bf16[64,256]{1,0:T(8,128)(2,1)S(1)}, bf16[64,256]{1,0:T(8,128)(2,1)S(1)}, u32[]{:S(2)}, u32[]{:S(2)}) %collective-permute-start.13) | collective-permute-done | bytes 32800 | tf_op jit(solution)/shard_map/ppermute | solution.py:432
  133.6 3.2 %collective-permute-start.14 = (bf16[64,256]{1,0:T(8,128)(2,1)S(1)}, bf16[64,256]{1,0:T(8,128)(2,1)S(1)}, u32[]{:S(2)}, u32[]{:S(2)}) collective-permute-start(bf16[64,256]{1,0:T(8,128)(2,1)S(1)} %multiply_convert_fusion), channel_id=1, source_target_pairs={{0,16},{16,0},{32,48},{48,32},{64,80},{80,64},{96,112},{112,96},{1... | collective-permute-start | bytes 98312 | tf_op jit(solution)/shard_map/ppermute | solution.py:435
  136.8 0.9 collective-permute-done.14
  137.8 0.4 collective-permute-start.16
  138.2 2.2 %collective-permute-start.17 = (bf16[64,512]{1,0:T(8,128)(2,1)S(1)}, bf16[64,512]{1,0:T(8,128)(2,1)S(1)}, u32[]{:S(2)}, u32[]{:S(2)}) collective-permute-start(bf16[64,512]{1,0:T(8,128)(2,1)S(1)} %pad_maximum_fusion.4.refs_0_), channel_id=1, source_target_pairs={{0,192},{16,208},{32,224},{48,240},{64,0},{80,16},{96,32},{112,48}... | collective-permute-start | bytes 196616 | tf_op jit(solution)/shard_map/ppermute | solution.py:440
  140.5 3.6 %collective-permute-done.15.refs_1_ = bf16[64,512]{1,0:T(8,128)(2,1)S(1)} collective-permute-done((bf16[64,512]{1,0:T(8,128)(2,1)S(1)}, bf16[64,512]{1,0:T(8,128)(2,1)S(1)}, u32[]{:S(2)}, u32[]{:S(2)}) %collective-permute-start.15) | collective-permute-done | bytes 65568 | tf_op jit(solution)/shard_map/ppermute | solution.py:440
  144.0 0.7 place_weights.1
  (30 shorter events, 0.8 us)
Async XLA Ops:
  1.2 8.0 %copy-start.3 = (s32[1,4]{1,0:T(1,128)S(1)}, s32[1,4]{1,0:T(1,128)}, u32[]{:S(2)}) copy-start(s32[1,4]{1,0:T(1,128)} %param.5) | copy-start | bytes 52
  6.0 15.0 %copy-start.1 = (bf16[1,1,2,96,1024]{4,3,2,1,0:T(8,128)(2,1)S(1)}, bf16[1,1,2,96,1024]{4,3,2,1,0:T(8,128)(2,1)}, u32[]{:S(2)}) copy-start(bf16[1,1,2,96,1024]{4,3,2,1,0:T(8,128)(2,1)} %param.4) | copy-start | bytes 1179652
  6.0 15.0 %copy-start.2 = (bf16[1,1,2,96,1024]{4,3,2,1,0:T(8,128)(2,1)S(1)}, bf16[1,1,2,96,1024]{4,3,2,1,0:T(8,128)(2,1)}, u32[]{:S(2)}) copy-start(bf16[1,1,2,96,1024]{4,3,2,1,0:T(8,128)(2,1)} %param.7) | copy-start | bytes 1179652
  6.0 4.9 %collective-permute-start = (bf16[8,192,128]{2,1,0:T(8,128)(2,1)}, bf16[8,192,128]{2,1,0:T(8,128)(2,1)S(1)}, u32[]{:S(2)}, u32[]{:S(2)}) collective-permute-start(bf16[8,192,128]{2,1,0:T(8,128)(2,1)} %get-tuple-element.31), channel_id=1, source_target_pairs={{0,16},{16,0},{32,48},{48,32},{64,80},{80,64},{96,112},{112,96},{1... | collective-permute-start | bytes 1179656 | tf_op jit(solution)/shard_map/ppermute | solution.py:383
  9.3 2.4 %collective-permute-start.1 = (s32[1,4]{1,0:T(1,128)S(1)}, s32[1,4]{1,0:T(1,128)S(1)}, u32[]{:S(2)}, u32[]{:S(2)}) collective-permute-start(s32[1,4]{1,0:T(1,128)S(1)} %copy-done.3), channel_id=1, source_target_pairs={{0,16},{16,0},{32,48},{48,32},{64,80},{80,64},{96,112},{112,96},{1... | collective-permute-start | bytes 56 | tf_op jit(solution)/shard_map/ppermute | solution.py:378
  11.7 30.7 %all-to-all-start = ((bf16[16,192,128]{2,1,0:T(8,128)(2,1)}), bf16[16,192,128]{2,1,0:T(8,128)(2,1)S(1)}, u32[]{:S(2)}, u32[]{:S(2)}) async-start(bf16[16,192,128]{2,1,0:T(8,128)(2,1)} %bitcast.30), calls=%async_computation | async-start | bytes 1572864 | tf_op jit(solution)/shard_map/all_to_all | solution.py:403
  21.1 2.0 %collective-permute-start.2 = (bf16[2,96,1024]{2,1,0:T(8,128)(2,1)S(1)}, bf16[2,96,1024]{2,1,0:T(8,128)(2,1)S(1)}, u32[]{:S(2)}, u32[]{:S(2)}) collective-permute-start(bf16[2,96,1024]{2,1,0:T(8,128)(2,1)S(1)} %pad_maximum_fusion.1), channel_id=1, source_target_pairs={{0,16},{16,0},{32,48},{48,32},{64,80},{80,64},{96,112},{112,96},{1... | collective-permute-start | bytes 1179656 | tf_op jit(solution)/shard_map/ppermute | solution.py:389
  23.2 10.7 %collective-permute-start.4 = (bf16[2,96,1024]{2,1,0:T(8,128)(2,1)S(1)}, bf16[2,96,1024]{2,1,0:T(8,128)(2,1)S(1)}, u32[]{:S(2)}, u32[]{:S(2)}) collective-permute-start(bf16[2,96,1024]{2,1,0:T(8,128)(2,1)S(1)} %get-tuple-element.58), channel_id=1, source_target_pairs={{0,192},{16,208},{32,224},{48,240},{64,0},{80,16},{96,32},{112,48}... | collective-permute-start | bytes 1179656 | tf_op jit(solution)/shard_map/ppermute | solution.py:401
  25.8 11.3 %collective-permute-start.3 = (bf16[2,96,1024]{2,1,0:T(8,128)(2,1)S(1)}, bf16[2,96,1024]{2,1,0:T(8,128)(2,1)S(1)}, u32[]{:S(2)}, u32[]{:S(2)}) collective-permute-start(bf16[2,96,1024]{2,1,0:T(8,128)(2,1)S(1)} %broadcast_select_fusion.3), channel_id=1, source_target_pairs={{0,64},{16,80},{32,96},{48,112},{64,128},{80,144},{96,160},{112,17... | collective-permute-start | bytes 1179656 | tf_op jit(solution)/shard_map/ppermute | solution.py:401
  42.4 3.5 %collective-permute-start.5 = (bf16[16,96,128]{2,1,0:T(8,128)(2,1)S(1)}, bf16[16,96,128]{2,1,0:T(8,128)(2,1)S(1)}, u32[]{:S(2)}, u32[]{:S(2)}) collective-permute-start(bf16[16,96,128]{2,1,0:T(8,128)(2,1)S(1)} %slice.11), channel_id=1, source_target_pairs={{0,16},{16,0},{32,48},{48,32},{64,80},{80,64},{96,112},{112,96},{1... | collective-permute-start | bytes 1179656 | tf_op jit(solution)/shard_map/ppermute | solution.py:405
  56.2 1.8 %collective-permute-start.6 = (bf16[16,96,128]{2,1,0:T(8,128)(2,1)S(1)}, bf16[16,96,128]{2,1,0:T(8,128)(2,1)S(1)}, u32[]{:S(2)}, u32[]{:S(2)}) collective-permute-start(bf16[16,96,128]{2,1,0:T(8,128)(2,1)S(1)} %get-tuple-element.37), channel_id=1, source_target_pairs={{0,16},{16,0},{32,48},{48,32},{64,80},{80,64},{96,112},{112,96},{1... | collective-permute-start | bytes 1179656 | tf_op jit(solution)/shard_map/ppermute | solution.py:408
  59.1 28.4 %all-to-all-start.1 = ((bf16[16,192,128]{2,1,0:T(8,128)(2,1)}), bf16[16,192,128]{2,1,0:T(8,128)(2,1)S(1)}, u32[]{:S(2)}, u32[]{:S(2)}) async-start(bf16[16,192,128]{2,1,0:T(8,128)(2,1)} %pad_maximum_fusion), calls=%async_computation.1 | async-start | bytes 1572864 | tf_op jit(solution)/shard_map/all_to_all | solution.py:410
  64.4 23.5 %collective-permute-start.7 = (bf16[2,96,1024]{2,1,0:T(8,128)(2,1)S(1)}, bf16[2,96,1024]{2,1,0:T(8,128)(2,1)S(1)}, u32[]{:S(2)}, u32[]{:S(2)}) collective-permute-start(bf16[2,96,1024]{2,1,0:T(8,128)(2,1)S(1)} %get-tuple-element.59), channel_id=1, source_target_pairs={{0,128},{16,144},{32,160},{48,176},{64,192},{80,208},{96,224},{112... | collective-permute-start | bytes 1179656 | tf_op jit(solution)/shard_map/ppermute | solution.py:401
  87.8 4.6 %collective-permute-start.10 = (bf16[2,96,512]{2,1,0:T(8,128)(2,1)S(1)}, bf16[2,96,512]{2,1,0:T(8,128)(2,1)S(1)}, u32[]{:S(2)}, u32[]{:S(2)}) collective-permute-start(bf16[2,96,512]{2,1,0:T(8,128)(2,1)S(1)} %get-tuple-element.45), channel_id=1, source_target_pairs={{0,192},{16,208},{32,224},{48,240},{64,0},{80,16},{96,32},{112,48}... | collective-permute-start | bytes 589832 | tf_op jit(solution)/shard_map/ppermute | solution.py:415
  89.6 8.2 %collective-permute-start.8 = (bf16[2,96,512]{2,1,0:T(8,128)(2,1)S(1)}, bf16[2,96,512]{2,1,0:T(8,128)(2,1)S(1)}, u32[]{:S(2)}, u32[]{:S(2)}) collective-permute-start(bf16[2,96,512]{2,1,0:T(8,128)(2,1)S(1)} %get-tuple-element.43), channel_id=1, source_target_pairs={{0,64},{16,80},{32,96},{48,112},{64,128},{80,144},{96,160},{112,17... | collective-permute-start | bytes 589832 | tf_op jit(solution)/shard_map/ppermute | solution.py:415
  89.6 8.3 %collective-permute-start.9 = (bf16[2,96,512]{2,1,0:T(8,128)(2,1)S(1)}, bf16[2,96,512]{2,1,0:T(8,128)(2,1)S(1)}, u32[]{:S(2)}, u32[]{:S(2)}) collective-permute-start(bf16[2,96,512]{2,1,0:T(8,128)(2,1)S(1)} %get-tuple-element.44), channel_id=1, source_target_pairs={{0,128},{16,144},{32,160},{48,176},{64,192},{80,208},{96,224},{112... | collective-permute-start | bytes 589832 | tf_op jit(solution)/shard_map/ppermute | solution.py:415
  100.1 7.0 %collective-permute-start.11 = (bf16[16,64,256]{2,1,0:T(8,128)(2,1)S(1)}, bf16[16,64,256]{2,1,0:T(8,128)(2,1)S(1)}, u32[]{:S(2)}, u32[]{:S(2)}) collective-permute-start(bf16[16,64,256]{2,1,0:T(8,128)(2,1)S(1)} %weight_terms.3), channel_id=1, source_target_pairs={{0,16},{16,0},{32,48},{48,32},{64,80},{80,64},{96,112},{112,96},{1... | collective-permute-start | bytes 1572872 | tf_op jit(solution)/shard_map/ppermute | solution.py:421
  108.0 22.7 %all-to-all-start.2 = ((bf16[16,64,256]{2,1,0:T(8,128)(2,1)}), bf16[16,64,256]{2,1,0:T(8,128)(2,1)S(1)}, u32[]{:S(2)}, u32[]{:S(2)}) async-start(bf16[16,64,256]{2,1,0:T(8,128)(2,1)} %add_convert_fusion), calls=%async_computation.2 | async-start | bytes 1048576 | tf_op jit(solution)/shard_map/all_to_all | solution.py:424
  112.8 1.8 %collective-permute-start.12 = (bf16[4,96,512]{2,1,0:T(8,128)(2,1)S(1)}, bf16[4,96,512]{2,1,0:T(8,128)(2,1)S(1)}, u32[]{:S(2)}, u32[]{:S(2)}) collective-permute-start(bf16[4,96,512]{2,1,0:T(8,128)(2,1)S(1)} %dynamic-slice_bitcast_fusion), channel_id=1, source_target_pairs={{0,16},{16,0},{32,48},{48,32},{64,80},{80,64},{96,112},{112,96},{1... | collective-permute-start | bytes 1179656 | tf_op jit(solution)/shard_map/ppermute | solution.py:425
  114.6 2.2 %copy-start = (bf16[4,1024,512]{2,1,0:T(8,128)(2,1)S(1)}, bf16[4,1024,512]{2,1,0:T(8,128)(2,1)}, u32[]{:S(2)}) copy-start(bf16[4,1024,512]{2,1,0:T(8,128)(2,1)} %weights_ref.3) | copy-start | bytes 12582916
  130.8 2.9 %collective-permute-start.13 = (bf16[64,256]{1,0:T(8,128)(2,1)S(1)}, bf16[64,256]{1,0:T(8,128)(2,1)S(1)}, u32[]{:S(2)}, u32[]{:S(2)}) collective-permute-start(bf16[64,256]{1,0:T(8,128)(2,1)S(1)} %reduce-precision_convert_fusion), channel_id=1, source_target_pairs={{0,32},{16,48},{32,0},{48,16},{64,96},{80,112},{96,64},{112,80},{1... | collective-permute-start | bytes 98312 | tf_op jit(solution)/shard_map/ppermute | solution.py:432
  133.6 4.0 %collective-permute-start.14 = (bf16[64,256]{1,0:T(8,128)(2,1)S(1)}, bf16[64,256]{1,0:T(8,128)(2,1)S(1)}, u32[]{:S(2)}, u32[]{:S(2)}) collective-permute-start(bf16[64,256]{1,0:T(8,128)(2,1)S(1)} %multiply_convert_fusion), channel_id=1, source_target_pairs={{0,16},{16,0},{32,48},{48,32},{64,80},{80,64},{96,112},{112,96},{1... | collective-permute-start | bytes 98312 | tf_op jit(solution)/shard_map/ppermute | solution.py:435
  137.7 6.3 %collective-permute-start.15 = (bf16[64,512]{1,0:T(8,128)(2,1)S(1)}, bf16[64,512]{1,0:T(8,128)(2,1)S(1)}, u32[]{:S(2)}, u32[]{:S(2)}) collective-permute-start(bf16[64,512]{1,0:T(8,128)(2,1)S(1)} %pad_maximum_fusion.4.refs_0_), channel_id=1, source_target_pairs={{0,64},{16,80},{32,96},{48,112},{64,128},{80,144},{96,160},{112,17... | collective-permute-start | bytes 196616 | tf_op jit(solution)/shard_map/ppermute | solution.py:440
  137.8 6.3 %collective-permute-start.16 = (bf16[64,512]{1,0:T(8,128)(2,1)S(1)}, bf16[64,512]{1,0:T(8,128)(2,1)S(1)}, u32[]{:S(2)}, u32[]{:S(2)}) collective-permute-start(bf16[64,512]{1,0:T(8,128)(2,1)S(1)} %pad_maximum_fusion.4.refs_0_), channel_id=1, source_target_pairs={{0,128},{16,144},{32,160},{48,176},{64,192},{80,208},{96,224},{112... | collective-permute-start | bytes 196616 | tf_op jit(solution)/shard_map/ppermute | solution.py:440
  138.2 5.8 %collective-permute-start.17 = (bf16[64,512]{1,0:T(8,128)(2,1)S(1)}, bf16[64,512]{1,0:T(8,128)(2,1)S(1)}, u32[]{:S(2)}, u32[]{:S(2)}) collective-permute-start(bf16[64,512]{1,0:T(8,128)(2,1)S(1)} %pad_maximum_fusion.4.refs_0_), channel_id=1, source_target_pairs={{0,192},{16,208},{32,224},{48,240},{64,0},{80,16},{96,32},{112,48}... | collective-permute-start | bytes 196616 | tf_op jit(solution)/shard_map/ppermute | solution.py:440
